TPU v7x, 32 devices: a whole 2x2x4 slice. The times are simulated.
32 devices in a mesh: blk: 16 (over z, y, x), mp: 2 (over core).
Axes of the slice: x: 2, y: 2, z: 4, core: 2. Of those that a mesh axis runs over, the one named last changes fastest.
Arguments:
- hidden: bfloat16 [144, 3584], replicated, may hold values from -6 to 6
- medusa_w: bfloat16 [2, 3584, 3584], P(None, 'blk', 'mp'), may hold values from -0.09375 to 0.09375
- embedding: bfloat16 [131072, 3584], P(('blk', 'mp')), may hold values from -0.5 to 0.5
- cand_ids: int32 [2, 144, 10], replicated, may hold values from 0 to 131071
- tree_q: bfloat16 [12, 48, 4096], P(None, None, 'mp'), may hold values from -6 to 6
- tree_key_value: bfloat16 [2, 12, 48, 2048], P(None, None, None, 'mp'), may hold values from -6 to 6
- prompt_key_value: bfloat16 [2, 16, 2048, 2048], P(None, 'blk', None, 'mp'), may hold values from -6 to 6
- block_group: int32 [16], P('blk'), may hold values from 0 to 11, as said below
- block_len: int32 [16], P('blk'), may hold values from 1 to 2048
- block_empty: int32 [16], P('blk'), may hold values 0 or 1
- parents: int32 [12, 48], replicated, may hold values from 0 to 46, as said below
- out_weight: bfloat16 [4096, 3584], P('mp'), may hold values from -0.09375 to 0.09375
- post_gain: float32 [3584], replicated, may hold values from 0.5 to 1.5
- resid: bfloat16 [576, 3584], P('blk'), may hold values from -6 to 6
Outputs:
- draft_logprob: float32 [2, 144, 10], replicated
- layer_out: bfloat16 [576, 3584], P('blk')
Inputs may be any that keep to these rules, and one draw needn't show every extreme that they name: `block_group`: every group number from 0 to min(12, 16) - 1 owns at least one block. `parents`: entry 0 of each row is 0; entry i for i >= 1 is below i; some group's last token has parent 48 - 2.
All inputs are finite; a program needn't handle non-finite values. No bound on the sum of `block_empty` on one device may be relied on, other than what follows from the above.
Results may differ from a plain program's by a relative error of at most 0.005.
Values may be sent and summed in bfloat16 or wider, within the bound.
No kernel may reach another device: no remote copies, remote signals or barrier semaphores. Data moves between devices by JAX's collectives and lax.ppermute only.
A program may use at most 192 MiB of HBM per device.

v0:
```python
import jax
import jax.numpy as jnp
from jax import lax
from jax.sharding import PartitionSpec as P

HEAD_SIZE = 256


def capped(values, limit):
    return limit * jnp.tanh(values / limit)


def ancestry(parents):
    count = parents.shape[1]
    column = jnp.arange(count, dtype=jnp.int32)
    linked = (parents[:, :, None] == column[None, None, :]) & (column[None, :, None] > 0)
    reach = jnp.eye(count, dtype=jnp.float32)[None] + linked.astype(jnp.float32)
    for sweep in range(count.bit_length()):
        reach = jnp.minimum(
            jnp.einsum("gij,gjk->gik", reach, reach, precision=lax.Precision.HIGHEST), 1.0
        )
    return reach


def attend(queries, keys, values, mask):
    rows = queries.shape[0]
    length = keys.shape[0]
    kv_heads = keys.shape[1] // HEAD_SIZE
    repeats = queries.shape[1] // keys.shape[1]
    query_view = queries.reshape(rows, kv_heads, repeats, HEAD_SIZE)
    key_view = keys.reshape(length, kv_heads, HEAD_SIZE)
    value_view = values.reshape(length, kv_heads, HEAD_SIZE)
    scores = jnp.einsum(
        "qhrd,khd->hrqk", query_view, key_view, preferred_element_type=jnp.float32
    ) * HEAD_SIZE ** (-0.5)
    weights = jnp.exp(capped(scores, 50.0)) * mask[None, None]
    denominator = jnp.sum(weights, -1).transpose(2, 0, 1).reshape(rows, kv_heads * repeats)
    numerator = jnp.einsum(
        "hrqk,khd->qhrd",
        weights.astype(jnp.bfloat16),
        value_view,
        preferred_element_type=jnp.float32,
    )
    return (numerator.reshape(rows, kv_heads * repeats * HEAD_SIZE), denominator)


def per_device(
    hidden,
    medusa_w,
    embedding,
    cand_ids,
    tree_q,
    tree_key_value,
    prompt_key_value,
    block_group,
    block_len,
    block_empty,
    parents,
    out_weight,
    post_gain,
    resid,
):
    units = medusa_w.shape[2]
    inner = jnp.einsum(
        "rd,mdu->mru",
        hidden,
        lax.all_gather(medusa_w, "blk", axis=1, tiled=True),
        preferred_element_type=jnp.float32,
    )
    own_cols = lax.dynamic_slice_in_dim(hidden, lax.axis_index("mp") * units, units, 1).astype(
        jnp.float32
    )
    fresh = (own_cols[None] + jax.nn.silu(inner)).astype(jnp.bfloat16)
    full_fresh = lax.all_gather(fresh, "mp", axis=2, tiled=True)
    logits = capped(
        jnp.einsum("mrd,vd->mrv", full_fresh, embedding, preferred_element_type=jnp.float32), 30.0
    )
    totals = jnp.sum(jnp.exp(logits), -1)
    vocab_dev = embedding.shape[0]
    first_id = lax.axis_index(("blk", "mp")) * vocab_dev
    local_ids = cand_ids - first_id
    match = local_ids[..., None] == jnp.arange(vocab_dev, dtype=jnp.int32)
    picked = jnp.sum(jnp.where(match, logits[:, :, None, :], 0.0), -1)
    totals, picked = lax.psum((totals, picked), ("blk", "mp"))
    draft_logprob = picked - jnp.log(totals)[..., None]
    groups, tree_size, features = tree_q.shape
    keys = prompt_key_value[0, 0]
    values = prompt_key_value[1, 0]
    length = keys.shape[0]
    group = block_group[0]
    key_ok = ((jnp.arange(length, dtype=jnp.int32) < block_len[0]) & (block_empty[0] == 0)).astype(
        jnp.float32
    )
    row_group = jnp.arange(groups * tree_size, dtype=jnp.int32) // tree_size
    mask = (row_group == group).astype(jnp.float32)[:, None] * key_ok[None, :]
    numer, denom = attend(tree_q.reshape(groups * tree_size, features), keys, values, mask)
    rows_dev = groups * tree_size // lax.axis_size("blk")
    first_row = lax.axis_index("blk") * rows_dev
    summed = lax.psum((numer, denom), "blk")
    numer = lax.dynamic_slice_in_dim(summed[0], first_row, rows_dev, 0)
    denom = lax.dynamic_slice_in_dim(summed[1], first_row, rows_dev, 0)
    reach = ancestry(parents)
    tree_numer, tree_denom = jax.vmap(attend)(tree_q, tree_key_value[0], tree_key_value[1], reach)
    heads_dev = tree_denom.shape[2]
    tree_numer = lax.dynamic_slice_in_dim(
        tree_numer.reshape(groups * tree_size, features), first_row, rows_dev, 0
    )
    tree_denom = lax.dynamic_slice_in_dim(
        tree_denom.reshape(groups * tree_size, heads_dev), first_row, rows_dev, 0
    )
    numer = numer + tree_numer
    denom = denom + tree_denom
    heads_out = (
        (numer.reshape(rows_dev, heads_dev, HEAD_SIZE) / denom[..., None])
        .reshape(rows_dev, features)
        .astype(jnp.bfloat16)
    )
    attn = lax.psum(jnp.dot(heads_out, out_weight, preferred_element_type=jnp.float32), "mp")
    normed = attn * lax.rsqrt(jnp.mean(attn * attn, -1, keepdims=True) + 1e-06) * post_gain
    layer_out = (normed + resid.astype(jnp.float32)).astype(jnp.bfloat16)
    return (draft_logprob, layer_out)


def solution(mesh):
    placed = (
        P(),
        P(None, "blk", "mp"),
        P(("blk", "mp"), None),
        P(),
        P(None, None, "mp"),
        P(None, None, None, "mp"),
        P(None, "blk", None, "mp"),
        P("blk"),
        P("blk"),
        P("blk"),
        P(),
        P("mp", None),
        P(),
        P("blk", None),
    )
    return jax.shard_map(
        per_device, mesh=mesh, in_specs=placed, out_specs=(P(), P("blk", None)), check_vma=False
    )
```

profile of v0, /device:TPU:0, one launch (start us, length us, event | category | flops | bytes accessed | tf_op | source)
XLA Modules:
  0.0 656.2 jit_solution(11298114023290017570)
XLA Ops:
  7.2 0.0 all-reduce.4.cloned.1.call-start
  7.2 5.9 fusion.47
  13.1 6.6 %copy.79 = bf16[1,1,2048,1024]{2,3,1,0:T(8,128)(2,1)} copy(bf16[1,1,2048,1024]{3,2,1,0:T(8,128)(2,1)} %get-tuple-element.7) | data formatting | bytes 8388608
  21.7 2.9 reshape_reshape.3
  24.7 6.5 copy.80
  31.2 2.5 broadcast_multiply_fusion
  33.7 21.1 %fusion.2 = (f32[4,2,576]{2,1,0:T(2,128)S(1)}, f32[4,2048,576,2]{1,2,3,0:T(8,128)}) fusion(f32[576,2048]{1,0:T(8,128)} %broadcast_multiply_fusion, bf16[2048,4,256,1]{0,2,3,1:T(8,128)(2,1)} %bitcast.80, bf16[576,4,2,256]{3,2,1,0:T(2,128)(2,1)} %reshape_reshape.3), kind=kOutput, calls=%fused_computation.5 | convolution fusion | flops 4869582336 | bytes 49039360 | tf_op jit(solution)/shard_map/qhrd,khd->hrqk/dot_general | solution.py:33
  54.8 20.7 %fusion.19 = f32[576,4,2,256]{3,0,2,1:T(8,128)} fusion(bf16[2048,4,256,1]{0,2,3,1:T(8,128)(2,1)} %bitcast.81, f32[4,2048,576,2]{1,2,3,0:T(8,128)} %get-tuple-element.15, f32[576,2048]{1,0:T(8,128)} %broadcast_multiply_fusion), kind=kOutput, calls=%fused_computation.19 | convolution fusion | flops 4869586944 | bytes 51380224 | tf_op jit(solution)/shard_map/hrqk,khd->qhrd/dot_general | solution.py:38
  75.5 8.1 %copy.56 = f32[576,4,2,256]{3,2,1,0:T(2,128)} copy(f32[576,4,2,256]{3,0,2,1:T(8,128)} %fusion.19) | data formatting | bytes 9437184 | tf_op jit(solution)/shard_map/hrqk,khd->qhrd/transpose | solution.py:38
  83.5 7.2 %reshape.101 = f32[576,2048]{1,0:T(8,128)} reshape(f32[576,4,2,256]{3,2,1,0:T(2,128)} %copy.56) | data formatting | bytes 9437184 | tf_op jit(solution)/shard_map/reshape | solution.py:44
  90.8 0.0 all-gather.3.cloned.1.call-start
  90.8 0.7 all-gather.3.cloned.1.call-update
  91.6 3.0 reshape.102
  94.6 0.6 reshape.104
  95.2 1.9 fusion.48
  97.1 0.9 reshape_squeeze.14
  98.1 0.6 convolution_minimum_fusion.5
  98.7 0.4 convolution_minimum_fusion.4
  99.1 0.4 convolution_minimum_fusion.3
  99.5 0.4 convolution_minimum_fusion.2
  100.0 0.4 convolution_minimum_fusion.1
  100.4 0.4 convolution_minimum_fusion
  100.8 0.1 copy.59
  101.0 4.3 fusion.49
  105.3 0.1 reshape.105
  105.4 81.1 %psum.38 = f32[576,8]{0,1:T(8,128)S(1)} all-reduce(f32[576,8]{0,1:T(8,128)S(1)} %copy-done.3), channel_id=1, replica_groups=mesh['blk'=16,'mp'=2] {'blk'}, use_global_device_ids=true, to_apply=%region_6.7 | all-reduce | flops 4608 | bytes 36864 | tf_op jit(solution)/shard_map/psum | solution.py:99
  186.5 0.1 dynamic-slice_add_fusion
  186.5 0.1 copy.64
  186.6 0.1 div.51
  186.8 0.1 copy.81
  186.9 0.9 reshape_squeeze.15
  187.8 2.1 convolution_bitcast_fusion.1
  189.9 5.8 copy.62
  195.7 7.3 %reshape.103 = f32[576,2048]{1,0:T(8,128)} reshape(f32[12,48,4,2,256]{4,3,2,1,0:T(2,128)} %copy.62) | data formatting | bytes 9437184 | tf_op jit(solution)/shard_map/reshape;vmap()/reshape | solution.py:106
  203.0 0.1 dynamic-slice_convert_fusion
  203.1 71.0 %all-reduce.4.cloned.1.call-done = f32[576,2048]{1,0:T(8,128)} async-done(((f32[576,2048]{1,0:T(8,128)}), f32[576,2048]{1,0:T(8,128)}) %all-reduce.4.cloned.1.call-update) | async-done | bytes 4718608 | tf_op jit(solution)/shard_map/psum | solution.py:99
  274.1 8.8 %fusion.32 = f32[36,3584]{1,0:T(8,128)} fusion(bf16[2048,3584]{1,0:T(8,128)(2,1)} %param.25, f32[36,2048]{1,0:T(8,128)S(1)} %bitcast.82, f32[576,2048]{1,0:T(8,128)} %reshape.103, s32[]{:T(128)S(6)} %select_n.25, f32[576,2048]{1,0:T(8,128)} %all-reduce.4.cloned.1.call-done), kind=kOutput, calls=%fused_computation.40 | convolution fusion | flops 528703488 | bytes 16146436 | tf_op jit(solution)/shard_map/dot_general | solution.py:118
  283.0 0.3 all-gather.5.cloned.1.call-start
  283.3 269.2 %all-gather.3.cloned.1.call-done = bf16[2,3584,1792]{2,1,0:T(8,128)(2,1)} async-done(((bf16[2,224,1792]{2,1,0:T(8,128)(2,1)}), bf16[2,3584,1792]{2,1,0:T(8,128)(2,1)}) %all-gather.3.cloned.1.call-update) | async-done | bytes 25690128 | tf_op jit(solution)/shard_map/all_gather | solution.py:67
  552.5 13.6 %add_convert_fusion = bf16[2,144,1792]{2,1,0:T(8,128)(2,1)} fusion(bf16[2,3584,1792]{2,1,0:T(8,128)(2,1)} %all-gather.3.cloned.1.call-done, bf16[144,3584]{1,0:T(8,128)(2,1)S(1)} %copy-done.2, f32[144,1792]{1,0:T(8,128)S(1)} %dynamic-slice_convert_fusion), kind=kOutput, calls=%fused_computation.21 | convolution fusion | flops 3702472704 | bytes 28786688 | tf_op jit(solution)/shard_map/rd,mdu->mru/dot_general | solution.py:64
  566.1 5.9 all-reduce.6.cloned.1.call-done
  572.0 1.2 multiply_reduce_fusion
  573.2 1.9 add_convert_fusion.1
  575.2 10.0 %all-gather.5.cloned.1.call-done = bf16[2,144,3584]{2,1,0:T(8,128)(2,1)} async-done(((bf16[2,144,1792]{2,1,0:T(8,128)(2,1)}), bf16[2,144,3584]{2,1,0:T(8,128)(2,1)}) %all-gather.5.cloned.1.call-update) | async-done | bytes 2064400 | tf_op jit(solution)/shard_map/all_gather | solution.py:74
  585.1 14.5 %exponential_reduce_fusion = (f32[2,144]{1,0:T(2,128)S(1)}, f32[2,144,4096]{2,1,0:T(8,128)S(1)}) fusion(bf16[2,144,3584]{2,1,0:T(8,128)(2,1)} %all-gather.5.cloned.1.call-done, bf16[4096,3584]{1,0:T(8,128)(2,1)} %param.16), kind=kOutput, calls=%fused_computation.11 | convolution fusion | flops 8459255296 | bytes 36144256 | tf_op jit(solution)/shard_map/mrd,vd->mrv/dot_general | solution.py:76
  599.7 8.0 %select_reduce_fusion = f32[2,144,10]{1,2,0:T(8,128)S(1)} fusion(f32[2,144,4096]{2,1,0:T(8,128)S(1)} %get-tuple-element.11, s32[2,144,10]{1,2,0:T(8,128)S(1)} %copy.50), kind=kLoop, calls=%fused_computation | loop fusion | flops 35386560 | bytes 4741632 | tf_op jit(solution)/shard_map/reduce_sum | solution.py:83
  607.7 40.9 %all-reduce = (f32[2,144,10]{1,2,0:T(8,128)S(1)}, f32[2,144]{1,0:T(2,128)S(1)}) all-reduce(f32[2,144,10]{1,2,0:T(8,128)S(1)} %select_reduce_fusion, f32[2,144]{1,0:T(2,128)S(1)} %get-tuple-element.10), channel_id=1, replica_groups=mesh['blk'=16,'mp'=2] {'blk','mp'}, use_global_device_ids=true, to_apply=%region_1.2 | all-reduce | flops 3168 | bytes 25344 | tf_op jit(solution)/shard_map/psum | solution.py:84
  648.6 0.6 copy.65
  (29 shorter events, 0.2 us)
Async XLA Ops:
  7.2 266.9 %all-reduce.4.cloned.1.call-start = ((), (), s32[]{:S(2)}) async-start(), calls=%async_computation.2 | async-start | bytes 9437184 | tf_op jit(solution)/shard_map/psum | solution.py:99
  13.1 8.6 %copy-start = (bf16[12,48,2048]{2,1,0:T(8,128)(2,1)S(1)}, bf16[12,48,2048]{2,1,0:T(8,128)(2,1)}, u32[]{:S(2)}) copy-start(bf16[12,48,2048]{2,1,0:T(8,128)(2,1)} %param.18) | copy-start | bytes 7077892
  90.8 461.7 %all-gather.3.cloned.1.call-start = ((), (), s32[]{:S(2)}) async-start(), calls=%async_computation | async-start | bytes 27295744 | tf_op jit(solution)/shard_map/all_gather | solution.py:67
  91.5 480.4 %all-reduce.6.cloned.1.call-start = ((), (), s32[]{:S(2)}) async-start(), calls=%async_computation.3 | async-start | bytes 1146880 | tf_op jit(solution)/shard_map/psum | solution.py:118
  94.6 3.5 copy-start.6
  100.8 4.6 copy-start.3
  195.7 7.3 %copy-start.2 = (bf16[144,3584]{1,0:T(8,128)(2,1)S(1)}, bf16[144,3584]{1,0:T(8,128)(2,1)}, u32[]{:S(2)}) copy-start(bf16[144,3584]{1,0:T(8,128)(2,1)} %param.14) | copy-start | bytes 3096580
  282.9 283.1 %copy-start.4 = (s32[2,144,10]{1,0,2:T(2,128)S(1)}, s32[2,144,10]{1,0,2:T(2,128)}, u32[]{:S(2)}) copy-start(s32[2,144,10]{1,0,2:T(2,128)} %param.17) | copy-start | bytes 34564
  283.0 290.2 %copy-start.1 = (bf16[36,3584]{1,0:T(8,128)(2,1)S(1)}, bf16[36,3584]{1,0:T(8,128)(2,1)}, u32[]{:S(2)}) copy-start(bf16[36,3584]{1,0:T(8,128)(2,1)} %param.27) | copy-start | bytes 774148
  283.0 290.2 %copy-start.5 = (f32[3584]{0:T(1024)S(1)}, f32[3584]{0:T(1024)}, u32[]{:S(2)}) copy-start(f32[3584]{0:T(1024)} %param.26) | copy-start | bytes 43012
  283.0 302.2 %all-gather.5.cloned.1.call-start = ((), (), s32[]{:S(2)}) async-start(), calls=%async_computation.1 | async-start | bytes 3096576 | tf_op jit(solution)/shard_map/all_gather | solution.py:74
Sparse Core Ops, SparseCore 0:
  90.9 183.1 all-reduce.3
  277.2 275.2 all-gather.2
  554.9 16.9 all-reduce.5
  573.4 11.7 all-gather.4
where the time goes:
time: 666 us; the launch traced here: 656 us
  waiting for transfers between devices  357 us (54%)
  blocking collectives  122 us (18%)
  matrix products  87.8 us (13%)
  local copies, waits for them, and re-layouts  58.9 us (9%)
  between operations  16.5 us (2%)
  other arithmetic  13.8 us (2%)
    all_gather x1, waiting for transfers between devices, per_device(): lax.all_gather(medusa_w, 'blk', axis=1, tiled=True)  269 us
    psum x1, blocking collectives, per_device(): summed = lax.psum((numer, denom), 'blk')  81.1 us
    psum x1, waiting for transfers between devices, per_device(): summed = lax.psum((numer, denom), 'blk')  71 us
    psum x1, blocking collectives, per_device(): totals, picked = lax.psum((totals, picked), ('blk', 'mp'))  40.9 us
    dot_general x2, matrix products, attend(): jnp.einsum('qhrd,khd->hrqk', query_view, key_view, preferred_element_type...  25.4 us
    dot_general x2, matrix products, attend(): jnp.einsum('hrqk,khd->qhrd', weights.astype(jnp.bfloat16), value_view, pr...  22.8 us
    dot_general x1, matrix products, per_device(): jnp.einsum('mrd,vd->mrv', full_fresh, embedding, preferred_element_type=j...  14.5 us
    unnamed x19, local copies, waits for them, and re-layouts  13.9 us
  transfers between devices with their start and end apart: 4, of which 4 were waited for; matrix products, arithmetic and copies ran while one was open for 9% of the time, Pallas kernels for 0%

commit v1 on v0

v1 whole, which is shorter than its diff:
```python
import functools

import jax
import jax.numpy as jnp
from jax import lax
from jax.experimental import pallas as pl
from jax.experimental.pallas import tpu as pltpu
from jax.sharding import PartitionSpec as P

HEAD_SIZE = 256
LANES = 128
MIB = 1 << 20

EXTRA = 16
HIGH, LOW, GROUP = 0, 4, 8


def swap_sum(value, axis, size):
    if size & (size - 1):
        return lax.psum(value, axis)
    step = 1
    while step < size:
        value = value + lax.ppermute(value, axis, [(i, i ^ step) for i in range(size)])
        step *= 2
    return value


def soft_weights(scores):
    return jnp.exp(50.0 * jnp.tanh(scores * (HEAD_SIZE**-0.5 / 50.0)))


def dot_t(left, right):
    return lax.dot_general(left, right, (((1,), (1,)), ((), ())), preferred_element_type=jnp.float32)


def prompt_kernel(tree_size, repeats, width, meta, q_ref, k_ref, v_ref, out_ref):
    group, used, empty = meta[0], meta[1], meta[2]
    limit = jnp.where(empty == 0, used, 0)
    queries = jnp.concatenate(
        [q_ref[0, :, r * HEAD_SIZE : (r + 1) * HEAD_SIZE] for r in range(repeats)], axis=0
    )
    rows = tree_size * repeats
    slots = k_ref.shape[2]
    scores = dot_t(queries, k_ref[0, 0])
    slot = lax.broadcasted_iota(jnp.int32, (rows, slots), 1)
    weights = jnp.where(slot < limit, soft_weights(scores), 0.0)
    denom = jnp.sum(weights, axis=1, keepdims=True)
    numer = jnp.dot(weights.astype(jnp.bfloat16), v_ref[0, 0], preferred_element_type=jnp.float32)
    per_head = HEAD_SIZE // width
    row_id = lax.broadcasted_iota(jnp.int32, (tree_size, width), 0)
    lane_id = lax.broadcasted_iota(jnp.int32, (tree_size, width), 1)
    extra_id = lax.broadcasted_iota(jnp.int32, (EXTRA, width), 0)
    for r in range(repeats):
        mine = jnp.broadcast_to(denom[r * tree_size : (r + 1) * tree_size], (tree_size, width))
        extra = jnp.where(extra_id == GROUP, group.astype(jnp.float32), 0.0)
        for c in range(-(-tree_size // width)):
            line = jnp.sum(
                jnp.where(row_id == lane_id + c * width, mine, 0.0), axis=0, keepdims=True
            )
            high = line.astype(jnp.bfloat16).astype(jnp.float32)
            extra = jnp.where(extra_id == HIGH + c, high, extra)
            extra = jnp.where(extra_id == LOW + c, line - high, extra)
        for part in range(per_head):
            out_ref[r * per_head + part, :tree_size, :] = numer[
                r * tree_size : (r + 1) * tree_size, part * width : (part + 1) * width
            ].astype(jnp.bfloat16)
            out_ref[r * per_head + part, tree_size:, :] = extra.astype(jnp.bfloat16)


def prompt_part(tree_q, prompt_key_value, meta, width, blocks):
    groups, tree_size, features = tree_q.shape
    slots, key_features = prompt_key_value.shape[2:]
    kv_heads = key_features // HEAD_SIZE
    repeats = features // key_features
    per_step = repeats * HEAD_SIZE // width
    return pl.pallas_call(
        functools.partial(prompt_kernel, tree_size, repeats, width),
        out_shape=jax.ShapeDtypeStruct((blocks, tree_size + EXTRA, width), jnp.bfloat16),
        grid_spec=pltpu.PrefetchScalarGridSpec(
            num_scalar_prefetch=1,
            grid=(kv_heads,),
            in_specs=[
                pl.BlockSpec((1, tree_size, repeats * HEAD_SIZE), lambda h, meta: (meta[0], 0, h)),
                pl.BlockSpec((1, 1, slots, HEAD_SIZE), lambda h, meta: (0, 0, 0, h)),
                pl.BlockSpec((1, 1, slots, HEAD_SIZE), lambda h, meta: (1, 0, 0, h)),
            ],
            out_specs=pl.BlockSpec((per_step, tree_size + EXTRA, width), lambda h, meta: (h, 0, 0)),
        ),
        compiler_params=pltpu.CompilerParams(vmem_limit_bytes=24 * MIB),
        cost_estimate=pl.CostEstimate(
            flops=4 * tree_size * features * slots,
            bytes_accessed=4 * slots * key_features,
            transcendentals=2 * tree_size * slots * features // HEAD_SIZE,
        ),
        name="prompt_part",
    )(meta, tree_q, prompt_key_value, prompt_key_value)


def tree_kernel(q_ref, k_ref, v_ref, reach_ref, numer_ref, denom_ref):
    for g in range(q_ref.shape[0]):
        weights = soft_weights(dot_t(q_ref[g], k_ref[g])) * reach_ref[g]
        denom_ref[g] = jnp.broadcast_to(
            jnp.sum(weights, axis=1, keepdims=True), denom_ref.shape[1:]
        )
        numer_ref[g] = jnp.dot(
            weights.astype(jnp.bfloat16), v_ref[g], preferred_element_type=jnp.float32
        )


def tree_part(queries, keys, values, reach):
    shape = values.shape
    return pl.pallas_call(
        tree_kernel,
        out_shape=[jax.ShapeDtypeStruct(shape, jnp.float32)] * 2,
        compiler_params=pltpu.CompilerParams(vmem_limit_bytes=24 * MIB),
        name="tree_part",
    )(queries, keys, values, reach)


def merge_kernel(got_ref, numer_ref, denom_ref, out_ref, hold):
    blocks = got_ref.shape[0]
    groups, tree_size, width = numer_ref.shape
    row_id = lax.broadcasted_iota(jnp.int32, (tree_size, width), 0)
    lane_id = lax.broadcasted_iota(jnp.int32, (tree_size, width), 1)
    lines = -(-tree_size // width)

    @pl.loop(0, groups)
    def _(g):
        def add(b, carry):
            numer, extra = carry
            more = got_ref[b, tree_size:, :].astype(jnp.float32)
            same = more[GROUP : GROUP + 1, :] == g.astype(jnp.float32)
            numer = numer + jnp.where(same, got_ref[b, :tree_size, :].astype(jnp.float32), 0.0)
            extra = extra + jnp.where(same, more, 0.0)
            return numer, extra

        start = (numer_ref[g], jnp.zeros((EXTRA, width), jnp.float32))
        numer, extra = lax.fori_loop(0, blocks, add, start, unroll=True)
        denom = denom_ref[g]
        for c in range(lines):
            line = extra[HIGH + c : HIGH + c + 1, :] + extra[LOW + c : LOW + c + 1, :]
            spread = jnp.where(row_id == lane_id + c * width, line, 0.0)
            denom = denom + jnp.sum(spread, axis=1, keepdims=True)
        hold[pl.ds(pl.multiple_of(g * tree_size, 8), tree_size), :] = numer / denom

    count = out_ref.shape[1]
    for d in range(out_ref.shape[0]):
        out_ref[d] = hold[d * count : (d + 1) * count, :].astype(jnp.bfloat16)


def merge_part(got, numer, denom):
    blocks, _, width = got.shape
    groups, tree_size, _ = numer.shape
    tokens = groups * tree_size
    return pl.pallas_call(
        merge_kernel,
        out_shape=jax.ShapeDtypeStruct((blocks, tokens // blocks, width), jnp.bfloat16),
        scratch_shapes=[pltpu.VMEM((tokens, width), jnp.float32)],
        compiler_params=pltpu.CompilerParams(vmem_limit_bytes=24 * MIB),
        name="merge_part",
    )(got, numer, denom)


def score_kernel(picks, ids_ref, fresh_ref, embed_ref, out_ref, total, picked):
    step = pl.program_id(0)

    @pl.when(step == 0)
    def _():
        total[...] = jnp.zeros_like(total)
        picked[...] = jnp.zeros_like(picked)

    tile = embed_ref.shape[0]
    logits = 30.0 * jnp.tanh(dot_t(fresh_ref[...], embed_ref[...]) * (1.0 / 30.0))
    local = ids_ref[...] - step * tile
    lane = local & (LANES - 1)
    chunk = local >> 7
    sums, found = total[...], picked[...]
    for c in range(tile // LANES):
        part = logits[:, c * LANES : (c + 1) * LANES]
        sums = sums + jnp.exp(part)
        there = jnp.take_along_axis(part, lane, axis=1, mode="promise_in_bounds")
        found = found + jnp.where(chunk == c, there, 0.0)
    total[...] = sums
    picked[...] = found

    @pl.when(step == pl.num_programs(0) - 1)
    def _():
        place = lax.broadcasted_iota(jnp.int32, sums.shape, 1)
        whole = jnp.sum(sums, axis=1, keepdims=True)
        out_ref[...] = jnp.where(place < picks, found, jnp.where(place == picks, whole, 0.0))


def score_part(fresh, embedding, ids, picks):
    rows, depth = fresh.shape
    vocab = embedding.shape[0]
    tile = min(512, vocab)
    return pl.pallas_call(
        functools.partial(score_kernel, picks),
        out_shape=jax.ShapeDtypeStruct((rows, LANES), jnp.float32),
        grid=(vocab // tile,),
        in_specs=[
            pl.BlockSpec((rows, LANES), lambda i: (0, 0)),
            pl.BlockSpec((rows, depth), lambda i: (0, 0)),
            pl.BlockSpec((tile, depth), lambda i: (i, 0)),
        ],
        out_specs=pl.BlockSpec((rows, LANES), lambda i: (0, 0)),
        scratch_shapes=[pltpu.VMEM((rows, LANES), jnp.float32)] * 2,
        compiler_params=pltpu.CompilerParams(vmem_limit_bytes=32 * MIB),
        cost_estimate=pl.CostEstimate(
            flops=2 * rows * depth * vocab,
            bytes_accessed=2 * vocab * depth,
            transcendentals=2 * rows * vocab,
        ),
        name="score_part",
    )(ids, fresh, embedding)


def ancestry(parents):
    count = parents.shape[1]
    column = jnp.arange(count, dtype=jnp.int32)
    linked = (parents[:, :, None] == column[None, None, :]) & (column[None, :, None] > 0)
    reach = jnp.eye(count, dtype=jnp.bfloat16)[None] + linked.astype(jnp.bfloat16)
    for sweep in range(count.bit_length()):
        met = jnp.einsum("gij,gjk->gik", reach, reach, preferred_element_type=jnp.float32)
        reach = jnp.minimum(met, 1.0).astype(jnp.bfloat16)
    return reach.astype(jnp.float32)


def per_device(
    hidden,
    medusa_w,
    embedding,
    cand_ids,
    tree_q,
    tree_key_value,
    prompt_key_value,
    block_group,
    block_len,
    block_empty,
    parents,
    out_weight,
    post_gain,
    resid,
):
    blocks, splits = lax.axis_size("blk"), lax.axis_size("mp")
    blk, mp = lax.axis_index("blk"), lax.axis_index("mp")
    drafts, depth, units = medusa_w.shape
    rows, model = hidden.shape
    lines = drafts * rows
    own = lines // blocks

    hidden_cols = lax.dynamic_slice_in_dim(hidden, blk * depth, depth, 1)
    partial = jnp.einsum("rd,mdu->mru", hidden_cols, medusa_w, preferred_element_type=jnp.float32)
    partial = partial.reshape(blocks, own, units).astype(jnp.bfloat16)
    inner = lax.psum_scatter(partial, "blk", scatter_dimension=0).astype(jnp.float32)
    base = lax.dynamic_slice(hidden, ((blk * own) % rows, mp * units), (own, units))
    fresh = (base.astype(jnp.float32) + jax.nn.silu(inner)).astype(jnp.bfloat16)
    fresh = lax.all_gather(fresh, "blk", axis=0, tiled=True)
    fresh = lax.all_gather(fresh, "mp", axis=1, tiled=True)

    groups, tree_size, features = tree_q.shape
    width = features // blocks
    meta = jnp.concatenate([block_group, block_len, block_empty])
    sent = prompt_part(tree_q, prompt_key_value, meta, width, blocks)
    got = lax.all_to_all(sent, "blk", 0, 0, tiled=True)

    repeats = features // tree_key_value.shape[3]
    column = blk * width
    head = column // HEAD_SIZE
    kv_head = head // repeats
    queries = lax.dynamic_slice_in_dim(tree_q, head * HEAD_SIZE, HEAD_SIZE, 2)
    keys = lax.dynamic_slice_in_dim(tree_key_value[0], kv_head * HEAD_SIZE, HEAD_SIZE, 2)
    values = lax.dynamic_slice_in_dim(
        tree_key_value[1], kv_head * HEAD_SIZE + column % HEAD_SIZE, width, 2
    )
    tree_numer, tree_denom = tree_part(queries, keys, values, ancestry(parents))
    heads_out = merge_part(got, tree_numer, tree_denom)
    heads_out = lax.all_to_all(heads_out, "blk", 0, 0, tiled=True)
    tokens = heads_out.shape[1]
    heads_out = heads_out.transpose(1, 0, 2).reshape(tokens, features)
    attn = swap_sum(jnp.dot(heads_out, out_weight, preferred_element_type=jnp.float32), "mp", splits)
    normed = attn * lax.rsqrt(jnp.mean(attn * attn, -1, keepdims=True) + 1e-06) * post_gain
    layer_out = (normed + resid.astype(jnp.float32)).astype(jnp.bfloat16)

    vocab = embedding.shape[0]
    picks = cand_ids.shape[2]
    ids = cand_ids.reshape(lines, picks) - (blk * splits + mp) * vocab
    ids = jnp.pad(ids, ((0, 0), (0, LANES - picks)), constant_values=-1)
    score = score_part(fresh, embedding, ids, picks)
    payload = score[:, : picks + 1].T.reshape(-1)
    payload = jnp.pad(payload, (0, -payload.shape[0] % 1024)).reshape(-1, LANES)
    spread = jnp.broadcast_to(payload[None], (blocks * splits,) + payload.shape)
    score = jnp.sum(lax.all_to_all(spread, ("blk", "mp"), 0, 0, tiled=True), 0)
    score = score.reshape(-1)[: (picks + 1) * lines].reshape(picks + 1, lines)
    draft_logprob = (score[:picks] - jnp.log(score[picks:])).T.reshape(drafts, rows, picks)
    return (draft_logprob, layer_out)


def solution(mesh):
    placed = (
        P(),
        P(None, "blk", "mp"),
        P(("blk", "mp"), None),
        P(),
        P(None, None, "mp"),
        P(None, None, None, "mp"),
        P(None, "blk", None, "mp"),
        P("blk"),
        P("blk"),
        P("blk"),
        P(),
        P("mp", None),
        P(),
        P("blk", None),
    )
    return jax.shard_map(
        per_device, mesh=mesh, in_specs=placed, out_specs=(P(), P("blk", None)), check_vma=False
    )
```

time: 666 us -> 260 us (0.39); the launches traced: 656 us -> 260 us
  waiting for transfers between devices: 357 us -> 121 us
  matrix products: 87.8 us -> 10.7 us
  blocking collectives: 122 us -> 58.1 us
  local copies, waits for them, and re-layouts: 58.9 us -> 16.4 us
  Pallas kernels: 0 us -> 23.7 us
  other arithmetic: 13.8 us -> 2.25 us
  starting transfers between devices: 0.41 us -> 11 us
    all_gather x2 -> x1, waiting for transfers between devices: 279 us -> 0.01 us  [per_device(): fresh = lax.all_gather(fresh, 'mp', axis=1, tiled=True)]
    psum x2 -> x0, blocking collectives: 122 us -> none  [the longest x1 81.1 us: per_device(): summed = lax.psum((numer, denom), 'blk')]
    reduce_scatter x0 -> x1, waiting for transfers between devices: none -> 105 us  [per_device(): lax.psum_scatter(partial, 'blk', scatter_dimension=0).astype(jnp.float32)]
    psum x2 -> x0, waiting for transfers between devices: 76.9 us -> none  [the longest x1 71 us: per_device(): summed = lax.psum((numer, denom), 'blk')]
    dot_general x12 -> x4, matrix products: 79 us -> 2.91 us  [the longest x3 1.55 us: ancestry(): jnp.einsum('gij,gjk->gik', reach, reach, preferred_element_type=jnp.float32)]
    all_gather x0 -> x1, blocking collectives: none -> 47.6 us  [per_device(): fresh = lax.all_gather(fresh, 'blk', axis=0, tiled=True)]
    pallas_call x0 -> x4, Pallas kernels: none -> 23.7 us  [the longest x1 16.4 us: score_part(): pl.pallas_call(functools.partial(score_kernel, picks), out_shape=jax.Shap...]
    reshape x5 -> x2, local copies, waits for them, and re-layouts: 18.2 us -> 0.79 us  [the longest x1 0.69 us: per_device(): (score[:picks] - jnp.log(score[picks:])).T.reshape(drafts, rows, picks)]
  transfers between devices with their start and end apart: 4 -> 5, of which waited for: 4 -> 3; matrix products, arithmetic and copies ran while one was open for 9% -> 7% of each run, Pallas kernels for 0% -> 3%
where the time goes in v1:
time: 260 us
  waiting for transfers between devices  121 us (47%)
  blocking collectives  58.1 us (22%)
  Pallas kernels  23.7 us (9%)
  local copies, waits for them, and re-layouts  16.4 us (6%)
  between operations  16.4 us (6%)
  starting transfers between devices  11 us (4%)
  matrix products  10.7 us (4%)
    reduce_scatter x1, waiting for transfers between devices, per_device(): lax.psum_scatter(partial, 'blk', scatter_dimension=0).astype(jnp.float32)  105 us
    all_gather x1, blocking collectives, per_device(): fresh = lax.all_gather(fresh, 'blk', axis=0, tiled=True)  47.6 us
    pallas_call x1, Pallas kernels, score_part(): pl.pallas_call(functools.partial(score_kernel, picks), out_shape=jax.Shap...  16.4 us
    all_to_all x1, waiting for transfers between devices, per_device(): score = jnp.sum(lax.all_to_all(spread, ('blk', 'mp'), 0, 0, tiled=True), 0)  14.6 us
    all_to_all x1, blocking collectives, per_device(): heads_out = lax.all_to_all(heads_out, 'blk', 0, 0, tiled=True)  10.5 us
    all_to_all x1, starting transfers between devices, per_device(): got = lax.all_to_all(sent, 'blk', 0, 0, tiled=True)  8.31 us
    dot_general x1, matrix products, per_device(): jnp.dot(heads_out, out_weight, preferred_element_type=jnp.float32)  7.74 us
    unnamed x21, local copies, waits for them, and re-layouts  7.58 us
  transfers between devices with their start and end apart: 5, of which 3 were waited for; matrix products, arithmetic and copies ran while one was open for 7% of the time, Pallas kernels for 3%

profile of v1, /device:TPU:0, one launch (start us, length us, event | category | flops | bytes accessed | tf_op | source)
XLA Modules:
  0.0 259.7 jit_solution(10491885501681797500)
XLA Ops:
  7.2 0.0 copy-start
  7.2 0.0 reduce-scatter.2.cloned.1.call-start
  7.2 1.4 copy-done
  8.6 1.4 fusion
  10.0 0.0 copy-start.3
  10.0 1.3 convert_element_type.63
  11.3 0.0 reduce-scatter.2.cloned.1.call-update
  13.2 0.1 pad_add_fusion.meta
  13.3 0.0 copy-done.3
  13.3 3.4 %copy-done.2 = bf16[2,1,2048,1024]{3,2,1,0:T(8,128)(2,1)S(1)} copy-done((bf16[2,1,2048,1024]{3,2,1,0:T(8,128)(2,1)S(1)}, bf16[2,1,2048,1024]{3,2,1,0:T(8,128)(2,1)}, u32[]{:S(2)}) %copy-start.2) | copy-done | bytes 8388632
  16.7 5.4 %prompt_part.1 = bf16[16,64,128]{2,1,0:T(8,128)(2,1)} custom-call(s32[3]{0:T(128)S(1)} %pad_add_fusion.meta, bf16[12,48,2048]{2,1,0:T(8,128)(2,1)S(1)} %copy-done.3, bf16[2,1,2048,1024]{3,2,1,0:T(8,128)(2,1)S(1)} %copy-done.2, bf16[2,1,2048,1024]{3,2,1,0:T(8,128)(2,1)S(1)} %copy-done.2), custom_call_target="tpu_custom_call" | custom-call | flops 805306368 | bytes 8388608 | tf_op jit(solution)/shard_map/prompt_part/pallas_call | solution.py:76
  22.0 8.3 %all-to-all-start.1 = ((bf16[16,64,128]{2,1,0:T(8,128)(2,1)}), bf16[16,64,128]{2,1,0:T(8,128)(2,1)S(1)}, u32[]{:S(2)}, u32[]{:S(2)}) async-start(bf16[16,64,128]{2,1,0:T(8,128)(2,1)} %prompt_part.1), calls=%async_computation.2 | async-start | bytes 524288 | tf_op jit(solution)/shard_map/all_to_all | solution.py:265
  30.4 0.0 all-gather.3.cloned.1.call-start
  30.6 0.7 fusion.2
  31.3 0.4 fusion.4
  31.7 0.4 fusion.7.reach_ref
  32.2 3.4 %fusion.35 = (bf16[1,12,48,1024]{3,2,1,0:T(8,128)(2,1)}, bf16[1,12,48,1024]{3,2,1,0:T(8,128)(2,1)}) fusion(bf16[2,12,48,1024]{3,2,1,0:T(8,128)(2,1)} %param.19), kind=kLoop, calls=%fused_computation.54 | loop fusion | bytes 4718592 | tf_op jit(solution)/shard_map/slice | solution.py:274
  35.5 104.7 %reduce-scatter.2.cloned.1.call-done = bf16[1,18,1792]{2,1,0:T(8,128)(2,1)} async-done(((bf16[16,18,1792]{2,1,0:T(8,128)(2,1)}), bf16[1,18,1792]{2,1,0:T(8,128)(2,1)}) %reduce-scatter.2.cloned.1.call-update) | async-done | bytes 64528 | tf_op jit(solution)/shard_map/reduce_scatter | solution.py:255
  140.2 1.0 fusion.25
  141.2 47.6 %all-gather = bf16[16,18,1792]{2,1,0:T(8,128)(2,1)S(1)} all-gather(bf16[1,18,1792]{2,1,0:T(8,128)(2,1)S(1)} %fusion.25), channel_id=1, replica_groups=mesh['blk'=16,'mp'=2] {'blk'}, dimensions={0}, use_global_device_ids=true | all-gather | bytes 1096704 | tf_op jit(solution)/shard_map/all_gather | solution.py:258
  188.8 1.2 reshape.62
  190.0 0.0 all-gather.3.cloned.1.call-update
  190.0 1.1 dynamic-slice_bitcast_fusion.1.v_ref
  191.1 1.0 dynamic-slice_bitcast_fusion.k_ref
  192.1 0.5 tree_part.1
  192.7 0.0 all-to-all-done.1.got_ref
  192.7 1.4 merge_part.1
  194.1 10.5 %all_to_all.15 = bf16[16,36,128]{2,1,0:T(8,128)(2,1)S(1)} all-to-all(bf16[16,36,128]{2,1,0:T(8,128)(2,1)S(1)} %merge_part.1), channel_id=1, replica_groups=mesh['blk'=16,'mp'=2] {'blk'}, dimensions={0} | all-to-all | bytes 294912 | tf_op jit(solution)/shard_map/all_to_all | solution.py:278
  204.7 0.0 copy-start.6
  204.7 7.7 %fusion.36 = f32[36,3584]{1,0:T(8,128)S(1)} fusion(bf16[36,2048]{1,0:T(8,128)(2,1)S(1)} %bitcast.37, bf16[2048,3584]{1,0:T(8,128)(2,1)} %param.25), kind=kOutput, calls=%fused_computation.55 | convolution fusion | flops 528482304 | bytes 15343616 | tf_op jit(solution)/shard_map/dot_general | solution.py:281
  212.4 0.0 collective-permute-start
  212.5 0.1 copy.23
  212.6 1.8 collective-permute-done
  214.4 0.2 multiply_reduce_fusion
  214.6 0.0 all-gather.3.cloned.1.call-done.fresh_ref
  214.6 1.6 copy-done.4
  216.2 16.4 %score_part.1 = f32[288,128]{1,0:T(8,128)S(1)} custom-call(s32[288,128]{1,0:T(8,128)S(1)} %pad.8.ids_ref, bf16[288,3584]{1,0:T(8,128)(2,1)S(1)} %copy-done.4, bf16[4096,3584]{1,0:T(8,128)(2,1)} %embed_ref.1), custom_call_target="tpu_custom_call" | custom-call | flops 8455716864 | bytes 29360128 | tf_op jit(solution)/shard_map/score_part/pallas_call | solution.py:197
  232.7 0.0 copy-start.5
  232.7 0.0 copy-start.7
  232.7 0.1 copy.24
  232.8 0.1 reshape.56
  232.9 0.9 broadcast_in_dim.5
  233.8 2.6 %all-to-all-start = ((f32[32,32,128]{2,1,0:T(8,128)}), f32[32,32,128]{2,1,0:T(8,128)S(1)}, u32[]{:S(2)}, u32[]{:S(2)}) async-start(f32[32,32,128]{2,1,0:T(8,128)} %broadcast_in_dim.5), calls=%async_computation.1 | async-start | bytes 1048576 | tf_op jit(solution)/shard_map/all_to_all | solution.py:293
  236.4 0.9 add_convert_fusion
  237.3 14.6 %all-to-all-done = f32[32,32,128]{2,1,0:T(8,128)S(1)} async-done(((f32[32,32,128]{2,1,0:T(8,128)}), f32[32,32,128]{2,1,0:T(8,128)S(1)}, u32[]{:S(2)}, u32[]{:S(2)}) %all-to-all-start) | async-done | bytes 524320 | tf_op jit(solution)/shard_map/all_to_all | solution.py:293
  252.0 0.1 slice_log_fusion
  252.1 0.1 slice.26
  252.2 0.7 reshape.58
  (23 shorter events, 0.3 us)
Async XLA Ops:
  7.2 1.4 copy-start
  7.2 133.0 %reduce-scatter.2.cloned.1.call-start = ((), (), s32[]{:S(2)}) async-start(), calls=%async_computation.4 | async-start | bytes 1462272 | tf_op jit(solution)/shard_map/reduce_scatter | solution.py:255
  10.0 3.3 %copy-start.3 = (bf16[12,48,2048]{2,1,0:T(8,128)(2,1)S(1)}, bf16[12,48,2048]{2,1,0:T(8,128)(2,1)}, u32[]{:S(2)}) copy-start(bf16[12,48,2048]{2,1,0:T(8,128)(2,1)} %q_ref.1) | copy-start | bytes 7077892
  13.3 3.4 %copy-start.2 = (bf16[2,1,2048,1024]{3,2,1,0:T(8,128)(2,1)S(1)}, bf16[2,1,2048,1024]{3,2,1,0:T(8,128)(2,1)}, u32[]{:S(2)}) copy-start(bf16[2,1,2048,1024]{3,2,1,0:T(8,128)(2,1)} %v_ref.1) | copy-start | bytes 25165828
  16.7 13.9 %copy-start.8 = (s32[12,48]{1,0:T(8,128)S(1)}, s32[12,48]{1,0:T(8,128)}, u32[]{:S(2)}) copy-start(s32[12,48]{1,0:T(8,128)} %param.24) | copy-start | bytes 6916
  22.0 170.6 %all-to-all-start.1 = ((bf16[16,64,128]{2,1,0:T(8,128)(2,1)}), bf16[16,64,128]{2,1,0:T(8,128)(2,1)S(1)}, u32[]{:S(2)}, u32[]{:S(2)}) async-start(bf16[16,64,128]{2,1,0:T(8,128)(2,1)} %prompt_part.1), calls=%async_computation.2 | async-start | bytes 524288 | tf_op jit(solution)/shard_map/all_to_all | solution.py:265
  30.4 184.3 %all-gather.3.cloned.1.call-start = ((), (), s32[]{:S(2)}) async-start(), calls=%async_computation.5 | async-start | bytes 3096576 | tf_op jit(solution)/shard_map/all_gather | solution.py:259
  204.7 7.8 %copy-start.6 = (s32[2,144,10]{1,0,2:T(2,128)S(1)}, s32[2,144,10]{1,0,2:T(2,128)}, u32[]{:S(2)}) copy-start(s32[2,144,10]{1,0,2:T(2,128)} %param.17) | copy-start | bytes 34564
  212.4 2.0 collective-permute-start
  214.6 1.6 copy-start.4
  216.2 36.6 %copy-start.1 = (bf16[2,224,1792]{2,1,0:T(8,128)(2,1)S(1)}, bf16[2,224,1792]{2,1,0:T(8,128)(2,1)}, u32[]{:S(2)}) copy-start(bf16[2,224,1792]{2,1,0:T(8,128)(2,1)} %param.15) | copy-start | bytes 4816900
  232.7 3.7 %copy-start.5 = (bf16[36,3584]{1,0:T(8,128)(2,1)S(1)}, bf16[36,3584]{1,0:T(8,128)(2,1)}, u32[]{:S(2)}) copy-start(bf16[36,3584]{1,0:T(8,128)(2,1)} %param.27) | copy-start | bytes 774148
  232.7 3.7 %copy-start.7 = (f32[3584]{0:T(1024)S(1)}, f32[3584]{0:T(1024)}, u32[]{:S(2)}) copy-start(f32[3584]{0:T(1024)} %param.26) | copy-start | bytes 43012
  233.8 18.2 %all-to-all-start = ((f32[32,32,128]{2,1,0:T(8,128)}), f32[32,32,128]{2,1,0:T(8,128)S(1)}, u32[]{:S(2)}, u32[]{:S(2)}) async-start(f32[32,32,128]{2,1,0:T(8,128)} %broadcast_in_dim.5), calls=%async_computation.1 | async-start | bytes 1048576 | tf_op jit(solution)/shard_map/all_to_all | solution.py:293
Sparse Core Ops, SparseCore 0:
  12.8 127.3 reduce-scatter.1
  190.1 6.7 all-gather.2

commit v2 on v1

--- a/solution.py
+++ b/solution.py
@@ -13,16 +13,6 @@
 
 EXTRA = 16
 HIGH, LOW, GROUP = 0, 4, 8
-
-
-def swap_sum(value, axis, size):
-    if size & (size - 1):
-        return lax.psum(value, axis)
-    step = 1
-    while step < size:
-        value = value + lax.ppermute(value, axis, [(i, i ^ step) for i in range(size)])
-        step *= 2
-    return value
 
 
 def soft_weights(scores):
@@ -161,16 +151,23 @@
     )(got, numer, denom)
 
 
-def score_kernel(picks, ids_ref, fresh_ref, embed_ref, out_ref, total, picked):
+def score_kernel(picks, count, places, ids_ref, *refs):
+    pieces, embed_ref, out_ref = refs[:count], refs[count], refs[count + 1]
+    fresh, total, picked = refs[count + 2 :]
     step = pl.program_id(0)
 
     @pl.when(step == 0)
     def _():
         total[...] = jnp.zeros_like(total)
         picked[...] = jnp.zeros_like(picked)
+        for n, piece in enumerate(pieces):
+            height, span = piece.shape
+            row = pl.multiple_of(places[2 * n] * height, 16)
+            col = pl.multiple_of(places[2 * n + 1] * span, LANES)
+            fresh[pl.ds(row, height), pl.ds(col, span)] = piece[...]
 
     tile = embed_ref.shape[0]
-    logits = 30.0 * jnp.tanh(dot_t(fresh_ref[...], embed_ref[...]) * (1.0 / 30.0))
+    logits = 30.0 * jnp.tanh(dot_t(fresh[...], embed_ref[...]) * (1.0 / 30.0))
     local = ids_ref[...] - step * tile
     lane = local & (LANES - 1)
     chunk = local >> 7
@@ -187,24 +184,28 @@
     def _():
         place = lax.broadcasted_iota(jnp.int32, sums.shape, 1)
         whole = jnp.sum(sums, axis=1, keepdims=True)
-        out_ref[...] = jnp.where(place < picks, found, jnp.where(place == picks, whole, 0.0))
-
-
-def score_part(fresh, embedding, ids, picks):
-    rows, depth = fresh.shape
-    vocab = embedding.shape[0]
+        both = jnp.where(place < picks, found, jnp.where(place == picks, whole, 0.0))
+        out_ref[...] = both.T[: out_ref.shape[0]]
+
+
+def score_part(pieces, places, embedding, ids, picks):
+    rows = ids.shape[0]
+    vocab, depth = embedding.shape
     tile = min(512, vocab)
-    return pl.pallas_call(
-        functools.partial(score_kernel, picks),
-        out_shape=jax.ShapeDtypeStruct((rows, LANES), jnp.float32),
-        grid=(vocab // tile,),
-        in_specs=[
-            pl.BlockSpec((rows, LANES), lambda i: (0, 0)),
-            pl.BlockSpec((rows, depth), lambda i: (0, 0)),
-            pl.BlockSpec((tile, depth), lambda i: (i, 0)),
-        ],
-        out_specs=pl.BlockSpec((rows, LANES), lambda i: (0, 0)),
-        scratch_shapes=[pltpu.VMEM((rows, LANES), jnp.float32)] * 2,
+    lines = -(-(picks + 1) // 8) * 8
+    return pl.pallas_call(
+        functools.partial(score_kernel, picks, len(pieces)),
+        out_shape=jax.ShapeDtypeStruct((lines, rows), jnp.float32),
+        grid_spec=pltpu.PrefetchScalarGridSpec(
+            num_scalar_prefetch=1,
+            grid=(vocab // tile,),
+            in_specs=[pl.BlockSpec((rows, LANES), lambda i, places: (0, 0))]
+            + [pl.BlockSpec(piece.shape, lambda i, places: (0, 0)) for piece in pieces]
+            + [pl.BlockSpec((tile, depth), lambda i, places: (i, 0))],
+            out_specs=pl.BlockSpec((lines, rows), lambda i, places: (0, 0)),
+            scratch_shapes=[pltpu.VMEM((rows, depth), jnp.bfloat16)]
+            + [pltpu.VMEM((rows, LANES), jnp.float32)] * 2,
+        ),
         compiler_params=pltpu.CompilerParams(vmem_limit_bytes=32 * MIB),
         cost_estimate=pl.CostEstimate(
             flops=2 * rows * depth * vocab,
@@ -212,7 +213,177 @@
             transcendentals=2 * rows * vocab,
         ),
         name="score_part",
-    )(ids, fresh, embedding)
+    )(places, ids, *pieces, embedding)
+
+
+def draft_kernel(meta, hidden_ref, weight_ref, *refs):
+    outs, padded = refs[:-1], refs[-1]
+    step = pl.program_id(0)
+    depth = weight_ref.shape[1]
+    window = padded.shape[0]
+
+    @pl.when(step == 0)
+    def _():
+        padded[...] = jnp.zeros_like(padded)
+
+    padded[pl.ds(pl.multiple_of(meta[1], 16), depth), :] = weight_ref[0]
+    columns = hidden_ref[:, pl.ds(pl.multiple_of(meta[0], LANES), window)]
+    partial = jnp.dot(columns, padded[...], preferred_element_type=jnp.float32)
+    for n, out in enumerate(outs):
+
+        @pl.when(step == n)
+        def _():
+            out[...] = partial.astype(out.dtype)
+
+
+def draft_part(hidden, medusa_w, blk):
+    rows, model = hidden.shape
+    depth, units = medusa_w.shape[1:]
+    half = units // 2
+    window = -(-depth // LANES) * LANES + LANES
+    start = blk * depth
+    first = jnp.minimum(start // LANES * LANES, model - window)
+    meta = jnp.stack([first, start - first] + [(blk & 3) ^ k for k in range(4)])
+    whole = pl.BlockSpec((rows, half), lambda k, meta: (0, 0))
+    return pl.pallas_call(
+        draft_kernel,
+        out_shape=[
+            jax.ShapeDtypeStruct((rows, half), jnp.bfloat16 if k else jnp.float32)
+            for k in range(4)
+        ],
+        grid_spec=pltpu.PrefetchScalarGridSpec(
+            num_scalar_prefetch=1,
+            grid=(4,),
+            in_specs=[
+                pl.BlockSpec((rows, model), lambda k, meta: (0, 0)),
+                pl.BlockSpec(
+                    (1, depth, half), lambda k, meta: (meta[2 + k] >> 1, 0, meta[2 + k] & 1)
+                ),
+            ],
+            out_specs=[whole] * 4,
+            scratch_shapes=[pltpu.VMEM((window, half), jnp.bfloat16)],
+        ),
+        compiler_params=pltpu.CompilerParams(vmem_limit_bytes=16 * MIB),
+        name="draft_part",
+    )(meta, hidden, medusa_w)
+
+
+def fold_kernel(place, own_ref, *refs):
+    got, outs, hold = refs[:3], refs[3:-1], refs[-1]
+    total = own_ref[...]
+    for one in got:
+        total = total + one[...].astype(jnp.float32)
+    height = hold.shape[1]
+    for j in range(len(outs)):
+        hold[j] = total[j * height : (j + 1) * height]
+    for k, out in enumerate(outs):
+        out[...] = hold[place[0] ^ k].astype(out.dtype)
+
+
+def fold_part(own, got, place, layers):
+    rows, half = own.shape
+    height = rows // layers
+    spec = pl.BlockSpec(memory_space=pltpu.VMEM)
+    return pl.pallas_call(
+        fold_kernel,
+        out_shape=[
+            jax.ShapeDtypeStruct((height, half), jnp.bfloat16 if k else jnp.float32)
+            for k in range(layers)
+        ],
+        in_specs=[pl.BlockSpec(memory_space=pltpu.SMEM)] + [spec] * 4,
+        out_specs=[spec] * layers,
+        scratch_shapes=[pltpu.VMEM((layers, height, half), jnp.float32)],
+        compiler_params=pltpu.CompilerParams(vmem_limit_bytes=16 * MIB),
+        name="fold_part",
+    )(place, own, *got)
+
+
+def stack_kernel(place, *refs):
+    parts, out_ref, hold, flat = refs[:-3], refs[-3], refs[-2], refs[-1]
+    height = hold.shape[1]
+    for k, part in enumerate(parts):
+        hold[place[0] ^ k] = part[...].astype(jnp.float32)
+    for j in range(len(parts)):
+        flat[j * height : (j + 1) * height, :] = hold[j]
+    out_ref[...] = flat[...].astype(jnp.bfloat16)
+
+
+def stack_part(parts, place):
+    layers = len(parts)
+    height, half = parts[0].shape
+    spec = pl.BlockSpec(memory_space=pltpu.VMEM)
+    return pl.pallas_call(
+        stack_kernel,
+        out_shape=jax.ShapeDtypeStruct((layers * height, half), jnp.bfloat16),
+        in_specs=[pl.BlockSpec(memory_space=pltpu.SMEM)] + [spec] * layers,
+        out_specs=spec,
+        scratch_shapes=[
+            pltpu.VMEM((layers, height, half), jnp.float32),
+            pltpu.VMEM((layers * height, half), jnp.float32),
+        ],
+        compiler_params=pltpu.CompilerParams(vmem_limit_bytes=16 * MIB),
+        name="stack_part",
+    )(place, *parts)
+
+
+def partner(value, axis, size, bits):
+    return lax.ppermute(value, axis, [(i, i ^ bits) for i in range(size)])
+
+
+def pair_sum(values):
+    while len(values) > 1:
+        values = [values[i] + values[i + 1] for i in range(0, len(values), 2)]
+    return values[0]
+
+
+def group_sum(value, axis, size, stride, count):
+    return pair_sum(
+        [value] + [partner(value, axis, size, k * stride) for k in range(1, count)]
+    )
+
+
+def fresh_by_permutes(hidden, medusa_w, blocks, blk, mp):
+    rows, model = hidden.shape
+    units = medusa_w.shape[2]
+    half = units // 2
+    layers = blocks // 4
+    height = rows // layers
+    layer = blk // 4
+    place = layer.reshape(1)
+    parts = draft_part(hidden, medusa_w, blk)
+    got = [partner(parts[k], "blk", blocks, k) for k in range(1, 4)]
+    parts = fold_part(parts[0], got, place, layers)
+    inner = parts[0]
+    for k in range(1, layers):
+        inner = inner + partner(parts[k], "blk", blocks, 4 * k).astype(jnp.float32)
+    base = lax.dynamic_slice(
+        hidden, (layer * height, mp * units + (blk & 1) * half), (height, half)
+    )
+    own = (base.astype(jnp.float32) + jax.nn.silu(inner)).astype(jnp.bfloat16)
+    chunks = [own] + [partner(own, "blk", blocks, 4 * k) for k in range(1, layers)]
+    quad = stack_part(chunks, place)
+    pieces = [quad] + [partner(quad, "blk", blocks, k) for k in range(1, 4)]
+    pieces = pieces + [partner(piece, "mp", 2, 1) for piece in pieces]
+    places = []
+    for side in (mp, 1 - mp):
+        for k in range(4):
+            which = (blk & 3) ^ k
+            places += [which >> 1, side * 2 + (which & 1)]
+    return pieces, jnp.stack(places)
+
+
+def fresh_by_collectives(hidden, medusa_w, blocks, blk, mp):
+    drafts, depth, units = medusa_w.shape
+    rows = hidden.shape[0]
+    own = drafts * rows // blocks
+    hidden_cols = lax.dynamic_slice_in_dim(hidden, blk * depth, depth, 1)
+    partial = jnp.einsum("rd,mdu->mru", hidden_cols, medusa_w, preferred_element_type=jnp.float32)
+    partial = partial.reshape(blocks, own, units).astype(jnp.bfloat16)
+    inner = lax.psum_scatter(partial, "blk", scatter_dimension=0).astype(jnp.float32)
+    base = lax.dynamic_slice(hidden, ((blk * own) % rows, mp * units), (own, units))
+    fresh = (base.astype(jnp.float32) + jax.nn.silu(inner)).astype(jnp.bfloat16)
+    fresh = lax.all_gather(fresh, "blk", axis=0, tiled=True)
+    return [lax.all_gather(fresh, "mp", axis=1, tiled=True)], jnp.zeros((2,), jnp.int32)
 
 
 def ancestry(parents):
@@ -247,16 +418,11 @@
     drafts, depth, units = medusa_w.shape
     rows, model = hidden.shape
     lines = drafts * rows
-    own = lines // blocks
-
-    hidden_cols = lax.dynamic_slice_in_dim(hidden, blk * depth, depth, 1)
-    partial = jnp.einsum("rd,mdu->mru", hidden_cols, medusa_w, preferred_element_type=jnp.float32)
-    partial = partial.reshape(blocks, own, units).astype(jnp.bfloat16)
-    inner = lax.psum_scatter(partial, "blk", scatter_dimension=0).astype(jnp.float32)
-    base = lax.dynamic_slice(hidden, ((blk * own) % rows, mp * units), (own, units))
-    fresh = (base.astype(jnp.float32) + jax.nn.silu(inner)).astype(jnp.bfloat16)
-    fresh = lax.all_gather(fresh, "blk", axis=0, tiled=True)
-    fresh = lax.all_gather(fresh, "mp", axis=1, tiled=True)
+
+    if splits == 2 and blocks % 4 == 0 and units % 256 == 0 and drafts == 2:
+        pieces, places = fresh_by_permutes(hidden, medusa_w, blocks, blk, mp)
+    else:
+        pieces, places = fresh_by_collectives(hidden, medusa_w, blocks, blk, mp)
 
     groups, tree_size, features = tree_q.shape
     width = features // blocks
@@ -278,7 +444,8 @@
     heads_out = lax.all_to_all(heads_out, "blk", 0, 0, tiled=True)
     tokens = heads_out.shape[1]
     heads_out = heads_out.transpose(1, 0, 2).reshape(tokens, features)
-    attn = swap_sum(jnp.dot(heads_out, out_weight, preferred_element_type=jnp.float32), "mp", splits)
+    attn = jnp.dot(heads_out, out_weight, preferred_element_type=jnp.float32)
+    attn = group_sum(attn, "mp", splits, 1, splits)
     normed = attn * lax.rsqrt(jnp.mean(attn * attn, -1, keepdims=True) + 1e-06) * post_gain
     layer_out = (normed + resid.astype(jnp.float32)).astype(jnp.bfloat16)
 
@@ -286,13 +453,12 @@
     picks = cand_ids.shape[2]
     ids = cand_ids.reshape(lines, picks) - (blk * splits + mp) * vocab
     ids = jnp.pad(ids, ((0, 0), (0, LANES - picks)), constant_values=-1)
-    score = score_part(fresh, embedding, ids, picks)
-    payload = score[:, : picks + 1].T.reshape(-1)
-    payload = jnp.pad(payload, (0, -payload.shape[0] % 1024)).reshape(-1, LANES)
-    spread = jnp.broadcast_to(payload[None], (blocks * splits,) + payload.shape)
-    score = jnp.sum(lax.all_to_all(spread, ("blk", "mp"), 0, 0, tiled=True), 0)
-    score = score.reshape(-1)[: (picks + 1) * lines].reshape(picks + 1, lines)
-    draft_logprob = (score[:picks] - jnp.log(score[picks:])).T.reshape(drafts, rows, picks)
+    score = score_part(pieces, places, embedding, ids, picks)
+    score = group_sum(score, "mp", splits, 1, splits)
+    score = group_sum(score, "blk", blocks, 1, 4)
+    score = group_sum(score, "blk", blocks, 4, blocks // 4)
+    draft_logprob = score[:picks] - jnp.log(score[picks : picks + 1])
+    draft_logprob = draft_logprob.T.reshape(drafts, rows, picks)
     return (draft_logprob, layer_out)
 
 

time: 260 us -> 122 us (0.47)
  waiting for transfers between devices: 121 us -> 29.4 us
  blocking collectives: 58.1 us -> 0 us
  starting transfers between devices: 11 us -> 36.7 us
  between operations: 16.4 us -> 3 us
  Pallas kernels: 23.7 us -> 28.8 us
  local copies, waits for them, and re-layouts: 16.4 us -> 12.6 us
    reduce_scatter x1 -> x0, waiting for transfers between devices: 105 us -> none  [per_device(): lax.psum_scatter(partial, 'blk', scatter_dimension=0).astype(jnp.float32)]
    all_gather x1 -> x0, blocking collectives: 47.6 us -> none  [per_device(): fresh = lax.all_gather(fresh, 'blk', axis=0, tiled=True)]
    ppermute x1 -> x24, waiting for transfers between devices: 1.8 us -> 29.4 us  [partner(): return lax.ppermute(value, axis, [(i, i ^ bits) for i in range(size)])]
    ppermute x1 -> x24, starting transfers between devices: 0.01 us -> 24.7 us  [partner(): return lax.ppermute(value, axis, [(i, i ^ bits) for i in range(size)])]
    all_to_all x1, waiting for transfers between devices: 14.6 us -> 0.01 us  [per_device(): heads_out = lax.all_to_all(heads_out, 'blk', 0, 0, tiled=True)]
    all_to_all x1 -> x0, blocking collectives: 10.5 us -> none  [per_device(): heads_out = lax.all_to_all(heads_out, 'blk', 0, 0, tiled=True)]
    pallas_call x1 -> x4, Pallas kernels: 16.4 us -> 20.9 us  [the longest x1 17.3 us: score_part(): pl.pallas_call(functools.partial(score_kernel, picks, len(pieces)), out_s...]
    unnamed x21 -> x18, local copies, waits for them, and re-layouts: 7.58 us -> 5.13 us
  transfers between devices with their start and end apart: 5 -> 26, of which waited for: 3 -> 14; matrix products, arithmetic and copies ran while one was open for 7% -> 14% of each run, Pallas kernels for 3% -> 19%
where the time goes in v2:
time: 122 us; the launch traced here: 121 us
  starting transfers between devices  36.7 us (30%)
  waiting for transfers between devices  29.4 us (24%)
  Pallas kernels  28.8 us (24%)
  local copies, waits for them, and re-layouts  12.6 us (10%)
  matrix products  9.33 us (8%)
  between operations  3 us (2%)
  other arithmetic  1.29 us (1%)
    ppermute x24, waiting for transfers between devices, partner(): return lax.ppermute(value, axis, [(i, i ^ bits) for i in range(size)])  29.4 us
    ppermute x24, starting transfers between devices, partner(): return lax.ppermute(value, axis, [(i, i ^ bits) for i in range(size)])  24.7 us
    pallas_call x1, Pallas kernels, score_part(): pl.pallas_call(functools.partial(score_kernel, picks, len(pieces)), out_s...  17.3 us
    all_to_all x1, starting transfers between devices, per_device(): got = lax.all_to_all(sent, 'blk', 0, 0, tiled=True)  8.31 us
    dot_general x1, matrix products, per_device(): attn = jnp.dot(heads_out, out_weight, preferred_element_type=jnp.float32)  7.77 us
    pallas_call x1, Pallas kernels, prompt_part(): pl.pallas_call(functools.partial(prompt_kernel, tree_size, repeats, width...  5.38 us
    unnamed x18, local copies, waits for them, and re-layouts  5.13 us
    all_to_all x1, starting transfers between devices, per_device(): heads_out = lax.all_to_all(heads_out, 'blk', 0, 0, tiled=True)  3.71 us
  transfers between devices with their start and end apart: 26, of which 14 were waited for; matrix products, arithmetic and copies ran while one was open for 14% of the time, Pallas kernels for 19%

profile of v2, /device:TPU:0, one launch (start us, length us, event | category | flops | bytes accessed | tf_op | source)
XLA Modules:
  0.0 121.1 jit_solution(17215267707865790880)
XLA Ops:
  2.6 3.4 %copy-done = bf16[2,1,2048,1024]{3,2,1,0:T(8,128)(2,1)S(1)} copy-done((bf16[2,1,2048,1024]{3,2,1,0:T(8,128)(2,1)S(1)}, bf16[2,1,2048,1024]{3,2,1,0:T(8,128)(2,1)}, u32[]{:S(2)}) %copy-start) | copy-done | bytes 8388632
  6.0 1.7 %copy-done.1 = bf16[12,48,2048]{2,1,0:T(8,128)(2,1)S(1)} copy-done((bf16[12,48,2048]{2,1,0:T(8,128)(2,1)S(1)}, bf16[12,48,2048]{2,1,0:T(8,128)(2,1)}, u32[]{:S(2)}) %copy-start.1) | copy-done | bytes 2359320
  7.7 5.4 %prompt_part.1 = bf16[16,64,128]{2,1,0:T(8,128)(2,1)} custom-call(s32[3]{0:T(128)S(1)} %pad_add_fusion.meta, bf16[12,48,2048]{2,1,0:T(8,128)(2,1)S(1)} %copy-done.1, bf16[2,1,2048,1024]{3,2,1,0:T(8,128)(2,1)S(1)} %copy-done, bf16[2,1,2048,1024]{3,2,1,0:T(8,128)(2,1)S(1)} %copy-done), custom_call_target="tpu_custom_call" | custom-call | flops 805306368 | bytes 8388608 | tf_op jit(solution)/shard_map/prompt_part/pallas_call | solution.py:66
  13.1 8.3 %all-to-all-start = ((bf16[16,64,128]{2,1,0:T(8,128)(2,1)}), bf16[16,64,128]{2,1,0:T(8,128)(2,1)S(1)}, u32[]{:S(2)}, u32[]{:S(2)}) async-start(bf16[16,64,128]{2,1,0:T(8,128)(2,1)} %prompt_part.1), calls=%async_computation | async-start | bytes 524288 | tf_op jit(solution)/shard_map/all_to_all | solution.py:431
  21.5 3.3 %draft_part.1 = (f32[144,896]{1,0:T(8,128)S(1)}, bf16[144,896]{1,0:T(8,128)(2,1)}, bf16[144,896]{1,0:T(8,128)(2,1)}, bf16[144,896]{1,0:T(8,128)(2,1)}) custom-call(s32[6]{0:T(128)S(1)} %stack.83.meta, bf16[144,3584]{1,0:T(8,128)(2,1)S(1)} %copy-done.3, bf16[2,224,1792]{2,1,0:T(8,128)(2,1)S(1)} %copy-done.2), custom_call_target="tpu_custom_call" | custom-call | tf_op jit(solution)/shard_map/draft_part/pallas_call | solution.py:248
  24.8 1.9 %collective-permute-start = (bf16[144,896]{1,0:T(8,128)(2,1)}, bf16[144,896]{1,0:T(8,128)(2,1)S(1)}, u32[]{:S(2)}, u32[]{:S(2)}) collective-permute-start(bf16[144,896]{1,0:T(8,128)(2,1)} %get-tuple-element.13), channel_id=1, source_target_pairs={{0,2},{2,0},{4,6},{6,4},{8,10},{10,8},{12,14},{14,12},{16,18},{18,... | collective-permute-start | bytes 774152 | tf_op jit(solution)/shard_map/ppermute | solution.py:330
  26.7 1.5 %collective-permute-start.1 = (bf16[144,896]{1,0:T(8,128)(2,1)}, bf16[144,896]{1,0:T(8,128)(2,1)S(1)}, u32[]{:S(2)}, u32[]{:S(2)}) collective-permute-start(bf16[144,896]{1,0:T(8,128)(2,1)} %get-tuple-element.14), channel_id=1, source_target_pairs={{0,4},{2,6},{4,0},{6,2},{8,12},{10,14},{12,8},{14,10},{16,20},{18,... | collective-permute-start | bytes 774152 | tf_op jit(solution)/shard_map/ppermute | solution.py:330
  28.3 3.4 %fusion.27 = (bf16[1,12,48,1024]{3,2,1,0:T(8,128)(2,1)}, bf16[1,12,48,1024]{3,2,1,0:T(8,128)(2,1)}) fusion(bf16[2,12,48,1024]{3,2,1,0:T(8,128)(2,1)} %param.19), kind=kLoop, calls=%fused_computation.44 | loop fusion | bytes 4718592 | tf_op jit(solution)/shard_map/slice | solution.py:440
  31.7 3.2 %collective-permute-done.refs_0_ = bf16[144,896]{1,0:T(8,128)(2,1)S(1)} collective-permute-done((bf16[144,896]{1,0:T(8,128)(2,1)}, bf16[144,896]{1,0:T(8,128)(2,1)S(1)}, u32[]{:S(2)}, u32[]{:S(2)}) %collective-permute-start) | collective-permute-done | bytes 258080 | tf_op jit(solution)/shard_map/ppermute | solution.py:330
  34.8 4.2 %collective-permute-done.1.refs_1_ = bf16[144,896]{1,0:T(8,128)(2,1)S(1)} collective-permute-done((bf16[144,896]{1,0:T(8,128)(2,1)}, bf16[144,896]{1,0:T(8,128)(2,1)S(1)}, u32[]{:S(2)}, u32[]{:S(2)}) %collective-permute-start.1) | collective-permute-done | bytes 258080 | tf_op jit(solution)/shard_map/ppermute | solution.py:330
  39.0 1.3 %collective-permute-done.2.refs_2_ = bf16[144,896]{1,0:T(8,128)(2,1)S(1)} collective-permute-done((bf16[144,896]{1,0:T(8,128)(2,1)}, bf16[144,896]{1,0:T(8,128)(2,1)S(1)}, u32[]{:S(2)}, u32[]{:S(2)}) %collective-permute-start.2) | collective-permute-done | bytes 258080 | tf_op jit(solution)/shard_map/ppermute | solution.py:330
  40.5 1.5 %collective-permute-start.3 = (bf16[36,896]{1,0:T(8,128)(2,1)S(1)}, bf16[36,896]{1,0:T(8,128)(2,1)S(1)}, u32[]{:S(2)}, u32[]{:S(2)}) collective-permute-start(bf16[36,896]{1,0:T(8,128)(2,1)S(1)} %get-tuple-element.17), channel_id=1, source_target_pairs={{0,8},{2,10},{4,12},{6,14},{8,0},{10,2},{12,4},{14,6},{16,24},{18,... | collective-permute-start | bytes 193544 | tf_op jit(solution)/shard_map/ppermute | solution.py:330
  42.0 2.4 %collective-permute-start.4 = (bf16[36,896]{1,0:T(8,128)(2,1)S(1)}, bf16[36,896]{1,0:T(8,128)(2,1)S(1)}, u32[]{:S(2)}, u32[]{:S(2)}) collective-permute-start(bf16[36,896]{1,0:T(8,128)(2,1)S(1)} %get-tuple-element.18), channel_id=1, source_target_pairs={{0,16},{2,18},{4,20},{6,22},{8,24},{10,26},{12,28},{14,30},{16,0},... | collective-permute-start | bytes 193544 | tf_op jit(solution)/shard_map/ppermute | solution.py:330
  44.4 0.6 collective-permute-start.5
  45.0 0.7 fusion.1
  45.7 3.1 %collective-permute-done.4 = bf16[36,896]{1,0:T(8,128)(2,1)S(1)} collective-permute-done((bf16[36,896]{1,0:T(8,128)(2,1)S(1)}, bf16[36,896]{1,0:T(8,128)(2,1)S(1)}, u32[]{:S(2)}, u32[]{:S(2)}) %collective-permute-start.4) | collective-permute-done | bytes 64544 | tf_op jit(solution)/shard_map/ppermute | solution.py:330
  48.9 1.7 %collective-permute-done.5 = bf16[36,896]{1,0:T(8,128)(2,1)S(1)} collective-permute-done((bf16[36,896]{1,0:T(8,128)(2,1)S(1)}, bf16[36,896]{1,0:T(8,128)(2,1)S(1)}, u32[]{:S(2)}, u32[]{:S(2)}) %collective-permute-start.5) | collective-permute-done | bytes 64544 | tf_op jit(solution)/shard_map/ppermute | solution.py:330
  50.7 2.1 %collective-permute-start.7 = (bf16[36,896]{1,0:T(8,128)(2,1)S(1)}, bf16[36,896]{1,0:T(8,128)(2,1)S(1)}, u32[]{:S(2)}, u32[]{:S(2)}) collective-permute-start(bf16[36,896]{1,0:T(8,128)(2,1)S(1)} %add_convert_fusion.1.refs_0_), channel_id=1, source_target_pairs={{0,16},{2,18},{4,20},{6,22},{8,24},{10,26},{12,28},{14,30},{16,0},... | collective-permute-start | bytes 193544 | tf_op jit(solution)/shard_map/ppermute | solution.py:330
  52.8 2.3 %collective-permute-start.8 = (bf16[36,896]{1,0:T(8,128)(2,1)S(1)}, bf16[36,896]{1,0:T(8,128)(2,1)S(1)}, u32[]{:S(2)}, u32[]{:S(2)}) collective-permute-start(bf16[36,896]{1,0:T(8,128)(2,1)S(1)} %add_convert_fusion.1.refs_0_), channel_id=1, source_target_pairs={{0,24},{2,26},{4,28},{6,30},{8,16},{10,18},{12,20},{14,22},{16,8},... | collective-permute-start | bytes 193544 | tf_op jit(solution)/shard_map/ppermute | solution.py:330
  55.1 0.4 fusion.3
  55.6 0.8 collective-permute-done.6.refs_1_
  56.4 2.5 %collective-permute-done.8.refs_3_ = bf16[36,896]{1,0:T(8,128)(2,1)S(1)} collective-permute-done((bf16[36,896]{1,0:T(8,128)(2,1)S(1)}, bf16[36,896]{1,0:T(8,128)(2,1)S(1)}, u32[]{:S(2)}, u32[]{:S(2)}) %collective-permute-start.8) | collective-permute-done | bytes 64544 | tf_op jit(solution)/shard_map/ppermute | solution.py:330
  59.0 1.1 collective-permute-start.9
  60.1 0.7 collective-permute-start.10
  60.8 1.8 %collective-permute-start.11 = (bf16[144,896]{1,0:T(8,128)(2,1)S(1)}, bf16[144,896]{1,0:T(8,128)(2,1)S(1)}, u32[]{:S(2)}, u32[]{:S(2)}) collective-permute-start(bf16[144,896]{1,0:T(8,128)(2,1)S(1)} %stack_part.1.refs_0_), channel_id=1, source_target_pairs={{0,6},{2,4},{4,2},{6,0},{8,14},{10,12},{12,10},{14,8},{16,22},{18,... | collective-permute-start | bytes 774152 | tf_op jit(solution)/shard_map/ppermute | solution.py:330
  62.6 1.0 constant_dynamic-slice_fusion.q_ref
  63.7 1.0 dynamic-slice_bitcast_fusion.k_ref
  64.7 1.6 %collective-permute-done.9.refs_1_ = bf16[144,896]{1,0:T(8,128)(2,1)S(1)} collective-permute-done((bf16[144,896]{1,0:T(8,128)(2,1)S(1)}, bf16[144,896]{1,0:T(8,128)(2,1)S(1)}, u32[]{:S(2)}, u32[]{:S(2)}) %collective-permute-start.9) | collective-permute-done | bytes 258080 | tf_op jit(solution)/shard_map/ppermute | solution.py:330
  66.3 4.2 %collective-permute-done.10.refs_2_ = bf16[144,896]{1,0:T(8,128)(2,1)S(1)} collective-permute-done((bf16[144,896]{1,0:T(8,128)(2,1)S(1)}, bf16[144,896]{1,0:T(8,128)(2,1)S(1)}, u32[]{:S(2)}, u32[]{:S(2)}) %collective-permute-start.10) | collective-permute-done | bytes 258080 | tf_op jit(solution)/shard_map/ppermute | solution.py:330
  70.5 0.5 collective-permute-start.15
  71.0 1.1 dynamic-slice_bitcast_fusion.1.v_ref
  72.3 0.4 fusion.6.reach_ref
  72.7 0.5 tree_part.1
  73.4 2.1 %merge_part.1 = bf16[16,36,128]{2,1,0:T(8,128)(2,1)} custom-call(bf16[16,64,128]{2,1,0:T(8,128)(2,1)S(1)} %all-to-all-done.got_ref, f32[12,48,128]{2,1,0:T(8,128)S(1)} %get-tuple-element.20.numer_ref, f32[12,48,128]{2,1,0:T(8,128)S(1)} %get-tuple-element.21.denom_ref), custom_call_target="tpu_custom_call" | custom-call | tf_op jit(solution)/shard_map/merge_part/pallas_call | solution.py:145
  75.4 3.7 %all-to-all-start.1 = ((bf16[16,36,128]{2,1,0:T(8,128)(2,1)}), bf16[16,36,128]{2,1,0:T(8,128)(2,1)S(1)}, u32[]{:S(2)}, u32[]{:S(2)}) async-start(bf16[16,36,128]{2,1,0:T(8,128)(2,1)} %merge_part.1), calls=%async_computation.1 | async-start | bytes 327680 | tf_op jit(solution)/shard_map/all_to_all | solution.py:444
  79.2 17.3 %score_part.1 = f32[16,288]{1,0:T(8,128)S(1)} custom-call(s32[16]{0:T(128)S(1)} %stack.76.places, s32[288,128]{1,0:T(8,128)S(1)} %pad.4.ids_ref, bf16[144,896]{1,0:T(8,128)(2,1)S(1)} %stack_part.1.refs_0_, bf16[144,896]{1,0:T(8,128)(2,1)S(1)} %collective-permute-done.9.refs_1_, bf16[144,896]{1,0:T(8,128)(2,1)S(1)} %collective-permute-done.10.refs_2_, ...), custom_call_target="tpu_custom_call" | custom-call | flops 8455716864 | bytes 29360128 | tf_op jit(solution)/shard_map/score_part/pallas_call | solution.py:196
  96.7 1.0 collective-permute-done.16
  97.7 1.9 %collective-permute-start.17 = (f32[16,288]{1,0:T(8,128)S(1)}, f32[16,288]{1,0:T(8,128)S(1)}, u32[]{:S(2)}, u32[]{:S(2)}) collective-permute-start(f32[16,288]{1,0:T(8,128)S(1)} %add.137), channel_id=1, source_target_pairs={{0,2},{2,0},{4,6},{6,4},{8,10},{10,8},{12,14},{14,12},{16,18},{18,... | collective-permute-start | bytes 55304 | tf_op jit(solution)/shard_map/ppermute | solution.py:330
  99.6 1.5 %collective-permute-start.18 = (f32[16,288]{1,0:T(8,128)S(1)}, f32[16,288]{1,0:T(8,128)S(1)}, u32[]{:S(2)}, u32[]{:S(2)}) collective-permute-start(f32[16,288]{1,0:T(8,128)S(1)} %add.137), channel_id=1, source_target_pairs={{0,4},{2,6},{4,0},{6,2},{8,12},{10,14},{12,8},{14,10},{16,20},{18,... | collective-permute-start | bytes 55304 | tf_op jit(solution)/shard_map/ppermute | solution.py:330
  101.5 1.9 %collective-permute-done.18 = f32[16,288]{1,0:T(8,128)S(1)} collective-permute-done((f32[16,288]{1,0:T(8,128)S(1)}, f32[16,288]{1,0:T(8,128)S(1)}, u32[]{:S(2)}, u32[]{:S(2)}) %collective-permute-start.18) | collective-permute-done | bytes 18464 | tf_op jit(solution)/shard_map/ppermute | solution.py:330
  103.5 2.4 %collective-permute-done.19 = f32[16,288]{1,0:T(8,128)S(1)} collective-permute-done((f32[16,288]{1,0:T(8,128)S(1)}, f32[16,288]{1,0:T(8,128)S(1)}, u32[]{:S(2)}, u32[]{:S(2)}) %collective-permute-start.19) | collective-permute-done | bytes 18464 | tf_op jit(solution)/shard_map/ppermute | solution.py:330
  105.8 1.5 %collective-permute-start.20 = (f32[16,288]{1,0:T(8,128)S(1)}, f32[16,288]{1,0:T(8,128)S(1)}, u32[]{:S(2)}, u32[]{:S(2)}) collective-permute-start(f32[16,288]{1,0:T(8,128)S(1)} %add_add_fusion.1), channel_id=1, source_target_pairs={{0,8},{2,10},{4,12},{6,14},{8,0},{10,2},{12,4},{14,6},{16,24},{18,... | collective-permute-start | bytes 55304 | tf_op jit(solution)/shard_map/ppermute | solution.py:330
  107.4 2.4 %collective-permute-start.21 = (f32[16,288]{1,0:T(8,128)S(1)}, f32[16,288]{1,0:T(8,128)S(1)}, u32[]{:S(2)}, u32[]{:S(2)}) collective-permute-start(f32[16,288]{1,0:T(8,128)S(1)} %add_add_fusion.1), channel_id=1, source_target_pairs={{0,16},{2,18},{4,20},{6,22},{8,24},{10,26},{12,28},{14,30},{16,0},... | collective-permute-start | bytes 55304 | tf_op jit(solution)/shard_map/ppermute | solution.py:330
  109.7 0.6 collective-permute-start.22
  110.3 7.8 %fusion.28 = f32[36,3584]{1,0:T(8,128)S(1)} fusion(bf16[36,2048]{1,0:T(8,128)(2,1)S(1)} %bitcast.38, bf16[2048,3584]{1,0:T(8,128)(2,1)} %param.25), kind=kOutput, calls=%fused_computation.45 | convolution fusion | flops 528482304 | bytes 15343616 | tf_op jit(solution)/shard_map/dot_general | solution.py:447
  118.2 0.7 reshape.42
  118.9 1.2 collective-permute-done.23
  120.3 0.9 add_convert_fusion
  (56 shorter events, 2.0 us)
Async XLA Ops:
  2.6 3.4 %copy-start = (bf16[2,1,2048,1024]{3,2,1,0:T(8,128)(2,1)S(1)}, bf16[2,1,2048,1024]{3,2,1,0:T(8,128)(2,1)}, u32[]{:S(2)}) copy-start(bf16[2,1,2048,1024]{3,2,1,0:T(8,128)(2,1)} %v_ref.1) | copy-start | bytes 25165828
  6.0 1.7 %copy-start.1 = (bf16[12,48,2048]{2,1,0:T(8,128)(2,1)S(1)}, bf16[12,48,2048]{2,1,0:T(8,128)(2,1)}, u32[]{:S(2)}) copy-start(bf16[12,48,2048]{2,1,0:T(8,128)(2,1)} %q_ref.1) | copy-start | bytes 7077892
  7.7 13.8 %copy-start.2 = (bf16[2,224,1792]{2,1,0:T(8,128)(2,1)S(1)}, bf16[2,224,1792]{2,1,0:T(8,128)(2,1)}, u32[]{:S(2)}) copy-start(bf16[2,224,1792]{2,1,0:T(8,128)(2,1)} %weight_ref.1) | copy-start | bytes 4816900
  7.7 13.8 %copy-start.3 = (bf16[144,3584]{1,0:T(8,128)(2,1)S(1)}, bf16[144,3584]{1,0:T(8,128)(2,1)}, u32[]{:S(2)}) copy-start(bf16[144,3584]{1,0:T(8,128)(2,1)} %hidden_ref.1) | copy-start | bytes 3096580
  13.1 60.3 %all-to-all-start = ((bf16[16,64,128]{2,1,0:T(8,128)(2,1)}), bf16[16,64,128]{2,1,0:T(8,128)(2,1)S(1)}, u32[]{:S(2)}, u32[]{:S(2)}) async-start(bf16[16,64,128]{2,1,0:T(8,128)(2,1)} %prompt_part.1), calls=%async_computation | async-start | bytes 524288 | tf_op jit(solution)/shard_map/all_to_all | solution.py:431
  24.8 10.1 %collective-permute-start = (bf16[144,896]{1,0:T(8,128)(2,1)}, bf16[144,896]{1,0:T(8,128)(2,1)S(1)}, u32[]{:S(2)}, u32[]{:S(2)}) collective-permute-start(bf16[144,896]{1,0:T(8,128)(2,1)} %get-tuple-element.13), channel_id=1, source_target_pairs={{0,2},{2,0},{4,6},{6,4},{8,10},{10,8},{12,14},{14,12},{16,18},{18,... | collective-permute-start | bytes 774152 | tf_op jit(solution)/shard_map/ppermute | solution.py:330
  26.7 12.3 %collective-permute-start.1 = (bf16[144,896]{1,0:T(8,128)(2,1)}, bf16[144,896]{1,0:T(8,128)(2,1)S(1)}, u32[]{:S(2)}, u32[]{:S(2)}) collective-permute-start(bf16[144,896]{1,0:T(8,128)(2,1)} %get-tuple-element.14), channel_id=1, source_target_pairs={{0,4},{2,6},{4,0},{6,2},{8,12},{10,14},{12,8},{14,10},{16,20},{18,... | collective-permute-start | bytes 774152 | tf_op jit(solution)/shard_map/ppermute | solution.py:330
  28.2 12.1 %collective-permute-start.2 = (bf16[144,896]{1,0:T(8,128)(2,1)}, bf16[144,896]{1,0:T(8,128)(2,1)S(1)}, u32[]{:S(2)}, u32[]{:S(2)}) collective-permute-start(bf16[144,896]{1,0:T(8,128)(2,1)} %get-tuple-element.15), channel_id=1, source_target_pairs={{0,6},{2,4},{4,2},{6,0},{8,14},{10,12},{12,10},{14,8},{16,22},{18,... | collective-permute-start | bytes 774152 | tf_op jit(solution)/shard_map/ppermute | solution.py:330
  28.3 16.7 %copy-start.7 = (s32[12,48]{1,0:T(8,128)S(1)}, s32[12,48]{1,0:T(8,128)}, u32[]{:S(2)}) copy-start(s32[12,48]{1,0:T(8,128)} %param.24) | copy-start | bytes 6916
  31.7 30.9 %copy-start.5 = (s32[2,144,10]{1,0,2:T(2,128)S(1)}, s32[2,144,10]{1,0,2:T(2,128)}, u32[]{:S(2)}) copy-start(s32[2,144,10]{1,0,2:T(2,128)} %param.17) | copy-start | bytes 34564
  40.5 5.2 %collective-permute-start.3 = (bf16[36,896]{1,0:T(8,128)(2,1)S(1)}, bf16[36,896]{1,0:T(8,128)(2,1)S(1)}, u32[]{:S(2)}, u32[]{:S(2)}) collective-permute-start(bf16[36,896]{1,0:T(8,128)(2,1)S(1)} %get-tuple-element.17), channel_id=1, source_target_pairs={{0,8},{2,10},{4,12},{6,14},{8,0},{10,2},{12,4},{14,6},{16,24},{18,... | collective-permute-start | bytes 193544 | tf_op jit(solution)/shard_map/ppermute | solution.py:330
  42.0 6.8 %collective-permute-start.4 = (bf16[36,896]{1,0:T(8,128)(2,1)S(1)}, bf16[36,896]{1,0:T(8,128)(2,1)S(1)}, u32[]{:S(2)}, u32[]{:S(2)}) collective-permute-start(bf16[36,896]{1,0:T(8,128)(2,1)S(1)} %get-tuple-element.18), channel_id=1, source_target_pairs={{0,16},{2,18},{4,20},{6,22},{8,24},{10,26},{12,28},{14,30},{16,0},... | collective-permute-start | bytes 193544 | tf_op jit(solution)/shard_map/ppermute | solution.py:330
  44.4 6.1 %collective-permute-start.5 = (bf16[36,896]{1,0:T(8,128)(2,1)S(1)}, bf16[36,896]{1,0:T(8,128)(2,1)S(1)}, u32[]{:S(2)}, u32[]{:S(2)}) collective-permute-start(bf16[36,896]{1,0:T(8,128)(2,1)S(1)} %get-tuple-element.19), channel_id=1, source_target_pairs={{0,24},{2,26},{4,28},{6,30},{8,16},{10,18},{12,20},{14,22},{16,8},... | collective-permute-start | bytes 193544 | tf_op jit(solution)/shard_map/ppermute | solution.py:330
  50.7 5.8 %collective-permute-start.6 = (bf16[36,896]{1,0:T(8,128)(2,1)S(1)}, bf16[36,896]{1,0:T(8,128)(2,1)S(1)}, u32[]{:S(2)}, u32[]{:S(2)}) collective-permute-start(bf16[36,896]{1,0:T(8,128)(2,1)S(1)} %add_convert_fusion.1.refs_0_), channel_id=1, source_target_pairs={{0,8},{2,10},{4,12},{6,14},{8,0},{10,2},{12,4},{14,6},{16,24},{18,... | collective-permute-start | bytes 193544 | tf_op jit(solution)/shard_map/ppermute | solution.py:330
  50.7 5.7 %collective-permute-start.7 = (bf16[36,896]{1,0:T(8,128)(2,1)S(1)}, bf16[36,896]{1,0:T(8,128)(2,1)S(1)}, u32[]{:S(2)}, u32[]{:S(2)}) collective-permute-start(bf16[36,896]{1,0:T(8,128)(2,1)S(1)} %add_convert_fusion.1.refs_0_), channel_id=1, source_target_pairs={{0,16},{2,18},{4,20},{6,22},{8,24},{10,26},{12,28},{14,30},{16,0},... | collective-permute-start | bytes 193544 | tf_op jit(solution)/shard_map/ppermute | solution.py:330
  52.8 6.1 %collective-permute-start.8 = (bf16[36,896]{1,0:T(8,128)(2,1)S(1)}, bf16[36,896]{1,0:T(8,128)(2,1)S(1)}, u32[]{:S(2)}, u32[]{:S(2)}) collective-permute-start(bf16[36,896]{1,0:T(8,128)(2,1)S(1)} %add_convert_fusion.1.refs_0_), channel_id=1, source_target_pairs={{0,24},{2,26},{4,28},{6,30},{8,16},{10,18},{12,20},{14,22},{16,8},... | collective-permute-start | bytes 193544 | tf_op jit(solution)/shard_map/ppermute | solution.py:330
  59.0 7.3 %collective-permute-start.9 = (bf16[144,896]{1,0:T(8,128)(2,1)S(1)}, bf16[144,896]{1,0:T(8,128)(2,1)S(1)}, u32[]{:S(2)}, u32[]{:S(2)}) collective-permute-start(bf16[144,896]{1,0:T(8,128)(2,1)S(1)} %stack_part.1.refs_0_), channel_id=1, source_target_pairs={{0,2},{2,0},{4,6},{6,4},{8,10},{10,8},{12,14},{14,12},{16,18},{18,... | collective-permute-start | bytes 774152 | tf_op jit(solution)/shard_map/ppermute | solution.py:330
  60.1 10.4 %collective-permute-start.10 = (bf16[144,896]{1,0:T(8,128)(2,1)S(1)}, bf16[144,896]{1,0:T(8,128)(2,1)S(1)}, u32[]{:S(2)}, u32[]{:S(2)}) collective-permute-start(bf16[144,896]{1,0:T(8,128)(2,1)S(1)} %stack_part.1.refs_0_), channel_id=1, source_target_pairs={{0,4},{2,6},{4,0},{6,2},{8,12},{10,14},{12,8},{14,10},{16,20},{18,... | collective-permute-start | bytes 774152 | tf_op jit(solution)/shard_map/ppermute | solution.py:330
  60.8 9.7 %collective-permute-start.11 = (bf16[144,896]{1,0:T(8,128)(2,1)S(1)}, bf16[144,896]{1,0:T(8,128)(2,1)S(1)}, u32[]{:S(2)}, u32[]{:S(2)}) collective-permute-start(bf16[144,896]{1,0:T(8,128)(2,1)S(1)} %stack_part.1.refs_0_), channel_id=1, source_target_pairs={{0,6},{2,4},{4,2},{6,0},{8,14},{10,12},{12,10},{14,8},{16,22},{18,... | collective-permute-start | bytes 774152 | tf_op jit(solution)/shard_map/ppermute | solution.py:330
  64.7 14.5 %collective-permute-start.12 = (bf16[144,896]{1,0:T(8,128)(2,1)S(1)}, bf16[144,896]{1,0:T(8,128)(2,1)S(1)}, u32[]{:S(2)}, u32[]{:S(2)}) collective-permute-start(bf16[144,896]{1,0:T(8,128)(2,1)S(1)} %stack_part.1.refs_0_), channel_id=1, source_target_pairs={{0,1},{1,0},{2,3},{3,2},{4,5},{5,4},{6,7},{7,6},{8,9},{9,8},{10,11... | collective-permute-start | bytes 774152 | tf_op jit(solution)/shard_map/ppermute | solution.py:330
  66.3 12.8 %collective-permute-start.13 = (bf16[144,896]{1,0:T(8,128)(2,1)S(1)}, bf16[144,896]{1,0:T(8,128)(2,1)}, u32[]{:S(2)}, u32[]{:S(2)}) collective-permute-start(bf16[144,896]{1,0:T(8,128)(2,1)S(1)} %collective-permute-done.9.refs_1_), channel_id=1, source_target_pairs={{0,1},{1,0},{2,3},{3,2},{4,5},{5,4},{6,7},{7,6},{8,9},{9,8},{10,11... | collective-permute-start | bytes 774152 | tf_op jit(solution)/shard_map/ppermute | solution.py:330
  70.5 8.7 %collective-permute-start.14 = (bf16[144,896]{1,0:T(8,128)(2,1)S(1)}, bf16[144,896]{1,0:T(8,128)(2,1)}, u32[]{:S(2)}, u32[]{:S(2)}) collective-permute-start(bf16[144,896]{1,0:T(8,128)(2,1)S(1)} %collective-permute-done.10.refs_2_), channel_id=1, source_target_pairs={{0,1},{1,0},{2,3},{3,2},{4,5},{5,4},{6,7},{7,6},{8,9},{9,8},{10,11... | collective-permute-start | bytes 774152 | tf_op jit(solution)/shard_map/ppermute | solution.py:330
  70.5 8.7 %collective-permute-start.15 = (bf16[144,896]{1,0:T(8,128)(2,1)S(1)}, bf16[144,896]{1,0:T(8,128)(2,1)}, u32[]{:S(2)}, u32[]{:S(2)}) collective-permute-start(bf16[144,896]{1,0:T(8,128)(2,1)S(1)} %collective-permute-done.11.refs_3_), channel_id=1, source_target_pairs={{0,1},{1,0},{2,3},{3,2},{4,5},{5,4},{6,7},{7,6},{8,9},{9,8},{10,11... | collective-permute-start | bytes 774152 | tf_op jit(solution)/shard_map/ppermute | solution.py:330
  75.4 25.8 %all-to-all-start.1 = ((bf16[16,36,128]{2,1,0:T(8,128)(2,1)}), bf16[16,36,128]{2,1,0:T(8,128)(2,1)S(1)}, u32[]{:S(2)}, u32[]{:S(2)}) async-start(bf16[16,36,128]{2,1,0:T(8,128)(2,1)} %merge_part.1), calls=%async_computation.1 | async-start | bytes 327680 | tf_op jit(solution)/shard_map/all_to_all | solution.py:444
  96.5 1.2 %collective-permute-start.16 = (f32[16,288]{1,0:T(8,128)S(1)}, f32[16,288]{1,0:T(8,128)S(1)}, u32[]{:S(2)}, u32[]{:S(2)}) collective-permute-start(f32[16,288]{1,0:T(8,128)S(1)} %score_part.1), channel_id=1, source_target_pairs={{0,1},{1,0},{2,3},{3,2},{4,5},{5,4},{6,7},{7,6},{8,9},{9,8},{10,11... | collective-permute-start | bytes 55304 | tf_op jit(solution)/shard_map/ppermute | solution.py:330
  97.7 3.8 %collective-permute-start.17 = (f32[16,288]{1,0:T(8,128)S(1)}, f32[16,288]{1,0:T(8,128)S(1)}, u32[]{:S(2)}, u32[]{:S(2)}) collective-permute-start(f32[16,288]{1,0:T(8,128)S(1)} %add.137), channel_id=1, source_target_pairs={{0,2},{2,0},{4,6},{6,4},{8,10},{10,8},{12,14},{14,12},{16,18},{18,... | collective-permute-start | bytes 55304 | tf_op jit(solution)/shard_map/ppermute | solution.py:330
  99.6 3.8 %collective-permute-start.18 = (f32[16,288]{1,0:T(8,128)S(1)}, f32[16,288]{1,0:T(8,128)S(1)}, u32[]{:S(2)}, u32[]{:S(2)}) collective-permute-start(f32[16,288]{1,0:T(8,128)S(1)} %add.137), channel_id=1, source_target_pairs={{0,4},{2,6},{4,0},{6,2},{8,12},{10,14},{12,8},{14,10},{16,20},{18,... | collective-permute-start | bytes 55304 | tf_op jit(solution)/shard_map/ppermute | solution.py:330
  101.1 4.7 %collective-permute-start.19 = (f32[16,288]{1,0:T(8,128)S(1)}, f32[16,288]{1,0:T(8,128)S(1)}, u32[]{:S(2)}, u32[]{:S(2)}) collective-permute-start(f32[16,288]{1,0:T(8,128)S(1)} %add.137), channel_id=1, source_target_pairs={{0,6},{2,4},{4,2},{6,0},{8,14},{10,12},{12,10},{14,8},{16,22},{18,... | collective-permute-start | bytes 55304 | tf_op jit(solution)/shard_map/ppermute | solution.py:330
  105.8 12.3 %collective-permute-start.20 = (f32[16,288]{1,0:T(8,128)S(1)}, f32[16,288]{1,0:T(8,128)S(1)}, u32[]{:S(2)}, u32[]{:S(2)}) collective-permute-start(f32[16,288]{1,0:T(8,128)S(1)} %add_add_fusion.1), channel_id=1, source_target_pairs={{0,8},{2,10},{4,12},{6,14},{8,0},{10,2},{12,4},{14,6},{16,24},{18,... | collective-permute-start | bytes 55304 | tf_op jit(solution)/shard_map/ppermute | solution.py:330
  107.4 10.7 %collective-permute-start.21 = (f32[16,288]{1,0:T(8,128)S(1)}, f32[16,288]{1,0:T(8,128)S(1)}, u32[]{:S(2)}, u32[]{:S(2)}) collective-permute-start(f32[16,288]{1,0:T(8,128)S(1)} %add_add_fusion.1), channel_id=1, source_target_pairs={{0,16},{2,18},{4,20},{6,22},{8,24},{10,26},{12,28},{14,30},{16,0},... | collective-permute-start | bytes 55304 | tf_op jit(solution)/shard_map/ppermute | solution.py:330
  109.7 8.4 %collective-permute-start.22 = (f32[16,288]{1,0:T(8,128)S(1)}, f32[16,288]{1,0:T(8,128)S(1)}, u32[]{:S(2)}, u32[]{:S(2)}) collective-permute-start(f32[16,288]{1,0:T(8,128)S(1)} %add_add_fusion.1), channel_id=1, source_target_pairs={{0,24},{2,26},{4,28},{6,30},{8,16},{10,18},{12,20},{14,22},{16,8},... | collective-permute-start | bytes 55304 | tf_op jit(solution)/shard_map/ppermute | solution.py:330
  110.3 10.0 %copy-start.4 = (bf16[36,3584]{1,0:T(8,128)(2,1)S(1)}, bf16[36,3584]{1,0:T(8,128)(2,1)}, u32[]{:S(2)}) copy-start(bf16[36,3584]{1,0:T(8,128)(2,1)} %param.27) | copy-start | bytes 774148
  110.3 10.0 %copy-start.6 = (f32[3584]{0:T(1024)S(1)}, f32[3584]{0:T(1024)}, u32[]{:S(2)}) copy-start(f32[3584]{0:T(1024)} %param.26) | copy-start | bytes 43012
  118.1 2.0 %collective-permute-start.23 = (f32[36,3584]{1,0:T(8,128)S(1)}, f32[36,3584]{1,0:T(8,128)S(1)}, u32[]{:S(2)}, u32[]{:S(2)}) collective-permute-start(f32[36,3584]{1,0:T(8,128)S(1)} %fusion.28), channel_id=1, source_target_pairs={{0,1},{1,0},{2,3},{3,2},{4,5},{5,4},{6,7},{7,6},{8,9},{9,8},{10,11... | collective-permute-start | bytes 1548296 | tf_op jit(solution)/shard_map/ppermute | solution.py:330

commit v3 on v1

--- a/solution.py
+++ b/solution.py
@@ -13,16 +13,6 @@
 
 EXTRA = 16
 HIGH, LOW, GROUP = 0, 4, 8
-
-
-def swap_sum(value, axis, size):
-    if size & (size - 1):
-        return lax.psum(value, axis)
-    step = 1
-    while step < size:
-        value = value + lax.ppermute(value, axis, [(i, i ^ step) for i in range(size)])
-        step *= 2
-    return value
 
 
 def soft_weights(scores):
@@ -96,25 +86,46 @@
     )(meta, tree_q, prompt_key_value, prompt_key_value)
 
 
-def tree_kernel(q_ref, k_ref, v_ref, reach_ref, numer_ref, denom_ref):
+def tree_kernel(meta, q_ref, k_ref, v_ref, reach_ref, numer_ref, denom_ref):
+    width = numer_ref.shape[2]
     for g in range(q_ref.shape[0]):
-        weights = soft_weights(dot_t(q_ref[g], k_ref[g])) * reach_ref[g]
+        weights = soft_weights(dot_t(q_ref[g], k_ref[0, g])) * reach_ref[g]
         denom_ref[g] = jnp.broadcast_to(
             jnp.sum(weights, axis=1, keepdims=True), denom_ref.shape[1:]
         )
-        numer_ref[g] = jnp.dot(
-            weights.astype(jnp.bfloat16), v_ref[g], preferred_element_type=jnp.float32
+        numer = jnp.dot(
+            weights.astype(jnp.bfloat16), v_ref[0, g], preferred_element_type=jnp.float32
         )
-
-
-def tree_part(queries, keys, values, reach):
-    shape = values.shape
+        mine = numer[:, :width]
+        for j in range(1, HEAD_SIZE // width):
+            mine = jnp.where(meta[2] == j, numer[:, j * width : (j + 1) * width], mine)
+        numer_ref[g] = mine
+
+
+def tree_part(tree_q, tree_key_value, reach, column, width):
+    groups, tree_size, features = tree_q.shape
+    repeats = features // tree_key_value.shape[3]
+    head = column // HEAD_SIZE
+    meta = jnp.stack([head, head // repeats, column % HEAD_SIZE // width])
+    shape = (groups, tree_size, width)
+    block = (1, groups, tree_size, HEAD_SIZE)
     return pl.pallas_call(
         tree_kernel,
         out_shape=[jax.ShapeDtypeStruct(shape, jnp.float32)] * 2,
-        compiler_params=pltpu.CompilerParams(vmem_limit_bytes=24 * MIB),
+        grid_spec=pltpu.PrefetchScalarGridSpec(
+            num_scalar_prefetch=1,
+            grid=(1,),
+            in_specs=[
+                pl.BlockSpec(block[1:], lambda i, meta: (0, 0, meta[0])),
+                pl.BlockSpec(block, lambda i, meta: (0, 0, 0, meta[1])),
+                pl.BlockSpec(block, lambda i, meta: (1, 0, 0, meta[1])),
+                pl.BlockSpec(reach.shape, lambda i, meta: (0, 0, 0)),
+            ],
+            out_specs=[pl.BlockSpec(shape, lambda i, meta: (0, 0, 0))] * 2,
+        ),
+        compiler_params=pltpu.CompilerParams(vmem_limit_bytes=16 * MIB),
         name="tree_part",
-    )(queries, keys, values, reach)
+    )(meta, tree_q, tree_key_value, tree_key_value, reach)
 
 
 def merge_kernel(got_ref, numer_ref, denom_ref, out_ref, hold):
@@ -161,58 +172,221 @@
     )(got, numer, denom)
 
 
-def score_kernel(picks, ids_ref, fresh_ref, embed_ref, out_ref, total, picked):
+def score_kernel(picks, side, ids_ref, *refs):
+    pieces, embed_ref, out_ref = refs[:-6], refs[-6], refs[-5]
+    fresh, total, picked, before = refs[-4:]
     step = pl.program_id(0)
+    tile = embed_ref.shape[0]
+    span = before.shape[1]
+    rows = fresh.shape[0]
+    band = 32 if rows % 32 == 0 else rows
 
     @pl.when(step == 0)
     def _():
-        total[...] = jnp.zeros_like(total)
-        picked[...] = jnp.zeros_like(picked)
-
-    tile = embed_ref.shape[0]
-    logits = 30.0 * jnp.tanh(dot_t(fresh_ref[...], embed_ref[...]) * (1.0 / 30.0))
-    local = ids_ref[...] - step * tile
-    lane = local & (LANES - 1)
-    chunk = local >> 7
-    sums, found = total[...], picked[...]
-    for c in range(tile // LANES):
-        part = logits[:, c * LANES : (c + 1) * LANES]
-        sums = sums + jnp.exp(part)
-        there = jnp.take_along_axis(part, lane, axis=1, mode="promise_in_bounds")
-        found = found + jnp.where(chunk == c, there, 0.0)
-    total[...] = sums
-    picked[...] = found
+        before[...] = jnp.zeros_like(before)
+        for n, piece in enumerate(pieces):
+            if len(piece.shape) == 2:
+                fresh[...] = piece[...]
+                continue
+            for q in range(4):
+                height, wide = piece.shape[1:]
+                row = q // 2 * height
+                col = pl.multiple_of(((side[0] ^ n) * 2 + q % 2) * wide, LANES)
+                fresh[row : row + height, pl.ds(col, wide)] = piece[q]
+
+    def absorb(raw, start, keep=None):
+        for r in range(0, rows, band):
+            ids = ids_ref[r : r + band] - start
+            lane = ids & (LANES - 1)
+            chunk = ids >> 7
+            sums, found = total[r : r + band], picked[r : r + band]
+            for c in range(span // LANES):
+                part = jnp.tanh(raw[r : r + band, c * LANES : (c + 1) * LANES] * (1.0 / 30.0))
+                sums = sums + jnp.exp(30.0 * part)
+                there = jnp.take_along_axis(part, lane, axis=1, mode="promise_in_bounds")
+                found = found + jnp.where(chunk == c, there, 0.0)
+            if keep is not None:
+                sums, found = jnp.where(keep, sums, 0.0), jnp.where(keep, found, 0.0)
+            total[r : r + band] = sums
+            picked[r : r + band] = found
+
+    base = step * tile
+    raw = dot_t(fresh[...], embed_ref[:span])
+    absorb(before[...], base - span, step > 0)
+    for n in range(1, tile // span):
+        more = dot_t(fresh[...], embed_ref[n * span : (n + 1) * span])
+        absorb(raw, base + (n - 1) * span)
+        raw = more
+    before[...] = raw
 
     @pl.when(step == pl.num_programs(0) - 1)
     def _():
+        absorb(before[...], base + tile - span)
+        sums, found = total[...], picked[...]
         place = lax.broadcasted_iota(jnp.int32, sums.shape, 1)
         whole = jnp.sum(sums, axis=1, keepdims=True)
-        out_ref[...] = jnp.where(place < picks, found, jnp.where(place == picks, whole, 0.0))
-
-
-def score_part(fresh, embedding, ids, picks):
-    rows, depth = fresh.shape
-    vocab = embedding.shape[0]
+        both = jnp.where(place < picks, 30.0 * found, jnp.where(place == picks, whole, 0.0))
+        out_ref[...] = both.T[: out_ref.shape[0]]
+
+
+def score_part(side, pieces, embedding, ids, picks):
+    rows = ids.shape[0]
+    vocab, depth = embedding.shape
     tile = min(512, vocab)
+    span = min(256, tile)
+    lines = -(-(picks + 1) // 8) * 8
     return pl.pallas_call(
         functools.partial(score_kernel, picks),
-        out_shape=jax.ShapeDtypeStruct((rows, LANES), jnp.float32),
-        grid=(vocab // tile,),
-        in_specs=[
-            pl.BlockSpec((rows, LANES), lambda i: (0, 0)),
-            pl.BlockSpec((rows, depth), lambda i: (0, 0)),
-            pl.BlockSpec((tile, depth), lambda i: (i, 0)),
-        ],
-        out_specs=pl.BlockSpec((rows, LANES), lambda i: (0, 0)),
-        scratch_shapes=[pltpu.VMEM((rows, LANES), jnp.float32)] * 2,
-        compiler_params=pltpu.CompilerParams(vmem_limit_bytes=32 * MIB),
+        out_shape=jax.ShapeDtypeStruct((lines, rows), jnp.float32),
+        grid_spec=pltpu.PrefetchScalarGridSpec(
+            num_scalar_prefetch=1,
+            grid=(vocab // tile,),
+            in_specs=[pl.BlockSpec((rows, LANES), lambda i, side: (0, 0))]
+            + [pl.BlockSpec(piece.shape, lambda i, side, n=piece.ndim: (0,) * n) for piece in pieces]
+            + [pl.BlockSpec((tile, depth), lambda i, side: (i, 0))],
+            out_specs=pl.BlockSpec((lines, rows), lambda i, side: (0, 0)),
+            scratch_shapes=[pltpu.VMEM((rows, depth), jnp.bfloat16)]
+            + [pltpu.VMEM((rows, LANES), jnp.float32)] * 2
+            + [pltpu.VMEM((rows, span), jnp.float32)],
+        ),
+        compiler_params=pltpu.CompilerParams(vmem_limit_bytes=28 * MIB),
         cost_estimate=pl.CostEstimate(
             flops=2 * rows * depth * vocab,
             bytes_accessed=2 * vocab * depth,
             transcendentals=2 * rows * vocab,
         ),
         name="score_part",
-    )(ids, fresh, embedding)
+    )(side, ids, *pieces, embedding)
+
+
+def draft_kernel(meta, hidden_ref, weight_ref, out_ref, padded):
+    depth = weight_ref.shape[1]
+    window = padded.shape[0]
+
+    @pl.when((pl.program_id(0) == 0) & (pl.program_id(1) == 0))
+    def _():
+        padded[...] = jnp.zeros_like(padded)
+
+    padded[pl.ds(pl.multiple_of(meta[1], 16), depth), :] = weight_ref[0]
+    columns = hidden_ref[:, pl.ds(pl.multiple_of(meta[0], LANES), window)]
+    partial = jnp.dot(columns, padded[...], preferred_element_type=jnp.float32)
+    out_ref[0] = partial.astype(jnp.bfloat16)
+
+
+def draft_part(hidden, medusa_w, blk):
+    rows, model = hidden.shape
+    depth, units = medusa_w.shape[1:]
+    half = units // 2
+    window = -(-depth // LANES) * LANES + LANES
+    start = blk * depth
+    first = jnp.minimum(start // LANES * LANES, model - window)
+    meta = jnp.stack([first, start - first])
+    return pl.pallas_call(
+        draft_kernel,
+        out_shape=jax.ShapeDtypeStruct((4, rows, half), jnp.bfloat16),
+        grid_spec=pltpu.PrefetchScalarGridSpec(
+            num_scalar_prefetch=1,
+            grid=(2, 2),
+            in_specs=[
+                pl.BlockSpec((rows, model), lambda m, c, meta: (0, 0)),
+                pl.BlockSpec((1, depth, half), lambda m, c, meta: (m, 0, c)),
+            ],
+            out_specs=pl.BlockSpec((1, rows, half), lambda m, c, meta: (m * 2 + c, 0, 0)),
+            scratch_shapes=[pltpu.VMEM((window, half), jnp.bfloat16)],
+        ),
+        compiler_params=pltpu.CompilerParams(vmem_limit_bytes=16 * MIB),
+        name="draft_part",
+    )(meta, hidden, medusa_w)
+
+
+def in_vmem(kernel, name, out_shape, args, scratch=()):
+    spec = pl.BlockSpec(memory_space=pltpu.VMEM)
+    return pl.pallas_call(
+        kernel,
+        out_shape=out_shape,
+        in_specs=[spec] * len(args),
+        out_specs=spec,
+        scratch_shapes=scratch,
+        compiler_params=pltpu.CompilerParams(vmem_limit_bytes=16 * MIB),
+        name=name,
+    )(*args)
+
+
+def fold_kernel(got_ref, out_ref, hold):
+    hold[...] = sum(got_ref[k].astype(jnp.float32) for k in range(got_ref.shape[0]))
+    height = out_ref.shape[1]
+    for j in range(out_ref.shape[0]):
+        out_ref[j] = hold[j * height : (j + 1) * height].astype(jnp.bfloat16)
+
+
+def silu_kernel(got_ref, base_ref, out_ref):
+    inner = sum(got_ref[k].astype(jnp.float32) for k in range(got_ref.shape[0]))
+    fresh = base_ref[...].astype(jnp.float32) + inner / (1.0 + jnp.exp(-inner))
+    for k in range(out_ref.shape[0]):
+        out_ref[k] = fresh.astype(jnp.bfloat16)
+
+
+def stack_kernel(got_ref, out_ref, hold):
+    height = got_ref.shape[1]
+    for j in range(got_ref.shape[0]):
+        hold[j * height : (j + 1) * height, :] = got_ref[j].astype(jnp.float32)
+    for k in range(out_ref.shape[0]):
+        out_ref[k] = hold[...].astype(jnp.bfloat16)
+
+
+PLANE = 4
+
+
+def plane_groups(blocks):
+    return [[base + k for k in range(PLANE)] for base in range(0, blocks, PLANE)]
+
+
+def layer_groups(blocks):
+    return [[base + k for k in range(0, blocks, PLANE)] for base in range(PLANE)]
+
+
+def exchange(value, axis, groups=None):
+    return lax.all_to_all(value, axis, 0, 0, axis_index_groups=groups, tiled=True)
+
+
+def group_sum(value, axis, size, groups=None):
+    if size == 2 and groups is None:
+        return value + lax.ppermute(value, axis, [(0, 1), (1, 0)])
+    return jnp.sum(exchange(jnp.broadcast_to(value[None], (size,) + value.shape), axis, groups), 0)
+
+
+def fresh_by_stages(hidden, parts, units, blocks, blk, mp):
+    rows = hidden.shape[0]
+    half = units // 2
+    layers = blocks // PLANE
+    height = rows // layers
+    planes, columns = plane_groups(blocks), layer_groups(blocks)
+    quads = jax.ShapeDtypeStruct((PLANE, rows, half), jnp.bfloat16)
+    chunks = jax.ShapeDtypeStruct((layers, height, half), jnp.bfloat16)
+    hold = [pltpu.VMEM((rows, half), jnp.float32)]
+    base = lax.dynamic_slice(
+        hidden, (blk // PLANE * height, mp * units + (blk & 1) * half), (height, half)
+    )
+    got = exchange(parts, "blk", planes)
+    got = exchange(in_vmem(fold_kernel, "fold_part", chunks, [got], hold), "blk", columns)
+    got = exchange(in_vmem(silu_kernel, "silu_part", chunks, [got, base]), "blk", columns)
+    got = exchange(in_vmem(stack_kernel, "stack_part", quads, [got], hold), "blk", planes)
+    other = lax.ppermute(got, "mp", [(0, 1), (1, 0)])
+    return [got, other]
+
+
+def fresh_by_collectives(hidden, medusa_w, blocks, blk, mp):
+    drafts, depth, units = medusa_w.shape
+    rows = hidden.shape[0]
+    own = drafts * rows // blocks
+    hidden_cols = lax.dynamic_slice_in_dim(hidden, blk * depth, depth, 1)
+    partial = jnp.einsum("rd,mdu->mru", hidden_cols, medusa_w, preferred_element_type=jnp.float32)
+    partial = partial.reshape(blocks, own, units).astype(jnp.bfloat16)
+    inner = lax.psum_scatter(partial, "blk", scatter_dimension=0).astype(jnp.float32)
+    base = lax.dynamic_slice(hidden, ((blk * own) % rows, mp * units), (own, units))
+    fresh = (base.astype(jnp.float32) + jax.nn.silu(inner)).astype(jnp.bfloat16)
+    fresh = lax.all_gather(fresh, "blk", axis=0, tiled=True)
+    return [lax.all_gather(fresh, "mp", axis=1, tiled=True)]
 
 
 def ancestry(parents):
@@ -247,38 +421,29 @@
     drafts, depth, units = medusa_w.shape
     rows, model = hidden.shape
     lines = drafts * rows
-    own = lines // blocks
-
-    hidden_cols = lax.dynamic_slice_in_dim(hidden, blk * depth, depth, 1)
-    partial = jnp.einsum("rd,mdu->mru", hidden_cols, medusa_w, preferred_element_type=jnp.float32)
-    partial = partial.reshape(blocks, own, units).astype(jnp.bfloat16)
-    inner = lax.psum_scatter(partial, "blk", scatter_dimension=0).astype(jnp.float32)
-    base = lax.dynamic_slice(hidden, ((blk * own) % rows, mp * units), (own, units))
-    fresh = (base.astype(jnp.float32) + jax.nn.silu(inner)).astype(jnp.bfloat16)
-    fresh = lax.all_gather(fresh, "blk", axis=0, tiled=True)
-    fresh = lax.all_gather(fresh, "mp", axis=1, tiled=True)
 
     groups, tree_size, features = tree_q.shape
     width = features // blocks
     meta = jnp.concatenate([block_group, block_len, block_empty])
+
+    if splits == 2 and blocks % PLANE == 0 and units % 256 == 0 and drafts == 2:
+        parts = draft_part(hidden, medusa_w, blk)
+        parts, meta = lax.optimization_barrier((parts, meta))
+        pieces = fresh_by_stages(hidden, parts, units, blocks, blk, mp)
+    else:
+        pieces = fresh_by_collectives(hidden, medusa_w, blocks, blk, mp)
+
     sent = prompt_part(tree_q, prompt_key_value, meta, width, blocks)
-    got = lax.all_to_all(sent, "blk", 0, 0, tiled=True)
-
-    repeats = features // tree_key_value.shape[3]
-    column = blk * width
-    head = column // HEAD_SIZE
-    kv_head = head // repeats
-    queries = lax.dynamic_slice_in_dim(tree_q, head * HEAD_SIZE, HEAD_SIZE, 2)
-    keys = lax.dynamic_slice_in_dim(tree_key_value[0], kv_head * HEAD_SIZE, HEAD_SIZE, 2)
-    values = lax.dynamic_slice_in_dim(
-        tree_key_value[1], kv_head * HEAD_SIZE + column % HEAD_SIZE, width, 2
+    got = exchange(sent, "blk")
+    tree_numer, tree_denom = tree_part(
+        tree_q, tree_key_value, ancestry(parents), blk * width, width
     )
-    tree_numer, tree_denom = tree_part(queries, keys, values, ancestry(parents))
-    heads_out = merge_part(got, tree_numer, tree_denom)
-    heads_out = lax.all_to_all(heads_out, "blk", 0, 0, tiled=True)
+    heads_out = exchange(merge_part(got, tree_numer, tree_denom), "blk")
     tokens = heads_out.shape[1]
     heads_out = heads_out.transpose(1, 0, 2).reshape(tokens, features)
-    attn = swap_sum(jnp.dot(heads_out, out_weight, preferred_element_type=jnp.float32), "mp", splits)
+    attn = jnp.dot(heads_out, out_weight, preferred_element_type=jnp.float32)
+    attn, pieces = lax.optimization_barrier((attn, pieces))
+    attn = group_sum(attn, "mp", splits)
     normed = attn * lax.rsqrt(jnp.mean(attn * attn, -1, keepdims=True) + 1e-06) * post_gain
     layer_out = (normed + resid.astype(jnp.float32)).astype(jnp.bfloat16)
 
@@ -286,13 +451,12 @@
     picks = cand_ids.shape[2]
     ids = cand_ids.reshape(lines, picks) - (blk * splits + mp) * vocab
     ids = jnp.pad(ids, ((0, 0), (0, LANES - picks)), constant_values=-1)
-    score = score_part(fresh, embedding, ids, picks)
-    payload = score[:, : picks + 1].T.reshape(-1)
-    payload = jnp.pad(payload, (0, -payload.shape[0] % 1024)).reshape(-1, LANES)
-    spread = jnp.broadcast_to(payload[None], (blocks * splits,) + payload.shape)
-    score = jnp.sum(lax.all_to_all(spread, ("blk", "mp"), 0, 0, tiled=True), 0)
-    score = score.reshape(-1)[: (picks + 1) * lines].reshape(picks + 1, lines)
-    draft_logprob = (score[:picks] - jnp.log(score[picks:])).T.reshape(drafts, rows, picks)
+    score = score_part(mp.reshape(1), pieces, embedding, ids, picks)
+    score = group_sum(score, "mp", splits)
+    score = group_sum(score, "blk", PLANE, plane_groups(blocks))
+    score = group_sum(score, "blk", blocks // PLANE, layer_groups(blocks))
+    draft_logprob = score[:picks] - jnp.log(score[picks : picks + 1])
+    draft_logprob = draft_logprob.T.reshape(drafts, rows, picks)
     return (draft_logprob, layer_out)
 
 

time: 260 us -> 142 us (0.55)
  waiting for transfers between devices: 121 us -> 22 us
  blocking collectives: 58.1 us -> 34.6 us
  between operations: 16.4 us -> 2.9 us
  starting transfers between devices: 11 us -> 23.8 us
  Pallas kernels: 23.7 us -> 28.9 us
    reduce_scatter x1 -> x0, waiting for transfers between devices: 105 us -> none  [per_device(): lax.psum_scatter(partial, 'blk', scatter_dimension=0).astype(jnp.float32)]
    all_gather x1 -> x0, blocking collectives: 47.6 us -> none  [per_device(): fresh = lax.all_gather(fresh, 'blk', axis=0, tiled=True)]
    all_to_all x1 -> x3, blocking collectives: 10.5 us -> 34.6 us  [exchange(): lax.all_to_all(value, axis, 0, 0, axis_index_groups=groups, tiled=True)]
    all_to_all x2 -> x5, starting transfers between devices: 10.9 us -> 23.1 us  [exchange(): lax.all_to_all(value, axis, 0, 0, axis_index_groups=groups, tiled=True)]
    all_to_all x2 -> x5, waiting for transfers between devices: 14.6 us -> 21.3 us  [exchange(): lax.all_to_all(value, axis, 0, 0, axis_index_groups=groups, tiled=True)]
    unnamed x21 -> x28, local copies, waits for them, and re-layouts: 7.58 us -> 13 us
    pallas_call x0 -> x4, Pallas kernels: none -> 4.11 us  [the longest x1 2.26 us: draft_part(): pl.pallas_call(draft_kernel, out_shape=jax.ShapeDtypeStruct((4, rows, hal...]
    slice x3 -> x0, local copies, waits for them, and re-layouts: 3.45 us -> none  [the longest x1 3.37 us: per_device(): tree_key_value[1]]
  transfers between devices with their start and end apart: 5 -> 8, of which waited for: 3 -> 4; matrix products, arithmetic and copies ran while one was open for 7% -> 10% of each run, Pallas kernels for 3% -> 6%
where the time goes in v3:
time: 142 us; the launch traced here: 141 us
  blocking collectives  34.6 us (24%)
  Pallas kernels  28.9 us (20%)
  starting transfers between devices  23.8 us (17%)
  waiting for transfers between devices  22 us (15%)
  local copies, waits for them, and re-layouts  14.9 us (10%)
  matrix products  11.8 us (8%)
  between operations  2.9 us (2%)
  other arithmetic  2.08 us (1%)
    all_to_all x3, blocking collectives, exchange(): lax.all_to_all(value, axis, 0, 0, axis_index_groups=groups, tiled=True)  34.6 us
    all_to_all x5, starting transfers between devices, exchange(): lax.all_to_all(value, axis, 0, 0, axis_index_groups=groups, tiled=True)  23.1 us
    all_to_all x5, waiting for transfers between devices, exchange(): lax.all_to_all(value, axis, 0, 0, axis_index_groups=groups, tiled=True)  21.3 us
    pallas_call x1, Pallas kernels, score_part(): pl.pallas_call(functools.partial(score_kernel, picks), out_shape=jax.Shap...  16.3 us
    unnamed x28, local copies, waits for them, and re-layouts  13 us
    dot_general x1, matrix products, per_device(): attn = jnp.dot(heads_out, out_weight, preferred_element_type=jnp.float32)  7.73 us
    pallas_call x1, Pallas kernels, prompt_part(): pl.pallas_call(functools.partial(prompt_kernel, tree_size, repeats, width...  5.34 us
    dot_general x3, matrix products, ancestry(): jnp.einsum('gij,gjk->gik', reach, reach, preferred_element_type=jnp.float32)  4.09 us
  transfers between devices with their start and end apart: 8, of which 4 were waited for; matrix products, arithmetic and copies ran while one was open for 10% of the time, Pallas kernels for 6%

profile of v3, /device:TPU:0, one launch (start us, length us, event | category | flops | bytes accessed | tf_op | source)
XLA Modules:
  0.0 140.9 jit_solution(10990296462728789654)
XLA Ops:
  2.6 0.1 pad_add_fusion.meta
  2.7 1.4 %copy-done.5 = bf16[2,224,1792]{2,1,0:T(8,128)(2,1)S(1)} copy-done((bf16[2,224,1792]{2,1,0:T(8,128)(2,1)S(1)}, bf16[2,224,1792]{2,1,0:T(8,128)(2,1)}, u32[]{:S(2)}) %copy-start.5) | copy-done | bytes 1605656
  4.1 1.2 copy-done.6
  5.3 2.3 %draft_part.1 = bf16[4,144,896]{2,1,0:T(8,128)(2,1)S(1)} custom-call(s32[2]{0:T(128)S(1)} %pad_add_fusion.meta, bf16[144,3584]{1,0:T(8,128)(2,1)S(1)} %copy-done.6, bf16[2,224,1792]{2,1,0:T(8,128)(2,1)S(1)} %copy-done.5), custom_call_target="tpu_custom_call" | custom-call | tf_op jit(solution)/shard_map/draft_part/pallas_call | solution.py:284
  7.6 0.0 copy-start.12
  7.6 0.1 pad_add_fusion.1.meta
  7.7 19.0 %all_to_all.40.got_ref = bf16[4,144,896]{2,1,0:T(8,128)(2,1)S(1)} all-to-all(bf16[4,144,896]{2,1,0:T(8,128)(2,1)S(1)} %draft_part.1), channel_id=1, replica_groups={{0,2,4,6},{8,10,12,14},{16,18,20,22},{24,26,28,30},{1,3,5,7},{9,11,13,1..., dimensions={0} | all-to-all | bytes 2064384 | tf_op jit(solution)/shard_map/all_to_all | solution.py:349
  26.6 0.9 fold_part.1
  27.6 4.9 %all-to-all-start.3 = ((bf16[4,36,896]{2,1,0:T(8,128)(2,1)}), bf16[4,36,896]{2,1,0:T(8,128)(2,1)S(1)}, u32[]{:S(2)}, u32[]{:S(2)}) async-start(bf16[4,36,896]{2,1,0:T(8,128)(2,1)} %fold_part.1), calls=%async_computation.3 | async-start | bytes 573440 | tf_op jit(solution)/shard_map/all_to_all | solution.py:349
  32.4 1.0 dynamic_slice.3.base_ref
  33.4 7.0 %all-to-all-done.3.got_ref = bf16[4,36,896]{2,1,0:T(8,128)(2,1)S(1)} async-done(((bf16[4,36,896]{2,1,0:T(8,128)(2,1)}), bf16[4,36,896]{2,1,0:T(8,128)(2,1)S(1)}, u32[]{:S(2)}, u32[]{:S(2)}) %all-to-all-start.3) | async-done | bytes 258080 | tf_op jit(solution)/shard_map/all_to_all | solution.py:349
  40.4 0.8 silu_part.1
  41.2 3.5 %all-to-all-start.4 = ((bf16[4,36,896]{2,1,0:T(8,128)(2,1)}), bf16[4,36,896]{2,1,0:T(8,128)(2,1)S(1)}, u32[]{:S(2)}, u32[]{:S(2)}) async-start(bf16[4,36,896]{2,1,0:T(8,128)(2,1)} %silu_part.1), calls=%async_computation.4 | async-start | bytes 573440 | tf_op jit(solution)/shard_map/all_to_all | solution.py:349
  44.7 3.4 %copy-done = bf16[2,1,2048,1024]{3,2,1,0:T(8,128)(2,1)S(1)} copy-done((bf16[2,1,2048,1024]{3,2,1,0:T(8,128)(2,1)S(1)}, bf16[2,1,2048,1024]{3,2,1,0:T(8,128)(2,1)}, u32[]{:S(2)}) %copy-start) | copy-done | bytes 8388632
  48.1 1.7 %copy-done.1 = bf16[12,48,2048]{2,1,0:T(8,128)(2,1)S(1)} copy-done((bf16[12,48,2048]{2,1,0:T(8,128)(2,1)S(1)}, bf16[12,48,2048]{2,1,0:T(8,128)(2,1)}, u32[]{:S(2)}) %copy-start.1) | copy-done | bytes 2359320
  49.7 5.3 %prompt_part.1 = bf16[16,64,128]{2,1,0:T(8,128)(2,1)} custom-call(s32[3]{0:T(128)S(1)} %pad_add_fusion.1.meta, bf16[12,48,2048]{2,1,0:T(8,128)(2,1)S(1)} %copy-done.1, bf16[2,1,2048,1024]{3,2,1,0:T(8,128)(2,1)S(1)} %copy-done, bf16[2,1,2048,1024]{3,2,1,0:T(8,128)(2,1)S(1)} %copy-done), custom_call_target="tpu_custom_call" | custom-call | flops 805306368 | bytes 8388608 | tf_op jit(solution)/shard_map/prompt_part/pallas_call | solution.py:66
  55.1 5.8 %all-to-all-start = ((bf16[16,64,128]{2,1,0:T(8,128)(2,1)}), bf16[16,64,128]{2,1,0:T(8,128)(2,1)S(1)}, u32[]{:S(2)}, u32[]{:S(2)}) async-start(bf16[16,64,128]{2,1,0:T(8,128)(2,1)} %prompt_part.1), calls=%async_computation | async-start | bytes 524288 | tf_op jit(solution)/shard_map/all_to_all | solution.py:349
  61.0 0.1 stack_part.1
  61.1 1.0 copy-done.4
  62.1 7.3 %all-to-all-done.got_ref = bf16[16,64,128]{2,1,0:T(8,128)(2,1)S(1)} async-done(((bf16[16,64,128]{2,1,0:T(8,128)(2,1)}), bf16[16,64,128]{2,1,0:T(8,128)(2,1)S(1)}, u32[]{:S(2)}, u32[]{:S(2)}) %all-to-all-start) | async-done | bytes 262176 | tf_op jit(solution)/shard_map/all_to_all | solution.py:349
  69.4 0.7 copy-done.8
  70.1 3.5 %all-to-all-start.5 = ((bf16[4,144,896]{2,1,0:T(8,128)(2,1)}), bf16[4,144,896]{2,1,0:T(8,128)(2,1)S(1)}, u32[]{:S(2)}, u32[]{:S(2)}) async-start(bf16[4,144,896]{2,1,0:T(8,128)(2,1)} %copy-done.4), calls=%async_computation.5 | async-start | bytes 2064384 | tf_op jit(solution)/shard_map/all_to_all | solution.py:349
  73.6 0.1 pad_add_fusion.2.meta
  73.7 1.3 fusion.1
  75.1 1.6 %fusion.3 = bf16[12,48,48]{2,1,0:T(8,128)(2,1)S(1)} fusion(bf16[12,48,48]{2,1,0:T(8,128)(2,1)} %fusion.1), kind=kOutput, calls=%fused_computation.9 | convolution fusion | flops 5419008 | bytes 110592 | tf_op jit(solution)/shard_map/gij,gjk->gik/dot_general | solution.py:398
  76.7 1.2 fusion.6.reach_ref
  77.8 1.7 %copy-done.3 = bf16[2,12,48,1024]{3,2,1,0:T(8,128)(2,1)S(1)} copy-done((bf16[2,12,48,1024]{3,2,1,0:T(8,128)(2,1)S(1)}, bf16[2,12,48,1024]{3,2,1,0:T(8,128)(2,1)}, u32[]{:S(2)}) %copy-start.3) | copy-done | bytes 2359320
  79.5 1.0 copy-done.7
  80.5 1.1 tree_part.1
  81.5 0.0 copy-start.9
  81.6 0.9 copy-done.9
  82.5 2.1 %merge_part.1 = bf16[16,36,128]{2,1,0:T(8,128)(2,1)} custom-call(bf16[16,64,128]{2,1,0:T(8,128)(2,1)S(1)} %copy-done.9, f32[12,48,128]{2,1,0:T(8,128)S(1)} %get-tuple-element.10.numer_ref, f32[12,48,128]{2,1,0:T(8,128)S(1)} %get-tuple-element.11.denom_ref), custom_call_target="tpu_custom_call" | custom-call | tf_op jit(solution)/shard_map/merge_part/pallas_call | solution.py:166
  84.6 5.5 %all-to-all-start.1 = ((bf16[16,36,128]{2,1,0:T(8,128)(2,1)}), bf16[16,36,128]{2,1,0:T(8,128)(2,1)S(1)}, u32[]{:S(2)}, u32[]{:S(2)}) async-start(bf16[16,36,128]{2,1,0:T(8,128)(2,1)} %merge_part.1), calls=%async_computation.1 | async-start | bytes 327680 | tf_op jit(solution)/shard_map/all_to_all | solution.py:349
  90.1 0.1 collective-permute-start
  90.1 0.7 broadcast_subtract_fusion
  90.9 0.1 copy.19
  91.0 7.0 %all-to-all-done.1 = bf16[16,36,128]{2,1,0:T(8,128)(2,1)S(1)} async-done(((bf16[16,36,128]{2,1,0:T(8,128)(2,1)}), bf16[16,36,128]{2,1,0:T(8,128)(2,1)S(1)}, u32[]{:S(2)}, u32[]{:S(2)}) %all-to-all-start.1) | async-done | bytes 147488 | tf_op jit(solution)/shard_map/all_to_all | solution.py:349
  98.1 7.7 %fusion.27 = f32[36,3584]{1,0:T(8,128)S(1)} fusion(bf16[36,2048]{1,0:T(8,128)(2,1)S(1)} %bitcast.21, bf16[2048,3584]{1,0:T(8,128)(2,1)} %param.25), kind=kOutput, calls=%fused_computation.40 | convolution fusion | flops 528482304 | bytes 15343616 | tf_op jit(solution)/shard_map/dot_general | solution.py:444
  105.8 0.0 collective-permute-done.refs_1_
  105.9 16.3 %score_part.1 = f32[16,288]{1,0:T(8,128)S(1)} custom-call(s32[1]{0:T(128)} %bitcast.side, s32[288,128]{1,0:T(8,128)S(1)} %pad.4.ids_ref, bf16[4,144,896]{2,1,0:T(8,128)(2,1)S(1)} %all-to-all-done.5.refs_0_, bf16[4,144,896]{2,1,0:T(8,128)(2,1)S(1)} %collective-permute-done.refs_1_, bf16[4096,3584]{1,0:T(8,128)(2,1)} %refs_2_.1), custom_call_target="tpu_custom_call" | custom-call | flops 8455716864 | bytes 29360128 | tf_op jit(solution)/shard_map/score_part/pallas_call | solution.py:238
  122.2 0.1 collective-permute-start.1
  122.2 0.5 collective-permute-start.2
  122.7 0.7 collective-permute-done.1
  123.4 7.3 %all_to_all.41 = f32[4,16,288]{2,1,0:T(8,128)S(1)} all-to-all(f32[4,16,288]{2,1,0:T(8,128)S(1)} %broadcast_in_dim.4), channel_id=1, replica_groups={{0,2,4,6},{8,10,12,14},{16,18,20,22},{24,26,28,30},{1,3,5,7},{9,11,13,1..., dimensions={0} | all-to-all | bytes 147456 | tf_op jit(solution)/shard_map/all_to_all | solution.py:349
  130.8 8.3 %all_to_all.42 = f32[4,16,288]{2,1,0:T(8,128)S(1)} all-to-all(f32[4,16,288]{2,1,0:T(8,128)S(1)} %broadcast_in_dim.5), channel_id=1, replica_groups={{0,8,16,24},{2,10,18,26},{4,12,20,28},{6,14,22,30},{1,9,17,25},{3,11,19..., dimensions={0} | all-to-all | bytes 147456 | tf_op jit(solution)/shard_map/all_to_all | solution.py:349
  139.2 0.7 reshape.43
  139.9 0.2 multiply_reduce_fusion
  140.1 0.9 add_convert_fusion
  (32 shorter events, 0.2 us)
Async XLA Ops:
  2.7 1.4 %copy-start.5 = (bf16[2,224,1792]{2,1,0:T(8,128)(2,1)S(1)}, bf16[2,224,1792]{2,1,0:T(8,128)(2,1)}, u32[]{:S(2)}) copy-start(bf16[2,224,1792]{2,1,0:T(8,128)(2,1)} %weight_ref.1) | copy-start | bytes 4816900
  4.1 1.2 copy-start.6
  7.6 66.2 %copy-start.12 = (s32[12,48]{1,0:T(8,128)S(1)}, s32[12,48]{1,0:T(8,128)}, u32[]{:S(2)}) copy-start(s32[12,48]{1,0:T(8,128)} %param.24) | copy-start | bytes 6916
  26.6 51.2 %copy-start.2 = (bf16[12,48,2048]{2,1,0:T(8,128)(2,1)S(1)}, bf16[12,48,2048]{2,1,0:T(8,128)(2,1)}, u32[]{:S(2)}) copy-start(bf16[12,48,2048]{2,1,0:T(8,128)(2,1)} %q_ref.3) | copy-start | bytes 7077892
  27.6 12.9 %all-to-all-start.3 = ((bf16[4,36,896]{2,1,0:T(8,128)(2,1)}), bf16[4,36,896]{2,1,0:T(8,128)(2,1)S(1)}, u32[]{:S(2)}, u32[]{:S(2)}) async-start(bf16[4,36,896]{2,1,0:T(8,128)(2,1)} %fold_part.1), calls=%async_computation.3 | async-start | bytes 573440 | tf_op jit(solution)/shard_map/all_to_all | solution.py:349
  41.2 13.9 %all-to-all-start.4 = ((bf16[4,36,896]{2,1,0:T(8,128)(2,1)}), bf16[4,36,896]{2,1,0:T(8,128)(2,1)S(1)}, u32[]{:S(2)}, u32[]{:S(2)}) async-start(bf16[4,36,896]{2,1,0:T(8,128)(2,1)} %silu_part.1), calls=%async_computation.4 | async-start | bytes 573440 | tf_op jit(solution)/shard_map/all_to_all | solution.py:349
  44.7 3.4 %copy-start = (bf16[2,1,2048,1024]{3,2,1,0:T(8,128)(2,1)S(1)}, bf16[2,1,2048,1024]{3,2,1,0:T(8,128)(2,1)}, u32[]{:S(2)}) copy-start(bf16[2,1,2048,1024]{3,2,1,0:T(8,128)(2,1)} %v_ref.2) | copy-start | bytes 25165828
  48.1 1.7 %copy-start.1 = (bf16[12,48,2048]{2,1,0:T(8,128)(2,1)S(1)}, bf16[12,48,2048]{2,1,0:T(8,128)(2,1)}, u32[]{:S(2)}) copy-start(bf16[12,48,2048]{2,1,0:T(8,128)(2,1)} %q_ref.3) | copy-start | bytes 7077892
  55.1 14.3 %all-to-all-start = ((bf16[16,64,128]{2,1,0:T(8,128)(2,1)}), bf16[16,64,128]{2,1,0:T(8,128)(2,1)S(1)}, u32[]{:S(2)}, u32[]{:S(2)}) async-start(bf16[16,64,128]{2,1,0:T(8,128)(2,1)} %prompt_part.1), calls=%async_computation | async-start | bytes 524288 | tf_op jit(solution)/shard_map/all_to_all | solution.py:349
  61.1 1.0 copy-start.4
  69.4 0.7 copy-start.8
  70.1 14.4 %all-to-all-start.5 = ((bf16[4,144,896]{2,1,0:T(8,128)(2,1)}), bf16[4,144,896]{2,1,0:T(8,128)(2,1)S(1)}, u32[]{:S(2)}, u32[]{:S(2)}) async-start(bf16[4,144,896]{2,1,0:T(8,128)(2,1)} %copy-done.4), calls=%async_computation.5 | async-start | bytes 2064384 | tf_op jit(solution)/shard_map/all_to_all | solution.py:349
  77.8 1.7 %copy-start.3 = (bf16[2,12,48,1024]{3,2,1,0:T(8,128)(2,1)S(1)}, bf16[2,12,48,1024]{3,2,1,0:T(8,128)(2,1)}, u32[]{:S(2)}) copy-start(bf16[2,12,48,1024]{3,2,1,0:T(8,128)(2,1)} %v_ref.3) | copy-start | bytes 7077892
  79.5 1.0 copy-start.7
  81.5 1.0 copy-start.9
  84.6 13.4 %all-to-all-start.1 = ((bf16[16,36,128]{2,1,0:T(8,128)(2,1)}), bf16[16,36,128]{2,1,0:T(8,128)(2,1)S(1)}, u32[]{:S(2)}, u32[]{:S(2)}) async-start(bf16[16,36,128]{2,1,0:T(8,128)(2,1)} %merge_part.1), calls=%async_computation.1 | async-start | bytes 327680 | tf_op jit(solution)/shard_map/all_to_all | solution.py:349
  90.1 15.8 %collective-permute-start = (bf16[4,144,896]{2,1,0:T(8,128)(2,1)S(1)}, bf16[4,144,896]{2,1,0:T(8,128)(2,1)S(1)}, u32[]{:S(2)}, u32[]{:S(2)}) collective-permute-start(bf16[4,144,896]{2,1,0:T(8,128)(2,1)S(1)} %all-to-all-done.5.refs_0_), channel_id=1, source_target_pairs={{0,1},{1,0},{2,3},{3,2},{4,5},{5,4},{6,7},{7,6},{8,9},{9,8},{10,11... | collective-permute-start | bytes 3096584 | tf_op jit(solution)/shard_map/ppermute | solution.py:374
  105.8 34.2 %copy-start.10 = (bf16[36,3584]{1,0:T(8,128)(2,1)S(1)}, bf16[36,3584]{1,0:T(8,128)(2,1)}, u32[]{:S(2)}) copy-start(bf16[36,3584]{1,0:T(8,128)(2,1)} %param.27) | copy-start | bytes 774148
  105.8 34.2 %copy-start.11 = (f32[3584]{0:T(1024)S(1)}, f32[3584]{0:T(1024)}, u32[]{:S(2)}) copy-start(f32[3584]{0:T(1024)} %param.26) | copy-start | bytes 43012
  122.2 1.3 collective-permute-start.1
  122.2 17.6 %collective-permute-start.2 = (f32[36,3584]{1,0:T(8,128)S(1)}, f32[36,3584]{1,0:T(8,128)S(1)}, u32[]{:S(2)}, u32[]{:S(2)}) collective-permute-start(f32[36,3584]{1,0:T(8,128)S(1)} %fusion.27), channel_id=1, source_target_pairs={{0,1},{1,0},{2,3},{3,2},{4,5},{5,4},{6,7},{7,6},{8,9},{9,8},{10,11... | collective-permute-start | bytes 1548296 | tf_op jit(solution)/shard_map/ppermute | solution.py:354

commit v4 on v2

v4 whole, which is shorter than its diff:
```python
import functools

import jax
import jax.numpy as jnp
from jax import lax
from jax.experimental import pallas as pl
from jax.experimental.pallas import tpu as pltpu
from jax.sharding import PartitionSpec as P

HEAD_SIZE = 256
LANES = 128
MIB = 1 << 20

EXTRA = 16
HIGH, LOW, GROUP = 0, 4, 8


def soft_weights(scores):
    return jnp.exp(50.0 * jnp.tanh(scores * (HEAD_SIZE**-0.5 / 50.0)))


def dot_t(left, right):
    return lax.dot_general(left, right, (((1,), (1,)), ((), ())), preferred_element_type=jnp.float32)


def in_hbm():
    return pl.BlockSpec(memory_space=pltpu.HBM)


def pin(value):
    return pltpu.with_memory_space_constraint(value, pltpu.HBM)


def in_vmem():
    return pl.BlockSpec(memory_space=pltpu.VMEM)


def in_smem():
    return pl.BlockSpec(memory_space=pltpu.SMEM)


def limit(mib):
    return pltpu.CompilerParams(vmem_limit_bytes=mib * MIB)


def prompt_kernel(meta, q_hbm, kv_hbm, out_ref, queries, held, sems):
    group, used, empty = meta[0], meta[1], meta[2]
    last = jnp.where(empty == 0, used, 0)
    kv_heads, slots = held.shape[1:3]
    tree_size, features = queries.shape
    repeats = features // HEAD_SIZE // kv_heads
    width = out_ref.shape[2]
    rows = tree_size * repeats
    ask = pltpu.make_async_copy(q_hbm.at[group], queries, sems.at[2 * kv_heads])
    ask.start()
    copies = []
    for h in range(kv_heads):
        for s in range(2):
            columns = pl.ds(h * HEAD_SIZE, HEAD_SIZE)
            copies.append(
                pltpu.make_async_copy(
                    kv_hbm.at[s, 0, :, columns], held.at[s, h], sems.at[2 * h + s]
                )
            )
            copies[-1].start()
    ask.wait()
    per_head = HEAD_SIZE // width
    row_id = lax.broadcasted_iota(jnp.int32, (tree_size, width), 0)
    lane_id = lax.broadcasted_iota(jnp.int32, (tree_size, width), 1)
    extra_id = lax.broadcasted_iota(jnp.int32, (EXTRA, width), 0)
    slot = lax.broadcasted_iota(jnp.int32, (rows, slots), 1)
    for h in range(kv_heads):
        asked = jnp.concatenate(
            [
                queries[:, (h * repeats + r) * HEAD_SIZE : (h * repeats + r + 1) * HEAD_SIZE]
                for r in range(repeats)
            ],
            axis=0,
        )
        copies[2 * h].wait()
        scores = dot_t(asked, held[0, h])
        weights = jnp.where(slot < last, soft_weights(scores), 0.0)
        denom = jnp.sum(weights, axis=1, keepdims=True)
        copies[2 * h + 1].wait()
        numer = jnp.dot(
            weights.astype(jnp.bfloat16), held[1, h], preferred_element_type=jnp.float32
        )
        for r in range(repeats):
            mine = jnp.broadcast_to(denom[r * tree_size : (r + 1) * tree_size], (tree_size, width))
            extra = jnp.where(extra_id == GROUP, group.astype(jnp.float32), 0.0)
            for c in range(-(-tree_size // width)):
                line = jnp.sum(
                    jnp.where(row_id == lane_id + c * width, mine, 0.0), axis=0, keepdims=True
                )
                high = line.astype(jnp.bfloat16).astype(jnp.float32)
                extra = jnp.where(extra_id == HIGH + c, high, extra)
                extra = jnp.where(extra_id == LOW + c, line - high, extra)
            for part in range(per_head):
                d = (h * repeats + r) * per_head + part
                out_ref[d, :tree_size, :] = numer[
                    r * tree_size : (r + 1) * tree_size, part * width : (part + 1) * width
                ].astype(jnp.bfloat16)
                out_ref[d, tree_size:, :] = extra.astype(jnp.bfloat16)


def prompt_part(tree_q, prompt_key_value, meta, width, blocks):
    groups, tree_size, features = tree_q.shape
    slots, key_features = prompt_key_value.shape[2:]
    kv_heads = key_features // HEAD_SIZE
    return pl.pallas_call(
        prompt_kernel,
        out_shape=jax.ShapeDtypeStruct((blocks, tree_size + EXTRA, width), jnp.bfloat16),
        in_specs=[in_smem(), in_hbm(), in_hbm()],
        out_specs=in_vmem(),
        scratch_shapes=[
            pltpu.VMEM((tree_size, features), jnp.bfloat16),
            pltpu.VMEM((2, kv_heads, slots, HEAD_SIZE), jnp.bfloat16),
            pltpu.SemaphoreType.DMA((2 * kv_heads + 1,)),
        ],
        compiler_params=limit(24),
        cost_estimate=pl.CostEstimate(
            flops=4 * tree_size * features * slots,
            bytes_accessed=4 * slots * key_features,
            transcendentals=2 * tree_size * slots * features // HEAD_SIZE,
        ),
        name="prompt_part",
    )(meta, pin(tree_q), pin(prompt_key_value))


def tree_kernel(meta, q_hbm, kv_hbm, reach_ref, numer_ref, denom_ref, held, sems):
    width = numer_ref.shape[2]
    query_columns = pl.ds(pl.multiple_of(meta[0] * HEAD_SIZE, HEAD_SIZE), HEAD_SIZE)
    key_columns = pl.ds(pl.multiple_of(meta[1] * HEAD_SIZE, HEAD_SIZE), HEAD_SIZE)
    copies = [
        pltpu.make_async_copy(q_hbm.at[:, :, query_columns], held.at[0], sems.at[0]),
        pltpu.make_async_copy(kv_hbm.at[0, :, :, key_columns], held.at[1], sems.at[1]),
        pltpu.make_async_copy(kv_hbm.at[1, :, :, key_columns], held.at[2], sems.at[2]),
    ]
    for copy in copies:
        copy.start()
    for copy in copies:
        copy.wait()
    for g in range(held.shape[1]):
        weights = soft_weights(dot_t(held[0, g], held[1, g])) * reach_ref[g]
        denom_ref[g] = jnp.broadcast_to(
            jnp.sum(weights, axis=1, keepdims=True), denom_ref.shape[1:]
        )
        numer = jnp.dot(
            weights.astype(jnp.bfloat16), held[2, g], preferred_element_type=jnp.float32
        )
        mine = numer[:, :width]
        for j in range(1, HEAD_SIZE // width):
            mine = jnp.where(meta[2] == j, numer[:, j * width : (j + 1) * width], mine)
        numer_ref[g] = mine


def tree_part(tree_q, tree_key_value, reach, column, width):
    groups, tree_size, features = tree_q.shape
    repeats = features // tree_key_value.shape[3]
    head = column // HEAD_SIZE
    meta = jnp.stack([head, head // repeats, column % HEAD_SIZE // width])
    return pl.pallas_call(
        tree_kernel,
        out_shape=[jax.ShapeDtypeStruct((groups, tree_size, width), jnp.float32)] * 2,
        in_specs=[in_smem(), in_hbm(), in_hbm(), in_vmem()],
        out_specs=[in_vmem()] * 2,
        scratch_shapes=[
            pltpu.VMEM((3, groups, tree_size, HEAD_SIZE), jnp.bfloat16),
            pltpu.SemaphoreType.DMA((3,)),
        ],
        compiler_params=limit(16),
        name="tree_part",
    )(meta, pin(tree_q), pin(tree_key_value), reach)


def merge_kernel(got_ref, numer_ref, denom_ref, out_ref, hold):
    blocks = got_ref.shape[0]
    groups, tree_size, width = numer_ref.shape
    row_id = lax.broadcasted_iota(jnp.int32, (tree_size, width), 0)
    lane_id = lax.broadcasted_iota(jnp.int32, (tree_size, width), 1)
    lines = -(-tree_size // width)

    @pl.loop(0, groups)
    def _(g):
        def add(b, carry):
            numer, extra = carry
            more = got_ref[b, tree_size:, :].astype(jnp.float32)
            same = more[GROUP : GROUP + 1, :] == g.astype(jnp.float32)
            numer = numer + jnp.where(same, got_ref[b, :tree_size, :].astype(jnp.float32), 0.0)
            extra = extra + jnp.where(same, more, 0.0)
            return numer, extra

        start = (numer_ref[g], jnp.zeros((EXTRA, width), jnp.float32))
        numer, extra = lax.fori_loop(0, blocks, add, start, unroll=True)
        denom = denom_ref[g]
        for c in range(lines):
            line = extra[HIGH + c : HIGH + c + 1, :] + extra[LOW + c : LOW + c + 1, :]
            spread = jnp.where(row_id == lane_id + c * width, line, 0.0)
            denom = denom + jnp.sum(spread, axis=1, keepdims=True)
        hold[pl.ds(pl.multiple_of(g * tree_size, 8), tree_size), :] = numer / denom

    count = out_ref.shape[1]
    for d in range(out_ref.shape[0]):
        out_ref[d] = hold[d * count : (d + 1) * count, :].astype(jnp.bfloat16)


def merge_part(got, numer, denom):
    blocks, _, width = got.shape
    groups, tree_size, _ = numer.shape
    tokens = groups * tree_size
    return pl.pallas_call(
        merge_kernel,
        out_shape=jax.ShapeDtypeStruct((blocks, tokens // blocks, width), jnp.bfloat16),
        scratch_shapes=[pltpu.VMEM((tokens, width), jnp.float32)],
        compiler_params=limit(16),
        name="merge_part",
    )(got, numer, denom)


def project_kernel(heads_ref, weight_hbm, out_ref, ring, sems):
    slots, span = ring.shape[:2]
    steps = weight_hbm.shape[0] // span
    per_step = span // heads_ref.shape[2]

    def copy(i):
        return pltpu.make_async_copy(
            weight_hbm.at[i * span : (i + 1) * span], ring.at[i % slots], sems.at[i % slots]
        )

    for i in range(min(slots, steps)):
        copy(i).start()
    for i in range(steps):
        left = jnp.concatenate([heads_ref[i * per_step + j] for j in range(per_step)], axis=1)
        copy(i).wait()
        more = jnp.dot(left, ring[i % slots], preferred_element_type=jnp.float32)
        out_ref[...] = more if i == 0 else out_ref[...] + more
        if i + slots < steps:
            copy(i + slots).start()


def project_part(heads_out, out_weight):
    blocks, tokens, width = heads_out.shape
    features, model = out_weight.shape
    if width % LANES or features % HEAD_SIZE:
        flat = heads_out.transpose(1, 0, 2).reshape(tokens, features)
        return jnp.dot(flat, out_weight, preferred_element_type=jnp.float32)
    slots = 4
    return pl.pallas_call(
        project_kernel,
        out_shape=jax.ShapeDtypeStruct((tokens, model), jnp.float32),
        in_specs=[in_vmem(), in_hbm()],
        out_specs=in_vmem(),
        scratch_shapes=[
            pltpu.VMEM((slots, HEAD_SIZE, model), jnp.bfloat16),
            pltpu.SemaphoreType.DMA((slots,)),
        ],
        compiler_params=limit(20),
        cost_estimate=pl.CostEstimate(
            flops=2 * tokens * features * model,
            bytes_accessed=2 * features * model,
            transcendentals=0,
        ),
        name="project_part",
    )(heads_out, pin(out_weight))


def score_kernel(picks, places, ids_ref, *refs):
    pieces, (embed_hbm, out_ref) = refs[:-8], refs[-8:-6]
    fresh, total, picked, raw, ring, sems = refs[-6:]
    slots, span = ring.shape[:2]
    rows = fresh.shape[0]
    chunks = embed_hbm.shape[0] // span
    band = 32 if rows % 32 == 0 else rows

    def copy(c):
        start = pl.multiple_of(c * span, span)
        return pltpu.make_async_copy(
            embed_hbm.at[pl.ds(start, span)], ring.at[c % slots], sems.at[c % slots]
        )

    def product(c):
        copy(c).wait()
        return dot_t(fresh[...], ring[c % slots])

    def refill(c):
        @pl.when(c + slots < chunks)
        def _():
            copy(c + slots).start()

    def absorb(side, start, keep=None):
        for r in range(0, rows, band):
            ids = ids_ref[r : r + band] - start
            lane = ids & (LANES - 1)
            chunk = ids >> 7
            sums, found = total[r : r + band], picked[r : r + band]
            for c in range(span // LANES):
                part = raw[side, r : r + band, c * LANES : (c + 1) * LANES]
                part = jnp.tanh(part * (1.0 / 30.0))
                sums = sums + jnp.exp(30.0 * part)
                there = jnp.take_along_axis(part, lane, axis=1, mode="promise_in_bounds")
                found = found + jnp.where(chunk == c, there, 0.0)
            if keep is not None:
                sums, found = jnp.where(keep, sums, 0.0), jnp.where(keep, found, 0.0)
            total[r : r + band] = sums
            picked[r : r + band] = found

    for c in range(min(slots, chunks)):
        copy(c).start()
    raw[1] = jnp.zeros(raw.shape[1:], jnp.float32)
    total[...] = jnp.zeros_like(total)
    picked[...] = jnp.zeros_like(picked)
    for n, piece in enumerate(pieces):
        height, wide = piece.shape
        row = pl.multiple_of(places[2 * n] * height, 16)
        col = pl.multiple_of(places[2 * n + 1] * wide, LANES)
        fresh[pl.ds(row, height), pl.ds(col, wide)] = piece[...]

    @pl.loop(0, chunks // 2)
    def _(pair):
        first = 2 * pair
        more = product(first)
        absorb(1, (first - 1) * span, pair > 0)
        raw[0] = more
        refill(first)
        more = product(first + 1)
        absorb(0, first * span)
        raw[1] = more
        refill(first + 1)

    absorb(1, (chunks - 1) * span)
    place = lax.broadcasted_iota(jnp.int32, total.shape, 1)
    whole = jnp.sum(total[...], axis=1, keepdims=True)
    both = jnp.where(place < picks, 30.0 * picked[...], jnp.where(place == picks, whole, 0.0))
    out_ref[...] = both.T[: out_ref.shape[0]]


def score_part(places, pieces, embedding, ids, picks):
    rows = ids.shape[0]
    vocab, depth = embedding.shape
    span, slots = HEAD_SIZE, 4
    lines = -(-(picks + 1) // 8) * 8
    return pl.pallas_call(
        functools.partial(score_kernel, picks),
        out_shape=jax.ShapeDtypeStruct((lines, rows), jnp.float32),
        in_specs=[in_smem()] + [in_vmem()] * (1 + len(pieces)) + [in_hbm()],
        out_specs=in_vmem(),
        scratch_shapes=[
            pltpu.VMEM((rows, depth), jnp.bfloat16),
            pltpu.VMEM((rows, LANES), jnp.float32),
            pltpu.VMEM((rows, LANES), jnp.float32),
            pltpu.VMEM((2, rows, span), jnp.float32),
            pltpu.VMEM((slots, span, depth), jnp.bfloat16),
            pltpu.SemaphoreType.DMA((slots,)),
        ],
        compiler_params=limit(24),
        cost_estimate=pl.CostEstimate(
            flops=2 * rows * depth * vocab,
            bytes_accessed=2 * vocab * depth,
            transcendentals=2 * rows * vocab,
        ),
        name="score_part",
    )(places, ids, *pieces, pin(embedding))


def draft_kernel(meta, hidden_hbm, weight_hbm, *refs):
    outs, columns, padded, sems = refs[:4], *refs[4:]
    depth = weight_hbm.shape[1]
    half = padded.shape[2]
    window = padded.shape[1]
    first = pl.multiple_of(meta[0], LANES)
    ask = pltpu.make_async_copy(hidden_hbm.at[:, pl.ds(first, window)], columns, sems.at[4])
    ask.start()
    padded[...] = jnp.zeros_like(padded)
    copies = []
    for k in (1, 2, 3, 0):
        quad = meta[2 + k]
        col = pl.multiple_of((quad & 1) * half, LANES)
        copies.append(
            pltpu.make_async_copy(
                weight_hbm.at[quad >> 1, :, pl.ds(col, half)],
                padded.at[k, pl.ds(pl.multiple_of(meta[1], 16), depth)],
                sems.at[k],
            )
        )
        copies[-1].start()
    ask.wait()
    for n, k in enumerate((1, 2, 3, 0)):
        copies[n].wait()
        partial = jnp.dot(columns[...], padded[k], preferred_element_type=jnp.float32)
        outs[k][...] = partial.astype(outs[k].dtype)


def draft_part(hidden, medusa_w, blk):
    rows, model = hidden.shape
    depth, units = medusa_w.shape[1:]
    half = units // 2
    window = -(-depth // LANES) * LANES + LANES
    start = blk * depth
    first = jnp.minimum(start // LANES * LANES, model - window)
    meta = jnp.stack([first, start - first] + [(blk & 3) ^ k for k in range(4)])
    return pl.pallas_call(
        draft_kernel,
        out_shape=[
            jax.ShapeDtypeStruct((rows, half), jnp.bfloat16 if k else jnp.float32)
            for k in range(4)
        ],
        in_specs=[in_smem(), in_hbm(), in_hbm()],
        out_specs=[in_vmem()] * 4,
        scratch_shapes=[
            pltpu.VMEM((rows, window), jnp.bfloat16),
            pltpu.VMEM((4, window, half), jnp.bfloat16),
            pltpu.SemaphoreType.DMA((5,)),
        ],
        compiler_params=limit(16),
        name="draft_part",
    )(meta, pin(hidden), pin(medusa_w))


def fold_kernel(place, own_ref, *refs):
    got, outs, hold = refs[:3], refs[3:-1], refs[-1]
    total = own_ref[...]
    for one in got:
        total = total + one[...].astype(jnp.float32)
    height = hold.shape[1]
    for j in range(len(outs)):
        hold[j] = total[j * height : (j + 1) * height]
    for k, out in enumerate(outs):
        out[...] = hold[place[0] ^ k].astype(out.dtype)


def fold_part(own, got, place, layers):
    rows, half = own.shape
    height = rows // layers
    return pl.pallas_call(
        fold_kernel,
        out_shape=[
            jax.ShapeDtypeStruct((height, half), jnp.bfloat16 if k else jnp.float32)
            for k in range(layers)
        ],
        in_specs=[in_smem()] + [in_vmem()] * 4,
        out_specs=[in_vmem()] * layers,
        scratch_shapes=[pltpu.VMEM((layers, height, half), jnp.float32)],
        compiler_params=limit(16),
        name="fold_part",
    )(place, own, *got)


def stack_kernel(place, *refs):
    parts, out_ref, hold, flat = refs[:-3], refs[-3], refs[-2], refs[-1]
    height = hold.shape[1]
    for k, part in enumerate(parts):
        hold[place[0] ^ k] = part[...].astype(jnp.float32)
    for j in range(len(parts)):
        flat[j * height : (j + 1) * height, :] = hold[j]
    out_ref[...] = flat[...].astype(jnp.bfloat16)


def stack_part(parts, place):
    layers = len(parts)
    height, half = parts[0].shape
    return pl.pallas_call(
        stack_kernel,
        out_shape=jax.ShapeDtypeStruct((layers * height, half), jnp.bfloat16),
        in_specs=[in_smem()] + [in_vmem()] * layers,
        out_specs=in_vmem(),
        scratch_shapes=[
            pltpu.VMEM((layers, height, half), jnp.float32),
            pltpu.VMEM((layers * height, half), jnp.float32),
        ],
        compiler_params=limit(16),
        name="stack_part",
    )(place, *parts)


def partner(value, axis, size, bits):
    return lax.ppermute(value, axis, [(i, i ^ bits) for i in range(size)])


def total_sum(value, sizes):
    for axis, size in sizes:
        step = 1
        while step < size:
            value = value + partner(value, axis, size, step)
            step *= 2
    return value


def both_by_stages(hidden, parts, units, blocks, blk, mp, prompt, merge):
    rows, model = hidden.shape
    half = units // 2
    layers = blocks // 4
    height = rows // layers
    layer = blk // 4
    place = layer.reshape(1)
    got = [partner(parts[k], "blk", blocks, k) for k in range(1, 4)]
    got, sent = lax.optimization_barrier((got, prompt()))
    parts = fold_part(parts[0], got, place, layers)
    more = [partner(parts[k], "blk", blocks, 4 * k) for k in range(1, layers)]
    more, partials = lax.optimization_barrier((more, spread(sent)))
    inner = parts[0] + sum(one.astype(jnp.float32) for one in more)
    base = lax.dynamic_slice(
        hidden, (layer * height, mp * units + (blk & 1) * half), (height, half)
    )
    own = (base.astype(jnp.float32) + jax.nn.silu(inner)).astype(jnp.bfloat16)
    chunks = [own] + [partner(own, "blk", blocks, 4 * k) for k in range(1, layers)]
    chunks, heads_out = lax.optimization_barrier((chunks, merge(partials)))
    quad = stack_part(chunks, place)
    pieces = [quad] + [partner(quad, "blk", blocks, k) for k in range(1, 4)]
    pieces = pieces + [partner(piece, "mp", 2, 1) for piece in pieces]
    places = []
    for side in (mp, 1 - mp):
        for k in range(4):
            which = (blk & 3) ^ k
            places += [which >> 1, side * 2 + (which & 1)]
    return pieces, jnp.stack(places), heads_out


def spread(value):
    return lax.all_to_all(value, "blk", 0, 0, tiled=True)


def fresh_by_collectives(hidden, medusa_w, blocks, blk, mp):
    drafts, depth, units = medusa_w.shape
    rows = hidden.shape[0]
    own = drafts * rows // blocks
    hidden_cols = lax.dynamic_slice_in_dim(hidden, blk * depth, depth, 1)
    partial = jnp.einsum("rd,mdu->mru", hidden_cols, medusa_w, preferred_element_type=jnp.float32)
    partial = partial.reshape(blocks, own, units).astype(jnp.bfloat16)
    inner = lax.psum_scatter(partial, "blk", scatter_dimension=0).astype(jnp.float32)
    base = lax.dynamic_slice(hidden, ((blk * own) % rows, mp * units), (own, units))
    fresh = (base.astype(jnp.float32) + jax.nn.silu(inner)).astype(jnp.bfloat16)
    fresh = lax.all_gather(fresh, "blk", axis=0, tiled=True)
    return [lax.all_gather(fresh, "mp", axis=1, tiled=True)]


def ancestry(parents):
    count = parents.shape[1]
    column = jnp.arange(count, dtype=jnp.int32)
    linked = (parents[:, :, None] == column[None, None, :]) & (column[None, :, None] > 0)
    reach = jnp.eye(count, dtype=jnp.bfloat16)[None] + linked.astype(jnp.bfloat16)
    for sweep in range(count.bit_length()):
        met = jnp.einsum("gij,gjk->gik", reach, reach, preferred_element_type=jnp.float32)
        reach = jnp.minimum(met, 1.0).astype(jnp.bfloat16)
    return reach.astype(jnp.float32)


def per_device(
    hidden,
    medusa_w,
    embedding,
    cand_ids,
    tree_q,
    tree_key_value,
    prompt_key_value,
    block_group,
    block_len,
    block_empty,
    parents,
    out_weight,
    post_gain,
    resid,
):
    blocks, splits = lax.axis_size("blk"), lax.axis_size("mp")
    blk, mp = lax.axis_index("blk"), lax.axis_index("mp")
    drafts, depth, units = medusa_w.shape
    rows, model = hidden.shape
    lines = drafts * rows

    groups, tree_size, features = tree_q.shape
    width = features // blocks
    meta = jnp.concatenate([block_group, block_len, block_empty])

    def prompt():
        return prompt_part(tree_q, prompt_key_value, meta, width, blocks)

    def merge(partials):
        reach = ancestry(parents)
        numer, denom = tree_part(tree_q, tree_key_value, reach, blk * width, width)
        return merge_part(partials, numer, denom)

    if splits == 2 and blocks % 4 == 0 and units % 256 == 0 and drafts == 2:
        parts = draft_part(hidden, medusa_w, blk)
        parts, meta = lax.optimization_barrier((parts, meta))
        pieces, places, heads_out = both_by_stages(
            hidden, parts, units, blocks, blk, mp, prompt, merge
        )
    else:
        pieces = fresh_by_collectives(hidden, medusa_w, blocks, blk, mp)
        places = jnp.zeros((2,), jnp.int32)
        heads_out = merge(spread(prompt()))
    heads_out = spread(heads_out)
    attn = project_part(heads_out, out_weight)
    attn, pieces = lax.optimization_barrier((attn, pieces))
    attn = total_sum(attn, [("mp", splits)])
    normed = attn * lax.rsqrt(jnp.mean(attn * attn, -1, keepdims=True) + 1e-06) * post_gain
    layer_out = (normed + resid.astype(jnp.float32)).astype(jnp.bfloat16)

    vocab = embedding.shape[0]
    picks = cand_ids.shape[2]
    ids = cand_ids.reshape(lines, picks) - (blk * splits + mp) * vocab
    ids = jnp.pad(ids, ((0, 0), (0, LANES - picks)), constant_values=-1)
    score = score_part(places, pieces, embedding, ids, picks)
    score = total_sum(score, [("mp", splits), ("blk", blocks)])
    draft_logprob = score[:picks] - jnp.log(score[picks : picks + 1])
    draft_logprob = draft_logprob.T.reshape(drafts, rows, picks)
    return (draft_logprob, layer_out)


def solution(mesh):
    placed = (
        P(),
        P(None, "blk", "mp"),
        P(("blk", "mp"), None),
        P(),
        P(None, None, "mp"),
        P(None, None, None, "mp"),
        P(None, "blk", None, "mp"),
        P("blk"),
        P("blk"),
        P("blk"),
        P(),
        P("mp", None),
        P(),
        P("blk", None),
    )
    return jax.shard_map(
        per_device, mesh=mesh, in_specs=placed, out_specs=(P(), P("blk", None)), check_vma=False
    )
```

time: 122 us -> 117 us (0.959)
  Pallas kernels: 28.8 us -> 43 us
  local copies, waits for them, and re-layouts: 12.6 us -> 1.04 us
  matrix products: 9.33 us -> 1.56 us
  starting transfers between devices: 36.7 us -> 33.4 us
  other arithmetic: 1.29 us -> 3.22 us
  waiting for transfers between devices: 29.4 us -> 31 us
    pallas_call x3 -> x4, Pallas kernels: 23.2 us -> 37.6 us  [the longest x1 22.4 us: score_part(): pl.pallas_call(functools.partial(score_kernel, picks), out_shape=jax.Shap...]
    dot_general x1 -> x0, matrix products: 7.77 us -> none  [per_device(): attn = jnp.dot(heads_out, out_weight, preferred_element_type=jnp.float32)]
    unnamed x18 -> x6, local copies, waits for them, and re-layouts: 5.13 us -> 0.01 us
    slice x1 -> x0, local copies, waits for them, and re-layouts: 3.37 us -> none  [per_device(): tree_key_value[1]]
    dynamic_slice x3 -> x0, local copies, waits for them, and re-layouts: 3.04 us -> none  [the longest x1 1.07 us: per_device(): lax.dynamic_slice_in_dim(tree_key_value[1], kv_head * HEAD_SIZE + column...]
    ppermute x24 -> x22, starting transfers between devices: 24.7 us -> 22.5 us  [partner(): return lax.ppermute(value, axis, [(i, i ^ bits) for i in range(size)])]
    all_to_all x2, waiting for transfers between devices: 0.01 us -> 2.13 us  [spread(): return lax.all_to_all(value, 'blk', 0, 0, tiled=True)]
    ppermute x24 -> x22, waiting for transfers between devices: 29.4 us -> 28.9 us  [partner(): return lax.ppermute(value, axis, [(i, i ^ bits) for i in range(size)])]
  transfers between devices with their start and end apart: 26 -> 24, of which waited for: 14 -> 10; matrix products, arithmetic and copies ran while one was open for 14% -> 2% of each run, Pallas kernels for 19% -> 34%
where the time goes in v4:
time: 117 us; the launch traced here: 116 us
  Pallas kernels  43 us (37%)
  starting transfers between devices  33.4 us (29%)
  waiting for transfers between devices  31 us (26%)
  other arithmetic  3.22 us (3%)
  between operations  2.97 us (3%)
  matrix products  1.56 us (1%)
    ppermute x22, waiting for transfers between devices, partner(): return lax.ppermute(value, axis, [(i, i ^ bits) for i in range(size)])  28.9 us
    ppermute x22, starting transfers between devices, partner(): return lax.ppermute(value, axis, [(i, i ^ bits) for i in range(size)])  22.5 us
    pallas_call x1, Pallas kernels, score_part(): pl.pallas_call(functools.partial(score_kernel, picks), out_shape=jax.Shap...  22.4 us
    all_to_all x2, starting transfers between devices, spread(): return lax.all_to_all(value, 'blk', 0, 0, tiled=True)  10.9 us
    pallas_call x1, Pallas kernels, prompt_part(): pl.pallas_call(prompt_kernel, out_shape=jax.ShapeDtypeStruct((blocks, tre...  7 us
    pallas_call x1, Pallas kernels, project_part(): pl.pallas_call(project_kernel, out_shape=jax.ShapeDtypeStruct((tokens, mo...  5.95 us
    pallas_call x1, Pallas kernels, draft_part(): pl.pallas_call(draft_kernel, out_shape=[jax.ShapeDtypeStruct((rows, half)...  3.08 us
  transfers between devices with their start and end apart: 24, of which 10 were waited for; matrix products, arithmetic and copies ran while one was open for 2% of the time, Pallas kernels for 34%

profile of v4, /device:TPU:0, one launch (start us, length us, event | category | flops | bytes accessed | tf_op | source)
XLA Modules:
  0.0 116.3 jit_solution(358283105340473673)
XLA Ops:
  2.6 0.1 stack.95.meta
  2.7 3.1 %draft_part.1 = (f32[144,896]{1,0:T(8,128)S(1)}, bf16[144,896]{1,0:T(8,128)(2,1)S(1)}, bf16[144,896]{1,0:T(8,128)(2,1)S(1)}, bf16[144,896]{1,0:T(8,128)(2,1)S(1)}) custom-call(s32[6]{0:T(128)S(1)} %stack.95.meta, bf16[144,3584]{1,0:T(8,128)(2,1)} %hidden_hbm.1, bf16[2,224,1792]{2,1,0:T(8,128)(2,1)} %weight_hbm.2), custom_call_target="tpu_custom_call" | custom-call | tf_op jit(solution)/shard_map/draft_part/pallas_call | solution.py:401
  5.9 3.0 %collective-permute-start = (bf16[144,896]{1,0:T(8,128)(2,1)S(1)}, bf16[144,896]{1,0:T(8,128)(2,1)S(1)}, u32[]{:S(2)}, u32[]{:S(2)}) collective-permute-start(bf16[144,896]{1,0:T(8,128)(2,1)S(1)} %get-tuple-element.44), channel_id=1, source_target_pairs={{0,2},{2,0},{4,6},{6,4},{8,10},{10,8},{12,14},{14,12},{16,18},{18,... | collective-permute-start | bytes 774152 | tf_op jit(solution)/shard_map/ppermute | solution.py:476
  8.8 1.5 %collective-permute-start.1 = (bf16[144,896]{1,0:T(8,128)(2,1)S(1)}, bf16[144,896]{1,0:T(8,128)(2,1)S(1)}, u32[]{:S(2)}, u32[]{:S(2)}) collective-permute-start(bf16[144,896]{1,0:T(8,128)(2,1)S(1)} %get-tuple-element.45), channel_id=1, source_target_pairs={{0,4},{2,6},{4,0},{6,2},{8,12},{10,14},{12,8},{14,10},{16,20},{18,... | collective-permute-start | bytes 774152 | tf_op jit(solution)/shard_map/ppermute | solution.py:476
  10.4 7.0 %prompt_part.1 = bf16[16,64,128]{2,1,0:T(8,128)(2,1)} custom-call(s32[3]{0:T(128)S(1)} %pad_add_fusion.meta, bf16[12,48,2048]{2,1,0:T(8,128)(2,1)} %q_hbm.3, bf16[2,1,2048,1024]{3,2,1,0:T(8,128)(2,1)} %kv_hbm.2), custom_call_target="tpu_custom_call" | custom-call | flops 805306368 | bytes 8388608 | tf_op jit(solution)/shard_map/prompt_part/pallas_call | solution.py:110
  17.4 4.6 %collective-permute-done.1.refs_1_ = bf16[144,896]{1,0:T(8,128)(2,1)S(1)} collective-permute-done((bf16[144,896]{1,0:T(8,128)(2,1)S(1)}, bf16[144,896]{1,0:T(8,128)(2,1)S(1)}, u32[]{:S(2)}, u32[]{:S(2)}) %collective-permute-start.1) | collective-permute-done | bytes 258080 | tf_op jit(solution)/shard_map/ppermute | solution.py:476
  22.0 5.9 %all-to-all-start = ((bf16[16,64,128]{2,1,0:T(8,128)(2,1)}), bf16[16,64,128]{2,1,0:T(8,128)(2,1)S(1)}, u32[]{:S(2)}, u32[]{:S(2)}) async-start(bf16[16,64,128]{2,1,0:T(8,128)(2,1)} %prompt_part.1), calls=%async_computation | async-start | bytes 524288 | tf_op jit(solution)/shard_map/all_to_all | solution.py:519
  28.0 0.7 fusion.1
  28.7 0.4 fusion.3
  29.1 0.2 fold_part.1
  29.4 2.0 %collective-permute-start.3 = (bf16[36,896]{1,0:T(8,128)(2,1)S(1)}, bf16[36,896]{1,0:T(8,128)(2,1)S(1)}, u32[]{:S(2)}, u32[]{:S(2)}) collective-permute-start(bf16[36,896]{1,0:T(8,128)(2,1)S(1)} %get-tuple-element.52), channel_id=1, source_target_pairs={{0,8},{2,10},{4,12},{6,14},{8,0},{10,2},{12,4},{14,6},{16,24},{18,... | collective-permute-start | bytes 193544 | tf_op jit(solution)/shard_map/ppermute | solution.py:476
  31.4 2.4 %collective-permute-start.4 = (bf16[36,896]{1,0:T(8,128)(2,1)S(1)}, bf16[36,896]{1,0:T(8,128)(2,1)S(1)}, u32[]{:S(2)}, u32[]{:S(2)}) collective-permute-start(bf16[36,896]{1,0:T(8,128)(2,1)S(1)} %get-tuple-element.53), channel_id=1, source_target_pairs={{0,16},{2,18},{4,20},{6,22},{8,24},{10,26},{12,28},{14,30},{16,0},... | collective-permute-start | bytes 193544 | tf_op jit(solution)/shard_map/ppermute | solution.py:476
  33.7 0.1 collective-permute-start.5
  33.8 0.4 fusion.6.reach_ref
  34.3 0.6 collective-permute-done.3
  34.9 6.0 %collective-permute-done.4 = bf16[36,896]{1,0:T(8,128)(2,1)S(1)} collective-permute-done((bf16[36,896]{1,0:T(8,128)(2,1)S(1)}, bf16[36,896]{1,0:T(8,128)(2,1)S(1)}, u32[]{:S(2)}, u32[]{:S(2)}) %collective-permute-start.4) | collective-permute-done | bytes 64544 | tf_op jit(solution)/shard_map/ppermute | solution.py:476
  41.0 1.0 add_convert_fusion.1.refs_0_
  41.9 1.4 %collective-permute-start.6 = (bf16[36,896]{1,0:T(8,128)(2,1)S(1)}, bf16[36,896]{1,0:T(8,128)(2,1)S(1)}, u32[]{:S(2)}, u32[]{:S(2)}) collective-permute-start(bf16[36,896]{1,0:T(8,128)(2,1)S(1)} %add_convert_fusion.1.refs_0_), channel_id=1, source_target_pairs={{0,8},{2,10},{4,12},{6,14},{8,0},{10,2},{12,4},{14,6},{16,24},{18,... | collective-permute-start | bytes 193544 | tf_op jit(solution)/shard_map/ppermute | solution.py:476
  43.3 0.7 collective-permute-start.7
  44.0 2.4 %collective-permute-start.8 = (bf16[36,896]{1,0:T(8,128)(2,1)S(1)}, bf16[36,896]{1,0:T(8,128)(2,1)S(1)}, u32[]{:S(2)}, u32[]{:S(2)}) collective-permute-start(bf16[36,896]{1,0:T(8,128)(2,1)S(1)} %add_convert_fusion.1.refs_0_), channel_id=1, source_target_pairs={{0,24},{2,26},{4,28},{6,30},{8,16},{10,18},{12,20},{14,22},{16,8},... | collective-permute-start | bytes 193544 | tf_op jit(solution)/shard_map/ppermute | solution.py:476
  46.5 2.3 %tree_part.1 = (f32[12,48,128]{2,1,0:T(8,128)S(1)}, f32[12,48,128]{2,1,0:T(8,128)S(1)}) custom-call(s32[3]{0:T(128)S(1)} %pad_add_fusion.1.meta, bf16[12,48,2048]{2,1,0:T(8,128)(2,1)} %q_hbm.3, bf16[2,12,48,1024]{3,2,1,0:T(8,128)(2,1)} %kv_hbm.3, f32[12,48,48]{2,1,0:T(8,128)S(1)} %fusion.6.reach_ref), custom_call_target="tpu_custom_call" | custom-call | tf_op jit(solution)/shard_map/tree_part/pallas_call | solution.py:162
  48.7 2.1 %merge_part.1 = bf16[16,36,128]{2,1,0:T(8,128)(2,1)} custom-call(bf16[16,64,128]{2,1,0:T(8,128)(2,1)S(1)} %all-to-all-done.got_ref, f32[12,48,128]{2,1,0:T(8,128)S(1)} %get-tuple-element.60.numer_ref, f32[12,48,128]{2,1,0:T(8,128)S(1)} %get-tuple-element.61.denom_ref), custom_call_target="tpu_custom_call" | custom-call | tf_op jit(solution)/shard_map/merge_part/pallas_call | solution.py:211
  50.8 0.1 stack_part.1.refs_0_
  50.9 1.5 %collective-permute-start.9 = (bf16[144,896]{1,0:T(8,128)(2,1)S(1)}, bf16[144,896]{1,0:T(8,128)(2,1)S(1)}, u32[]{:S(2)}, u32[]{:S(2)}) collective-permute-start(bf16[144,896]{1,0:T(8,128)(2,1)S(1)} %stack_part.1.refs_0_), channel_id=1, source_target_pairs={{0,2},{2,0},{4,6},{6,4},{8,10},{10,8},{12,14},{14,12},{16,18},{18,... | collective-permute-start | bytes 774152 | tf_op jit(solution)/shard_map/ppermute | solution.py:476
  52.4 1.5 %collective-permute-start.10 = (bf16[144,896]{1,0:T(8,128)(2,1)S(1)}, bf16[144,896]{1,0:T(8,128)(2,1)S(1)}, u32[]{:S(2)}, u32[]{:S(2)}) collective-permute-start(bf16[144,896]{1,0:T(8,128)(2,1)S(1)} %stack_part.1.refs_0_), channel_id=1, source_target_pairs={{0,4},{2,6},{4,0},{6,2},{8,12},{10,14},{12,8},{14,10},{16,20},{18,... | collective-permute-start | bytes 774152 | tf_op jit(solution)/shard_map/ppermute | solution.py:476
  53.9 0.6 collective-permute-start.11
  54.5 5.0 %all-to-all-start.1 = ((bf16[16,36,128]{2,1,0:T(8,128)(2,1)}), bf16[16,36,128]{2,1,0:T(8,128)(2,1)S(1)}, u32[]{:S(2)}, u32[]{:S(2)}) async-start(bf16[16,36,128]{2,1,0:T(8,128)(2,1)} %merge_part.1), calls=%async_computation.1 | async-start | bytes 327680 | tf_op jit(solution)/shard_map/all_to_all | solution.py:519
  59.6 0.5 collective-permute-start.13
  60.1 4.4 %collective-permute-done.10.refs_2_ = bf16[144,896]{1,0:T(8,128)(2,1)S(1)} collective-permute-done((bf16[144,896]{1,0:T(8,128)(2,1)S(1)}, bf16[144,896]{1,0:T(8,128)(2,1)S(1)}, u32[]{:S(2)}, u32[]{:S(2)}) %collective-permute-start.10) | collective-permute-done | bytes 258080 | tf_op jit(solution)/shard_map/ppermute | solution.py:476
  64.5 0.5 collective-permute-start.15
  65.0 0.1 copy.16
  65.2 0.1 stack.88.places
  65.3 2.1 %all-to-all-done.1.heads_ref = bf16[16,36,128]{2,1,0:T(8,128)(2,1)S(1)} async-done(((bf16[16,36,128]{2,1,0:T(8,128)(2,1)}), bf16[16,36,128]{2,1,0:T(8,128)(2,1)S(1)}, u32[]{:S(2)}, u32[]{:S(2)}) %all-to-all-start.1) | async-done | bytes 147488 | tf_op jit(solution)/shard_map/all_to_all | solution.py:519
  67.4 5.9 %project_part.1 = f32[36,3584]{1,0:T(8,128)S(1)} custom-call(bf16[16,36,128]{2,1,0:T(8,128)(2,1)S(1)} %all-to-all-done.1.heads_ref, bf16[2048,3584]{1,0:T(8,128)(2,1)} %weight_hbm.3), custom_call_target="tpu_custom_call" | custom-call | flops 528482304 | bytes 14680064 | tf_op jit(solution)/shard_map/project_part/pallas_call | solution.py:248
  73.5 22.4 %score_part.1 = f32[16,288]{1,0:T(8,128)S(1)} custom-call(s32[16]{0:T(128)S(1)} %stack.88.places, s32[288,128]{1,0:T(8,128)S(1)} %pad.4.ids_ref, bf16[144,896]{1,0:T(8,128)(2,1)S(1)} %stack_part.1.refs_0_, bf16[144,896]{1,0:T(8,128)(2,1)S(1)} %collective-permute-done.9.refs_1_, bf16[144,896]{1,0:T(8,128)(2,1)S(1)} %collective-permute-done.10.refs_2_, ...), custom_call_target="tpu_custom_call" | custom-call | flops 8455716864 | bytes 29360128 | tf_op jit(solution)/shard_map/score_part/pallas_call | solution.py:342
  95.9 0.6 collective-permute-start.16
  96.4 0.8 collective-permute-done.16
  97.3 1.2 %collective-permute-start.17 = (f32[16,288]{1,0:T(8,128)S(1)}, f32[16,288]{1,0:T(8,128)S(1)}, u32[]{:S(2)}, u32[]{:S(2)}) collective-permute-start(f32[16,288]{1,0:T(8,128)S(1)} %add.123), channel_id=1, source_target_pairs={{0,2},{2,0},{4,6},{6,4},{8,10},{10,8},{12,14},{14,12},{16,18},{18,... | collective-permute-start | bytes 55304 | tf_op jit(solution)/shard_map/ppermute | solution.py:476
  98.5 2.6 %collective-permute-done.17 = f32[16,288]{1,0:T(8,128)S(1)} collective-permute-done((f32[16,288]{1,0:T(8,128)S(1)}, f32[16,288]{1,0:T(8,128)S(1)}, u32[]{:S(2)}, u32[]{:S(2)}) %collective-permute-start.17) | collective-permute-done | bytes 18464 | tf_op jit(solution)/shard_map/ppermute | solution.py:476
  101.1 0.8 collective-permute-start.18
  101.9 3.0 %collective-permute-done.18 = f32[16,288]{1,0:T(8,128)S(1)} collective-permute-done((f32[16,288]{1,0:T(8,128)S(1)}, f32[16,288]{1,0:T(8,128)S(1)}, u32[]{:S(2)}, u32[]{:S(2)}) %collective-permute-start.18) | collective-permute-done | bytes 18464 | tf_op jit(solution)/shard_map/ppermute | solution.py:476
  104.9 0.8 collective-permute-start.19
  105.7 3.0 %collective-permute-done.19 = f32[16,288]{1,0:T(8,128)S(1)} collective-permute-done((f32[16,288]{1,0:T(8,128)S(1)}, f32[16,288]{1,0:T(8,128)S(1)}, u32[]{:S(2)}, u32[]{:S(2)}) %collective-permute-start.19) | collective-permute-done | bytes 18464 | tf_op jit(solution)/shard_map/ppermute | solution.py:476
  108.8 1.0 collective-permute-start.20
  109.8 3.7 %collective-permute-done.20 = f32[16,288]{1,0:T(8,128)S(1)} collective-permute-done((f32[16,288]{1,0:T(8,128)S(1)}, f32[16,288]{1,0:T(8,128)S(1)}, u32[]{:S(2)}, u32[]{:S(2)}) %collective-permute-start.20) | collective-permute-done | bytes 18464 | tf_op jit(solution)/shard_map/ppermute | solution.py:476
  113.5 0.7 reshape.37
  114.2 0.2 multiply_reduce_fusion
  114.4 1.8 %add_convert_fusion = bf16[36,3584]{1,0:T(8,128)(2,1)} fusion(bf16[36,3584]{1,0:T(8,128)(2,1)} %param.27, f32[36,3584]{1,0:T(8,128)S(1)} %get-tuple-element.77, f32[3584]{0:T(1024)S(1)} %copy-done.1, f32[36]{0:T(128)S(1)} %add_rsqrt_fusion), kind=kLoop, calls=%fused_computation.13 | loop fusion | flops 645120 | bytes 1046672 | tf_op jit(solution)/shard_map/convert_element_type | solution.py:596
  (38 shorter events, 0.5 us)
Async XLA Ops:
  0.6 27.3 %copy-start.2 = (s32[12,48]{1,0:T(8,128)S(1)}, s32[12,48]{1,0:T(8,128)}, u32[]{:S(2)}) copy-start(s32[12,48]{1,0:T(8,128)} %param.24) | copy-start | bytes 6916
  5.9 59.2 %copy-start = (s32[2,144,10]{1,0,2:T(2,128)S(1)}, s32[2,144,10]{1,0,2:T(2,128)}, u32[]{:S(2)}) copy-start(s32[2,144,10]{1,0,2:T(2,128)} %param.17) | copy-start | bytes 34564
  5.9 11.5 %collective-permute-start = (bf16[144,896]{1,0:T(8,128)(2,1)S(1)}, bf16[144,896]{1,0:T(8,128)(2,1)S(1)}, u32[]{:S(2)}, u32[]{:S(2)}) collective-permute-start(bf16[144,896]{1,0:T(8,128)(2,1)S(1)} %get-tuple-element.44), channel_id=1, source_target_pairs={{0,2},{2,0},{4,6},{6,4},{8,10},{10,8},{12,14},{14,12},{16,18},{18,... | collective-permute-start | bytes 774152 | tf_op jit(solution)/shard_map/ppermute | solution.py:476
  8.8 13.2 %collective-permute-start.1 = (bf16[144,896]{1,0:T(8,128)(2,1)S(1)}, bf16[144,896]{1,0:T(8,128)(2,1)S(1)}, u32[]{:S(2)}, u32[]{:S(2)}) collective-permute-start(bf16[144,896]{1,0:T(8,128)(2,1)S(1)} %get-tuple-element.45), channel_id=1, source_target_pairs={{0,4},{2,6},{4,0},{6,2},{8,12},{10,14},{12,8},{14,10},{16,20},{18,... | collective-permute-start | bytes 774152 | tf_op jit(solution)/shard_map/ppermute | solution.py:476
  10.3 11.7 %collective-permute-start.2 = (bf16[144,896]{1,0:T(8,128)(2,1)S(1)}, bf16[144,896]{1,0:T(8,128)(2,1)S(1)}, u32[]{:S(2)}, u32[]{:S(2)}) collective-permute-start(bf16[144,896]{1,0:T(8,128)(2,1)S(1)} %get-tuple-element.46), channel_id=1, source_target_pairs={{0,6},{2,4},{4,2},{6,0},{8,14},{10,12},{12,10},{14,8},{16,22},{18,... | collective-permute-start | bytes 774152 | tf_op jit(solution)/shard_map/ppermute | solution.py:476
  22.0 18.9 %all-to-all-start = ((bf16[16,64,128]{2,1,0:T(8,128)(2,1)}), bf16[16,64,128]{2,1,0:T(8,128)(2,1)S(1)}, u32[]{:S(2)}, u32[]{:S(2)}) async-start(bf16[16,64,128]{2,1,0:T(8,128)(2,1)} %prompt_part.1), calls=%async_computation | async-start | bytes 524288 | tf_op jit(solution)/shard_map/all_to_all | solution.py:519
  29.4 5.5 %collective-permute-start.3 = (bf16[36,896]{1,0:T(8,128)(2,1)S(1)}, bf16[36,896]{1,0:T(8,128)(2,1)S(1)}, u32[]{:S(2)}, u32[]{:S(2)}) collective-permute-start(bf16[36,896]{1,0:T(8,128)(2,1)S(1)} %get-tuple-element.52), channel_id=1, source_target_pairs={{0,8},{2,10},{4,12},{6,14},{8,0},{10,2},{12,4},{14,6},{16,24},{18,... | collective-permute-start | bytes 193544 | tf_op jit(solution)/shard_map/ppermute | solution.py:476
  31.4 9.6 %collective-permute-start.4 = (bf16[36,896]{1,0:T(8,128)(2,1)S(1)}, bf16[36,896]{1,0:T(8,128)(2,1)S(1)}, u32[]{:S(2)}, u32[]{:S(2)}) collective-permute-start(bf16[36,896]{1,0:T(8,128)(2,1)S(1)} %get-tuple-element.53), channel_id=1, source_target_pairs={{0,16},{2,18},{4,20},{6,22},{8,24},{10,26},{12,28},{14,30},{16,0},... | collective-permute-start | bytes 193544 | tf_op jit(solution)/shard_map/ppermute | solution.py:476
  33.7 7.2 %collective-permute-start.5 = (bf16[36,896]{1,0:T(8,128)(2,1)S(1)}, bf16[36,896]{1,0:T(8,128)(2,1)S(1)}, u32[]{:S(2)}, u32[]{:S(2)}) collective-permute-start(bf16[36,896]{1,0:T(8,128)(2,1)S(1)} %get-tuple-element.54), channel_id=1, source_target_pairs={{0,24},{2,26},{4,28},{6,30},{8,16},{10,18},{12,20},{14,22},{16,8},... | collective-permute-start | bytes 193544 | tf_op jit(solution)/shard_map/ppermute | solution.py:476
  41.9 8.9 %collective-permute-start.6 = (bf16[36,896]{1,0:T(8,128)(2,1)S(1)}, bf16[36,896]{1,0:T(8,128)(2,1)S(1)}, u32[]{:S(2)}, u32[]{:S(2)}) collective-permute-start(bf16[36,896]{1,0:T(8,128)(2,1)S(1)} %add_convert_fusion.1.refs_0_), channel_id=1, source_target_pairs={{0,8},{2,10},{4,12},{6,14},{8,0},{10,2},{12,4},{14,6},{16,24},{18,... | collective-permute-start | bytes 193544 | tf_op jit(solution)/shard_map/ppermute | solution.py:476
  43.3 7.5 %collective-permute-start.7 = (bf16[36,896]{1,0:T(8,128)(2,1)S(1)}, bf16[36,896]{1,0:T(8,128)(2,1)S(1)}, u32[]{:S(2)}, u32[]{:S(2)}) collective-permute-start(bf16[36,896]{1,0:T(8,128)(2,1)S(1)} %add_convert_fusion.1.refs_0_), channel_id=1, source_target_pairs={{0,16},{2,18},{4,20},{6,22},{8,24},{10,26},{12,28},{14,30},{16,0},... | collective-permute-start | bytes 193544 | tf_op jit(solution)/shard_map/ppermute | solution.py:476
  44.0 6.8 %collective-permute-start.8 = (bf16[36,896]{1,0:T(8,128)(2,1)S(1)}, bf16[36,896]{1,0:T(8,128)(2,1)S(1)}, u32[]{:S(2)}, u32[]{:S(2)}) collective-permute-start(bf16[36,896]{1,0:T(8,128)(2,1)S(1)} %add_convert_fusion.1.refs_0_), channel_id=1, source_target_pairs={{0,24},{2,26},{4,28},{6,30},{8,16},{10,18},{12,20},{14,22},{16,8},... | collective-permute-start | bytes 193544 | tf_op jit(solution)/shard_map/ppermute | solution.py:476
  50.9 8.7 %collective-permute-start.9 = (bf16[144,896]{1,0:T(8,128)(2,1)S(1)}, bf16[144,896]{1,0:T(8,128)(2,1)S(1)}, u32[]{:S(2)}, u32[]{:S(2)}) collective-permute-start(bf16[144,896]{1,0:T(8,128)(2,1)S(1)} %stack_part.1.refs_0_), channel_id=1, source_target_pairs={{0,2},{2,0},{4,6},{6,4},{8,10},{10,8},{12,14},{14,12},{16,18},{18,... | collective-permute-start | bytes 774152 | tf_op jit(solution)/shard_map/ppermute | solution.py:476
  52.4 12.1 %collective-permute-start.10 = (bf16[144,896]{1,0:T(8,128)(2,1)S(1)}, bf16[144,896]{1,0:T(8,128)(2,1)S(1)}, u32[]{:S(2)}, u32[]{:S(2)}) collective-permute-start(bf16[144,896]{1,0:T(8,128)(2,1)S(1)} %stack_part.1.refs_0_), channel_id=1, source_target_pairs={{0,4},{2,6},{4,0},{6,2},{8,12},{10,14},{12,8},{14,10},{16,20},{18,... | collective-permute-start | bytes 774152 | tf_op jit(solution)/shard_map/ppermute | solution.py:476
  53.9 10.6 %collective-permute-start.11 = (bf16[144,896]{1,0:T(8,128)(2,1)S(1)}, bf16[144,896]{1,0:T(8,128)(2,1)S(1)}, u32[]{:S(2)}, u32[]{:S(2)}) collective-permute-start(bf16[144,896]{1,0:T(8,128)(2,1)S(1)} %stack_part.1.refs_0_), channel_id=1, source_target_pairs={{0,6},{2,4},{4,2},{6,0},{8,14},{10,12},{12,10},{14,8},{16,22},{18,... | collective-permute-start | bytes 774152 | tf_op jit(solution)/shard_map/ppermute | solution.py:476
  54.5 12.9 %all-to-all-start.1 = ((bf16[16,36,128]{2,1,0:T(8,128)(2,1)}), bf16[16,36,128]{2,1,0:T(8,128)(2,1)S(1)}, u32[]{:S(2)}, u32[]{:S(2)}) async-start(bf16[16,36,128]{2,1,0:T(8,128)(2,1)} %merge_part.1), calls=%async_computation.1 | async-start | bytes 327680 | tf_op jit(solution)/shard_map/all_to_all | solution.py:519
  59.5 13.9 %collective-permute-start.12 = (bf16[144,896]{1,0:T(8,128)(2,1)S(1)}, bf16[144,896]{1,0:T(8,128)(2,1)S(1)}, u32[]{:S(2)}, u32[]{:S(2)}) collective-permute-start(bf16[144,896]{1,0:T(8,128)(2,1)S(1)} %stack_part.1.refs_0_), channel_id=1, source_target_pairs={{0,1},{1,0},{2,3},{3,2},{4,5},{5,4},{6,7},{7,6},{8,9},{9,8},{10,11... | collective-permute-start | bytes 774152 | tf_op jit(solution)/shard_map/ppermute | solution.py:476
  59.6 13.8 %collective-permute-start.13 = (bf16[144,896]{1,0:T(8,128)(2,1)S(1)}, bf16[144,896]{1,0:T(8,128)(2,1)S(1)}, u32[]{:S(2)}, u32[]{:S(2)}) collective-permute-start(bf16[144,896]{1,0:T(8,128)(2,1)S(1)} %collective-permute-done.9.refs_1_), channel_id=1, source_target_pairs={{0,1},{1,0},{2,3},{3,2},{4,5},{5,4},{6,7},{7,6},{8,9},{9,8},{10,11... | collective-permute-start | bytes 774152 | tf_op jit(solution)/shard_map/ppermute | solution.py:476
  64.5 8.9 %collective-permute-start.14 = (bf16[144,896]{1,0:T(8,128)(2,1)S(1)}, bf16[144,896]{1,0:T(8,128)(2,1)S(1)}, u32[]{:S(2)}, u32[]{:S(2)}) collective-permute-start(bf16[144,896]{1,0:T(8,128)(2,1)S(1)} %collective-permute-done.10.refs_2_), channel_id=1, source_target_pairs={{0,1},{1,0},{2,3},{3,2},{4,5},{5,4},{6,7},{7,6},{8,9},{9,8},{10,11... | collective-permute-start | bytes 774152 | tf_op jit(solution)/shard_map/ppermute | solution.py:476
  64.5 8.9 %collective-permute-start.15 = (bf16[144,896]{1,0:T(8,128)(2,1)S(1)}, bf16[144,896]{1,0:T(8,128)(2,1)S(1)}, u32[]{:S(2)}, u32[]{:S(2)}) collective-permute-start(bf16[144,896]{1,0:T(8,128)(2,1)S(1)} %collective-permute-done.11.refs_3_), channel_id=1, source_target_pairs={{0,1},{1,0},{2,3},{3,2},{4,5},{5,4},{6,7},{7,6},{8,9},{9,8},{10,11... | collective-permute-start | bytes 774152 | tf_op jit(solution)/shard_map/ppermute | solution.py:476
  73.4 41.1 %copy-start.1 = (f32[3584]{0:T(1024)S(1)}, f32[3584]{0:T(1024)}, u32[]{:S(2)}) copy-start(f32[3584]{0:T(1024)} %param.26) | copy-start | bytes 43012
  73.4 40.8 %collective-permute-start.21 = (f32[36,3584]{1,0:T(8,128)S(1)}, f32[36,3584]{1,0:T(8,128)S(1)}, u32[]{:S(2)}, u32[]{:S(2)}) collective-permute-start(f32[36,3584]{1,0:T(8,128)S(1)} %project_part.1), channel_id=1, source_target_pairs={{0,1},{1,0},{2,3},{3,2},{4,5},{5,4},{6,7},{7,6},{8,9},{9,8},{10,11... | collective-permute-start | bytes 1548296 | tf_op jit(solution)/shard_map/ppermute | solution.py:476
  95.9 1.4 %collective-permute-start.16 = (f32[16,288]{1,0:T(8,128)S(1)}, f32[16,288]{1,0:T(8,128)S(1)}, u32[]{:S(2)}, u32[]{:S(2)}) collective-permute-start(f32[16,288]{1,0:T(8,128)S(1)} %score_part.1), channel_id=1, source_target_pairs={{0,1},{1,0},{2,3},{3,2},{4,5},{5,4},{6,7},{7,6},{8,9},{9,8},{10,11... | collective-permute-start | bytes 55304 | tf_op jit(solution)/shard_map/ppermute | solution.py:476
  97.3 3.8 %collective-permute-start.17 = (f32[16,288]{1,0:T(8,128)S(1)}, f32[16,288]{1,0:T(8,128)S(1)}, u32[]{:S(2)}, u32[]{:S(2)}) collective-permute-start(f32[16,288]{1,0:T(8,128)S(1)} %add.123), channel_id=1, source_target_pairs={{0,2},{2,0},{4,6},{6,4},{8,10},{10,8},{12,14},{14,12},{16,18},{18,... | collective-permute-start | bytes 55304 | tf_op jit(solution)/shard_map/ppermute | solution.py:476
  101.1 3.8 %collective-permute-start.18 = (f32[16,288]{1,0:T(8,128)S(1)}, f32[16,288]{1,0:T(8,128)S(1)}, u32[]{:S(2)}, u32[]{:S(2)}) collective-permute-start(f32[16,288]{1,0:T(8,128)S(1)} %add.124), channel_id=1, source_target_pairs={{0,4},{2,6},{4,0},{6,2},{8,12},{10,14},{12,8},{14,10},{16,20},{18,... | collective-permute-start | bytes 55304 | tf_op jit(solution)/shard_map/ppermute | solution.py:476
  104.9 3.8 %collective-permute-start.19 = (f32[16,288]{1,0:T(8,128)S(1)}, f32[16,288]{1,0:T(8,128)S(1)}, u32[]{:S(2)}, u32[]{:S(2)}) collective-permute-start(f32[16,288]{1,0:T(8,128)S(1)} %add.125), channel_id=1, source_target_pairs={{0,8},{2,10},{4,12},{6,14},{8,0},{10,2},{12,4},{14,6},{16,24},{18,... | collective-permute-start | bytes 55304 | tf_op jit(solution)/shard_map/ppermute | solution.py:476
  108.8 4.7 %collective-permute-start.20 = (f32[16,288]{1,0:T(8,128)S(1)}, f32[16,288]{1,0:T(8,128)S(1)}, u32[]{:S(2)}, u32[]{:S(2)}) collective-permute-start(f32[16,288]{1,0:T(8,128)S(1)} %add.126), channel_id=1, source_target_pairs={{0,16},{2,18},{4,20},{6,22},{8,24},{10,26},{12,28},{14,30},{16,0},... | collective-permute-start | bytes 55304 | tf_op jit(solution)/shard_map/ppermute | solution.py:476

commit v5 on v4

--- a/solution.py
+++ b/solution.py
@@ -53,16 +53,16 @@
     rows = tree_size * repeats
     ask = pltpu.make_async_copy(q_hbm.at[group], queries, sems.at[2 * kv_heads])
     ask.start()
-    copies = []
-    for h in range(kv_heads):
-        for s in range(2):
-            columns = pl.ds(h * HEAD_SIZE, HEAD_SIZE)
-            copies.append(
-                pltpu.make_async_copy(
-                    kv_hbm.at[s, 0, :, columns], held.at[s, h], sems.at[2 * h + s]
-                )
-            )
-            copies[-1].start()
+    copies = [
+        pltpu.make_async_copy(
+            kv_hbm.at[s, 0, :, pl.ds(h * HEAD_SIZE, HEAD_SIZE)], held.at[s, h], sems.at[2 * h + s]
+        )
+        for h in range(kv_heads)
+        for s in range(2)
+    ]
+    ahead = 4
+    for copy in copies[:ahead]:
+        copy.start()
     ask.wait()
     per_head = HEAD_SIZE // width
     row_id = lax.broadcasted_iota(jnp.int32, (tree_size, width), 0)
@@ -78,10 +78,14 @@
             axis=0,
         )
         copies[2 * h].wait()
+        if 2 * h + ahead < len(copies):
+            copies[2 * h + ahead].start()
         scores = dot_t(asked, held[0, h])
         weights = jnp.where(slot < last, soft_weights(scores), 0.0)
         denom = jnp.sum(weights, axis=1, keepdims=True)
         copies[2 * h + 1].wait()
+        if 2 * h + 1 + ahead < len(copies):
+            copies[2 * h + 1 + ahead].start()
         numer = jnp.dot(
             weights.astype(jnp.bfloat16), held[1, h], preferred_element_type=jnp.float32
         )
@@ -264,38 +268,36 @@
     )(heads_out, pin(out_weight))
 
 
-def score_kernel(picks, places, ids_ref, *refs):
-    pieces, (embed_hbm, out_ref) = refs[:-8], refs[-8:-6]
-    fresh, total, picked, raw, ring, sems = refs[-6:]
-    slots, span = ring.shape[:2]
+def score_kernel(picks, streams, places, ids_ref, *refs):
+    pieces, embeds, out_ref = refs[: -5 - 2 * streams], refs[-5 - 2 * streams : -5], refs[-5]
+    fresh, total, picked, before = refs[-4:]
+    step = pl.program_id(0)
+    span = embeds[0].shape[0]
     rows = fresh.shape[0]
-    chunks = embed_hbm.shape[0] // span
     band = 32 if rows % 32 == 0 else rows
 
-    def copy(c):
-        start = pl.multiple_of(c * span, span)
-        return pltpu.make_async_copy(
-            embed_hbm.at[pl.ds(start, span)], ring.at[c % slots], sems.at[c % slots]
-        )
-
-    def product(c):
-        copy(c).wait()
-        return dot_t(fresh[...], ring[c % slots])
-
-    def refill(c):
-        @pl.when(c + slots < chunks)
-        def _():
-            copy(c + slots).start()
-
-    def absorb(side, start, keep=None):
+    @pl.when(step == 0)
+    def _():
+        before[...] = jnp.zeros_like(before)
+        for n, piece in enumerate(pieces):
+            height, wide = piece.shape
+            row = pl.multiple_of(places[2 * n] * height, 16)
+            col = pl.multiple_of(places[2 * n + 1] * wide, LANES)
+            fresh[pl.ds(row, height), pl.ds(col, wide)] = piece[...]
+
+    def product(n):
+        half = fresh.shape[1] // 2
+        low, high = embeds[2 * n], embeds[2 * n + 1]
+        return dot_t(fresh[:, :half], low[...]) + dot_t(fresh[:, half:], high[...])
+
+    def absorb(raw, start, keep=None):
         for r in range(0, rows, band):
             ids = ids_ref[r : r + band] - start
             lane = ids & (LANES - 1)
             chunk = ids >> 7
             sums, found = total[r : r + band], picked[r : r + band]
             for c in range(span // LANES):
-                part = raw[side, r : r + band, c * LANES : (c + 1) * LANES]
-                part = jnp.tanh(part * (1.0 / 30.0))
+                part = jnp.tanh(raw[r : r + band, c * LANES : (c + 1) * LANES] * (1.0 / 30.0))
                 sums = sums + jnp.exp(30.0 * part)
                 there = jnp.take_along_axis(part, lane, axis=1, mode="promise_in_bounds")
                 found = found + jnp.where(chunk == c, there, 0.0)
@@ -304,62 +306,59 @@
             total[r : r + band] = sums
             picked[r : r + band] = found
 
-    for c in range(min(slots, chunks)):
-        copy(c).start()
-    raw[1] = jnp.zeros(raw.shape[1:], jnp.float32)
-    total[...] = jnp.zeros_like(total)
-    picked[...] = jnp.zeros_like(picked)
-    for n, piece in enumerate(pieces):
-        height, wide = piece.shape
-        row = pl.multiple_of(places[2 * n] * height, 16)
-        col = pl.multiple_of(places[2 * n + 1] * wide, LANES)
-        fresh[pl.ds(row, height), pl.ds(col, wide)] = piece[...]
-
-    @pl.loop(0, chunks // 2)
-    def _(pair):
-        first = 2 * pair
-        more = product(first)
-        absorb(1, (first - 1) * span, pair > 0)
-        raw[0] = more
-        refill(first)
-        more = product(first + 1)
-        absorb(0, first * span)
-        raw[1] = more
-        refill(first + 1)
-
-    absorb(1, (chunks - 1) * span)
-    place = lax.broadcasted_iota(jnp.int32, total.shape, 1)
-    whole = jnp.sum(total[...], axis=1, keepdims=True)
-    both = jnp.where(place < picks, 30.0 * picked[...], jnp.where(place == picks, whole, 0.0))
-    out_ref[...] = both.T[: out_ref.shape[0]]
+    base = step * streams * span
+    raw = product(0)
+    absorb(before[...], base - span, step > 0)
+    for n in range(1, streams):
+        more = product(n)
+        absorb(raw, base + (n - 1) * span)
+        raw = more
+    before[...] = raw
+
+    @pl.when(step == pl.num_programs(0) - 1)
+    def _():
+        absorb(before[...], base + (streams - 1) * span)
+        sums, found = total[...], picked[...]
+        place = lax.broadcasted_iota(jnp.int32, sums.shape, 1)
+        whole = jnp.sum(sums, axis=1, keepdims=True)
+        both = jnp.where(place < picks, 30.0 * found, jnp.where(place == picks, whole, 0.0))
+        out_ref[...] = both.T[: out_ref.shape[0]]
 
 
 def score_part(places, pieces, embedding, ids, picks):
     rows = ids.shape[0]
     vocab, depth = embedding.shape
-    span, slots = HEAD_SIZE, 4
+    span, streams = HEAD_SIZE, 2
     lines = -(-(picks + 1) // 8) * 8
-    return pl.pallas_call(
-        functools.partial(score_kernel, picks),
+    fixed = lambda i, places: (0, 0)
+    return pl.pallas_call(
+        functools.partial(score_kernel, picks, streams),
         out_shape=jax.ShapeDtypeStruct((lines, rows), jnp.float32),
-        in_specs=[in_smem()] + [in_vmem()] * (1 + len(pieces)) + [in_hbm()],
-        out_specs=in_vmem(),
-        scratch_shapes=[
-            pltpu.VMEM((rows, depth), jnp.bfloat16),
-            pltpu.VMEM((rows, LANES), jnp.float32),
-            pltpu.VMEM((rows, LANES), jnp.float32),
-            pltpu.VMEM((2, rows, span), jnp.float32),
-            pltpu.VMEM((slots, span, depth), jnp.bfloat16),
-            pltpu.SemaphoreType.DMA((slots,)),
-        ],
-        compiler_params=limit(24),
+        grid_spec=pltpu.PrefetchScalarGridSpec(
+            num_scalar_prefetch=1,
+            grid=(vocab // (span * streams),),
+            in_specs=[pl.BlockSpec((rows, LANES), fixed)]
+            + [pl.BlockSpec(piece.shape, fixed) for piece in pieces]
+            + [
+                pl.BlockSpec(
+                    (span, depth // 2), lambda i, places, n=n, k=k: (i * streams + n, k)
+                )
+                for n in range(streams)
+                for k in range(2)
+            ],
+            out_specs=pl.BlockSpec((lines, rows), fixed),
+            scratch_shapes=[pltpu.VMEM((rows, depth), jnp.bfloat16)]
+            + [pltpu.VMEM((rows, LANES), jnp.float32)] * 2
+            + [pltpu.VMEM((rows, span), jnp.float32)],
+        ),
+        compiler_params=limit(32),
         cost_estimate=pl.CostEstimate(
             flops=2 * rows * depth * vocab,
             bytes_accessed=2 * vocab * depth,
             transcendentals=2 * rows * vocab,
         ),
         name="score_part",
-    )(places, ids, *pieces, pin(embedding))
+    )(places, ids, *pieces, *[pin(embedding)] * (2 * streams))
 
 
 def draft_kernel(meta, hidden_hbm, weight_hbm, *refs):
@@ -476,16 +475,14 @@
     return lax.ppermute(value, axis, [(i, i ^ bits) for i in range(size)])
 
 
-def total_sum(value, sizes):
-    for axis, size in sizes:
-        step = 1
-        while step < size:
-            value = value + partner(value, axis, size, step)
-            step *= 2
-    return value
-
-
-def both_by_stages(hidden, parts, units, blocks, blk, mp, prompt, merge):
+def group_sum(value, axis, size, stride, count):
+    values = [value] + [partner(value, axis, size, k * stride) for k in range(1, count)]
+    while len(values) > 1:
+        values = [values[i] + values[i + 1] for i in range(0, len(values), 2)]
+    return values[0]
+
+
+def both_by_stages(hidden, parts, parents, units, blocks, blk, mp, prompt, merge):
     rows, model = hidden.shape
     half = units // 2
     layers = blocks // 4
@@ -493,17 +490,20 @@
     layer = blk // 4
     place = layer.reshape(1)
     got = [partner(parts[k], "blk", blocks, k) for k in range(1, 4)]
-    got, sent = lax.optimization_barrier((got, prompt()))
+    sent = prompt()
+    partials = spread(sent)
+    got, sent = lax.optimization_barrier((got, sent))
     parts = fold_part(parts[0], got, place, layers)
+    parts, parents = lax.optimization_barrier((parts, parents))
     more = [partner(parts[k], "blk", blocks, 4 * k) for k in range(1, layers)]
-    more, partials = lax.optimization_barrier((more, spread(sent)))
+    more, heads_out = lax.optimization_barrier((more, merge(partials, parents)))
     inner = parts[0] + sum(one.astype(jnp.float32) for one in more)
     base = lax.dynamic_slice(
         hidden, (layer * height, mp * units + (blk & 1) * half), (height, half)
     )
     own = (base.astype(jnp.float32) + jax.nn.silu(inner)).astype(jnp.bfloat16)
+    own, heads_out = lax.optimization_barrier((own, heads_out))
     chunks = [own] + [partner(own, "blk", blocks, 4 * k) for k in range(1, layers)]
-    chunks, heads_out = lax.optimization_barrier((chunks, merge(partials)))
     quad = stack_part(chunks, place)
     pieces = [quad] + [partner(quad, "blk", blocks, k) for k in range(1, 4)]
     pieces = pieces + [partner(piece, "mp", 2, 1) for piece in pieces]
@@ -573,7 +573,7 @@
     def prompt():
         return prompt_part(tree_q, prompt_key_value, meta, width, blocks)
 
-    def merge(partials):
+    def merge(partials, parents):
         reach = ancestry(parents)
         numer, denom = tree_part(tree_q, tree_key_value, reach, blk * width, width)
         return merge_part(partials, numer, denom)
@@ -582,16 +582,16 @@
         parts = draft_part(hidden, medusa_w, blk)
         parts, meta = lax.optimization_barrier((parts, meta))
         pieces, places, heads_out = both_by_stages(
-            hidden, parts, units, blocks, blk, mp, prompt, merge
+            hidden, parts, parents, units, blocks, blk, mp, prompt, merge
         )
     else:
         pieces = fresh_by_collectives(hidden, medusa_w, blocks, blk, mp)
         places = jnp.zeros((2,), jnp.int32)
-        heads_out = merge(spread(prompt()))
+        heads_out = merge(spread(prompt()), parents)
     heads_out = spread(heads_out)
     attn = project_part(heads_out, out_weight)
     attn, pieces = lax.optimization_barrier((attn, pieces))
-    attn = total_sum(attn, [("mp", splits)])
+    attn = group_sum(attn, "mp", splits, 1, splits)
     normed = attn * lax.rsqrt(jnp.mean(attn * attn, -1, keepdims=True) + 1e-06) * post_gain
     layer_out = (normed + resid.astype(jnp.float32)).astype(jnp.bfloat16)
 
@@ -600,7 +600,9 @@
     ids = cand_ids.reshape(lines, picks) - (blk * splits + mp) * vocab
     ids = jnp.pad(ids, ((0, 0), (0, LANES - picks)), constant_values=-1)
     score = score_part(places, pieces, embedding, ids, picks)
-    score = total_sum(score, [("mp", splits), ("blk", blocks)])
+    score = group_sum(score, "mp", splits, 1, splits)
+    score = group_sum(score, "blk", blocks, 1, 4)
+    score = group_sum(score, "blk", blocks, 4, blocks // 4)
     draft_logprob = score[:picks] - jnp.log(score[picks : picks + 1])
     draft_logprob = draft_logprob.T.reshape(drafts, rows, picks)
     return (draft_logprob, layer_out)

time: 117 us -> 104 us (0.89)
  waiting for transfers between devices: 31 us -> 21.1 us
  Pallas kernels: 43 us -> 37.4 us
  starting transfers between devices: 33.4 us -> 36.9 us
    ppermute x22 -> x24, waiting for transfers between devices: 28.9 us -> 15.4 us  [partner(): return lax.ppermute(value, axis, [(i, i ^ bits) for i in range(size)])]
    pallas_call x1, Pallas kernels: 22.4 us -> 16.7 us  [score_part(): pl.pallas_call(functools.partial(score_kernel, picks, streams), out_shape...]
    all_to_all x2, waiting for transfers between devices: 2.13 us -> 5.67 us  [spread(): return lax.all_to_all(value, 'blk', 0, 0, tiled=True)]
    ppermute x22 -> x24, starting transfers between devices: 22.5 us -> 25.1 us  [partner(): return lax.ppermute(value, axis, [(i, i ^ bits) for i in range(size)])]
  transfers between devices with their start and end apart: 24 -> 26, of which waited for: 10 -> 14; matrix products, arithmetic and copies ran while one was open for 2% -> 3% of each run, Pallas kernels for 34% -> 17%
where the time goes in v5:
time: 104 us; the launch traced here: 103 us
  Pallas kernels  37.4 us (36%)
  starting transfers between devices  36.9 us (35%)
  waiting for transfers between devices  21.1 us (20%)
  between operations  2.97 us (3%)
  other arithmetic  2.25 us (2%)
  matrix products  1.56 us (2%)
  local copies, waits for them, and re-layouts  1.05 us (1%)
    ppermute x24, starting transfers between devices, partner(): return lax.ppermute(value, axis, [(i, i ^ bits) for i in range(size)])  25.1 us
    pallas_call x1, Pallas kernels, score_part(): pl.pallas_call(functools.partial(score_kernel, picks, streams), out_shape...  16.7 us
    ppermute x24, waiting for transfers between devices, partner(): return lax.ppermute(value, axis, [(i, i ^ bits) for i in range(size)])  15.4 us
    all_to_all x2, starting transfers between devices, spread(): return lax.all_to_all(value, 'blk', 0, 0, tiled=True)  11.8 us
    pallas_call x1, Pallas kernels, prompt_part(): pl.pallas_call(prompt_kernel, out_shape=jax.ShapeDtypeStruct((blocks, tre...  7.01 us
    pallas_call x1, Pallas kernels, project_part(): pl.pallas_call(project_kernel, out_shape=jax.ShapeDtypeStruct((tokens, mo...  5.95 us
    all_to_all x2, waiting for transfers between devices, spread(): return lax.all_to_all(value, 'blk', 0, 0, tiled=True)  5.67 us
    pallas_call x1, Pallas kernels, draft_part(): pl.pallas_call(draft_kernel, out_shape=[jax.ShapeDtypeStruct((rows, half)...  3.08 us
  transfers between devices with their start and end apart: 26, of which 14 were waited for; matrix products, arithmetic and copies ran while one was open for 3% of the time, Pallas kernels for 17%

profile of v5, /device:TPU:0, one launch (start us, length us, event | category | flops | bytes accessed | tf_op | source)
XLA Modules:
  0.0 103.2 jit_solution(3510089854270700696)
XLA Ops:
  2.7 3.1 %draft_part.1 = (f32[144,896]{1,0:T(8,128)S(1)}, bf16[144,896]{1,0:T(8,128)(2,1)S(1)}, bf16[144,896]{1,0:T(8,128)(2,1)S(1)}, bf16[144,896]{1,0:T(8,128)(2,1)S(1)}) custom-call(s32[6]{0:T(128)S(1)} %stack.95.meta, bf16[144,3584]{1,0:T(8,128)(2,1)} %hidden_hbm.1, bf16[2,224,1792]{2,1,0:T(8,128)(2,1)} %weight_hbm.2), custom_call_target="tpu_custom_call" | custom-call | tf_op jit(solution)/shard_map/draft_part/pallas_call | solution.py:400
  5.9 3.0 %collective-permute-start = (bf16[144,896]{1,0:T(8,128)(2,1)S(1)}, bf16[144,896]{1,0:T(8,128)(2,1)S(1)}, u32[]{:S(2)}, u32[]{:S(2)}) collective-permute-start(bf16[144,896]{1,0:T(8,128)(2,1)S(1)} %get-tuple-element.45), channel_id=1, source_target_pairs={{0,2},{2,0},{4,6},{6,4},{8,10},{10,8},{12,14},{14,12},{16,18},{18,... | collective-permute-start | bytes 774152 | tf_op jit(solution)/shard_map/ppermute | solution.py:475
  8.8 1.5 %collective-permute-start.1 = (bf16[144,896]{1,0:T(8,128)(2,1)S(1)}, bf16[144,896]{1,0:T(8,128)(2,1)S(1)}, u32[]{:S(2)}, u32[]{:S(2)}) collective-permute-start(bf16[144,896]{1,0:T(8,128)(2,1)S(1)} %get-tuple-element.46), channel_id=1, source_target_pairs={{0,4},{2,6},{4,0},{6,2},{8,12},{10,14},{12,8},{14,10},{16,20},{18,... | collective-permute-start | bytes 774152 | tf_op jit(solution)/shard_map/ppermute | solution.py:475
  10.4 7.0 %prompt_part.1 = bf16[16,64,128]{2,1,0:T(8,128)(2,1)} custom-call(s32[3]{0:T(128)S(1)} %pad_add_fusion.meta, bf16[12,48,2048]{2,1,0:T(8,128)(2,1)} %q_hbm.3, bf16[2,1,2048,1024]{3,2,1,0:T(8,128)(2,1)} %kv_hbm.2), custom_call_target="tpu_custom_call" | custom-call | flops 805306368 | bytes 8388608 | tf_op jit(solution)/shard_map/prompt_part/pallas_call | solution.py:114
  17.4 7.3 %all-to-all-start = ((bf16[16,64,128]{2,1,0:T(8,128)(2,1)}), bf16[16,64,128]{2,1,0:T(8,128)(2,1)S(1)}, u32[]{:S(2)}, u32[]{:S(2)}) async-start(bf16[16,64,128]{2,1,0:T(8,128)(2,1)} %prompt_part.1), calls=%async_computation | async-start | bytes 524288 | tf_op jit(solution)/shard_map/all_to_all | solution.py:519
  24.9 0.2 fold_part.1
  25.2 2.0 %collective-permute-start.3 = (bf16[36,896]{1,0:T(8,128)(2,1)S(1)}, bf16[36,896]{1,0:T(8,128)(2,1)S(1)}, u32[]{:S(2)}, u32[]{:S(2)}) collective-permute-start(bf16[36,896]{1,0:T(8,128)(2,1)S(1)} %get-tuple-element.57), channel_id=1, source_target_pairs={{0,8},{2,10},{4,12},{6,14},{8,0},{10,2},{12,4},{14,6},{16,24},{18,... | collective-permute-start | bytes 193544 | tf_op jit(solution)/shard_map/ppermute | solution.py:475
  27.1 2.4 %collective-permute-start.4 = (bf16[36,896]{1,0:T(8,128)(2,1)S(1)}, bf16[36,896]{1,0:T(8,128)(2,1)S(1)}, u32[]{:S(2)}, u32[]{:S(2)}) collective-permute-start(bf16[36,896]{1,0:T(8,128)(2,1)S(1)} %get-tuple-element.58), channel_id=1, source_target_pairs={{0,16},{2,18},{4,20},{6,22},{8,24},{10,26},{12,28},{14,30},{16,0},... | collective-permute-start | bytes 193544 | tf_op jit(solution)/shard_map/ppermute | solution.py:475
  29.6 0.7 fusion.1
  30.3 0.4 fusion.3
  30.7 0.4 fusion.6.reach_ref
  31.2 2.3 %tree_part.1 = (f32[12,48,128]{2,1,0:T(8,128)S(1)}, f32[12,48,128]{2,1,0:T(8,128)S(1)}) custom-call(s32[3]{0:T(128)S(1)} %pad_add_fusion.1.meta, bf16[12,48,2048]{2,1,0:T(8,128)(2,1)} %q_hbm.3, bf16[2,12,48,1024]{3,2,1,0:T(8,128)(2,1)} %kv_hbm.3, f32[12,48,48]{2,1,0:T(8,128)S(1)} %fusion.6.reach_ref), custom_call_target="tpu_custom_call" | custom-call | tf_op jit(solution)/shard_map/tree_part/pallas_call | solution.py:166
  33.5 2.4 %all-to-all-done.got_ref = bf16[16,64,128]{2,1,0:T(8,128)(2,1)S(1)} async-done(((bf16[16,64,128]{2,1,0:T(8,128)(2,1)}), bf16[16,64,128]{2,1,0:T(8,128)(2,1)S(1)}, u32[]{:S(2)}, u32[]{:S(2)}) %all-to-all-start) | async-done | bytes 262176 | tf_op jit(solution)/shard_map/all_to_all | solution.py:519
  35.9 2.1 %merge_part.1 = bf16[16,36,128]{2,1,0:T(8,128)(2,1)} custom-call(bf16[16,64,128]{2,1,0:T(8,128)(2,1)S(1)} %all-to-all-done.got_ref, f32[12,48,128]{2,1,0:T(8,128)S(1)} %get-tuple-element.61.numer_ref, f32[12,48,128]{2,1,0:T(8,128)S(1)} %get-tuple-element.62.denom_ref), custom_call_target="tpu_custom_call" | custom-call | tf_op jit(solution)/shard_map/merge_part/pallas_call | solution.py:215
  38.0 1.0 add_convert_fusion.1.refs_0_
  39.0 1.6 %collective-permute-start.6 = (bf16[36,896]{1,0:T(8,128)(2,1)S(1)}, bf16[36,896]{1,0:T(8,128)(2,1)S(1)}, u32[]{:S(2)}, u32[]{:S(2)}) collective-permute-start(bf16[36,896]{1,0:T(8,128)(2,1)S(1)} %add_convert_fusion.1.refs_0_), channel_id=1, source_target_pairs={{0,8},{2,10},{4,12},{6,14},{8,0},{10,2},{12,4},{14,6},{16,24},{18,... | collective-permute-start | bytes 193544 | tf_op jit(solution)/shard_map/ppermute | solution.py:475
  40.6 1.7 %collective-permute-start.7 = (bf16[36,896]{1,0:T(8,128)(2,1)S(1)}, bf16[36,896]{1,0:T(8,128)(2,1)S(1)}, u32[]{:S(2)}, u32[]{:S(2)}) collective-permute-start(bf16[36,896]{1,0:T(8,128)(2,1)S(1)} %add_convert_fusion.1.refs_0_), channel_id=1, source_target_pairs={{0,16},{2,18},{4,20},{6,22},{8,24},{10,26},{12,28},{14,30},{16,0},... | collective-permute-start | bytes 193544 | tf_op jit(solution)/shard_map/ppermute | solution.py:475
  42.3 1.1 %collective-permute-start.8 = (bf16[36,896]{1,0:T(8,128)(2,1)S(1)}, bf16[36,896]{1,0:T(8,128)(2,1)S(1)}, u32[]{:S(2)}, u32[]{:S(2)}) collective-permute-start(bf16[36,896]{1,0:T(8,128)(2,1)S(1)} %add_convert_fusion.1.refs_0_), channel_id=1, source_target_pairs={{0,24},{2,26},{4,28},{6,30},{8,16},{10,18},{12,20},{14,22},{16,8},... | collective-permute-start | bytes 193544 | tf_op jit(solution)/shard_map/ppermute | solution.py:475
  43.5 1.4 %collective-permute-done.6.refs_1_ = bf16[36,896]{1,0:T(8,128)(2,1)S(1)} collective-permute-done((bf16[36,896]{1,0:T(8,128)(2,1)S(1)}, bf16[36,896]{1,0:T(8,128)(2,1)S(1)}, u32[]{:S(2)}, u32[]{:S(2)}) %collective-permute-start.6) | collective-permute-done | bytes 64544 | tf_op jit(solution)/shard_map/ppermute | solution.py:475
  44.9 1.9 %collective-permute-done.7.refs_2_ = bf16[36,896]{1,0:T(8,128)(2,1)S(1)} collective-permute-done((bf16[36,896]{1,0:T(8,128)(2,1)S(1)}, bf16[36,896]{1,0:T(8,128)(2,1)S(1)}, u32[]{:S(2)}, u32[]{:S(2)}) %collective-permute-start.7) | collective-permute-done | bytes 64544 | tf_op jit(solution)/shard_map/ppermute | solution.py:475
  46.8 1.7 %collective-permute-done.8.refs_3_ = bf16[36,896]{1,0:T(8,128)(2,1)S(1)} collective-permute-done((bf16[36,896]{1,0:T(8,128)(2,1)S(1)}, bf16[36,896]{1,0:T(8,128)(2,1)S(1)}, u32[]{:S(2)}, u32[]{:S(2)}) %collective-permute-start.8) | collective-permute-done | bytes 64544 | tf_op jit(solution)/shard_map/ppermute | solution.py:475
  48.5 0.7 collective-permute-start.9
  49.3 1.8 %collective-permute-start.10 = (bf16[144,896]{1,0:T(8,128)(2,1)S(1)}, bf16[144,896]{1,0:T(8,128)(2,1)S(1)}, u32[]{:S(2)}, u32[]{:S(2)}) collective-permute-start(bf16[144,896]{1,0:T(8,128)(2,1)S(1)} %stack_part.1.refs_0_), channel_id=1, source_target_pairs={{0,4},{2,6},{4,0},{6,2},{8,12},{10,14},{12,8},{14,10},{16,20},{18,... | collective-permute-start | bytes 774152 | tf_op jit(solution)/shard_map/ppermute | solution.py:475
  51.1 1.0 collective-permute-start.11
  52.1 4.4 %all-to-all-start.1 = ((bf16[16,36,128]{2,1,0:T(8,128)(2,1)}), bf16[16,36,128]{2,1,0:T(8,128)(2,1)S(1)}, u32[]{:S(2)}, u32[]{:S(2)}) async-start(bf16[16,36,128]{2,1,0:T(8,128)(2,1)} %merge_part.1), calls=%async_computation.1 | async-start | bytes 327680 | tf_op jit(solution)/shard_map/all_to_all | solution.py:519
  56.7 0.5 collective-permute-start.13
  57.1 3.3 %collective-permute-done.10.refs_2_ = bf16[144,896]{1,0:T(8,128)(2,1)S(1)} collective-permute-done((bf16[144,896]{1,0:T(8,128)(2,1)S(1)}, bf16[144,896]{1,0:T(8,128)(2,1)S(1)}, u32[]{:S(2)}, u32[]{:S(2)}) %collective-permute-start.10) | collective-permute-done | bytes 258080 | tf_op jit(solution)/shard_map/ppermute | solution.py:475
  60.5 0.5 collective-permute-start.15
  61.0 0.1 copy.16
  61.2 3.2 %all-to-all-done.1.heads_ref = bf16[16,36,128]{2,1,0:T(8,128)(2,1)S(1)} async-done(((bf16[16,36,128]{2,1,0:T(8,128)(2,1)}), bf16[16,36,128]{2,1,0:T(8,128)(2,1)S(1)}, u32[]{:S(2)}, u32[]{:S(2)}) %all-to-all-start.1) | async-done | bytes 147488 | tf_op jit(solution)/shard_map/all_to_all | solution.py:519
  64.5 5.9 %project_part.1 = f32[36,3584]{1,0:T(8,128)S(1)} custom-call(bf16[16,36,128]{2,1,0:T(8,128)(2,1)S(1)} %all-to-all-done.1.heads_ref, bf16[2048,3584]{1,0:T(8,128)(2,1)} %weight_hbm.3), custom_call_target="tpu_custom_call" | custom-call | flops 528482304 | bytes 14680064 | tf_op jit(solution)/shard_map/project_part/pallas_call | solution.py:252
  70.5 16.7 %score_part.1 = f32[16,288]{1,0:T(8,128)S(1)} custom-call(s32[16]{0:T(128)S(1)} %stack.88.places, s32[288,128]{1,0:T(8,128)S(1)} %pad.4.ids_ref, bf16[144,896]{1,0:T(8,128)(2,1)S(1)} %stack_part.1.refs_0_, bf16[144,896]{1,0:T(8,128)(2,1)S(1)} %collective-permute-done.9.refs_1_, bf16[144,896]{1,0:T(8,128)(2,1)S(1)} %collective-permute-done.10.refs_2_, ...), custom_call_target="tpu_custom_call" | custom-call | flops 8455716864 | bytes 29360128 | tf_op jit(solution)/shard_map/score_part/pallas_call | solution.py:334
  87.3 1.2 %collective-permute-done.16 = f32[16,288]{1,0:T(8,128)S(1)} collective-permute-done((f32[16,288]{1,0:T(8,128)S(1)}, f32[16,288]{1,0:T(8,128)S(1)}, u32[]{:S(2)}, u32[]{:S(2)}) %collective-permute-start.16) | collective-permute-done | bytes 18464 | tf_op jit(solution)/shard_map/ppermute | solution.py:475
  88.5 0.8 collective-permute-start.18
  89.2 1.9 %collective-permute-start.19 = (f32[16,288]{1,0:T(8,128)S(1)}, f32[16,288]{1,0:T(8,128)S(1)}, u32[]{:S(2)}, u32[]{:S(2)}) collective-permute-start(f32[16,288]{1,0:T(8,128)S(1)} %add.129), channel_id=1, source_target_pairs={{0,6},{2,4},{4,2},{6,0},{8,14},{10,12},{12,10},{14,8},{16,22},{18,... | collective-permute-start | bytes 55304 | tf_op jit(solution)/shard_map/ppermute | solution.py:475
  91.1 0.8 collective-permute-start.17
  91.9 0.3 collective-permute-done.18
  92.3 1.7 %collective-permute-done.19 = f32[16,288]{1,0:T(8,128)S(1)} collective-permute-done((f32[16,288]{1,0:T(8,128)S(1)}, f32[16,288]{1,0:T(8,128)S(1)}, u32[]{:S(2)}, u32[]{:S(2)}) %collective-permute-start.19) | collective-permute-done | bytes 18464 | tf_op jit(solution)/shard_map/ppermute | solution.py:475
  94.0 1.0 collective-permute-done.17
  95.0 0.4 collective-permute-start.21
  95.4 2.1 %collective-permute-start.22 = (f32[16,288]{1,0:T(8,128)S(1)}, f32[16,288]{1,0:T(8,128)S(1)}, u32[]{:S(2)}, u32[]{:S(2)}) collective-permute-start(f32[16,288]{1,0:T(8,128)S(1)} %add_add_fusion.1), channel_id=1, source_target_pairs={{0,24},{2,26},{4,28},{6,30},{8,16},{10,18},{12,20},{14,22},{16,8},... | collective-permute-start | bytes 55304 | tf_op jit(solution)/shard_map/ppermute | solution.py:475
  97.5 1.0 collective-permute-start.20
  98.5 1.2 %collective-permute-done.21 = f32[16,288]{1,0:T(8,128)S(1)} collective-permute-done((f32[16,288]{1,0:T(8,128)S(1)}, f32[16,288]{1,0:T(8,128)S(1)}, u32[]{:S(2)}, u32[]{:S(2)}) %collective-permute-start.21) | collective-permute-done | bytes 18464 | tf_op jit(solution)/shard_map/ppermute | solution.py:475
  99.8 1.2 %collective-permute-done.22 = f32[16,288]{1,0:T(8,128)S(1)} collective-permute-done((f32[16,288]{1,0:T(8,128)S(1)}, f32[16,288]{1,0:T(8,128)S(1)}, u32[]{:S(2)}, u32[]{:S(2)}) %collective-permute-start.22) | collective-permute-done | bytes 18464 | tf_op jit(solution)/shard_map/ppermute | solution.py:475
  101.0 0.3 collective-permute-done.20
  101.4 0.7 reshape.37
  102.1 0.2 multiply_reduce_fusion
  102.3 0.9 add_convert_fusion
  (42 shorter events, 0.9 us)
Async XLA Ops:
  0.6 29.0 %copy-start.3 = (s32[12,48]{1,0:T(8,128)S(1)}, s32[12,48]{1,0:T(8,128)}, u32[]{:S(2)}) copy-start(s32[12,48]{1,0:T(8,128)} %param.24) | copy-start | bytes 6916
  5.9 55.1 %copy-start.1 = (s32[2,144,10]{1,0,2:T(2,128)S(1)}, s32[2,144,10]{1,0,2:T(2,128)}, u32[]{:S(2)}) copy-start(s32[2,144,10]{1,0,2:T(2,128)} %param.17) | copy-start | bytes 34564
  5.9 19.0 %collective-permute-start = (bf16[144,896]{1,0:T(8,128)(2,1)S(1)}, bf16[144,896]{1,0:T(8,128)(2,1)S(1)}, u32[]{:S(2)}, u32[]{:S(2)}) collective-permute-start(bf16[144,896]{1,0:T(8,128)(2,1)S(1)} %get-tuple-element.45), channel_id=1, source_target_pairs={{0,2},{2,0},{4,6},{6,4},{8,10},{10,8},{12,14},{14,12},{16,18},{18,... | collective-permute-start | bytes 774152 | tf_op jit(solution)/shard_map/ppermute | solution.py:475
  8.8 16.1 %collective-permute-start.1 = (bf16[144,896]{1,0:T(8,128)(2,1)S(1)}, bf16[144,896]{1,0:T(8,128)(2,1)S(1)}, u32[]{:S(2)}, u32[]{:S(2)}) collective-permute-start(bf16[144,896]{1,0:T(8,128)(2,1)S(1)} %get-tuple-element.46), channel_id=1, source_target_pairs={{0,4},{2,6},{4,0},{6,2},{8,12},{10,14},{12,8},{14,10},{16,20},{18,... | collective-permute-start | bytes 774152 | tf_op jit(solution)/shard_map/ppermute | solution.py:475
  10.3 14.6 %collective-permute-start.2 = (bf16[144,896]{1,0:T(8,128)(2,1)S(1)}, bf16[144,896]{1,0:T(8,128)(2,1)S(1)}, u32[]{:S(2)}, u32[]{:S(2)}) collective-permute-start(bf16[144,896]{1,0:T(8,128)(2,1)S(1)} %get-tuple-element.47), channel_id=1, source_target_pairs={{0,6},{2,4},{4,2},{6,0},{8,14},{10,12},{12,10},{14,8},{16,22},{18,... | collective-permute-start | bytes 774152 | tf_op jit(solution)/shard_map/ppermute | solution.py:475
  17.4 18.5 %all-to-all-start = ((bf16[16,64,128]{2,1,0:T(8,128)(2,1)}), bf16[16,64,128]{2,1,0:T(8,128)(2,1)S(1)}, u32[]{:S(2)}, u32[]{:S(2)}) async-start(bf16[16,64,128]{2,1,0:T(8,128)(2,1)} %prompt_part.1), calls=%async_computation | async-start | bytes 524288 | tf_op jit(solution)/shard_map/all_to_all | solution.py:519
  25.2 12.8 %collective-permute-start.3 = (bf16[36,896]{1,0:T(8,128)(2,1)S(1)}, bf16[36,896]{1,0:T(8,128)(2,1)S(1)}, u32[]{:S(2)}, u32[]{:S(2)}) collective-permute-start(bf16[36,896]{1,0:T(8,128)(2,1)S(1)} %get-tuple-element.57), channel_id=1, source_target_pairs={{0,8},{2,10},{4,12},{6,14},{8,0},{10,2},{12,4},{14,6},{16,24},{18,... | collective-permute-start | bytes 193544 | tf_op jit(solution)/shard_map/ppermute | solution.py:475
  27.1 10.9 %collective-permute-start.4 = (bf16[36,896]{1,0:T(8,128)(2,1)S(1)}, bf16[36,896]{1,0:T(8,128)(2,1)S(1)}, u32[]{:S(2)}, u32[]{:S(2)}) collective-permute-start(bf16[36,896]{1,0:T(8,128)(2,1)S(1)} %get-tuple-element.58), channel_id=1, source_target_pairs={{0,16},{2,18},{4,20},{6,22},{8,24},{10,26},{12,28},{14,30},{16,0},... | collective-permute-start | bytes 193544 | tf_op jit(solution)/shard_map/ppermute | solution.py:475
  29.5 8.5 %collective-permute-start.5 = (bf16[36,896]{1,0:T(8,128)(2,1)S(1)}, bf16[36,896]{1,0:T(8,128)(2,1)S(1)}, u32[]{:S(2)}, u32[]{:S(2)}) collective-permute-start(bf16[36,896]{1,0:T(8,128)(2,1)S(1)} %get-tuple-element.59), channel_id=1, source_target_pairs={{0,24},{2,26},{4,28},{6,30},{8,16},{10,18},{12,20},{14,22},{16,8},... | collective-permute-start | bytes 193544 | tf_op jit(solution)/shard_map/ppermute | solution.py:475
  39.0 5.9 %collective-permute-start.6 = (bf16[36,896]{1,0:T(8,128)(2,1)S(1)}, bf16[36,896]{1,0:T(8,128)(2,1)S(1)}, u32[]{:S(2)}, u32[]{:S(2)}) collective-permute-start(bf16[36,896]{1,0:T(8,128)(2,1)S(1)} %add_convert_fusion.1.refs_0_), channel_id=1, source_target_pairs={{0,8},{2,10},{4,12},{6,14},{8,0},{10,2},{12,4},{14,6},{16,24},{18,... | collective-permute-start | bytes 193544 | tf_op jit(solution)/shard_map/ppermute | solution.py:475
  40.6 6.1 %collective-permute-start.7 = (bf16[36,896]{1,0:T(8,128)(2,1)S(1)}, bf16[36,896]{1,0:T(8,128)(2,1)S(1)}, u32[]{:S(2)}, u32[]{:S(2)}) collective-permute-start(bf16[36,896]{1,0:T(8,128)(2,1)S(1)} %add_convert_fusion.1.refs_0_), channel_id=1, source_target_pairs={{0,16},{2,18},{4,20},{6,22},{8,24},{10,26},{12,28},{14,30},{16,0},... | collective-permute-start | bytes 193544 | tf_op jit(solution)/shard_map/ppermute | solution.py:475
  42.3 6.1 %collective-permute-start.8 = (bf16[36,896]{1,0:T(8,128)(2,1)S(1)}, bf16[36,896]{1,0:T(8,128)(2,1)S(1)}, u32[]{:S(2)}, u32[]{:S(2)}) collective-permute-start(bf16[36,896]{1,0:T(8,128)(2,1)S(1)} %add_convert_fusion.1.refs_0_), channel_id=1, source_target_pairs={{0,24},{2,26},{4,28},{6,30},{8,16},{10,18},{12,20},{14,22},{16,8},... | collective-permute-start | bytes 193544 | tf_op jit(solution)/shard_map/ppermute | solution.py:475
  48.5 8.1 %collective-permute-start.9 = (bf16[144,896]{1,0:T(8,128)(2,1)S(1)}, bf16[144,896]{1,0:T(8,128)(2,1)S(1)}, u32[]{:S(2)}, u32[]{:S(2)}) collective-permute-start(bf16[144,896]{1,0:T(8,128)(2,1)S(1)} %stack_part.1.refs_0_), channel_id=1, source_target_pairs={{0,2},{2,0},{4,6},{6,4},{8,10},{10,8},{12,14},{14,12},{16,18},{18,... | collective-permute-start | bytes 774152 | tf_op jit(solution)/shard_map/ppermute | solution.py:475
  49.3 11.2 %collective-permute-start.10 = (bf16[144,896]{1,0:T(8,128)(2,1)S(1)}, bf16[144,896]{1,0:T(8,128)(2,1)S(1)}, u32[]{:S(2)}, u32[]{:S(2)}) collective-permute-start(bf16[144,896]{1,0:T(8,128)(2,1)S(1)} %stack_part.1.refs_0_), channel_id=1, source_target_pairs={{0,4},{2,6},{4,0},{6,2},{8,12},{10,14},{12,8},{14,10},{16,20},{18,... | collective-permute-start | bytes 774152 | tf_op jit(solution)/shard_map/ppermute | solution.py:475
  51.1 9.3 %collective-permute-start.11 = (bf16[144,896]{1,0:T(8,128)(2,1)S(1)}, bf16[144,896]{1,0:T(8,128)(2,1)S(1)}, u32[]{:S(2)}, u32[]{:S(2)}) collective-permute-start(bf16[144,896]{1,0:T(8,128)(2,1)S(1)} %stack_part.1.refs_0_), channel_id=1, source_target_pairs={{0,6},{2,4},{4,2},{6,0},{8,14},{10,12},{12,10},{14,8},{16,22},{18,... | collective-permute-start | bytes 774152 | tf_op jit(solution)/shard_map/ppermute | solution.py:475
  52.1 12.4 %all-to-all-start.1 = ((bf16[16,36,128]{2,1,0:T(8,128)(2,1)}), bf16[16,36,128]{2,1,0:T(8,128)(2,1)S(1)}, u32[]{:S(2)}, u32[]{:S(2)}) async-start(bf16[16,36,128]{2,1,0:T(8,128)(2,1)} %merge_part.1), calls=%async_computation.1 | async-start | bytes 327680 | tf_op jit(solution)/shard_map/all_to_all | solution.py:519
  56.6 13.9 %collective-permute-start.12 = (bf16[144,896]{1,0:T(8,128)(2,1)S(1)}, bf16[144,896]{1,0:T(8,128)(2,1)S(1)}, u32[]{:S(2)}, u32[]{:S(2)}) collective-permute-start(bf16[144,896]{1,0:T(8,128)(2,1)S(1)} %stack_part.1.refs_0_), channel_id=1, source_target_pairs={{0,1},{1,0},{2,3},{3,2},{4,5},{5,4},{6,7},{7,6},{8,9},{9,8},{10,11... | collective-permute-start | bytes 774152 | tf_op jit(solution)/shard_map/ppermute | solution.py:475
  56.7 13.8 %collective-permute-start.13 = (bf16[144,896]{1,0:T(8,128)(2,1)S(1)}, bf16[144,896]{1,0:T(8,128)(2,1)S(1)}, u32[]{:S(2)}, u32[]{:S(2)}) collective-permute-start(bf16[144,896]{1,0:T(8,128)(2,1)S(1)} %collective-permute-done.9.refs_1_), channel_id=1, source_target_pairs={{0,1},{1,0},{2,3},{3,2},{4,5},{5,4},{6,7},{7,6},{8,9},{9,8},{10,11... | collective-permute-start | bytes 774152 | tf_op jit(solution)/shard_map/ppermute | solution.py:475
  60.5 10.0 %collective-permute-start.14 = (bf16[144,896]{1,0:T(8,128)(2,1)S(1)}, bf16[144,896]{1,0:T(8,128)(2,1)S(1)}, u32[]{:S(2)}, u32[]{:S(2)}) collective-permute-start(bf16[144,896]{1,0:T(8,128)(2,1)S(1)} %collective-permute-done.10.refs_2_), channel_id=1, source_target_pairs={{0,1},{1,0},{2,3},{3,2},{4,5},{5,4},{6,7},{7,6},{8,9},{9,8},{10,11... | collective-permute-start | bytes 774152 | tf_op jit(solution)/shard_map/ppermute | solution.py:475
  60.5 10.0 %collective-permute-start.15 = (bf16[144,896]{1,0:T(8,128)(2,1)S(1)}, bf16[144,896]{1,0:T(8,128)(2,1)S(1)}, u32[]{:S(2)}, u32[]{:S(2)}) collective-permute-start(bf16[144,896]{1,0:T(8,128)(2,1)S(1)} %collective-permute-done.11.refs_3_), channel_id=1, source_target_pairs={{0,1},{1,0},{2,3},{3,2},{4,5},{5,4},{6,7},{7,6},{8,9},{9,8},{10,11... | collective-permute-start | bytes 774152 | tf_op jit(solution)/shard_map/ppermute | solution.py:475
  70.4 31.9 %copy-start = (bf16[36,3584]{1,0:T(8,128)(2,1)S(1)}, bf16[36,3584]{1,0:T(8,128)(2,1)}, u32[]{:S(2)}) copy-start(bf16[36,3584]{1,0:T(8,128)(2,1)} %param.27) | copy-start | bytes 774148
  70.4 31.9 %copy-start.2 = (f32[3584]{0:T(1024)S(1)}, f32[3584]{0:T(1024)}, u32[]{:S(2)}) copy-start(f32[3584]{0:T(1024)} %param.26) | copy-start | bytes 43012
  87.2 1.3 %collective-permute-start.16 = (f32[16,288]{1,0:T(8,128)S(1)}, f32[16,288]{1,0:T(8,128)S(1)}, u32[]{:S(2)}, u32[]{:S(2)}) collective-permute-start(f32[16,288]{1,0:T(8,128)S(1)} %score_part.1), channel_id=1, source_target_pairs={{0,1},{1,0},{2,3},{3,2},{4,5},{5,4},{6,7},{7,6},{8,9},{9,8},{10,11... | collective-permute-start | bytes 55304 | tf_op jit(solution)/shard_map/ppermute | solution.py:475
  88.5 3.8 %collective-permute-start.18 = (f32[16,288]{1,0:T(8,128)S(1)}, f32[16,288]{1,0:T(8,128)S(1)}, u32[]{:S(2)}, u32[]{:S(2)}) collective-permute-start(f32[16,288]{1,0:T(8,128)S(1)} %add.129), channel_id=1, source_target_pairs={{0,4},{2,6},{4,0},{6,2},{8,12},{10,14},{12,8},{14,10},{16,20},{18,... | collective-permute-start | bytes 55304 | tf_op jit(solution)/shard_map/ppermute | solution.py:475
  89.2 4.7 %collective-permute-start.19 = (f32[16,288]{1,0:T(8,128)S(1)}, f32[16,288]{1,0:T(8,128)S(1)}, u32[]{:S(2)}, u32[]{:S(2)}) collective-permute-start(f32[16,288]{1,0:T(8,128)S(1)} %add.129), channel_id=1, source_target_pairs={{0,6},{2,4},{4,2},{6,0},{8,14},{10,12},{12,10},{14,8},{16,22},{18,... | collective-permute-start | bytes 55304 | tf_op jit(solution)/shard_map/ppermute | solution.py:475
  91.1 3.8 %collective-permute-start.17 = (f32[16,288]{1,0:T(8,128)S(1)}, f32[16,288]{1,0:T(8,128)S(1)}, u32[]{:S(2)}, u32[]{:S(2)}) collective-permute-start(f32[16,288]{1,0:T(8,128)S(1)} %add.129), channel_id=1, source_target_pairs={{0,2},{2,0},{4,6},{6,4},{8,10},{10,8},{12,14},{14,12},{16,18},{18,... | collective-permute-start | bytes 55304 | tf_op jit(solution)/shard_map/ppermute | solution.py:475
  95.0 4.8 %collective-permute-start.21 = (f32[16,288]{1,0:T(8,128)S(1)}, f32[16,288]{1,0:T(8,128)S(1)}, u32[]{:S(2)}, u32[]{:S(2)}) collective-permute-start(f32[16,288]{1,0:T(8,128)S(1)} %add_add_fusion.1), channel_id=1, source_target_pairs={{0,16},{2,18},{4,20},{6,22},{8,24},{10,26},{12,28},{14,30},{16,0},... | collective-permute-start | bytes 55304 | tf_op jit(solution)/shard_map/ppermute | solution.py:475
  95.4 5.6 %collective-permute-start.22 = (f32[16,288]{1,0:T(8,128)S(1)}, f32[16,288]{1,0:T(8,128)S(1)}, u32[]{:S(2)}, u32[]{:S(2)}) collective-permute-start(f32[16,288]{1,0:T(8,128)S(1)} %add_add_fusion.1), channel_id=1, source_target_pairs={{0,24},{2,26},{4,28},{6,30},{8,16},{10,18},{12,20},{14,22},{16,8},... | collective-permute-start | bytes 55304 | tf_op jit(solution)/shard_map/ppermute | solution.py:475
  97.5 3.8 %collective-permute-start.20 = (f32[16,288]{1,0:T(8,128)S(1)}, f32[16,288]{1,0:T(8,128)S(1)}, u32[]{:S(2)}, u32[]{:S(2)}) collective-permute-start(f32[16,288]{1,0:T(8,128)S(1)} %add_add_fusion.1), channel_id=1, source_target_pairs={{0,8},{2,10},{4,12},{6,14},{8,0},{10,2},{12,4},{14,6},{16,24},{18,... | collective-permute-start | bytes 55304 | tf_op jit(solution)/shard_map/ppermute | solution.py:475
  98.5 3.6 %collective-permute-start.23 = (f32[36,3584]{1,0:T(8,128)S(1)}, f32[36,3584]{1,0:T(8,128)S(1)}, u32[]{:S(2)}, u32[]{:S(2)}) collective-permute-start(f32[36,3584]{1,0:T(8,128)S(1)} %project_part.1), channel_id=1, source_target_pairs={{0,1},{1,0},{2,3},{3,2},{4,5},{5,4},{6,7},{7,6},{8,9},{9,8},{10,11... | collective-permute-start | bytes 1548296 | tf_op jit(solution)/shard_map/ppermute | solution.py:475

commit v6 on v5

--- a/solution.py
+++ b/solution.py
@@ -68,7 +68,8 @@
     row_id = lax.broadcasted_iota(jnp.int32, (tree_size, width), 0)
     lane_id = lax.broadcasted_iota(jnp.int32, (tree_size, width), 1)
     extra_id = lax.broadcasted_iota(jnp.int32, (EXTRA, width), 0)
-    slot = lax.broadcasted_iota(jnp.int32, (rows, slots), 1)
+    span = min(512, slots)
+    slot = lax.broadcasted_iota(jnp.int32, (rows, span), 1)
     for h in range(kv_heads):
         asked = jnp.concatenate(
             [
@@ -80,15 +81,23 @@
         copies[2 * h].wait()
         if 2 * h + ahead < len(copies):
             copies[2 * h + ahead].start()
-        scores = dot_t(asked, held[0, h])
-        weights = jnp.where(slot < last, soft_weights(scores), 0.0)
-        denom = jnp.sum(weights, axis=1, keepdims=True)
-        copies[2 * h + 1].wait()
-        if 2 * h + 1 + ahead < len(copies):
-            copies[2 * h + 1 + ahead].start()
-        numer = jnp.dot(
-            weights.astype(jnp.bfloat16), held[1, h], preferred_element_type=jnp.float32
-        )
+        numer = jnp.zeros((rows, HEAD_SIZE), jnp.float32)
+        sums = jnp.zeros((rows, LANES), jnp.float32)
+        for start in range(0, slots, span):
+            scores = dot_t(asked, held[0, h, start : start + span])
+            weights = jnp.where(slot < last - start, soft_weights(scores), 0.0)
+            for c in range(0, span, LANES):
+                sums = sums + weights[:, c : c + LANES]
+            if start == 0:
+                copies[2 * h + 1].wait()
+                if 2 * h + 1 + ahead < len(copies):
+                    copies[2 * h + 1 + ahead].start()
+            numer = numer + jnp.dot(
+                weights.astype(jnp.bfloat16),
+                held[1, h, start : start + span],
+                preferred_element_type=jnp.float32,
+            )
+        denom = jnp.sum(sums, axis=1, keepdims=True)
         for r in range(repeats):
             mine = jnp.broadcast_to(denom[r * tree_size : (r + 1) * tree_size], (tree_size, width))
             extra = jnp.where(extra_id == GROUP, group.astype(jnp.float32), 0.0)
@@ -131,7 +140,7 @@
     )(meta, pin(tree_q), pin(prompt_key_value))
 
 
-def tree_kernel(meta, q_hbm, kv_hbm, reach_ref, numer_ref, denom_ref, held, sems):
+def tree_kernel(meta, q_hbm, kv_hbm, parents_ref, numer_ref, denom_ref, held, sems):
     width = numer_ref.shape[2]
     query_columns = pl.ds(pl.multiple_of(meta[0] * HEAD_SIZE, HEAD_SIZE), HEAD_SIZE)
     key_columns = pl.ds(pl.multiple_of(meta[1] * HEAD_SIZE, HEAD_SIZE), HEAD_SIZE)
@@ -142,10 +151,25 @@
     ]
     for copy in copies:
         copy.start()
+    groups, count = parents_ref.shape
+    above = lax.broadcasted_iota(jnp.int32, (count, count), 0)
+    token = lax.broadcasted_iota(jnp.int32, (count, count), 1)
+    met = [
+        jnp.where(
+            (above == token) | ((parents_ref[g : g + 1, :] == above) & (token > 0)), 1.0, 0.0
+        )
+        for g in range(groups)
+    ]
+    for sweep in range(count.bit_length()):
+        small = [one.astype(jnp.bfloat16) for one in met]
+        met = [
+            jnp.minimum(jnp.dot(one, one, preferred_element_type=jnp.float32), 1.0)
+            for one in small
+        ]
     for copy in copies:
         copy.wait()
-    for g in range(held.shape[1]):
-        weights = soft_weights(dot_t(held[0, g], held[1, g])) * reach_ref[g]
+    for g in range(groups):
+        weights = soft_weights(dot_t(held[0, g], held[1, g])) * met[g].T
         denom_ref[g] = jnp.broadcast_to(
             jnp.sum(weights, axis=1, keepdims=True), denom_ref.shape[1:]
         )
@@ -158,7 +182,7 @@
         numer_ref[g] = mine
 
 
-def tree_part(tree_q, tree_key_value, reach, column, width):
+def tree_part(tree_q, tree_key_value, parents, column, width):
     groups, tree_size, features = tree_q.shape
     repeats = features // tree_key_value.shape[3]
     head = column // HEAD_SIZE
@@ -174,34 +198,30 @@
         ],
         compiler_params=limit(16),
         name="tree_part",
-    )(meta, pin(tree_q), pin(tree_key_value), reach)
-
-
-def merge_kernel(got_ref, numer_ref, denom_ref, out_ref, hold):
+    )(meta, pin(tree_q), pin(tree_key_value), parents)
+
+
+def merge_kernel(got_ref, numer_ref, denom_ref, out_ref, hold, sums, lines):
     blocks = got_ref.shape[0]
     groups, tree_size, width = numer_ref.shape
     row_id = lax.broadcasted_iota(jnp.int32, (tree_size, width), 0)
     lane_id = lax.broadcasted_iota(jnp.int32, (tree_size, width), 1)
-    lines = -(-tree_size // width)
-
-    @pl.loop(0, groups)
-    def _(g):
-        def add(b, carry):
-            numer, extra = carry
-            more = got_ref[b, tree_size:, :].astype(jnp.float32)
-            same = more[GROUP : GROUP + 1, :] == g.astype(jnp.float32)
-            numer = numer + jnp.where(same, got_ref[b, :tree_size, :].astype(jnp.float32), 0.0)
-            extra = extra + jnp.where(same, more, 0.0)
-            return numer, extra
-
-        start = (numer_ref[g], jnp.zeros((EXTRA, width), jnp.float32))
-        numer, extra = lax.fori_loop(0, blocks, add, start, unroll=True)
+    sums[...] = numer_ref[...]
+    lines[...] = jnp.zeros_like(lines)
+    owners = []
+    for b in range(blocks):
+        extra = got_ref[b, tree_size:, :].astype(jnp.float32)
+        owners.append(jnp.max(extra[GROUP : GROUP + 1, :]).astype(jnp.int32))
+    for b in range(blocks):
+        sums[owners[b]] += got_ref[b, :tree_size, :].astype(jnp.float32)
+        lines[owners[b]] += got_ref[b, tree_size:, :].astype(jnp.float32)
+    for g in range(groups):
         denom = denom_ref[g]
-        for c in range(lines):
-            line = extra[HIGH + c : HIGH + c + 1, :] + extra[LOW + c : LOW + c + 1, :]
+        for c in range(-(-tree_size // width)):
+            line = lines[g, HIGH + c : HIGH + c + 1, :] + lines[g, LOW + c : LOW + c + 1, :]
             spread = jnp.where(row_id == lane_id + c * width, line, 0.0)
             denom = denom + jnp.sum(spread, axis=1, keepdims=True)
-        hold[pl.ds(pl.multiple_of(g * tree_size, 8), tree_size), :] = numer / denom
+        hold[g * tree_size : (g + 1) * tree_size, :] = sums[g] / denom
 
     count = out_ref.shape[1]
     for d in range(out_ref.shape[0]):
@@ -215,7 +235,11 @@
     return pl.pallas_call(
         merge_kernel,
         out_shape=jax.ShapeDtypeStruct((blocks, tokens // blocks, width), jnp.bfloat16),
-        scratch_shapes=[pltpu.VMEM((tokens, width), jnp.float32)],
+        scratch_shapes=[
+            pltpu.VMEM((tokens, width), jnp.float32),
+            pltpu.VMEM((groups, tree_size, width), jnp.float32),
+            pltpu.VMEM((groups, EXTRA, width), jnp.float32),
+        ],
         compiler_params=limit(16),
         name="merge_part",
     )(got, numer, denom)
@@ -328,7 +352,7 @@
 def score_part(places, pieces, embedding, ids, picks):
     rows = ids.shape[0]
     vocab, depth = embedding.shape
-    span, streams = HEAD_SIZE, 2
+    span, streams = min(512, vocab), 1
     lines = -(-(picks + 1) // 8) * 8
     fixed = lambda i, places: (0, 0)
     return pl.pallas_call(
@@ -475,8 +499,10 @@
     return lax.ppermute(value, axis, [(i, i ^ bits) for i in range(size)])
 
 
-def group_sum(value, axis, size, stride, count):
+def group_sum(value, axis, size, stride, count, beside=None):
     values = [value] + [partner(value, axis, size, k * stride) for k in range(1, count)]
+    if beside is not None:
+        values, _ = lax.optimization_barrier((values, beside))
     while len(values) > 1:
         values = [values[i] + values[i + 1] for i in range(0, len(values), 2)]
     return values[0]
@@ -492,18 +518,19 @@
     got = [partner(parts[k], "blk", blocks, k) for k in range(1, 4)]
     sent = prompt()
     partials = spread(sent)
-    got, sent = lax.optimization_barrier((got, sent))
+    base = lax.dynamic_slice(
+        hidden, (layer * height, mp * units + (blk & 1) * half), (height, half)
+    )
+    got, sent, base = lax.optimization_barrier((got, sent, base))
     parts = fold_part(parts[0], got, place, layers)
     parts, parents = lax.optimization_barrier((parts, parents))
     more = [partner(parts[k], "blk", blocks, 4 * k) for k in range(1, layers)]
     more, heads_out = lax.optimization_barrier((more, merge(partials, parents)))
     inner = parts[0] + sum(one.astype(jnp.float32) for one in more)
-    base = lax.dynamic_slice(
-        hidden, (layer * height, mp * units + (blk & 1) * half), (height, half)
-    )
     own = (base.astype(jnp.float32) + jax.nn.silu(inner)).astype(jnp.bfloat16)
     own, heads_out = lax.optimization_barrier((own, heads_out))
     chunks = [own] + [partner(own, "blk", blocks, 4 * k) for k in range(1, layers)]
+    chunks, heads_out = lax.optimization_barrier((chunks, spread(heads_out)))
     quad = stack_part(chunks, place)
     pieces = [quad] + [partner(quad, "blk", blocks, k) for k in range(1, 4)]
     pieces = pieces + [partner(piece, "mp", 2, 1) for piece in pieces]
@@ -531,17 +558,6 @@
     fresh = (base.astype(jnp.float32) + jax.nn.silu(inner)).astype(jnp.bfloat16)
     fresh = lax.all_gather(fresh, "blk", axis=0, tiled=True)
     return [lax.all_gather(fresh, "mp", axis=1, tiled=True)]
-
-
-def ancestry(parents):
-    count = parents.shape[1]
-    column = jnp.arange(count, dtype=jnp.int32)
-    linked = (parents[:, :, None] == column[None, None, :]) & (column[None, :, None] > 0)
-    reach = jnp.eye(count, dtype=jnp.bfloat16)[None] + linked.astype(jnp.bfloat16)
-    for sweep in range(count.bit_length()):
-        met = jnp.einsum("gij,gjk->gik", reach, reach, preferred_element_type=jnp.float32)
-        reach = jnp.minimum(met, 1.0).astype(jnp.bfloat16)
-    return reach.astype(jnp.float32)
 
 
 def per_device(
@@ -574,8 +590,7 @@
         return prompt_part(tree_q, prompt_key_value, meta, width, blocks)
 
     def merge(partials, parents):
-        reach = ancestry(parents)
-        numer, denom = tree_part(tree_q, tree_key_value, reach, blk * width, width)
+        numer, denom = tree_part(tree_q, tree_key_value, parents, blk * width, width)
         return merge_part(partials, numer, denom)
 
     if splits == 2 and blocks % 4 == 0 and units % 256 == 0 and drafts == 2:
@@ -587,8 +602,7 @@
     else:
         pieces = fresh_by_collectives(hidden, medusa_w, blocks, blk, mp)
         places = jnp.zeros((2,), jnp.int32)
-        heads_out = merge(spread(prompt()), parents)
-    heads_out = spread(heads_out)
+        heads_out = spread(merge(spread(prompt()), parents))
     attn = project_part(heads_out, out_weight)
     attn, pieces = lax.optimization_barrier((attn, pieces))
     attn = group_sum(attn, "mp", splits, 1, splits)
@@ -601,7 +615,7 @@
     ids = jnp.pad(ids, ((0, 0), (0, LANES - picks)), constant_values=-1)
     score = score_part(places, pieces, embedding, ids, picks)
     score = group_sum(score, "mp", splits, 1, splits)
-    score = group_sum(score, "blk", blocks, 1, 4)
+    score = group_sum(score, "blk", blocks, 1, 4, layer_out)
     score = group_sum(score, "blk", blocks, 4, blocks // 4)
     draft_logprob = score[:picks] - jnp.log(score[picks : picks + 1])
     draft_logprob = draft_logprob.T.reshape(drafts, rows, picks)

time: 104 us -> 116 us (1.12)
  waiting for transfers between devices: 21.1 us -> 37 us
  matrix products: 1.56 us -> 0 us
  Pallas kernels: 37.4 us -> 35.9 us
    ppermute x24, waiting for transfers between devices: 15.4 us -> 37 us  [partner(): return lax.ppermute(value, axis, [(i, i ^ bits) for i in range(size)])]
    all_to_all x2, waiting for transfers between devices: 5.67 us -> 0.01 us  [spread(): return lax.all_to_all(value, 'blk', 0, 0, tiled=True)]
    dot_general x3 -> x0, matrix products: 1.56 us -> none  [ancestry(): jnp.einsum('gij,gjk->gik', reach, reach, preferred_element_type=jnp.float32)]
  transfers between devices with their start and end apart: 26 -> 26, of which waited for: 14 -> 15; matrix products, arithmetic and copies ran while one was open for 3% -> 2% of each run, Pallas kernels for 17% -> 22%
where the time goes in v6:
time: 116 us
  waiting for transfers between devices  37 us (32%)
  starting transfers between devices  36.5 us (31%)
  Pallas kernels  35.9 us (31%)
  between operations  2.82 us (2%)
  local copies, waits for them, and re-layouts  2.03 us (2%)
  other arithmetic  1.36 us (1%)
    ppermute x24, waiting for transfers between devices, partner(): return lax.ppermute(value, axis, [(i, i ^ bits) for i in range(size)])  37 us
    ppermute x24, starting transfers between devices, partner(): return lax.ppermute(value, axis, [(i, i ^ bits) for i in range(size)])  24.4 us
    pallas_call x1, Pallas kernels, score_part(): pl.pallas_call(functools.partial(score_kernel, picks, streams), out_shape...  16.3 us
    all_to_all x2, starting transfers between devices, spread(): return lax.all_to_all(value, 'blk', 0, 0, tiled=True)  12.1 us
    pallas_call x1, Pallas kernels, prompt_part(): pl.pallas_call(prompt_kernel, out_shape=jax.ShapeDtypeStruct((blocks, tre...  6.91 us
    pallas_call x1, Pallas kernels, project_part(): pl.pallas_call(project_kernel, out_shape=jax.ShapeDtypeStruct((tokens, mo...  5.95 us
    pallas_call x1, Pallas kernels, draft_part(): pl.pallas_call(draft_kernel, out_shape=[jax.ShapeDtypeStruct((rows, half)...  3.08 us
  transfers between devices with their start and end apart: 26, of which 15 were waited for; matrix products, arithmetic and copies ran while one was open for 2% of the time, Pallas kernels for 22%

profile of v6, /device:TPU:0, one launch (start us, length us, event | category | flops | bytes accessed | tf_op | source)
XLA Modules:
  0.0 115.5 jit_solution(3671388807308293881)
XLA Ops:
  2.7 3.1 %draft_part.1 = (f32[144,896]{1,0:T(8,128)S(1)}, bf16[144,896]{1,0:T(8,128)(2,1)S(1)}, bf16[144,896]{1,0:T(8,128)(2,1)S(1)}, bf16[144,896]{1,0:T(8,128)(2,1)S(1)}) custom-call(s32[6]{0:T(128)S(1)} %stack.95.meta, bf16[144,3584]{1,0:T(8,128)(2,1)} %hidden_hbm.1, bf16[2,224,1792]{2,1,0:T(8,128)(2,1)} %weight_hbm.2), custom_call_target="tpu_custom_call" | custom-call | tf_op jit(solution)/shard_map/draft_part/pallas_call | solution.py:424
  5.9 6.9 %prompt_part.1 = bf16[16,64,128]{2,1,0:T(8,128)(2,1)} custom-call(s32[3]{0:T(128)S(1)} %pad_add_fusion.meta, bf16[12,48,2048]{2,1,0:T(8,128)(2,1)} %q_hbm.3, bf16[2,1,2048,1024]{3,2,1,0:T(8,128)(2,1)} %kv_hbm.2), custom_call_target="tpu_custom_call" | custom-call | flops 805306368 | bytes 8388608 | tf_op jit(solution)/shard_map/prompt_part/pallas_call | solution.py:123
  12.8 8.3 %all-to-all-start = ((bf16[16,64,128]{2,1,0:T(8,128)(2,1)}), bf16[16,64,128]{2,1,0:T(8,128)(2,1)S(1)}, u32[]{:S(2)}, u32[]{:S(2)}) async-start(bf16[16,64,128]{2,1,0:T(8,128)(2,1)} %prompt_part.1), calls=%async_computation | async-start | bytes 524288 | tf_op jit(solution)/shard_map/all_to_all | solution.py:546
  21.1 1.9 %collective-permute-start = (bf16[144,896]{1,0:T(8,128)(2,1)S(1)}, bf16[144,896]{1,0:T(8,128)(2,1)S(1)}, u32[]{:S(2)}, u32[]{:S(2)}) collective-permute-start(bf16[144,896]{1,0:T(8,128)(2,1)S(1)} %get-tuple-element.54), channel_id=1, source_target_pairs={{0,2},{2,0},{4,6},{6,4},{8,10},{10,8},{12,14},{14,12},{16,18},{18,... | collective-permute-start | bytes 774152 | tf_op jit(solution)/shard_map/ppermute | solution.py:499
  23.0 1.5 %collective-permute-start.1 = (bf16[144,896]{1,0:T(8,128)(2,1)S(1)}, bf16[144,896]{1,0:T(8,128)(2,1)S(1)}, u32[]{:S(2)}, u32[]{:S(2)}) collective-permute-start(bf16[144,896]{1,0:T(8,128)(2,1)S(1)} %get-tuple-element.55), channel_id=1, source_target_pairs={{0,4},{2,6},{4,0},{6,2},{8,12},{10,14},{12,8},{14,10},{16,20},{18,... | collective-permute-start | bytes 774152 | tf_op jit(solution)/shard_map/ppermute | solution.py:499
  24.5 0.2 collective-permute-start.2
  24.7 1.0 dynamic_slice.3
  25.7 7.4 %collective-permute-done.refs_0_ = bf16[144,896]{1,0:T(8,128)(2,1)S(1)} collective-permute-done((bf16[144,896]{1,0:T(8,128)(2,1)S(1)}, bf16[144,896]{1,0:T(8,128)(2,1)S(1)}, u32[]{:S(2)}, u32[]{:S(2)}) %collective-permute-start) | collective-permute-done | bytes 258080 | tf_op jit(solution)/shard_map/ppermute | solution.py:499
  33.1 3.5 %collective-permute-done.1.refs_1_ = bf16[144,896]{1,0:T(8,128)(2,1)S(1)} collective-permute-done((bf16[144,896]{1,0:T(8,128)(2,1)S(1)}, bf16[144,896]{1,0:T(8,128)(2,1)S(1)}, u32[]{:S(2)}, u32[]{:S(2)}) %collective-permute-start.1) | collective-permute-done | bytes 258080 | tf_op jit(solution)/shard_map/ppermute | solution.py:499
  36.6 1.5 %collective-permute-done.2.refs_2_ = bf16[144,896]{1,0:T(8,128)(2,1)S(1)} collective-permute-done((bf16[144,896]{1,0:T(8,128)(2,1)S(1)}, bf16[144,896]{1,0:T(8,128)(2,1)S(1)}, u32[]{:S(2)}, u32[]{:S(2)}) %collective-permute-start.2) | collective-permute-done | bytes 258080 | tf_op jit(solution)/shard_map/ppermute | solution.py:499
  38.1 0.2 fold_part.1
  38.4 1.5 %collective-permute-start.3 = (bf16[36,896]{1,0:T(8,128)(2,1)S(1)}, bf16[36,896]{1,0:T(8,128)(2,1)S(1)}, u32[]{:S(2)}, u32[]{:S(2)}) collective-permute-start(bf16[36,896]{1,0:T(8,128)(2,1)S(1)} %get-tuple-element.68), channel_id=1, source_target_pairs={{0,8},{2,10},{4,12},{6,14},{8,0},{10,2},{12,4},{14,6},{16,24},{18,... | collective-permute-start | bytes 193544 | tf_op jit(solution)/shard_map/ppermute | solution.py:499
  39.9 2.4 %collective-permute-start.4 = (bf16[36,896]{1,0:T(8,128)(2,1)S(1)}, bf16[36,896]{1,0:T(8,128)(2,1)S(1)}, u32[]{:S(2)}, u32[]{:S(2)}) collective-permute-start(bf16[36,896]{1,0:T(8,128)(2,1)S(1)} %get-tuple-element.69), channel_id=1, source_target_pairs={{0,16},{2,18},{4,20},{6,22},{8,24},{10,26},{12,28},{14,30},{16,0},... | collective-permute-start | bytes 193544 | tf_op jit(solution)/shard_map/ppermute | solution.py:499
  42.2 0.6 collective-permute-start.5
  42.9 2.2 %tree_part.1 = (f32[12,48,128]{2,1,0:T(8,128)S(1)}, f32[12,48,128]{2,1,0:T(8,128)S(1)}) custom-call(s32[3]{0:T(128)S(1)} %pad_add_fusion.1.meta, bf16[12,48,2048]{2,1,0:T(8,128)(2,1)} %q_hbm.3, bf16[2,12,48,1024]{3,2,1,0:T(8,128)(2,1)} %kv_hbm.3, s32[12,48]{1,0:T(8,128)S(1)} %copy-done), custom_call_target="tpu_custom_call" | custom-call | tf_op jit(solution)/shard_map/tree_part/pallas_call | solution.py:190
  45.1 1.1 merge_part.1
  46.2 0.5 collective-permute-done.4
  46.7 1.7 %collective-permute-done.5 = bf16[36,896]{1,0:T(8,128)(2,1)S(1)} collective-permute-done((bf16[36,896]{1,0:T(8,128)(2,1)S(1)}, bf16[36,896]{1,0:T(8,128)(2,1)S(1)}, u32[]{:S(2)}, u32[]{:S(2)}) %collective-permute-start.5) | collective-permute-done | bytes 64544 | tf_op jit(solution)/shard_map/ppermute | solution.py:499
  48.5 3.7 %all-to-all-start.1 = ((bf16[16,36,128]{2,1,0:T(8,128)(2,1)}), bf16[16,36,128]{2,1,0:T(8,128)(2,1)S(1)}, u32[]{:S(2)}, u32[]{:S(2)}) async-start(bf16[16,36,128]{2,1,0:T(8,128)(2,1)} %merge_part.1), calls=%async_computation.1 | async-start | bytes 327680 | tf_op jit(solution)/shard_map/all_to_all | solution.py:546
  52.2 1.9 %collective-permute-start.6 = (bf16[36,896]{1,0:T(8,128)(2,1)S(1)}, bf16[36,896]{1,0:T(8,128)(2,1)S(1)}, u32[]{:S(2)}, u32[]{:S(2)}) collective-permute-start(bf16[36,896]{1,0:T(8,128)(2,1)S(1)} %add_convert_fusion.1.refs_0_), channel_id=1, source_target_pairs={{0,8},{2,10},{4,12},{6,14},{8,0},{10,2},{12,4},{14,6},{16,24},{18,... | collective-permute-start | bytes 193544 | tf_op jit(solution)/shard_map/ppermute | solution.py:499
  54.2 2.4 %collective-permute-start.7 = (bf16[36,896]{1,0:T(8,128)(2,1)S(1)}, bf16[36,896]{1,0:T(8,128)(2,1)S(1)}, u32[]{:S(2)}, u32[]{:S(2)}) collective-permute-start(bf16[36,896]{1,0:T(8,128)(2,1)S(1)} %add_convert_fusion.1.refs_0_), channel_id=1, source_target_pairs={{0,16},{2,18},{4,20},{6,22},{8,24},{10,26},{12,28},{14,30},{16,0},... | collective-permute-start | bytes 193544 | tf_op jit(solution)/shard_map/ppermute | solution.py:499
  56.5 0.1 collective-permute-start.8
  56.7 0.9 collective-permute-done.6.refs_1_
  57.6 4.4 %collective-permute-done.7.refs_2_ = bf16[36,896]{1,0:T(8,128)(2,1)S(1)} collective-permute-done((bf16[36,896]{1,0:T(8,128)(2,1)S(1)}, bf16[36,896]{1,0:T(8,128)(2,1)S(1)}, u32[]{:S(2)}, u32[]{:S(2)}) %collective-permute-start.7) | collective-permute-done | bytes 64544 | tf_op jit(solution)/shard_map/ppermute | solution.py:499
  61.9 0.8 collective-permute-done.8.refs_3_
  62.9 1.5 %collective-permute-start.9 = (bf16[144,896]{1,0:T(8,128)(2,1)S(1)}, bf16[144,896]{1,0:T(8,128)(2,1)S(1)}, u32[]{:S(2)}, u32[]{:S(2)}) collective-permute-start(bf16[144,896]{1,0:T(8,128)(2,1)S(1)} %stack_part.1.refs_0_), channel_id=1, source_target_pairs={{0,2},{2,0},{4,6},{6,4},{8,10},{10,8},{12,14},{14,12},{16,18},{18,... | collective-permute-start | bytes 774152 | tf_op jit(solution)/shard_map/ppermute | solution.py:499
  64.4 1.5 %collective-permute-start.10 = (bf16[144,896]{1,0:T(8,128)(2,1)S(1)}, bf16[144,896]{1,0:T(8,128)(2,1)S(1)}, u32[]{:S(2)}, u32[]{:S(2)}) collective-permute-start(bf16[144,896]{1,0:T(8,128)(2,1)S(1)} %stack_part.1.refs_0_), channel_id=1, source_target_pairs={{0,4},{2,6},{4,0},{6,2},{8,12},{10,14},{12,8},{14,10},{16,20},{18,... | collective-permute-start | bytes 774152 | tf_op jit(solution)/shard_map/ppermute | solution.py:499
  65.9 0.5 collective-permute-start.11
  66.4 4.3 %collective-permute-done.9.refs_1_ = bf16[144,896]{1,0:T(8,128)(2,1)S(1)} collective-permute-done((bf16[144,896]{1,0:T(8,128)(2,1)S(1)}, bf16[144,896]{1,0:T(8,128)(2,1)S(1)}, u32[]{:S(2)}, u32[]{:S(2)}) %collective-permute-start.9) | collective-permute-done | bytes 258080 | tf_op jit(solution)/shard_map/ppermute | solution.py:499
  70.8 3.9 %collective-permute-done.10.refs_2_ = bf16[144,896]{1,0:T(8,128)(2,1)S(1)} collective-permute-done((bf16[144,896]{1,0:T(8,128)(2,1)S(1)}, bf16[144,896]{1,0:T(8,128)(2,1)S(1)}, u32[]{:S(2)}, u32[]{:S(2)}) %collective-permute-start.10) | collective-permute-done | bytes 258080 | tf_op jit(solution)/shard_map/ppermute | solution.py:499
  74.7 0.5 collective-permute-start.15
  75.2 0.1 copy.16
  75.4 6.0 %project_part.1 = f32[36,3584]{1,0:T(8,128)S(1)} custom-call(bf16[16,36,128]{2,1,0:T(8,128)(2,1)S(1)} %all-to-all-done.1.heads_ref, bf16[2048,3584]{1,0:T(8,128)(2,1)} %weight_hbm.3), custom_call_target="tpu_custom_call" | custom-call | flops 528482304 | bytes 14680064 | tf_op jit(solution)/shard_map/project_part/pallas_call | solution.py:276
  81.5 16.3 %score_part.1 = f32[16,288]{1,0:T(8,128)S(1)} custom-call(s32[16]{0:T(128)S(1)} %stack.88.places, s32[288,128]{1,0:T(8,128)S(1)} %pad.4.ids_ref, bf16[144,896]{1,0:T(8,128)(2,1)S(1)} %stack_part.1.refs_0_, bf16[144,896]{1,0:T(8,128)(2,1)S(1)} %collective-permute-done.9.refs_1_, bf16[144,896]{1,0:T(8,128)(2,1)S(1)} %collective-permute-done.10.refs_2_, ...), custom_call_target="tpu_custom_call" | custom-call | flops 8455716864 | bytes 29360128 | tf_op jit(solution)/shard_map/score_part/pallas_call | solution.py:358
  97.9 0.5 collective-permute-start.16
  98.4 0.8 collective-permute-done.16
  99.3 1.0 collective-permute-start.17
  100.3 1.0 collective-permute-start.18
  101.3 1.5 %collective-permute-start.19 = (f32[16,288]{1,0:T(8,128)S(1)}, f32[16,288]{1,0:T(8,128)S(1)}, u32[]{:S(2)}, u32[]{:S(2)}) collective-permute-start(f32[16,288]{1,0:T(8,128)S(1)} %add.119), channel_id=1, source_target_pairs={{0,6},{2,4},{4,2},{6,0},{8,14},{10,12},{12,10},{14,8},{16,22},{18,... | collective-permute-start | bytes 55304 | tf_op jit(solution)/shard_map/ppermute | solution.py:499
  102.8 0.2 multiply_reduce_fusion
  103.0 0.9 add_convert_fusion
  103.9 0.2 collective-permute-done.18
  104.1 1.9 %collective-permute-done.19 = f32[16,288]{1,0:T(8,128)S(1)} collective-permute-done((f32[16,288]{1,0:T(8,128)S(1)}, f32[16,288]{1,0:T(8,128)S(1)}, u32[]{:S(2)}, u32[]{:S(2)}) %collective-permute-start.19) | collective-permute-done | bytes 18464 | tf_op jit(solution)/shard_map/ppermute | solution.py:499
  106.0 3.1 %collective-permute-start.22 = (f32[16,288]{1,0:T(8,128)S(1)}, f32[16,288]{1,0:T(8,128)S(1)}, u32[]{:S(2)}, u32[]{:S(2)}) collective-permute-start(f32[16,288]{1,0:T(8,128)S(1)} %add_add_fusion.1), channel_id=1, source_target_pairs={{0,16},{2,18},{4,20},{6,22},{8,24},{10,26},{12,28},{14,30},{16,0},... | collective-permute-start | bytes 55304 | tf_op jit(solution)/shard_map/ppermute | solution.py:499
  109.2 0.7 collective-permute-start.23
  109.8 1.2 %collective-permute-done.22 = f32[16,288]{1,0:T(8,128)S(1)} collective-permute-done((f32[16,288]{1,0:T(8,128)S(1)}, f32[16,288]{1,0:T(8,128)S(1)}, u32[]{:S(2)}, u32[]{:S(2)}) %collective-permute-start.22) | collective-permute-done | bytes 18464 | tf_op jit(solution)/shard_map/ppermute | solution.py:499
  111.0 3.8 %collective-permute-done.23 = f32[16,288]{1,0:T(8,128)S(1)} collective-permute-done((f32[16,288]{1,0:T(8,128)S(1)}, f32[16,288]{1,0:T(8,128)S(1)}, u32[]{:S(2)}, u32[]{:S(2)}) %collective-permute-start.23) | collective-permute-done | bytes 18464 | tf_op jit(solution)/shard_map/ppermute | solution.py:499
  114.8 0.7 reshape.23
  (38 shorter events, 0.7 us)
Async XLA Ops:
  0.6 42.3 %copy-start = (s32[12,48]{1,0:T(8,128)S(1)}, s32[12,48]{1,0:T(8,128)}, u32[]{:S(2)}) copy-start(s32[12,48]{1,0:T(8,128)} %parents_ref) | copy-start | bytes 6916
  5.9 69.3 %copy-start.2 = (s32[2,144,10]{1,0,2:T(2,128)S(1)}, s32[2,144,10]{1,0,2:T(2,128)}, u32[]{:S(2)}) copy-start(s32[2,144,10]{1,0,2:T(2,128)} %param.17) | copy-start | bytes 34564
  12.8 32.4 %all-to-all-start = ((bf16[16,64,128]{2,1,0:T(8,128)(2,1)}), bf16[16,64,128]{2,1,0:T(8,128)(2,1)S(1)}, u32[]{:S(2)}, u32[]{:S(2)}) async-start(bf16[16,64,128]{2,1,0:T(8,128)(2,1)} %prompt_part.1), calls=%async_computation | async-start | bytes 524288 | tf_op jit(solution)/shard_map/all_to_all | solution.py:546
  21.1 12.0 %collective-permute-start = (bf16[144,896]{1,0:T(8,128)(2,1)S(1)}, bf16[144,896]{1,0:T(8,128)(2,1)S(1)}, u32[]{:S(2)}, u32[]{:S(2)}) collective-permute-start(bf16[144,896]{1,0:T(8,128)(2,1)S(1)} %get-tuple-element.54), channel_id=1, source_target_pairs={{0,2},{2,0},{4,6},{6,4},{8,10},{10,8},{12,14},{14,12},{16,18},{18,... | collective-permute-start | bytes 774152 | tf_op jit(solution)/shard_map/ppermute | solution.py:499
  23.0 13.6 %collective-permute-start.1 = (bf16[144,896]{1,0:T(8,128)(2,1)S(1)}, bf16[144,896]{1,0:T(8,128)(2,1)S(1)}, u32[]{:S(2)}, u32[]{:S(2)}) collective-permute-start(bf16[144,896]{1,0:T(8,128)(2,1)S(1)} %get-tuple-element.55), channel_id=1, source_target_pairs={{0,4},{2,6},{4,0},{6,2},{8,12},{10,14},{12,8},{14,10},{16,20},{18,... | collective-permute-start | bytes 774152 | tf_op jit(solution)/shard_map/ppermute | solution.py:499
  24.5 13.6 %collective-permute-start.2 = (bf16[144,896]{1,0:T(8,128)(2,1)S(1)}, bf16[144,896]{1,0:T(8,128)(2,1)S(1)}, u32[]{:S(2)}, u32[]{:S(2)}) collective-permute-start(bf16[144,896]{1,0:T(8,128)(2,1)S(1)} %get-tuple-element.56), channel_id=1, source_target_pairs={{0,6},{2,4},{4,2},{6,0},{8,14},{10,12},{12,10},{14,8},{16,22},{18,... | collective-permute-start | bytes 774152 | tf_op jit(solution)/shard_map/ppermute | solution.py:499
  38.4 7.8 %collective-permute-start.3 = (bf16[36,896]{1,0:T(8,128)(2,1)S(1)}, bf16[36,896]{1,0:T(8,128)(2,1)S(1)}, u32[]{:S(2)}, u32[]{:S(2)}) collective-permute-start(bf16[36,896]{1,0:T(8,128)(2,1)S(1)} %get-tuple-element.68), channel_id=1, source_target_pairs={{0,8},{2,10},{4,12},{6,14},{8,0},{10,2},{12,4},{14,6},{16,24},{18,... | collective-permute-start | bytes 193544 | tf_op jit(solution)/shard_map/ppermute | solution.py:499
  39.9 6.8 %collective-permute-start.4 = (bf16[36,896]{1,0:T(8,128)(2,1)S(1)}, bf16[36,896]{1,0:T(8,128)(2,1)S(1)}, u32[]{:S(2)}, u32[]{:S(2)}) collective-permute-start(bf16[36,896]{1,0:T(8,128)(2,1)S(1)} %get-tuple-element.69), channel_id=1, source_target_pairs={{0,16},{2,18},{4,20},{6,22},{8,24},{10,26},{12,28},{14,30},{16,0},... | collective-permute-start | bytes 193544 | tf_op jit(solution)/shard_map/ppermute | solution.py:499
  42.2 6.1 %collective-permute-start.5 = (bf16[36,896]{1,0:T(8,128)(2,1)S(1)}, bf16[36,896]{1,0:T(8,128)(2,1)S(1)}, u32[]{:S(2)}, u32[]{:S(2)}) collective-permute-start(bf16[36,896]{1,0:T(8,128)(2,1)S(1)} %get-tuple-element.70), channel_id=1, source_target_pairs={{0,24},{2,26},{4,28},{6,30},{8,16},{10,18},{12,20},{14,22},{16,8},... | collective-permute-start | bytes 193544 | tf_op jit(solution)/shard_map/ppermute | solution.py:499
  48.5 14.3 %all-to-all-start.1 = ((bf16[16,36,128]{2,1,0:T(8,128)(2,1)}), bf16[16,36,128]{2,1,0:T(8,128)(2,1)S(1)}, u32[]{:S(2)}, u32[]{:S(2)}) async-start(bf16[16,36,128]{2,1,0:T(8,128)(2,1)} %merge_part.1), calls=%async_computation.1 | async-start | bytes 327680 | tf_op jit(solution)/shard_map/all_to_all | solution.py:546
  52.2 5.3 %collective-permute-start.6 = (bf16[36,896]{1,0:T(8,128)(2,1)S(1)}, bf16[36,896]{1,0:T(8,128)(2,1)S(1)}, u32[]{:S(2)}, u32[]{:S(2)}) collective-permute-start(bf16[36,896]{1,0:T(8,128)(2,1)S(1)} %add_convert_fusion.1.refs_0_), channel_id=1, source_target_pairs={{0,8},{2,10},{4,12},{6,14},{8,0},{10,2},{12,4},{14,6},{16,24},{18,... | collective-permute-start | bytes 193544 | tf_op jit(solution)/shard_map/ppermute | solution.py:499
  54.2 7.8 %collective-permute-start.7 = (bf16[36,896]{1,0:T(8,128)(2,1)S(1)}, bf16[36,896]{1,0:T(8,128)(2,1)S(1)}, u32[]{:S(2)}, u32[]{:S(2)}) collective-permute-start(bf16[36,896]{1,0:T(8,128)(2,1)S(1)} %add_convert_fusion.1.refs_0_), channel_id=1, source_target_pairs={{0,16},{2,18},{4,20},{6,22},{8,24},{10,26},{12,28},{14,30},{16,0},... | collective-permute-start | bytes 193544 | tf_op jit(solution)/shard_map/ppermute | solution.py:499
  56.5 6.2 %collective-permute-start.8 = (bf16[36,896]{1,0:T(8,128)(2,1)S(1)}, bf16[36,896]{1,0:T(8,128)(2,1)S(1)}, u32[]{:S(2)}, u32[]{:S(2)}) collective-permute-start(bf16[36,896]{1,0:T(8,128)(2,1)S(1)} %add_convert_fusion.1.refs_0_), channel_id=1, source_target_pairs={{0,24},{2,26},{4,28},{6,30},{8,16},{10,18},{12,20},{14,22},{16,8},... | collective-permute-start | bytes 193544 | tf_op jit(solution)/shard_map/ppermute | solution.py:499
  62.9 7.9 %collective-permute-start.9 = (bf16[144,896]{1,0:T(8,128)(2,1)S(1)}, bf16[144,896]{1,0:T(8,128)(2,1)S(1)}, u32[]{:S(2)}, u32[]{:S(2)}) collective-permute-start(bf16[144,896]{1,0:T(8,128)(2,1)S(1)} %stack_part.1.refs_0_), channel_id=1, source_target_pairs={{0,2},{2,0},{4,6},{6,4},{8,10},{10,8},{12,14},{14,12},{16,18},{18,... | collective-permute-start | bytes 774152 | tf_op jit(solution)/shard_map/ppermute | solution.py:499
  64.4 10.3 %collective-permute-start.10 = (bf16[144,896]{1,0:T(8,128)(2,1)S(1)}, bf16[144,896]{1,0:T(8,128)(2,1)S(1)}, u32[]{:S(2)}, u32[]{:S(2)}) collective-permute-start(bf16[144,896]{1,0:T(8,128)(2,1)S(1)} %stack_part.1.refs_0_), channel_id=1, source_target_pairs={{0,4},{2,6},{4,0},{6,2},{8,12},{10,14},{12,8},{14,10},{16,20},{18,... | collective-permute-start | bytes 774152 | tf_op jit(solution)/shard_map/ppermute | solution.py:499
  65.9 8.8 %collective-permute-start.11 = (bf16[144,896]{1,0:T(8,128)(2,1)S(1)}, bf16[144,896]{1,0:T(8,128)(2,1)S(1)}, u32[]{:S(2)}, u32[]{:S(2)}) collective-permute-start(bf16[144,896]{1,0:T(8,128)(2,1)S(1)} %stack_part.1.refs_0_), channel_id=1, source_target_pairs={{0,6},{2,4},{4,2},{6,0},{8,14},{10,12},{12,10},{14,8},{16,22},{18,... | collective-permute-start | bytes 774152 | tf_op jit(solution)/shard_map/ppermute | solution.py:499
  66.4 15.0 %collective-permute-start.12 = (bf16[144,896]{1,0:T(8,128)(2,1)S(1)}, bf16[144,896]{1,0:T(8,128)(2,1)S(1)}, u32[]{:S(2)}, u32[]{:S(2)}) collective-permute-start(bf16[144,896]{1,0:T(8,128)(2,1)S(1)} %stack_part.1.refs_0_), channel_id=1, source_target_pairs={{0,1},{1,0},{2,3},{3,2},{4,5},{5,4},{6,7},{7,6},{8,9},{9,8},{10,11... | collective-permute-start | bytes 774152 | tf_op jit(solution)/shard_map/ppermute | solution.py:499
  70.7 10.7 %collective-permute-start.13 = (bf16[144,896]{1,0:T(8,128)(2,1)S(1)}, bf16[144,896]{1,0:T(8,128)(2,1)S(1)}, u32[]{:S(2)}, u32[]{:S(2)}) collective-permute-start(bf16[144,896]{1,0:T(8,128)(2,1)S(1)} %collective-permute-done.9.refs_1_), channel_id=1, source_target_pairs={{0,1},{1,0},{2,3},{3,2},{4,5},{5,4},{6,7},{7,6},{8,9},{9,8},{10,11... | collective-permute-start | bytes 774152 | tf_op jit(solution)/shard_map/ppermute | solution.py:499
  74.7 6.8 %collective-permute-start.14 = (bf16[144,896]{1,0:T(8,128)(2,1)S(1)}, bf16[144,896]{1,0:T(8,128)(2,1)S(1)}, u32[]{:S(2)}, u32[]{:S(2)}) collective-permute-start(bf16[144,896]{1,0:T(8,128)(2,1)S(1)} %collective-permute-done.10.refs_2_), channel_id=1, source_target_pairs={{0,1},{1,0},{2,3},{3,2},{4,5},{5,4},{6,7},{7,6},{8,9},{9,8},{10,11... | collective-permute-start | bytes 774152 | tf_op jit(solution)/shard_map/ppermute | solution.py:499
  74.7 6.8 %collective-permute-start.15 = (bf16[144,896]{1,0:T(8,128)(2,1)S(1)}, bf16[144,896]{1,0:T(8,128)(2,1)S(1)}, u32[]{:S(2)}, u32[]{:S(2)}) collective-permute-start(bf16[144,896]{1,0:T(8,128)(2,1)S(1)} %collective-permute-done.11.refs_3_), channel_id=1, source_target_pairs={{0,1},{1,0},{2,3},{3,2},{4,5},{5,4},{6,7},{7,6},{8,9},{9,8},{10,11... | collective-permute-start | bytes 774152 | tf_op jit(solution)/shard_map/ppermute | solution.py:499
  81.4 21.6 %copy-start.1 = (bf16[36,3584]{1,0:T(8,128)(2,1)S(1)}, bf16[36,3584]{1,0:T(8,128)(2,1)}, u32[]{:S(2)}) copy-start(bf16[36,3584]{1,0:T(8,128)(2,1)} %param.27) | copy-start | bytes 774148
  81.4 21.6 %copy-start.3 = (f32[3584]{0:T(1024)S(1)}, f32[3584]{0:T(1024)}, u32[]{:S(2)}) copy-start(f32[3584]{0:T(1024)} %param.26) | copy-start | bytes 43012
  81.5 21.3 %collective-permute-start.20 = (f32[36,3584]{1,0:T(8,128)S(1)}, f32[36,3584]{1,0:T(8,128)S(1)}, u32[]{:S(2)}, u32[]{:S(2)}) collective-permute-start(f32[36,3584]{1,0:T(8,128)S(1)} %project_part.1), channel_id=1, source_target_pairs={{0,1},{1,0},{2,3},{3,2},{4,5},{5,4},{6,7},{7,6},{8,9},{9,8},{10,11... | collective-permute-start | bytes 1548296 | tf_op jit(solution)/shard_map/ppermute | solution.py:499
  97.9 1.4 %collective-permute-start.16 = (f32[16,288]{1,0:T(8,128)S(1)}, f32[16,288]{1,0:T(8,128)S(1)}, u32[]{:S(2)}, u32[]{:S(2)}) collective-permute-start(f32[16,288]{1,0:T(8,128)S(1)} %score_part.1), channel_id=1, source_target_pairs={{0,1},{1,0},{2,3},{3,2},{4,5},{5,4},{6,7},{7,6},{8,9},{9,8},{10,11... | collective-permute-start | bytes 55304 | tf_op jit(solution)/shard_map/ppermute | solution.py:499
  99.3 4.6 %collective-permute-start.17 = (f32[16,288]{1,0:T(8,128)S(1)}, f32[16,288]{1,0:T(8,128)S(1)}, u32[]{:S(2)}, u32[]{:S(2)}) collective-permute-start(f32[16,288]{1,0:T(8,128)S(1)} %add.119), channel_id=1, source_target_pairs={{0,2},{2,0},{4,6},{6,4},{8,10},{10,8},{12,14},{14,12},{16,18},{18,... | collective-permute-start | bytes 55304 | tf_op jit(solution)/shard_map/ppermute | solution.py:499
  100.3 3.8 %collective-permute-start.18 = (f32[16,288]{1,0:T(8,128)S(1)}, f32[16,288]{1,0:T(8,128)S(1)}, u32[]{:S(2)}, u32[]{:S(2)}) collective-permute-start(f32[16,288]{1,0:T(8,128)S(1)} %add.119), channel_id=1, source_target_pairs={{0,4},{2,6},{4,0},{6,2},{8,12},{10,14},{12,8},{14,10},{16,20},{18,... | collective-permute-start | bytes 55304 | tf_op jit(solution)/shard_map/ppermute | solution.py:499
  101.3 4.7 %collective-permute-start.19 = (f32[16,288]{1,0:T(8,128)S(1)}, f32[16,288]{1,0:T(8,128)S(1)}, u32[]{:S(2)}, u32[]{:S(2)}) collective-permute-start(f32[16,288]{1,0:T(8,128)S(1)} %add.119), channel_id=1, source_target_pairs={{0,6},{2,4},{4,2},{6,0},{8,14},{10,12},{12,10},{14,8},{16,22},{18,... | collective-permute-start | bytes 55304 | tf_op jit(solution)/shard_map/ppermute | solution.py:499
  106.0 5.0 %collective-permute-start.22 = (f32[16,288]{1,0:T(8,128)S(1)}, f32[16,288]{1,0:T(8,128)S(1)}, u32[]{:S(2)}, u32[]{:S(2)}) collective-permute-start(f32[16,288]{1,0:T(8,128)S(1)} %add_add_fusion.1), channel_id=1, source_target_pairs={{0,16},{2,18},{4,20},{6,22},{8,24},{10,26},{12,28},{14,30},{16,0},... | collective-permute-start | bytes 55304 | tf_op jit(solution)/shard_map/ppermute | solution.py:499
  109.2 5.6 %collective-permute-start.23 = (f32[16,288]{1,0:T(8,128)S(1)}, f32[16,288]{1,0:T(8,128)S(1)}, u32[]{:S(2)}, u32[]{:S(2)}) collective-permute-start(f32[16,288]{1,0:T(8,128)S(1)} %add_add_fusion.1), channel_id=1, source_target_pairs={{0,24},{2,26},{4,28},{6,30},{8,16},{10,18},{12,20},{14,22},{16,8},... | collective-permute-start | bytes 55304 | tf_op jit(solution)/shard_map/ppermute | solution.py:499
  109.8 5.0 %collective-permute-start.21 = (f32[16,288]{1,0:T(8,128)S(1)}, f32[16,288]{1,0:T(8,128)S(1)}, u32[]{:S(2)}, u32[]{:S(2)}) collective-permute-start(f32[16,288]{1,0:T(8,128)S(1)} %add_add_fusion.1), channel_id=1, source_target_pairs={{0,8},{2,10},{4,12},{6,14},{8,0},{10,2},{12,4},{14,6},{16,24},{18,... | collective-permute-start | bytes 55304 | tf_op jit(solution)/shard_map/ppermute | solution.py:499

commit v7 on v6

--- a/solution.py
+++ b/solution.py
@@ -386,7 +386,7 @@
 
 
 def draft_kernel(meta, hidden_hbm, weight_hbm, *refs):
-    outs, columns, padded, sems = refs[:4], *refs[4:]
+    outs, base_ref, columns, padded, sems = refs[:4], *refs[4:]
     depth = weight_hbm.shape[1]
     half = padded.shape[2]
     window = padded.shape[1]
@@ -406,66 +406,75 @@
             )
         )
         copies[-1].start()
+    base_columns = pl.ds(pl.multiple_of(meta[6], LANES), half)
+    base = pltpu.make_async_copy(hidden_hbm.at[:, base_columns], base_ref, sems.at[5])
+    base.start()
     ask.wait()
     for n, k in enumerate((1, 2, 3, 0)):
         copies[n].wait()
         partial = jnp.dot(columns[...], padded[k], preferred_element_type=jnp.float32)
         outs[k][...] = partial.astype(outs[k].dtype)
-
-
-def draft_part(hidden, medusa_w, blk):
+    base.wait()
+
+
+def draft_part(hidden, medusa_w, blk, mp):
     rows, model = hidden.shape
     depth, units = medusa_w.shape[1:]
     half = units // 2
     window = -(-depth // LANES) * LANES + LANES
     start = blk * depth
     first = jnp.minimum(start // LANES * LANES, model - window)
-    meta = jnp.stack([first, start - first] + [(blk & 3) ^ k for k in range(4)])
+    meta = [first, start - first] + [(blk & 3) ^ k for k in range(4)]
+    meta = jnp.stack(meta + [mp * units + (blk & 1) * half])
     return pl.pallas_call(
         draft_kernel,
         out_shape=[
             jax.ShapeDtypeStruct((rows, half), jnp.bfloat16 if k else jnp.float32)
-            for k in range(4)
+            for k in range(5)
         ],
         in_specs=[in_smem(), in_hbm(), in_hbm()],
-        out_specs=[in_vmem()] * 4,
+        out_specs=[in_vmem()] * 5,
         scratch_shapes=[
             pltpu.VMEM((rows, window), jnp.bfloat16),
             pltpu.VMEM((4, window, half), jnp.bfloat16),
-            pltpu.SemaphoreType.DMA((5,)),
+            pltpu.SemaphoreType.DMA((6,)),
         ],
         compiler_params=limit(16),
         name="draft_part",
     )(meta, pin(hidden), pin(medusa_w))
 
 
-def fold_kernel(place, own_ref, *refs):
-    got, outs, hold = refs[:3], refs[3:-1], refs[-1]
+def fold_kernel(place, base_ref, own_ref, *refs):
+    got, chunk_ref, outs, hold = refs[:3], refs[3], refs[4:-1], refs[-1]
+    height = hold.shape[1]
+
+    def cut(whole):
+        for j in range(len(outs)):
+            hold[j] = whole[j * height : (j + 1) * height]
+
+    cut(base_ref[...].astype(jnp.float32))
+    chunk_ref[...] = hold[place[0]]
     total = own_ref[...]
     for one in got:
         total = total + one[...].astype(jnp.float32)
-    height = hold.shape[1]
-    for j in range(len(outs)):
-        hold[j] = total[j * height : (j + 1) * height]
+    cut(total)
     for k, out in enumerate(outs):
         out[...] = hold[place[0] ^ k].astype(out.dtype)
 
 
-def fold_part(own, got, place, layers):
+def fold_part(base, own, got, place, layers):
     rows, half = own.shape
     height = rows // layers
+    kinds = [jnp.float32, jnp.float32] + [jnp.bfloat16] * (layers - 1)
     return pl.pallas_call(
         fold_kernel,
-        out_shape=[
-            jax.ShapeDtypeStruct((height, half), jnp.bfloat16 if k else jnp.float32)
-            for k in range(layers)
-        ],
-        in_specs=[in_smem()] + [in_vmem()] * 4,
-        out_specs=[in_vmem()] * layers,
+        out_shape=[jax.ShapeDtypeStruct((height, half), kind) for kind in kinds],
+        in_specs=[in_smem()] + [in_vmem()] * 5,
+        out_specs=[in_vmem()] * (1 + layers),
         scratch_shapes=[pltpu.VMEM((layers, height, half), jnp.float32)],
         compiler_params=limit(16),
         name="fold_part",
-    )(place, own, *got)
+    )(place, base, own, *got)
 
 
 def stack_kernel(place, *refs):
@@ -499,38 +508,28 @@
     return lax.ppermute(value, axis, [(i, i ^ bits) for i in range(size)])
 
 
-def group_sum(value, axis, size, stride, count, beside=None):
+def group_sum(value, axis, size, stride, count):
     values = [value] + [partner(value, axis, size, k * stride) for k in range(1, count)]
-    if beside is not None:
-        values, _ = lax.optimization_barrier((values, beside))
     while len(values) > 1:
         values = [values[i] + values[i + 1] for i in range(0, len(values), 2)]
     return values[0]
 
 
-def both_by_stages(hidden, parts, parents, units, blocks, blk, mp, prompt, merge):
-    rows, model = hidden.shape
-    half = units // 2
+def both_by_stages(parts, parents, blocks, blk, mp, prompt, merge):
     layers = blocks // 4
-    height = rows // layers
-    layer = blk // 4
-    place = layer.reshape(1)
+    place = (blk // 4).reshape(1)
     got = [partner(parts[k], "blk", blocks, k) for k in range(1, 4)]
     sent = prompt()
     partials = spread(sent)
-    base = lax.dynamic_slice(
-        hidden, (layer * height, mp * units + (blk & 1) * half), (height, half)
-    )
-    got, sent, base = lax.optimization_barrier((got, sent, base))
-    parts = fold_part(parts[0], got, place, layers)
+    got, sent = lax.optimization_barrier((got, sent))
+    parts = fold_part(parts[4], parts[0], got, place, layers)
     parts, parents = lax.optimization_barrier((parts, parents))
-    more = [partner(parts[k], "blk", blocks, 4 * k) for k in range(1, layers)]
+    more = [partner(parts[1 + k], "blk", blocks, 4 * k) for k in range(1, layers)]
     more, heads_out = lax.optimization_barrier((more, merge(partials, parents)))
-    inner = parts[0] + sum(one.astype(jnp.float32) for one in more)
-    own = (base.astype(jnp.float32) + jax.nn.silu(inner)).astype(jnp.bfloat16)
+    inner = parts[1] + sum(one.astype(jnp.float32) for one in more)
+    own = (parts[0] + jax.nn.silu(inner)).astype(jnp.bfloat16)
     own, heads_out = lax.optimization_barrier((own, heads_out))
     chunks = [own] + [partner(own, "blk", blocks, 4 * k) for k in range(1, layers)]
-    chunks, heads_out = lax.optimization_barrier((chunks, spread(heads_out)))
     quad = stack_part(chunks, place)
     pieces = [quad] + [partner(quad, "blk", blocks, k) for k in range(1, 4)]
     pieces = pieces + [partner(piece, "mp", 2, 1) for piece in pieces]
@@ -539,7 +538,7 @@
         for k in range(4):
             which = (blk & 3) ^ k
             places += [which >> 1, side * 2 + (which & 1)]
-    return pieces, jnp.stack(places), heads_out
+    return pieces, jnp.stack(places), spread(heads_out)
 
 
 def spread(value):
@@ -594,31 +593,31 @@
         return merge_part(partials, numer, denom)
 
     if splits == 2 and blocks % 4 == 0 and units % 256 == 0 and drafts == 2:
-        parts = draft_part(hidden, medusa_w, blk)
+        parts = draft_part(hidden, medusa_w, blk, mp)
         parts, meta = lax.optimization_barrier((parts, meta))
         pieces, places, heads_out = both_by_stages(
-            hidden, parts, parents, units, blocks, blk, mp, prompt, merge
+            parts, parents, blocks, blk, mp, prompt, merge
         )
     else:
         pieces = fresh_by_collectives(hidden, medusa_w, blocks, blk, mp)
         places = jnp.zeros((2,), jnp.int32)
         heads_out = spread(merge(spread(prompt()), parents))
-    attn = project_part(heads_out, out_weight)
-    attn, pieces = lax.optimization_barrier((attn, pieces))
-    attn = group_sum(attn, "mp", splits, 1, splits)
-    normed = attn * lax.rsqrt(jnp.mean(attn * attn, -1, keepdims=True) + 1e-06) * post_gain
-    layer_out = (normed + resid.astype(jnp.float32)).astype(jnp.bfloat16)
-
     vocab = embedding.shape[0]
     picks = cand_ids.shape[2]
     ids = cand_ids.reshape(lines, picks) - (blk * splits + mp) * vocab
     ids = jnp.pad(ids, ((0, 0), (0, LANES - picks)), constant_values=-1)
     score = score_part(places, pieces, embedding, ids, picks)
     score = group_sum(score, "mp", splits, 1, splits)
-    score = group_sum(score, "blk", blocks, 1, 4, layer_out)
+    score, heads_out = lax.optimization_barrier((score, heads_out))
+    score = group_sum(score, "blk", blocks, 1, 4)
     score = group_sum(score, "blk", blocks, 4, blocks // 4)
     draft_logprob = score[:picks] - jnp.log(score[picks : picks + 1])
     draft_logprob = draft_logprob.T.reshape(drafts, rows, picks)
+
+    attn = project_part(heads_out, out_weight)
+    attn = group_sum(attn, "mp", splits, 1, splits)
+    normed = attn * lax.rsqrt(jnp.mean(attn * attn, -1, keepdims=True) + 1e-06) * post_gain
+    layer_out = (normed + resid.astype(jnp.float32)).astype(jnp.bfloat16)
     return (draft_logprob, layer_out)
 
 

time: 116 us -> 111 us (0.957)
  waiting for transfers between devices: 37 us -> 33.4 us
    ppermute x24, waiting for transfers between devices: 37 us -> 33.4 us  [partner(): return lax.ppermute(value, axis, [(i, i ^ bits) for i in range(size)])]
  transfers between devices with their start and end apart: 26 -> 26, of which waited for: 15 -> 14; matrix products, arithmetic and copies ran while one was open for 2% -> 1% of each run, Pallas kernels for 22% -> 23%
where the time goes in v7:
time: 111 us
  starting transfers between devices  36.2 us (33%)
  Pallas kernels  35.9 us (32%)
  waiting for transfers between devices  33.4 us (30%)
  between operations  2.84 us (3%)
  other arithmetic  1.32 us (1%)
    ppermute x24, waiting for transfers between devices, partner(): return lax.ppermute(value, axis, [(i, i ^ bits) for i in range(size)])  33.4 us
    ppermute x24, starting transfers between devices, partner(): return lax.ppermute(value, axis, [(i, i ^ bits) for i in range(size)])  24.2 us
    pallas_call x1, Pallas kernels, score_part(): pl.pallas_call(functools.partial(score_kernel, picks, streams), out_shape...  16.3 us
    all_to_all x2, starting transfers between devices, spread(): return lax.all_to_all(value, 'blk', 0, 0, tiled=True)  12 us
    pallas_call x1, Pallas kernels, prompt_part(): pl.pallas_call(prompt_kernel, out_shape=jax.ShapeDtypeStruct((blocks, tre...  6.91 us
    pallas_call x1, Pallas kernels, project_part(): pl.pallas_call(project_kernel, out_shape=jax.ShapeDtypeStruct((tokens, mo...  5.95 us
    pallas_call x1, Pallas kernels, draft_part(): pl.pallas_call(draft_kernel, out_shape=[jax.ShapeDtypeStruct((rows, half)...  3.09 us
    pallas_call x1, Pallas kernels, tree_part(): pl.pallas_call(tree_kernel, out_shape=[jax.ShapeDtypeStruct((groups, tree...  2.23 us
  transfers between devices with their start and end apart: 26, of which 14 were waited for; matrix products, arithmetic and copies ran while one was open for 1% of the time, Pallas kernels for 23%

profile of v7, /device:TPU:0, one launch (start us, length us, event | category | flops | bytes accessed | tf_op | source)
XLA Modules:
  0.0 110.8 jit_solution(10820295545002035877)
XLA Ops:
  2.6 0.1 stack.99.meta
  2.7 3.1 %draft_part.1 = (f32[144,896]{1,0:T(8,128)S(1)}, bf16[144,896]{1,0:T(8,128)(2,1)S(1)}, bf16[144,896]{1,0:T(8,128)(2,1)S(1)}, bf16[144,896]{1,0:T(8,128)(2,1)S(1)}, bf16[144,896]{1,0:T(8,128)(2,1)S(1)}) custom-call(s32[7]{0:T(128)S(1)} %stack.99.meta, bf16[144,3584]{1,0:T(8,128)(2,1)} %hidden_hbm.1, bf16[2,224,1792]{2,1,0:T(8,128)(2,1)} %weight_hbm.2), custom_call_target="tpu_custom_call" | custom-call | tf_op jit(solution)/shard_map/draft_part/pallas_call | solution.py:429
  5.9 6.9 %prompt_part.1 = bf16[16,64,128]{2,1,0:T(8,128)(2,1)} custom-call(s32[3]{0:T(128)S(1)} %pad_add_fusion.meta, bf16[12,48,2048]{2,1,0:T(8,128)(2,1)} %q_hbm.3, bf16[2,1,2048,1024]{3,2,1,0:T(8,128)(2,1)} %kv_hbm.2), custom_call_target="tpu_custom_call" | custom-call | flops 805306368 | bytes 8388608 | tf_op jit(solution)/shard_map/prompt_part/pallas_call | solution.py:123
  12.8 8.3 %all-to-all-start = ((bf16[16,64,128]{2,1,0:T(8,128)(2,1)}), bf16[16,64,128]{2,1,0:T(8,128)(2,1)S(1)}, u32[]{:S(2)}, u32[]{:S(2)}) async-start(bf16[16,64,128]{2,1,0:T(8,128)(2,1)} %prompt_part.1), calls=%async_computation | async-start | bytes 524288 | tf_op jit(solution)/shard_map/all_to_all | solution.py:545
  21.1 1.9 %collective-permute-start = (bf16[144,896]{1,0:T(8,128)(2,1)S(1)}, bf16[144,896]{1,0:T(8,128)(2,1)S(1)}, u32[]{:S(2)}, u32[]{:S(2)}) collective-permute-start(bf16[144,896]{1,0:T(8,128)(2,1)S(1)} %get-tuple-element.44), channel_id=1, source_target_pairs={{0,2},{2,0},{4,6},{6,4},{8,10},{10,8},{12,14},{14,12},{16,18},{18,... | collective-permute-start | bytes 774152 | tf_op jit(solution)/shard_map/ppermute | solution.py:508
  23.0 1.5 %collective-permute-start.1 = (bf16[144,896]{1,0:T(8,128)(2,1)S(1)}, bf16[144,896]{1,0:T(8,128)(2,1)S(1)}, u32[]{:S(2)}, u32[]{:S(2)}) collective-permute-start(bf16[144,896]{1,0:T(8,128)(2,1)S(1)} %get-tuple-element.45), channel_id=1, source_target_pairs={{0,4},{2,6},{4,0},{6,2},{8,12},{10,14},{12,8},{14,10},{16,20},{18,... | collective-permute-start | bytes 774152 | tf_op jit(solution)/shard_map/ppermute | solution.py:508
  24.5 0.2 collective-permute-start.2
  24.7 8.5 %collective-permute-done.refs_0_ = bf16[144,896]{1,0:T(8,128)(2,1)S(1)} collective-permute-done((bf16[144,896]{1,0:T(8,128)(2,1)S(1)}, bf16[144,896]{1,0:T(8,128)(2,1)S(1)}, u32[]{:S(2)}, u32[]{:S(2)}) %collective-permute-start) | collective-permute-done | bytes 258080 | tf_op jit(solution)/shard_map/ppermute | solution.py:508
  33.1 3.5 %collective-permute-done.1.refs_1_ = bf16[144,896]{1,0:T(8,128)(2,1)S(1)} collective-permute-done((bf16[144,896]{1,0:T(8,128)(2,1)S(1)}, bf16[144,896]{1,0:T(8,128)(2,1)S(1)}, u32[]{:S(2)}, u32[]{:S(2)}) %collective-permute-start.1) | collective-permute-done | bytes 258080 | tf_op jit(solution)/shard_map/ppermute | solution.py:508
  36.6 1.5 %collective-permute-done.2.refs_2_ = bf16[144,896]{1,0:T(8,128)(2,1)S(1)} collective-permute-done((bf16[144,896]{1,0:T(8,128)(2,1)S(1)}, bf16[144,896]{1,0:T(8,128)(2,1)S(1)}, u32[]{:S(2)}, u32[]{:S(2)}) %collective-permute-start.2) | collective-permute-done | bytes 258080 | tf_op jit(solution)/shard_map/ppermute | solution.py:508
  38.1 0.3 fold_part.1
  38.4 1.5 %collective-permute-start.3 = (bf16[36,896]{1,0:T(8,128)(2,1)S(1)}, bf16[36,896]{1,0:T(8,128)(2,1)S(1)}, u32[]{:S(2)}, u32[]{:S(2)}) collective-permute-start(bf16[36,896]{1,0:T(8,128)(2,1)S(1)} %get-tuple-element.58), channel_id=1, source_target_pairs={{0,8},{2,10},{4,12},{6,14},{8,0},{10,2},{12,4},{14,6},{16,24},{18,... | collective-permute-start | bytes 193544 | tf_op jit(solution)/shard_map/ppermute | solution.py:508
  39.9 2.4 %collective-permute-start.4 = (bf16[36,896]{1,0:T(8,128)(2,1)S(1)}, bf16[36,896]{1,0:T(8,128)(2,1)S(1)}, u32[]{:S(2)}, u32[]{:S(2)}) collective-permute-start(bf16[36,896]{1,0:T(8,128)(2,1)S(1)} %get-tuple-element.59), channel_id=1, source_target_pairs={{0,16},{2,18},{4,20},{6,22},{8,24},{10,26},{12,28},{14,30},{16,0},... | collective-permute-start | bytes 193544 | tf_op jit(solution)/shard_map/ppermute | solution.py:508
  42.3 0.6 collective-permute-start.5
  42.9 2.2 %tree_part.1 = (f32[12,48,128]{2,1,0:T(8,128)S(1)}, f32[12,48,128]{2,1,0:T(8,128)S(1)}) custom-call(s32[3]{0:T(128)S(1)} %pad_add_fusion.1.meta, bf16[12,48,2048]{2,1,0:T(8,128)(2,1)} %q_hbm.3, bf16[2,12,48,1024]{3,2,1,0:T(8,128)(2,1)} %kv_hbm.3, s32[12,48]{1,0:T(8,128)S(1)} %copy-done), custom_call_target="tpu_custom_call" | custom-call | tf_op jit(solution)/shard_map/tree_part/pallas_call | solution.py:190
  45.2 1.1 merge_part.1
  46.3 0.5 collective-permute-done.4
  46.8 1.7 %collective-permute-done.5 = bf16[36,896]{1,0:T(8,128)(2,1)S(1)} collective-permute-done((bf16[36,896]{1,0:T(8,128)(2,1)S(1)}, bf16[36,896]{1,0:T(8,128)(2,1)S(1)}, u32[]{:S(2)}, u32[]{:S(2)}) %collective-permute-start.5) | collective-permute-done | bytes 64544 | tf_op jit(solution)/shard_map/ppermute | solution.py:508
  48.6 2.0 %collective-permute-start.7 = (bf16[36,896]{1,0:T(8,128)(2,1)S(1)}, bf16[36,896]{1,0:T(8,128)(2,1)S(1)}, u32[]{:S(2)}, u32[]{:S(2)}) collective-permute-start(bf16[36,896]{1,0:T(8,128)(2,1)S(1)} %add_convert_fusion.1.refs_0_), channel_id=1, source_target_pairs={{0,16},{2,18},{4,20},{6,22},{8,24},{10,26},{12,28},{14,30},{16,0},... | collective-permute-start | bytes 193544 | tf_op jit(solution)/shard_map/ppermute | solution.py:508
  50.6 2.3 %collective-permute-start.8 = (bf16[36,896]{1,0:T(8,128)(2,1)S(1)}, bf16[36,896]{1,0:T(8,128)(2,1)S(1)}, u32[]{:S(2)}, u32[]{:S(2)}) collective-permute-start(bf16[36,896]{1,0:T(8,128)(2,1)S(1)} %add_convert_fusion.1.refs_0_), channel_id=1, source_target_pairs={{0,24},{2,26},{4,28},{6,30},{8,16},{10,18},{12,20},{14,22},{16,8},... | collective-permute-start | bytes 193544 | tf_op jit(solution)/shard_map/ppermute | solution.py:508
  53.0 1.5 %collective-permute-done.6.refs_1_ = bf16[36,896]{1,0:T(8,128)(2,1)S(1)} collective-permute-done((bf16[36,896]{1,0:T(8,128)(2,1)S(1)}, bf16[36,896]{1,0:T(8,128)(2,1)S(1)}, u32[]{:S(2)}, u32[]{:S(2)}) %collective-permute-start.6) | collective-permute-done | bytes 64544 | tf_op jit(solution)/shard_map/ppermute | solution.py:508
  54.5 2.4 %collective-permute-done.8.refs_3_ = bf16[36,896]{1,0:T(8,128)(2,1)S(1)} collective-permute-done((bf16[36,896]{1,0:T(8,128)(2,1)S(1)}, bf16[36,896]{1,0:T(8,128)(2,1)S(1)}, u32[]{:S(2)}, u32[]{:S(2)}) %collective-permute-start.8) | collective-permute-done | bytes 64544 | tf_op jit(solution)/shard_map/ppermute | solution.py:508
  56.8 0.1 stack_part.1.refs_0_
  56.9 1.4 %collective-permute-start.9 = (bf16[144,896]{1,0:T(8,128)(2,1)S(1)}, bf16[144,896]{1,0:T(8,128)(2,1)S(1)}, u32[]{:S(2)}, u32[]{:S(2)}) collective-permute-start(bf16[144,896]{1,0:T(8,128)(2,1)S(1)} %stack_part.1.refs_0_), channel_id=1, source_target_pairs={{0,2},{2,0},{4,6},{6,4},{8,10},{10,8},{12,14},{14,12},{16,18},{18,... | collective-permute-start | bytes 774152 | tf_op jit(solution)/shard_map/ppermute | solution.py:508
  58.3 0.5 collective-permute-start.10
  58.8 1.6 %collective-permute-start.11 = (bf16[144,896]{1,0:T(8,128)(2,1)S(1)}, bf16[144,896]{1,0:T(8,128)(2,1)S(1)}, u32[]{:S(2)}, u32[]{:S(2)}) collective-permute-start(bf16[144,896]{1,0:T(8,128)(2,1)S(1)} %stack_part.1.refs_0_), channel_id=1, source_target_pairs={{0,6},{2,4},{4,2},{6,0},{8,14},{10,12},{12,10},{14,8},{16,22},{18,... | collective-permute-start | bytes 774152 | tf_op jit(solution)/shard_map/ppermute | solution.py:508
  60.5 3.9 %collective-permute-done.9.refs_1_ = bf16[144,896]{1,0:T(8,128)(2,1)S(1)} collective-permute-done((bf16[144,896]{1,0:T(8,128)(2,1)S(1)}, bf16[144,896]{1,0:T(8,128)(2,1)S(1)}, u32[]{:S(2)}, u32[]{:S(2)}) %collective-permute-start.9) | collective-permute-done | bytes 258080 | tf_op jit(solution)/shard_map/ppermute | solution.py:508
  64.4 4.2 %collective-permute-done.10.refs_2_ = bf16[144,896]{1,0:T(8,128)(2,1)S(1)} collective-permute-done((bf16[144,896]{1,0:T(8,128)(2,1)S(1)}, bf16[144,896]{1,0:T(8,128)(2,1)S(1)}, u32[]{:S(2)}, u32[]{:S(2)}) %collective-permute-start.10) | collective-permute-done | bytes 258080 | tf_op jit(solution)/shard_map/ppermute | solution.py:508
  68.6 0.5 collective-permute-start.15
  69.1 0.1 copy.16
  69.3 0.1 stack.91.places
  69.4 3.7 %all-to-all-start.1 = ((bf16[16,36,128]{2,1,0:T(8,128)(2,1)}), bf16[16,36,128]{2,1,0:T(8,128)(2,1)S(1)}, u32[]{:S(2)}, u32[]{:S(2)}) async-start(bf16[16,36,128]{2,1,0:T(8,128)(2,1)} %merge_part.1), calls=%async_computation.1 | async-start | bytes 327680 | tf_op jit(solution)/shard_map/all_to_all | solution.py:545
  73.1 16.3 %score_part.1 = f32[16,288]{1,0:T(8,128)S(1)} custom-call(s32[16]{0:T(128)S(1)} %stack.91.places, s32[288,128]{1,0:T(8,128)S(1)} %pad.4.ids_ref, bf16[144,896]{1,0:T(8,128)(2,1)S(1)} %stack_part.1.refs_0_, bf16[144,896]{1,0:T(8,128)(2,1)S(1)} %collective-permute-done.9.refs_1_, bf16[144,896]{1,0:T(8,128)(2,1)S(1)} %collective-permute-done.10.refs_2_, ...), custom_call_target="tpu_custom_call" | custom-call | flops 8455716864 | bytes 29360128 | tf_op jit(solution)/shard_map/score_part/pallas_call | solution.py:358
  89.5 0.1 collective-permute-start.16
  89.6 1.1 %collective-permute-done.16 = f32[16,288]{1,0:T(8,128)S(1)} collective-permute-done((f32[16,288]{1,0:T(8,128)S(1)}, f32[16,288]{1,0:T(8,128)S(1)}, u32[]{:S(2)}, u32[]{:S(2)}) %collective-permute-start.16) | collective-permute-done | bytes 18464 | tf_op jit(solution)/shard_map/ppermute | solution.py:508
  90.7 1.7 %collective-permute-start.18 = (f32[16,288]{1,0:T(8,128)S(1)}, f32[16,288]{1,0:T(8,128)S(1)}, u32[]{:S(2)}, u32[]{:S(2)}) collective-permute-start(f32[16,288]{1,0:T(8,128)S(1)} %add.111), channel_id=1, source_target_pairs={{0,4},{2,6},{4,0},{6,2},{8,12},{10,14},{12,8},{14,10},{16,20},{18,... | collective-permute-start | bytes 55304 | tf_op jit(solution)/shard_map/ppermute | solution.py:508
  92.4 1.5 %collective-permute-start.19 = (f32[16,288]{1,0:T(8,128)S(1)}, f32[16,288]{1,0:T(8,128)S(1)}, u32[]{:S(2)}, u32[]{:S(2)}) collective-permute-start(f32[16,288]{1,0:T(8,128)S(1)} %add.111), channel_id=1, source_target_pairs={{0,6},{2,4},{4,2},{6,0},{8,14},{10,12},{12,10},{14,8},{16,22},{18,... | collective-permute-start | bytes 55304 | tf_op jit(solution)/shard_map/ppermute | solution.py:508
  93.9 0.4 collective-permute-start.17
  94.3 0.3 collective-permute-done.18
  94.6 2.7 %collective-permute-done.19 = f32[16,288]{1,0:T(8,128)S(1)} collective-permute-done((f32[16,288]{1,0:T(8,128)S(1)}, f32[16,288]{1,0:T(8,128)S(1)}, u32[]{:S(2)}, u32[]{:S(2)}) %collective-permute-start.19) | collective-permute-done | bytes 18464 | tf_op jit(solution)/shard_map/ppermute | solution.py:508
  97.3 0.4 collective-permute-done.17
  97.8 2.4 %collective-permute-start.21 = (f32[16,288]{1,0:T(8,128)S(1)}, f32[16,288]{1,0:T(8,128)S(1)}, u32[]{:S(2)}, u32[]{:S(2)}) collective-permute-start(f32[16,288]{1,0:T(8,128)S(1)} %add_add_fusion.1), channel_id=1, source_target_pairs={{0,16},{2,18},{4,20},{6,22},{8,24},{10,26},{12,28},{14,30},{16,0},... | collective-permute-start | bytes 55304 | tf_op jit(solution)/shard_map/ppermute | solution.py:508
  100.2 1.4 %collective-permute-start.22 = (f32[16,288]{1,0:T(8,128)S(1)}, f32[16,288]{1,0:T(8,128)S(1)}, u32[]{:S(2)}, u32[]{:S(2)}) collective-permute-start(f32[16,288]{1,0:T(8,128)S(1)} %add_add_fusion.1), channel_id=1, source_target_pairs={{0,24},{2,26},{4,28},{6,30},{8,16},{10,18},{12,20},{14,22},{16,8},... | collective-permute-start | bytes 55304 | tf_op jit(solution)/shard_map/ppermute | solution.py:508
  101.7 5.9 %project_part.1 = f32[36,3584]{1,0:T(8,128)S(1)} custom-call(bf16[16,36,128]{2,1,0:T(8,128)(2,1)S(1)} %all-to-all-done.1.heads_ref, bf16[2048,3584]{1,0:T(8,128)(2,1)} %weight_hbm.3), custom_call_target="tpu_custom_call" | custom-call | flops 528482304 | bytes 14680064 | tf_op jit(solution)/shard_map/project_part/pallas_call | solution.py:276
  107.8 0.7 reshape.23
  108.5 1.2 %collective-permute-done.23 = f32[36,3584]{1,0:T(8,128)S(1)} collective-permute-done((f32[36,3584]{1,0:T(8,128)S(1)}, f32[36,3584]{1,0:T(8,128)S(1)}, u32[]{:S(2)}, u32[]{:S(2)}) %collective-permute-start.23) | collective-permute-done | bytes 516128 | tf_op jit(solution)/shard_map/ppermute | solution.py:508
  109.7 0.2 multiply_reduce_fusion
  109.9 0.9 add_convert_fusion
  (37 shorter events, 0.6 us)
Async XLA Ops:
  0.6 42.3 %copy-start = (s32[12,48]{1,0:T(8,128)S(1)}, s32[12,48]{1,0:T(8,128)}, u32[]{:S(2)}) copy-start(s32[12,48]{1,0:T(8,128)} %parents_ref) | copy-start | bytes 6916
  5.9 63.2 %copy-start.2 = (s32[2,144,10]{1,0,2:T(2,128)S(1)}, s32[2,144,10]{1,0,2:T(2,128)}, u32[]{:S(2)}) copy-start(s32[2,144,10]{1,0,2:T(2,128)} %param.17) | copy-start | bytes 34564
  12.8 32.4 %all-to-all-start = ((bf16[16,64,128]{2,1,0:T(8,128)(2,1)}), bf16[16,64,128]{2,1,0:T(8,128)(2,1)S(1)}, u32[]{:S(2)}, u32[]{:S(2)}) async-start(bf16[16,64,128]{2,1,0:T(8,128)(2,1)} %prompt_part.1), calls=%async_computation | async-start | bytes 524288 | tf_op jit(solution)/shard_map/all_to_all | solution.py:545
  21.1 12.0 %collective-permute-start = (bf16[144,896]{1,0:T(8,128)(2,1)S(1)}, bf16[144,896]{1,0:T(8,128)(2,1)S(1)}, u32[]{:S(2)}, u32[]{:S(2)}) collective-permute-start(bf16[144,896]{1,0:T(8,128)(2,1)S(1)} %get-tuple-element.44), channel_id=1, source_target_pairs={{0,2},{2,0},{4,6},{6,4},{8,10},{10,8},{12,14},{14,12},{16,18},{18,... | collective-permute-start | bytes 774152 | tf_op jit(solution)/shard_map/ppermute | solution.py:508
  23.0 13.6 %collective-permute-start.1 = (bf16[144,896]{1,0:T(8,128)(2,1)S(1)}, bf16[144,896]{1,0:T(8,128)(2,1)S(1)}, u32[]{:S(2)}, u32[]{:S(2)}) collective-permute-start(bf16[144,896]{1,0:T(8,128)(2,1)S(1)} %get-tuple-element.45), channel_id=1, source_target_pairs={{0,4},{2,6},{4,0},{6,2},{8,12},{10,14},{12,8},{14,10},{16,20},{18,... | collective-permute-start | bytes 774152 | tf_op jit(solution)/shard_map/ppermute | solution.py:508
  24.5 13.6 %collective-permute-start.2 = (bf16[144,896]{1,0:T(8,128)(2,1)S(1)}, bf16[144,896]{1,0:T(8,128)(2,1)S(1)}, u32[]{:S(2)}, u32[]{:S(2)}) collective-permute-start(bf16[144,896]{1,0:T(8,128)(2,1)S(1)} %get-tuple-element.46), channel_id=1, source_target_pairs={{0,6},{2,4},{4,2},{6,0},{8,14},{10,12},{12,10},{14,8},{16,22},{18,... | collective-permute-start | bytes 774152 | tf_op jit(solution)/shard_map/ppermute | solution.py:508
  38.4 7.8 %collective-permute-start.3 = (bf16[36,896]{1,0:T(8,128)(2,1)S(1)}, bf16[36,896]{1,0:T(8,128)(2,1)S(1)}, u32[]{:S(2)}, u32[]{:S(2)}) collective-permute-start(bf16[36,896]{1,0:T(8,128)(2,1)S(1)} %get-tuple-element.58), channel_id=1, source_target_pairs={{0,8},{2,10},{4,12},{6,14},{8,0},{10,2},{12,4},{14,6},{16,24},{18,... | collective-permute-start | bytes 193544 | tf_op jit(solution)/shard_map/ppermute | solution.py:508
  39.9 6.8 %collective-permute-start.4 = (bf16[36,896]{1,0:T(8,128)(2,1)S(1)}, bf16[36,896]{1,0:T(8,128)(2,1)S(1)}, u32[]{:S(2)}, u32[]{:S(2)}) collective-permute-start(bf16[36,896]{1,0:T(8,128)(2,1)S(1)} %get-tuple-element.59), channel_id=1, source_target_pairs={{0,16},{2,18},{4,20},{6,22},{8,24},{10,26},{12,28},{14,30},{16,0},... | collective-permute-start | bytes 193544 | tf_op jit(solution)/shard_map/ppermute | solution.py:508
  42.3 6.1 %collective-permute-start.5 = (bf16[36,896]{1,0:T(8,128)(2,1)S(1)}, bf16[36,896]{1,0:T(8,128)(2,1)S(1)}, u32[]{:S(2)}, u32[]{:S(2)}) collective-permute-start(bf16[36,896]{1,0:T(8,128)(2,1)S(1)} %get-tuple-element.60), channel_id=1, source_target_pairs={{0,24},{2,26},{4,28},{6,30},{8,16},{10,18},{12,20},{14,22},{16,8},... | collective-permute-start | bytes 193544 | tf_op jit(solution)/shard_map/ppermute | solution.py:508
  48.5 5.9 %collective-permute-start.6 = (bf16[36,896]{1,0:T(8,128)(2,1)S(1)}, bf16[36,896]{1,0:T(8,128)(2,1)S(1)}, u32[]{:S(2)}, u32[]{:S(2)}) collective-permute-start(bf16[36,896]{1,0:T(8,128)(2,1)S(1)} %add_convert_fusion.1.refs_0_), channel_id=1, source_target_pairs={{0,8},{2,10},{4,12},{6,14},{8,0},{10,2},{12,4},{14,6},{16,24},{18,... | collective-permute-start | bytes 193544 | tf_op jit(solution)/shard_map/ppermute | solution.py:508
  48.6 5.9 %collective-permute-start.7 = (bf16[36,896]{1,0:T(8,128)(2,1)S(1)}, bf16[36,896]{1,0:T(8,128)(2,1)S(1)}, u32[]{:S(2)}, u32[]{:S(2)}) collective-permute-start(bf16[36,896]{1,0:T(8,128)(2,1)S(1)} %add_convert_fusion.1.refs_0_), channel_id=1, source_target_pairs={{0,16},{2,18},{4,20},{6,22},{8,24},{10,26},{12,28},{14,30},{16,0},... | collective-permute-start | bytes 193544 | tf_op jit(solution)/shard_map/ppermute | solution.py:508
  50.6 6.2 %collective-permute-start.8 = (bf16[36,896]{1,0:T(8,128)(2,1)S(1)}, bf16[36,896]{1,0:T(8,128)(2,1)S(1)}, u32[]{:S(2)}, u32[]{:S(2)}) collective-permute-start(bf16[36,896]{1,0:T(8,128)(2,1)S(1)} %add_convert_fusion.1.refs_0_), channel_id=1, source_target_pairs={{0,24},{2,26},{4,28},{6,30},{8,16},{10,18},{12,20},{14,22},{16,8},... | collective-permute-start | bytes 193544 | tf_op jit(solution)/shard_map/ppermute | solution.py:508
  56.9 7.5 %collective-permute-start.9 = (bf16[144,896]{1,0:T(8,128)(2,1)S(1)}, bf16[144,896]{1,0:T(8,128)(2,1)S(1)}, u32[]{:S(2)}, u32[]{:S(2)}) collective-permute-start(bf16[144,896]{1,0:T(8,128)(2,1)S(1)} %stack_part.1.refs_0_), channel_id=1, source_target_pairs={{0,2},{2,0},{4,6},{6,4},{8,10},{10,8},{12,14},{14,12},{16,18},{18,... | collective-permute-start | bytes 774152 | tf_op jit(solution)/shard_map/ppermute | solution.py:508
  58.3 10.3 %collective-permute-start.10 = (bf16[144,896]{1,0:T(8,128)(2,1)S(1)}, bf16[144,896]{1,0:T(8,128)(2,1)S(1)}, u32[]{:S(2)}, u32[]{:S(2)}) collective-permute-start(bf16[144,896]{1,0:T(8,128)(2,1)S(1)} %stack_part.1.refs_0_), channel_id=1, source_target_pairs={{0,4},{2,6},{4,0},{6,2},{8,12},{10,14},{12,8},{14,10},{16,20},{18,... | collective-permute-start | bytes 774152 | tf_op jit(solution)/shard_map/ppermute | solution.py:508
  58.8 9.8 %collective-permute-start.11 = (bf16[144,896]{1,0:T(8,128)(2,1)S(1)}, bf16[144,896]{1,0:T(8,128)(2,1)S(1)}, u32[]{:S(2)}, u32[]{:S(2)}) collective-permute-start(bf16[144,896]{1,0:T(8,128)(2,1)S(1)} %stack_part.1.refs_0_), channel_id=1, source_target_pairs={{0,6},{2,4},{4,2},{6,0},{8,14},{10,12},{12,10},{14,8},{16,22},{18,... | collective-permute-start | bytes 774152 | tf_op jit(solution)/shard_map/ppermute | solution.py:508
  60.5 12.6 %collective-permute-start.12 = (bf16[144,896]{1,0:T(8,128)(2,1)S(1)}, bf16[144,896]{1,0:T(8,128)(2,1)S(1)}, u32[]{:S(2)}, u32[]{:S(2)}) collective-permute-start(bf16[144,896]{1,0:T(8,128)(2,1)S(1)} %stack_part.1.refs_0_), channel_id=1, source_target_pairs={{0,1},{1,0},{2,3},{3,2},{4,5},{5,4},{6,7},{7,6},{8,9},{9,8},{10,11... | collective-permute-start | bytes 774152 | tf_op jit(solution)/shard_map/ppermute | solution.py:508
  64.4 8.7 %collective-permute-start.13 = (bf16[144,896]{1,0:T(8,128)(2,1)S(1)}, bf16[144,896]{1,0:T(8,128)(2,1)S(1)}, u32[]{:S(2)}, u32[]{:S(2)}) collective-permute-start(bf16[144,896]{1,0:T(8,128)(2,1)S(1)} %collective-permute-done.9.refs_1_), channel_id=1, source_target_pairs={{0,1},{1,0},{2,3},{3,2},{4,5},{5,4},{6,7},{7,6},{8,9},{9,8},{10,11... | collective-permute-start | bytes 774152 | tf_op jit(solution)/shard_map/ppermute | solution.py:508
  68.6 4.5 %collective-permute-start.14 = (bf16[144,896]{1,0:T(8,128)(2,1)S(1)}, bf16[144,896]{1,0:T(8,128)(2,1)S(1)}, u32[]{:S(2)}, u32[]{:S(2)}) collective-permute-start(bf16[144,896]{1,0:T(8,128)(2,1)S(1)} %collective-permute-done.10.refs_2_), channel_id=1, source_target_pairs={{0,1},{1,0},{2,3},{3,2},{4,5},{5,4},{6,7},{7,6},{8,9},{9,8},{10,11... | collective-permute-start | bytes 774152 | tf_op jit(solution)/shard_map/ppermute | solution.py:508
  68.6 4.5 %collective-permute-start.15 = (bf16[144,896]{1,0:T(8,128)(2,1)S(1)}, bf16[144,896]{1,0:T(8,128)(2,1)S(1)}, u32[]{:S(2)}, u32[]{:S(2)}) collective-permute-start(bf16[144,896]{1,0:T(8,128)(2,1)S(1)} %collective-permute-done.11.refs_3_), channel_id=1, source_target_pairs={{0,1},{1,0},{2,3},{3,2},{4,5},{5,4},{6,7},{7,6},{8,9},{9,8},{10,11... | collective-permute-start | bytes 774152 | tf_op jit(solution)/shard_map/ppermute | solution.py:508
  69.4 21.4 %all-to-all-start.1 = ((bf16[16,36,128]{2,1,0:T(8,128)(2,1)}), bf16[16,36,128]{2,1,0:T(8,128)(2,1)S(1)}, u32[]{:S(2)}, u32[]{:S(2)}) async-start(bf16[16,36,128]{2,1,0:T(8,128)(2,1)} %merge_part.1), calls=%async_computation.1 | async-start | bytes 327680 | tf_op jit(solution)/shard_map/all_to_all | solution.py:545
  89.5 1.3 %collective-permute-start.16 = (f32[16,288]{1,0:T(8,128)S(1)}, f32[16,288]{1,0:T(8,128)S(1)}, u32[]{:S(2)}, u32[]{:S(2)}) collective-permute-start(f32[16,288]{1,0:T(8,128)S(1)} %score_part.1), channel_id=1, source_target_pairs={{0,1},{1,0},{2,3},{3,2},{4,5},{5,4},{6,7},{7,6},{8,9},{9,8},{10,11... | collective-permute-start | bytes 55304 | tf_op jit(solution)/shard_map/ppermute | solution.py:508
  90.7 3.9 %collective-permute-start.18 = (f32[16,288]{1,0:T(8,128)S(1)}, f32[16,288]{1,0:T(8,128)S(1)}, u32[]{:S(2)}, u32[]{:S(2)}) collective-permute-start(f32[16,288]{1,0:T(8,128)S(1)} %add.111), channel_id=1, source_target_pairs={{0,4},{2,6},{4,0},{6,2},{8,12},{10,14},{12,8},{14,10},{16,20},{18,... | collective-permute-start | bytes 55304 | tf_op jit(solution)/shard_map/ppermute | solution.py:508
  92.4 4.9 %collective-permute-start.19 = (f32[16,288]{1,0:T(8,128)S(1)}, f32[16,288]{1,0:T(8,128)S(1)}, u32[]{:S(2)}, u32[]{:S(2)}) collective-permute-start(f32[16,288]{1,0:T(8,128)S(1)} %add.111), channel_id=1, source_target_pairs={{0,6},{2,4},{4,2},{6,0},{8,14},{10,12},{12,10},{14,8},{16,22},{18,... | collective-permute-start | bytes 55304 | tf_op jit(solution)/shard_map/ppermute | solution.py:508
  93.9 3.8 %collective-permute-start.17 = (f32[16,288]{1,0:T(8,128)S(1)}, f32[16,288]{1,0:T(8,128)S(1)}, u32[]{:S(2)}, u32[]{:S(2)}) collective-permute-start(f32[16,288]{1,0:T(8,128)S(1)} %add.111), channel_id=1, source_target_pairs={{0,2},{2,0},{4,6},{6,4},{8,10},{10,8},{12,14},{14,12},{16,18},{18,... | collective-permute-start | bytes 55304 | tf_op jit(solution)/shard_map/ppermute | solution.py:508
  97.7 12.2 %copy-start.1 = (bf16[36,3584]{1,0:T(8,128)(2,1)S(1)}, bf16[36,3584]{1,0:T(8,128)(2,1)}, u32[]{:S(2)}) copy-start(bf16[36,3584]{1,0:T(8,128)(2,1)} %param.27) | copy-start | bytes 774148
  97.8 12.2 %copy-start.3 = (f32[3584]{0:T(1024)S(1)}, f32[3584]{0:T(1024)}, u32[]{:S(2)}) copy-start(f32[3584]{0:T(1024)} %param.26) | copy-start | bytes 43012
  97.8 10.0 %collective-permute-start.21 = (f32[16,288]{1,0:T(8,128)S(1)}, f32[16,288]{1,0:T(8,128)S(1)}, u32[]{:S(2)}, u32[]{:S(2)}) collective-permute-start(f32[16,288]{1,0:T(8,128)S(1)} %add_add_fusion.1), channel_id=1, source_target_pairs={{0,16},{2,18},{4,20},{6,22},{8,24},{10,26},{12,28},{14,30},{16,0},... | collective-permute-start | bytes 55304 | tf_op jit(solution)/shard_map/ppermute | solution.py:508
  100.2 7.6 %collective-permute-start.22 = (f32[16,288]{1,0:T(8,128)S(1)}, f32[16,288]{1,0:T(8,128)S(1)}, u32[]{:S(2)}, u32[]{:S(2)}) collective-permute-start(f32[16,288]{1,0:T(8,128)S(1)} %add_add_fusion.1), channel_id=1, source_target_pairs={{0,24},{2,26},{4,28},{6,30},{8,16},{10,18},{12,20},{14,22},{16,8},... | collective-permute-start | bytes 55304 | tf_op jit(solution)/shard_map/ppermute | solution.py:508
  101.7 6.1 %collective-permute-start.20 = (f32[16,288]{1,0:T(8,128)S(1)}, f32[16,288]{1,0:T(8,128)S(1)}, u32[]{:S(2)}, u32[]{:S(2)}) collective-permute-start(f32[16,288]{1,0:T(8,128)S(1)} %add_add_fusion.1), channel_id=1, source_target_pairs={{0,8},{2,10},{4,12},{6,14},{8,0},{10,2},{12,4},{14,6},{16,24},{18,... | collective-permute-start | bytes 55304 | tf_op jit(solution)/shard_map/ppermute | solution.py:508
  107.7 2.0 %collective-permute-start.23 = (f32[36,3584]{1,0:T(8,128)S(1)}, f32[36,3584]{1,0:T(8,128)S(1)}, u32[]{:S(2)}, u32[]{:S(2)}) collective-permute-start(f32[36,3584]{1,0:T(8,128)S(1)} %project_part.1), channel_id=1, source_target_pairs={{0,1},{1,0},{2,3},{3,2},{4,5},{5,4},{6,7},{7,6},{8,9},{9,8},{10,11... | collective-permute-start | bytes 1548296 | tf_op jit(solution)/shard_map/ppermute | solution.py:508

commit v8 on v7

--- a/solution.py
+++ b/solution.py
@@ -10,6 +10,7 @@
 HEAD_SIZE = 256
 LANES = 128
 MIB = 1 << 20
+LOG2_E = 1.4426950408889634
 
 EXTRA = 16
 HIGH, LOW, GROUP = 0, 4, 8
@@ -197,6 +198,7 @@
             pltpu.SemaphoreType.DMA((3,)),
         ],
         compiler_params=limit(16),
+        cost_estimate=pl.CostEstimate(flops=0, bytes_accessed=20 * MIB, transcendentals=0),
         name="tree_part",
     )(meta, pin(tree_q), pin(tree_key_value), parents)
 
@@ -322,7 +324,7 @@
             sums, found = total[r : r + band], picked[r : r + band]
             for c in range(span // LANES):
                 part = jnp.tanh(raw[r : r + band, c * LANES : (c + 1) * LANES] * (1.0 / 30.0))
-                sums = sums + jnp.exp(30.0 * part)
+                sums = sums + jnp.exp2(part * (30.0 * LOG2_E))
                 there = jnp.take_along_axis(part, lane, axis=1, mode="promise_in_bounds")
                 found = found + jnp.where(chunk == c, there, 0.0)
             if keep is not None:
@@ -508,8 +510,10 @@
     return lax.ppermute(value, axis, [(i, i ^ bits) for i in range(size)])
 
 
-def group_sum(value, axis, size, stride, count):
+def group_sum(value, axis, size, stride, count, beside=None):
     values = [value] + [partner(value, axis, size, k * stride) for k in range(1, count)]
+    if beside is not None:
+        values, _ = lax.optimization_barrier((values, beside))
     while len(values) > 1:
         values = [values[i] + values[i + 1] for i in range(0, len(values), 2)]
     return values[0]
@@ -609,12 +613,12 @@
     score = score_part(places, pieces, embedding, ids, picks)
     score = group_sum(score, "mp", splits, 1, splits)
     score, heads_out = lax.optimization_barrier((score, heads_out))
-    score = group_sum(score, "blk", blocks, 1, 4)
+    attn = project_part(heads_out, out_weight)
+    score = group_sum(score, "blk", blocks, 1, 4, attn)
     score = group_sum(score, "blk", blocks, 4, blocks // 4)
     draft_logprob = score[:picks] - jnp.log(score[picks : picks + 1])
     draft_logprob = draft_logprob.T.reshape(drafts, rows, picks)
 
-    attn = project_part(heads_out, out_weight)
     attn = group_sum(attn, "mp", splits, 1, splits)
     normed = attn * lax.rsqrt(jnp.mean(attn * attn, -1, keepdims=True) + 1e-06) * post_gain
     layer_out = (normed + resid.astype(jnp.float32)).astype(jnp.bfloat16)

time: 111 us -> 111 us (level)
  transfers between devices with their start and end apart: 26 -> 26, of which waited for: 14 -> 12; matrix products, arithmetic and copies ran while one was open for 1% -> 1% of each run, Pallas kernels for 23% -> 23%
where the time goes in v8:
time: 111 us; the launch traced here: 110 us
  starting transfers between devices  36.3 us (33%)
  Pallas kernels  36 us (32%)
  waiting for transfers between devices  32.9 us (30%)
  between operations  2.83 us (3%)
  other arithmetic  1.32 us (1%)
    ppermute x24, waiting for transfers between devices, partner(): return lax.ppermute(value, axis, [(i, i ^ bits) for i in range(size)])  32.9 us
    ppermute x24, starting transfers between devices, partner(): return lax.ppermute(value, axis, [(i, i ^ bits) for i in range(size)])  24.3 us
    pallas_call x1, Pallas kernels, score_part(): pl.pallas_call(functools.partial(score_kernel, picks, streams), out_shape...  16.4 us
    all_to_all x2, starting transfers between devices, spread(): return lax.all_to_all(value, 'blk', 0, 0, tiled=True)  12 us
    pallas_call x1, Pallas kernels, prompt_part(): pl.pallas_call(prompt_kernel, out_shape=jax.ShapeDtypeStruct((blocks, tre...  6.91 us
    pallas_call x1, Pallas kernels, project_part(): pl.pallas_call(project_kernel, out_shape=jax.ShapeDtypeStruct((tokens, mo...  5.95 us
    pallas_call x1, Pallas kernels, draft_part(): pl.pallas_call(draft_kernel, out_shape=[jax.ShapeDtypeStruct((rows, half)...  3.09 us
    pallas_call x1, Pallas kernels, tree_part(): pl.pallas_call(tree_kernel, out_shape=[jax.ShapeDtypeStruct((groups, tree...  2.23 us
  transfers between devices with their start and end apart: 26, of which 12 were waited for; matrix products, arithmetic and copies ran while one was open for 1% of the time, Pallas kernels for 23%

profile of v8, /device:TPU:0, one launch (start us, length us, event | category | flops | bytes accessed | tf_op | source)
XLA Modules:
  0.0 110.4 jit_solution(15782217460031361231)
XLA Ops:
  2.6 0.1 stack.99.meta
  2.7 3.1 %draft_part.1 = (f32[144,896]{1,0:T(8,128)S(1)}, bf16[144,896]{1,0:T(8,128)(2,1)S(1)}, bf16[144,896]{1,0:T(8,128)(2,1)S(1)}, bf16[144,896]{1,0:T(8,128)(2,1)S(1)}, bf16[144,896]{1,0:T(8,128)(2,1)S(1)}) custom-call(s32[7]{0:T(128)S(1)} %stack.99.meta, bf16[144,3584]{1,0:T(8,128)(2,1)} %hidden_hbm.1, bf16[2,224,1792]{2,1,0:T(8,128)(2,1)} %weight_hbm.2), custom_call_target="tpu_custom_call" | custom-call | tf_op jit(solution)/shard_map/draft_part/pallas_call | solution.py:431
  5.8 0.1 pad_add_fusion.meta
  5.9 6.9 %prompt_part.1 = bf16[16,64,128]{2,1,0:T(8,128)(2,1)} custom-call(s32[3]{0:T(128)S(1)} %pad_add_fusion.meta, bf16[12,48,2048]{2,1,0:T(8,128)(2,1)} %q_hbm.3, bf16[2,1,2048,1024]{3,2,1,0:T(8,128)(2,1)} %kv_hbm.2), custom_call_target="tpu_custom_call" | custom-call | flops 805306368 | bytes 8388608 | tf_op jit(solution)/shard_map/prompt_part/pallas_call | solution.py:124
  12.8 8.3 %all-to-all-start = ((bf16[16,64,128]{2,1,0:T(8,128)(2,1)}), bf16[16,64,128]{2,1,0:T(8,128)(2,1)S(1)}, u32[]{:S(2)}, u32[]{:S(2)}) async-start(bf16[16,64,128]{2,1,0:T(8,128)(2,1)} %prompt_part.1), calls=%async_computation | async-start | bytes 524288 | tf_op jit(solution)/shard_map/all_to_all | solution.py:549
  21.1 1.9 %collective-permute-start = (bf16[144,896]{1,0:T(8,128)(2,1)S(1)}, bf16[144,896]{1,0:T(8,128)(2,1)S(1)}, u32[]{:S(2)}, u32[]{:S(2)}) collective-permute-start(bf16[144,896]{1,0:T(8,128)(2,1)S(1)} %get-tuple-element.48), channel_id=1, source_target_pairs={{0,2},{2,0},{4,6},{6,4},{8,10},{10,8},{12,14},{14,12},{16,18},{18,... | collective-permute-start | bytes 774152 | tf_op jit(solution)/shard_map/ppermute | solution.py:510
  23.0 1.5 %collective-permute-start.1 = (bf16[144,896]{1,0:T(8,128)(2,1)S(1)}, bf16[144,896]{1,0:T(8,128)(2,1)S(1)}, u32[]{:S(2)}, u32[]{:S(2)}) collective-permute-start(bf16[144,896]{1,0:T(8,128)(2,1)S(1)} %get-tuple-element.49), channel_id=1, source_target_pairs={{0,4},{2,6},{4,0},{6,2},{8,12},{10,14},{12,8},{14,10},{16,20},{18,... | collective-permute-start | bytes 774152 | tf_op jit(solution)/shard_map/ppermute | solution.py:510
  24.5 0.2 collective-permute-start.2
  24.7 8.5 %collective-permute-done.refs_0_ = bf16[144,896]{1,0:T(8,128)(2,1)S(1)} collective-permute-done((bf16[144,896]{1,0:T(8,128)(2,1)S(1)}, bf16[144,896]{1,0:T(8,128)(2,1)S(1)}, u32[]{:S(2)}, u32[]{:S(2)}) %collective-permute-start) | collective-permute-done | bytes 258080 | tf_op jit(solution)/shard_map/ppermute | solution.py:510
  33.1 3.5 %collective-permute-done.1.refs_1_ = bf16[144,896]{1,0:T(8,128)(2,1)S(1)} collective-permute-done((bf16[144,896]{1,0:T(8,128)(2,1)S(1)}, bf16[144,896]{1,0:T(8,128)(2,1)S(1)}, u32[]{:S(2)}, u32[]{:S(2)}) %collective-permute-start.1) | collective-permute-done | bytes 258080 | tf_op jit(solution)/shard_map/ppermute | solution.py:510
  36.6 1.5 %collective-permute-done.2.refs_2_ = bf16[144,896]{1,0:T(8,128)(2,1)S(1)} collective-permute-done((bf16[144,896]{1,0:T(8,128)(2,1)S(1)}, bf16[144,896]{1,0:T(8,128)(2,1)S(1)}, u32[]{:S(2)}, u32[]{:S(2)}) %collective-permute-start.2) | collective-permute-done | bytes 258080 | tf_op jit(solution)/shard_map/ppermute | solution.py:510
  38.1 0.3 fold_part.1
  38.4 1.5 %collective-permute-start.3 = (bf16[36,896]{1,0:T(8,128)(2,1)S(1)}, bf16[36,896]{1,0:T(8,128)(2,1)S(1)}, u32[]{:S(2)}, u32[]{:S(2)}) collective-permute-start(bf16[36,896]{1,0:T(8,128)(2,1)S(1)} %get-tuple-element.62), channel_id=1, source_target_pairs={{0,8},{2,10},{4,12},{6,14},{8,0},{10,2},{12,4},{14,6},{16,24},{18,... | collective-permute-start | bytes 193544 | tf_op jit(solution)/shard_map/ppermute | solution.py:510
  39.9 2.4 %collective-permute-start.4 = (bf16[36,896]{1,0:T(8,128)(2,1)S(1)}, bf16[36,896]{1,0:T(8,128)(2,1)S(1)}, u32[]{:S(2)}, u32[]{:S(2)}) collective-permute-start(bf16[36,896]{1,0:T(8,128)(2,1)S(1)} %get-tuple-element.63), channel_id=1, source_target_pairs={{0,16},{2,18},{4,20},{6,22},{8,24},{10,26},{12,28},{14,30},{16,0},... | collective-permute-start | bytes 193544 | tf_op jit(solution)/shard_map/ppermute | solution.py:510
  42.3 0.6 collective-permute-start.5
  42.9 0.1 pad_add_fusion.1.meta
  42.9 2.2 %tree_part.1 = (f32[12,48,128]{2,1,0:T(8,128)S(1)}, f32[12,48,128]{2,1,0:T(8,128)S(1)}) custom-call(s32[3]{0:T(128)S(1)} %pad_add_fusion.1.meta, bf16[12,48,2048]{2,1,0:T(8,128)(2,1)} %q_hbm.3, bf16[2,12,48,1024]{3,2,1,0:T(8,128)(2,1)} %kv_hbm.3, s32[12,48]{1,0:T(8,128)S(1)} %copy-done), custom_call_target="tpu_custom_call" | custom-call | bytes 20971520 | tf_op jit(solution)/shard_map/tree_part/pallas_call | solution.py:191
  45.2 1.1 merge_part.1
  46.3 0.5 collective-permute-done.4
  46.8 1.7 %collective-permute-done.5 = bf16[36,896]{1,0:T(8,128)(2,1)S(1)} collective-permute-done((bf16[36,896]{1,0:T(8,128)(2,1)S(1)}, bf16[36,896]{1,0:T(8,128)(2,1)S(1)}, u32[]{:S(2)}, u32[]{:S(2)}) %collective-permute-start.5) | collective-permute-done | bytes 64544 | tf_op jit(solution)/shard_map/ppermute | solution.py:510
  48.6 2.0 %collective-permute-start.7 = (bf16[36,896]{1,0:T(8,128)(2,1)S(1)}, bf16[36,896]{1,0:T(8,128)(2,1)S(1)}, u32[]{:S(2)}, u32[]{:S(2)}) collective-permute-start(bf16[36,896]{1,0:T(8,128)(2,1)S(1)} %add_convert_fusion.1.refs_0_), channel_id=1, source_target_pairs={{0,16},{2,18},{4,20},{6,22},{8,24},{10,26},{12,28},{14,30},{16,0},... | collective-permute-start | bytes 193544 | tf_op jit(solution)/shard_map/ppermute | solution.py:510
  50.6 2.3 %collective-permute-start.8 = (bf16[36,896]{1,0:T(8,128)(2,1)S(1)}, bf16[36,896]{1,0:T(8,128)(2,1)S(1)}, u32[]{:S(2)}, u32[]{:S(2)}) collective-permute-start(bf16[36,896]{1,0:T(8,128)(2,1)S(1)} %add_convert_fusion.1.refs_0_), channel_id=1, source_target_pairs={{0,24},{2,26},{4,28},{6,30},{8,16},{10,18},{12,20},{14,22},{16,8},... | collective-permute-start | bytes 193544 | tf_op jit(solution)/shard_map/ppermute | solution.py:510
  53.0 1.5 %collective-permute-done.6.refs_1_ = bf16[36,896]{1,0:T(8,128)(2,1)S(1)} collective-permute-done((bf16[36,896]{1,0:T(8,128)(2,1)S(1)}, bf16[36,896]{1,0:T(8,128)(2,1)S(1)}, u32[]{:S(2)}, u32[]{:S(2)}) %collective-permute-start.6) | collective-permute-done | bytes 64544 | tf_op jit(solution)/shard_map/ppermute | solution.py:510
  54.5 2.4 %collective-permute-done.8.refs_3_ = bf16[36,896]{1,0:T(8,128)(2,1)S(1)} collective-permute-done((bf16[36,896]{1,0:T(8,128)(2,1)S(1)}, bf16[36,896]{1,0:T(8,128)(2,1)S(1)}, u32[]{:S(2)}, u32[]{:S(2)}) %collective-permute-start.8) | collective-permute-done | bytes 64544 | tf_op jit(solution)/shard_map/ppermute | solution.py:510
  56.8 0.1 stack_part.1.refs_0_
  56.9 1.4 %collective-permute-start.9 = (bf16[144,896]{1,0:T(8,128)(2,1)S(1)}, bf16[144,896]{1,0:T(8,128)(2,1)S(1)}, u32[]{:S(2)}, u32[]{:S(2)}) collective-permute-start(bf16[144,896]{1,0:T(8,128)(2,1)S(1)} %stack_part.1.refs_0_), channel_id=1, source_target_pairs={{0,2},{2,0},{4,6},{6,4},{8,10},{10,8},{12,14},{14,12},{16,18},{18,... | collective-permute-start | bytes 774152 | tf_op jit(solution)/shard_map/ppermute | solution.py:510
  58.3 0.5 collective-permute-start.10
  58.8 1.6 %collective-permute-start.11 = (bf16[144,896]{1,0:T(8,128)(2,1)S(1)}, bf16[144,896]{1,0:T(8,128)(2,1)S(1)}, u32[]{:S(2)}, u32[]{:S(2)}) collective-permute-start(bf16[144,896]{1,0:T(8,128)(2,1)S(1)} %stack_part.1.refs_0_), channel_id=1, source_target_pairs={{0,6},{2,4},{4,2},{6,0},{8,14},{10,12},{12,10},{14,8},{16,22},{18,... | collective-permute-start | bytes 774152 | tf_op jit(solution)/shard_map/ppermute | solution.py:510
  60.5 3.9 %collective-permute-done.9.refs_1_ = bf16[144,896]{1,0:T(8,128)(2,1)S(1)} collective-permute-done((bf16[144,896]{1,0:T(8,128)(2,1)S(1)}, bf16[144,896]{1,0:T(8,128)(2,1)S(1)}, u32[]{:S(2)}, u32[]{:S(2)}) %collective-permute-start.9) | collective-permute-done | bytes 258080 | tf_op jit(solution)/shard_map/ppermute | solution.py:510
  64.4 4.2 %collective-permute-done.10.refs_2_ = bf16[144,896]{1,0:T(8,128)(2,1)S(1)} collective-permute-done((bf16[144,896]{1,0:T(8,128)(2,1)S(1)}, bf16[144,896]{1,0:T(8,128)(2,1)S(1)}, u32[]{:S(2)}, u32[]{:S(2)}) %collective-permute-start.10) | collective-permute-done | bytes 258080 | tf_op jit(solution)/shard_map/ppermute | solution.py:510
  68.6 0.5 collective-permute-start.15
  69.1 0.1 copy.16
  69.3 0.1 stack.91.places
  69.4 3.7 %all-to-all-start.1 = ((bf16[16,36,128]{2,1,0:T(8,128)(2,1)}), bf16[16,36,128]{2,1,0:T(8,128)(2,1)S(1)}, u32[]{:S(2)}, u32[]{:S(2)}) async-start(bf16[16,36,128]{2,1,0:T(8,128)(2,1)} %merge_part.1), calls=%async_computation.1 | async-start | bytes 327680 | tf_op jit(solution)/shard_map/all_to_all | solution.py:549
  73.1 16.4 %score_part.1 = f32[16,288]{1,0:T(8,128)S(1)} custom-call(s32[16]{0:T(128)S(1)} %stack.91.places, s32[288,128]{1,0:T(8,128)S(1)} %pad.4.ids_ref, bf16[144,896]{1,0:T(8,128)(2,1)S(1)} %stack_part.1.refs_0_, bf16[144,896]{1,0:T(8,128)(2,1)S(1)} %collective-permute-done.9.refs_1_, bf16[144,896]{1,0:T(8,128)(2,1)S(1)} %collective-permute-done.10.refs_2_, ...), custom_call_target="tpu_custom_call" | custom-call | flops 8455716864 | bytes 29360128 | tf_op jit(solution)/shard_map/score_part/pallas_call | solution.py:360
  89.5 0.1 collective-permute-start.16
  89.6 1.2 %collective-permute-done.16 = f32[16,288]{1,0:T(8,128)S(1)} collective-permute-done((f32[16,288]{1,0:T(8,128)S(1)}, f32[16,288]{1,0:T(8,128)S(1)}, u32[]{:S(2)}, u32[]{:S(2)}) %collective-permute-start.16) | collective-permute-done | bytes 18464 | tf_op jit(solution)/shard_map/ppermute | solution.py:510
  90.8 1.7 %collective-permute-start.17 = (f32[16,288]{1,0:T(8,128)S(1)}, f32[16,288]{1,0:T(8,128)S(1)}, u32[]{:S(2)}, u32[]{:S(2)}) collective-permute-start(f32[16,288]{1,0:T(8,128)S(1)} %add.111), channel_id=1, source_target_pairs={{0,2},{2,0},{4,6},{6,4},{8,10},{10,8},{12,14},{14,12},{16,18},{18,... | collective-permute-start | bytes 55304 | tf_op jit(solution)/shard_map/ppermute | solution.py:510
  92.5 1.5 %collective-permute-start.18 = (f32[16,288]{1,0:T(8,128)S(1)}, f32[16,288]{1,0:T(8,128)S(1)}, u32[]{:S(2)}, u32[]{:S(2)}) collective-permute-start(f32[16,288]{1,0:T(8,128)S(1)} %add.111), channel_id=1, source_target_pairs={{0,4},{2,6},{4,0},{6,2},{8,12},{10,14},{12,8},{14,10},{16,20},{18,... | collective-permute-start | bytes 55304 | tf_op jit(solution)/shard_map/ppermute | solution.py:510
  93.9 0.4 collective-permute-start.19
  94.3 5.9 %project_part.1 = f32[36,3584]{1,0:T(8,128)S(1)} custom-call(bf16[16,36,128]{2,1,0:T(8,128)(2,1)S(1)} %all-to-all-done.1.heads_ref, bf16[2048,3584]{1,0:T(8,128)(2,1)} %weight_hbm.3), custom_call_target="tpu_custom_call" | custom-call | flops 528482304 | bytes 14680064 | tf_op jit(solution)/shard_map/project_part/pallas_call | solution.py:278
  100.3 2.6 %collective-permute-start.21 = (f32[16,288]{1,0:T(8,128)S(1)}, f32[16,288]{1,0:T(8,128)S(1)}, u32[]{:S(2)}, u32[]{:S(2)}) collective-permute-start(f32[16,288]{1,0:T(8,128)S(1)} %add_add_fusion.1), channel_id=1, source_target_pairs={{0,16},{2,18},{4,20},{6,22},{8,24},{10,26},{12,28},{14,30},{16,0},... | collective-permute-start | bytes 55304 | tf_op jit(solution)/shard_map/ppermute | solution.py:510
  103.0 1.4 %collective-permute-start.22 = (f32[16,288]{1,0:T(8,128)S(1)}, f32[16,288]{1,0:T(8,128)S(1)}, u32[]{:S(2)}, u32[]{:S(2)}) collective-permute-start(f32[16,288]{1,0:T(8,128)S(1)} %add_add_fusion.1), channel_id=1, source_target_pairs={{0,24},{2,26},{4,28},{6,30},{8,16},{10,18},{12,20},{14,22},{16,8},... | collective-permute-start | bytes 55304 | tf_op jit(solution)/shard_map/ppermute | solution.py:510
  104.5 0.7 collective-permute-done.21
  105.1 3.5 %collective-permute-done.22 = f32[16,288]{1,0:T(8,128)S(1)} collective-permute-done((f32[16,288]{1,0:T(8,128)S(1)}, f32[16,288]{1,0:T(8,128)S(1)}, u32[]{:S(2)}, u32[]{:S(2)}) %collective-permute-start.22) | collective-permute-done | bytes 18464 | tf_op jit(solution)/shard_map/ppermute | solution.py:510
  108.6 0.7 reshape.23
  109.3 0.2 multiply_reduce_fusion
  109.5 0.9 add_convert_fusion
  (37 shorter events, 0.3 us)
Async XLA Ops:
  0.6 42.3 %copy-start = (s32[12,48]{1,0:T(8,128)S(1)}, s32[12,48]{1,0:T(8,128)}, u32[]{:S(2)}) copy-start(s32[12,48]{1,0:T(8,128)} %parents_ref) | copy-start | bytes 6916
  5.9 63.2 %copy-start.2 = (s32[2,144,10]{1,0,2:T(2,128)S(1)}, s32[2,144,10]{1,0,2:T(2,128)}, u32[]{:S(2)}) copy-start(s32[2,144,10]{1,0,2:T(2,128)} %param.17) | copy-start | bytes 34564
  12.8 32.4 %all-to-all-start = ((bf16[16,64,128]{2,1,0:T(8,128)(2,1)}), bf16[16,64,128]{2,1,0:T(8,128)(2,1)S(1)}, u32[]{:S(2)}, u32[]{:S(2)}) async-start(bf16[16,64,128]{2,1,0:T(8,128)(2,1)} %prompt_part.1), calls=%async_computation | async-start | bytes 524288 | tf_op jit(solution)/shard_map/all_to_all | solution.py:549
  21.1 12.0 %collective-permute-start = (bf16[144,896]{1,0:T(8,128)(2,1)S(1)}, bf16[144,896]{1,0:T(8,128)(2,1)S(1)}, u32[]{:S(2)}, u32[]{:S(2)}) collective-permute-start(bf16[144,896]{1,0:T(8,128)(2,1)S(1)} %get-tuple-element.48), channel_id=1, source_target_pairs={{0,2},{2,0},{4,6},{6,4},{8,10},{10,8},{12,14},{14,12},{16,18},{18,... | collective-permute-start | bytes 774152 | tf_op jit(solution)/shard_map/ppermute | solution.py:510
  23.0 13.6 %collective-permute-start.1 = (bf16[144,896]{1,0:T(8,128)(2,1)S(1)}, bf16[144,896]{1,0:T(8,128)(2,1)S(1)}, u32[]{:S(2)}, u32[]{:S(2)}) collective-permute-start(bf16[144,896]{1,0:T(8,128)(2,1)S(1)} %get-tuple-element.49), channel_id=1, source_target_pairs={{0,4},{2,6},{4,0},{6,2},{8,12},{10,14},{12,8},{14,10},{16,20},{18,... | collective-permute-start | bytes 774152 | tf_op jit(solution)/shard_map/ppermute | solution.py:510
  24.5 13.6 %collective-permute-start.2 = (bf16[144,896]{1,0:T(8,128)(2,1)S(1)}, bf16[144,896]{1,0:T(8,128)(2,1)S(1)}, u32[]{:S(2)}, u32[]{:S(2)}) collective-permute-start(bf16[144,896]{1,0:T(8,128)(2,1)S(1)} %get-tuple-element.50), channel_id=1, source_target_pairs={{0,6},{2,4},{4,2},{6,0},{8,14},{10,12},{12,10},{14,8},{16,22},{18,... | collective-permute-start | bytes 774152 | tf_op jit(solution)/shard_map/ppermute | solution.py:510
  38.4 7.9 %collective-permute-start.3 = (bf16[36,896]{1,0:T(8,128)(2,1)S(1)}, bf16[36,896]{1,0:T(8,128)(2,1)S(1)}, u32[]{:S(2)}, u32[]{:S(2)}) collective-permute-start(bf16[36,896]{1,0:T(8,128)(2,1)S(1)} %get-tuple-element.62), channel_id=1, source_target_pairs={{0,8},{2,10},{4,12},{6,14},{8,0},{10,2},{12,4},{14,6},{16,24},{18,... | collective-permute-start | bytes 193544 | tf_op jit(solution)/shard_map/ppermute | solution.py:510
  39.9 6.8 %collective-permute-start.4 = (bf16[36,896]{1,0:T(8,128)(2,1)S(1)}, bf16[36,896]{1,0:T(8,128)(2,1)S(1)}, u32[]{:S(2)}, u32[]{:S(2)}) collective-permute-start(bf16[36,896]{1,0:T(8,128)(2,1)S(1)} %get-tuple-element.63), channel_id=1, source_target_pairs={{0,16},{2,18},{4,20},{6,22},{8,24},{10,26},{12,28},{14,30},{16,0},... | collective-permute-start | bytes 193544 | tf_op jit(solution)/shard_map/ppermute | solution.py:510
  42.3 6.1 %collective-permute-start.5 = (bf16[36,896]{1,0:T(8,128)(2,1)S(1)}, bf16[36,896]{1,0:T(8,128)(2,1)S(1)}, u32[]{:S(2)}, u32[]{:S(2)}) collective-permute-start(bf16[36,896]{1,0:T(8,128)(2,1)S(1)} %get-tuple-element.64), channel_id=1, source_target_pairs={{0,24},{2,26},{4,28},{6,30},{8,16},{10,18},{12,20},{14,22},{16,8},... | collective-permute-start | bytes 193544 | tf_op jit(solution)/shard_map/ppermute | solution.py:510
  48.5 5.9 %collective-permute-start.6 = (bf16[36,896]{1,0:T(8,128)(2,1)S(1)}, bf16[36,896]{1,0:T(8,128)(2,1)S(1)}, u32[]{:S(2)}, u32[]{:S(2)}) collective-permute-start(bf16[36,896]{1,0:T(8,128)(2,1)S(1)} %add_convert_fusion.1.refs_0_), channel_id=1, source_target_pairs={{0,8},{2,10},{4,12},{6,14},{8,0},{10,2},{12,4},{14,6},{16,24},{18,... | collective-permute-start | bytes 193544 | tf_op jit(solution)/shard_map/ppermute | solution.py:510
  48.6 5.9 %collective-permute-start.7 = (bf16[36,896]{1,0:T(8,128)(2,1)S(1)}, bf16[36,896]{1,0:T(8,128)(2,1)S(1)}, u32[]{:S(2)}, u32[]{:S(2)}) collective-permute-start(bf16[36,896]{1,0:T(8,128)(2,1)S(1)} %add_convert_fusion.1.refs_0_), channel_id=1, source_target_pairs={{0,16},{2,18},{4,20},{6,22},{8,24},{10,26},{12,28},{14,30},{16,0},... | collective-permute-start | bytes 193544 | tf_op jit(solution)/shard_map/ppermute | solution.py:510
  50.6 6.2 %collective-permute-start.8 = (bf16[36,896]{1,0:T(8,128)(2,1)S(1)}, bf16[36,896]{1,0:T(8,128)(2,1)S(1)}, u32[]{:S(2)}, u32[]{:S(2)}) collective-permute-start(bf16[36,896]{1,0:T(8,128)(2,1)S(1)} %add_convert_fusion.1.refs_0_), channel_id=1, source_target_pairs={{0,24},{2,26},{4,28},{6,30},{8,16},{10,18},{12,20},{14,22},{16,8},... | collective-permute-start | bytes 193544 | tf_op jit(solution)/shard_map/ppermute | solution.py:510
  56.9 7.5 %collective-permute-start.9 = (bf16[144,896]{1,0:T(8,128)(2,1)S(1)}, bf16[144,896]{1,0:T(8,128)(2,1)S(1)}, u32[]{:S(2)}, u32[]{:S(2)}) collective-permute-start(bf16[144,896]{1,0:T(8,128)(2,1)S(1)} %stack_part.1.refs_0_), channel_id=1, source_target_pairs={{0,2},{2,0},{4,6},{6,4},{8,10},{10,8},{12,14},{14,12},{16,18},{18,... | collective-permute-start | bytes 774152 | tf_op jit(solution)/shard_map/ppermute | solution.py:510
  58.3 10.3 %collective-permute-start.10 = (bf16[144,896]{1,0:T(8,128)(2,1)S(1)}, bf16[144,896]{1,0:T(8,128)(2,1)S(1)}, u32[]{:S(2)}, u32[]{:S(2)}) collective-permute-start(bf16[144,896]{1,0:T(8,128)(2,1)S(1)} %stack_part.1.refs_0_), channel_id=1, source_target_pairs={{0,4},{2,6},{4,0},{6,2},{8,12},{10,14},{12,8},{14,10},{16,20},{18,... | collective-permute-start | bytes 774152 | tf_op jit(solution)/shard_map/ppermute | solution.py:510
  58.8 9.8 %collective-permute-start.11 = (bf16[144,896]{1,0:T(8,128)(2,1)S(1)}, bf16[144,896]{1,0:T(8,128)(2,1)S(1)}, u32[]{:S(2)}, u32[]{:S(2)}) collective-permute-start(bf16[144,896]{1,0:T(8,128)(2,1)S(1)} %stack_part.1.refs_0_), channel_id=1, source_target_pairs={{0,6},{2,4},{4,2},{6,0},{8,14},{10,12},{12,10},{14,8},{16,22},{18,... | collective-permute-start | bytes 774152 | tf_op jit(solution)/shard_map/ppermute | solution.py:510
  60.5 12.6 %collective-permute-start.12 = (bf16[144,896]{1,0:T(8,128)(2,1)S(1)}, bf16[144,896]{1,0:T(8,128)(2,1)S(1)}, u32[]{:S(2)}, u32[]{:S(2)}) collective-permute-start(bf16[144,896]{1,0:T(8,128)(2,1)S(1)} %stack_part.1.refs_0_), channel_id=1, source_target_pairs={{0,1},{1,0},{2,3},{3,2},{4,5},{5,4},{6,7},{7,6},{8,9},{9,8},{10,11... | collective-permute-start | bytes 774152 | tf_op jit(solution)/shard_map/ppermute | solution.py:510
  64.4 8.7 %collective-permute-start.13 = (bf16[144,896]{1,0:T(8,128)(2,1)S(1)}, bf16[144,896]{1,0:T(8,128)(2,1)S(1)}, u32[]{:S(2)}, u32[]{:S(2)}) collective-permute-start(bf16[144,896]{1,0:T(8,128)(2,1)S(1)} %collective-permute-done.9.refs_1_), channel_id=1, source_target_pairs={{0,1},{1,0},{2,3},{3,2},{4,5},{5,4},{6,7},{7,6},{8,9},{9,8},{10,11... | collective-permute-start | bytes 774152 | tf_op jit(solution)/shard_map/ppermute | solution.py:510
  68.6 4.5 %collective-permute-start.14 = (bf16[144,896]{1,0:T(8,128)(2,1)S(1)}, bf16[144,896]{1,0:T(8,128)(2,1)S(1)}, u32[]{:S(2)}, u32[]{:S(2)}) collective-permute-start(bf16[144,896]{1,0:T(8,128)(2,1)S(1)} %collective-permute-done.10.refs_2_), channel_id=1, source_target_pairs={{0,1},{1,0},{2,3},{3,2},{4,5},{5,4},{6,7},{7,6},{8,9},{9,8},{10,11... | collective-permute-start | bytes 774152 | tf_op jit(solution)/shard_map/ppermute | solution.py:510
  68.6 4.5 %collective-permute-start.15 = (bf16[144,896]{1,0:T(8,128)(2,1)S(1)}, bf16[144,896]{1,0:T(8,128)(2,1)S(1)}, u32[]{:S(2)}, u32[]{:S(2)}) collective-permute-start(bf16[144,896]{1,0:T(8,128)(2,1)S(1)} %collective-permute-done.11.refs_3_), channel_id=1, source_target_pairs={{0,1},{1,0},{2,3},{3,2},{4,5},{5,4},{6,7},{7,6},{8,9},{9,8},{10,11... | collective-permute-start | bytes 774152 | tf_op jit(solution)/shard_map/ppermute | solution.py:510
  69.4 21.4 %all-to-all-start.1 = ((bf16[16,36,128]{2,1,0:T(8,128)(2,1)}), bf16[16,36,128]{2,1,0:T(8,128)(2,1)S(1)}, u32[]{:S(2)}, u32[]{:S(2)}) async-start(bf16[16,36,128]{2,1,0:T(8,128)(2,1)} %merge_part.1), calls=%async_computation.1 | async-start | bytes 327680 | tf_op jit(solution)/shard_map/all_to_all | solution.py:549
  89.5 1.3 %collective-permute-start.16 = (f32[16,288]{1,0:T(8,128)S(1)}, f32[16,288]{1,0:T(8,128)S(1)}, u32[]{:S(2)}, u32[]{:S(2)}) collective-permute-start(f32[16,288]{1,0:T(8,128)S(1)} %score_part.1), channel_id=1, source_target_pairs={{0,1},{1,0},{2,3},{3,2},{4,5},{5,4},{6,7},{7,6},{8,9},{9,8},{10,11... | collective-permute-start | bytes 55304 | tf_op jit(solution)/shard_map/ppermute | solution.py:510
  90.7 18.8 %copy-start.1 = (bf16[36,3584]{1,0:T(8,128)(2,1)S(1)}, bf16[36,3584]{1,0:T(8,128)(2,1)}, u32[]{:S(2)}) copy-start(bf16[36,3584]{1,0:T(8,128)(2,1)} %param.27) | copy-start | bytes 774148
  90.7 18.8 %copy-start.3 = (f32[3584]{0:T(1024)S(1)}, f32[3584]{0:T(1024)}, u32[]{:S(2)}) copy-start(f32[3584]{0:T(1024)} %param.26) | copy-start | bytes 43012
  90.8 9.5 %collective-permute-start.17 = (f32[16,288]{1,0:T(8,128)S(1)}, f32[16,288]{1,0:T(8,128)S(1)}, u32[]{:S(2)}, u32[]{:S(2)}) collective-permute-start(f32[16,288]{1,0:T(8,128)S(1)} %add.111), channel_id=1, source_target_pairs={{0,2},{2,0},{4,6},{6,4},{8,10},{10,8},{12,14},{14,12},{16,18},{18,... | collective-permute-start | bytes 55304 | tf_op jit(solution)/shard_map/ppermute | solution.py:510
  92.5 7.8 %collective-permute-start.18 = (f32[16,288]{1,0:T(8,128)S(1)}, f32[16,288]{1,0:T(8,128)S(1)}, u32[]{:S(2)}, u32[]{:S(2)}) collective-permute-start(f32[16,288]{1,0:T(8,128)S(1)} %add.111), channel_id=1, source_target_pairs={{0,4},{2,6},{4,0},{6,2},{8,12},{10,14},{12,8},{14,10},{16,20},{18,... | collective-permute-start | bytes 55304 | tf_op jit(solution)/shard_map/ppermute | solution.py:510
  93.9 6.4 %collective-permute-start.19 = (f32[16,288]{1,0:T(8,128)S(1)}, f32[16,288]{1,0:T(8,128)S(1)}, u32[]{:S(2)}, u32[]{:S(2)}) collective-permute-start(f32[16,288]{1,0:T(8,128)S(1)} %add.111), channel_id=1, source_target_pairs={{0,6},{2,4},{4,2},{6,0},{8,14},{10,12},{12,10},{14,8},{16,22},{18,... | collective-permute-start | bytes 55304 | tf_op jit(solution)/shard_map/ppermute | solution.py:510
  100.3 4.8 %collective-permute-start.21 = (f32[16,288]{1,0:T(8,128)S(1)}, f32[16,288]{1,0:T(8,128)S(1)}, u32[]{:S(2)}, u32[]{:S(2)}) collective-permute-start(f32[16,288]{1,0:T(8,128)S(1)} %add_add_fusion.1), channel_id=1, source_target_pairs={{0,16},{2,18},{4,20},{6,22},{8,24},{10,26},{12,28},{14,30},{16,0},... | collective-permute-start | bytes 55304 | tf_op jit(solution)/shard_map/ppermute | solution.py:510
  103.0 5.6 %collective-permute-start.22 = (f32[16,288]{1,0:T(8,128)S(1)}, f32[16,288]{1,0:T(8,128)S(1)}, u32[]{:S(2)}, u32[]{:S(2)}) collective-permute-start(f32[16,288]{1,0:T(8,128)S(1)} %add_add_fusion.1), channel_id=1, source_target_pairs={{0,24},{2,26},{4,28},{6,30},{8,16},{10,18},{12,20},{14,22},{16,8},... | collective-permute-start | bytes 55304 | tf_op jit(solution)/shard_map/ppermute | solution.py:510
  104.4 4.2 %collective-permute-start.20 = (f32[16,288]{1,0:T(8,128)S(1)}, f32[16,288]{1,0:T(8,128)S(1)}, u32[]{:S(2)}, u32[]{:S(2)}) collective-permute-start(f32[16,288]{1,0:T(8,128)S(1)} %add_add_fusion.1), channel_id=1, source_target_pairs={{0,8},{2,10},{4,12},{6,14},{8,0},{10,2},{12,4},{14,6},{16,24},{18,... | collective-permute-start | bytes 55304 | tf_op jit(solution)/shard_map/ppermute | solution.py:510
  104.4 4.9 %collective-permute-start.23 = (f32[36,3584]{1,0:T(8,128)S(1)}, f32[36,3584]{1,0:T(8,128)S(1)}, u32[]{:S(2)}, u32[]{:S(2)}) collective-permute-start(f32[36,3584]{1,0:T(8,128)S(1)} %project_part.1), channel_id=1, source_target_pairs={{0,1},{1,0},{2,3},{3,2},{4,5},{5,4},{6,7},{7,6},{8,9},{9,8},{10,11... | collective-permute-start | bytes 1548296 | tf_op jit(solution)/shard_map/ppermute | solution.py:510

commit v9 on v5

--- a/solution.py
+++ b/solution.py
@@ -10,6 +10,7 @@
 HEAD_SIZE = 256
 LANES = 128
 MIB = 1 << 20
+LOG2_E = 1.4426950408889634
 
 EXTRA = 16
 HIGH, LOW, GROUP = 0, 4, 8
@@ -177,31 +178,27 @@
     )(meta, pin(tree_q), pin(tree_key_value), reach)
 
 
-def merge_kernel(got_ref, numer_ref, denom_ref, out_ref, hold):
+def merge_kernel(got_ref, numer_ref, denom_ref, out_ref, hold, sums, lines):
     blocks = got_ref.shape[0]
     groups, tree_size, width = numer_ref.shape
     row_id = lax.broadcasted_iota(jnp.int32, (tree_size, width), 0)
     lane_id = lax.broadcasted_iota(jnp.int32, (tree_size, width), 1)
-    lines = -(-tree_size // width)
-
-    @pl.loop(0, groups)
-    def _(g):
-        def add(b, carry):
-            numer, extra = carry
-            more = got_ref[b, tree_size:, :].astype(jnp.float32)
-            same = more[GROUP : GROUP + 1, :] == g.astype(jnp.float32)
-            numer = numer + jnp.where(same, got_ref[b, :tree_size, :].astype(jnp.float32), 0.0)
-            extra = extra + jnp.where(same, more, 0.0)
-            return numer, extra
-
-        start = (numer_ref[g], jnp.zeros((EXTRA, width), jnp.float32))
-        numer, extra = lax.fori_loop(0, blocks, add, start, unroll=True)
+    sums[...] = numer_ref[...]
+    lines[...] = jnp.zeros_like(lines)
+    owners = []
+    for b in range(blocks):
+        extra = got_ref[b, tree_size:, :].astype(jnp.float32)
+        owners.append(jnp.max(extra[GROUP : GROUP + 1, :]).astype(jnp.int32))
+    for b in range(blocks):
+        sums[owners[b]] += got_ref[b, :tree_size, :].astype(jnp.float32)
+        lines[owners[b]] += got_ref[b, tree_size:, :].astype(jnp.float32)
+    for g in range(groups):
         denom = denom_ref[g]
-        for c in range(lines):
-            line = extra[HIGH + c : HIGH + c + 1, :] + extra[LOW + c : LOW + c + 1, :]
+        for c in range(-(-tree_size // width)):
+            line = lines[g, HIGH + c : HIGH + c + 1, :] + lines[g, LOW + c : LOW + c + 1, :]
             spread = jnp.where(row_id == lane_id + c * width, line, 0.0)
             denom = denom + jnp.sum(spread, axis=1, keepdims=True)
-        hold[pl.ds(pl.multiple_of(g * tree_size, 8), tree_size), :] = numer / denom
+        hold[g * tree_size : (g + 1) * tree_size, :] = sums[g] / denom
 
     count = out_ref.shape[1]
     for d in range(out_ref.shape[0]):
@@ -215,7 +212,11 @@
     return pl.pallas_call(
         merge_kernel,
         out_shape=jax.ShapeDtypeStruct((blocks, tokens // blocks, width), jnp.bfloat16),
-        scratch_shapes=[pltpu.VMEM((tokens, width), jnp.float32)],
+        scratch_shapes=[
+            pltpu.VMEM((tokens, width), jnp.float32),
+            pltpu.VMEM((groups, tree_size, width), jnp.float32),
+            pltpu.VMEM((groups, EXTRA, width), jnp.float32),
+        ],
         compiler_params=limit(16),
         name="merge_part",
     )(got, numer, denom)
@@ -298,7 +299,7 @@
             sums, found = total[r : r + band], picked[r : r + band]
             for c in range(span // LANES):
                 part = jnp.tanh(raw[r : r + band, c * LANES : (c + 1) * LANES] * (1.0 / 30.0))
-                sums = sums + jnp.exp(30.0 * part)
+                sums = sums + jnp.exp2(part * (30.0 * LOG2_E))
                 there = jnp.take_along_axis(part, lane, axis=1, mode="promise_in_bounds")
                 found = found + jnp.where(chunk == c, there, 0.0)
             if keep is not None:
@@ -328,7 +329,7 @@
 def score_part(places, pieces, embedding, ids, picks):
     rows = ids.shape[0]
     vocab, depth = embedding.shape
-    span, streams = HEAD_SIZE, 2
+    span, streams = min(512, vocab), 1
     lines = -(-(picks + 1) // 8) * 8
     fixed = lambda i, places: (0, 0)
     return pl.pallas_call(
@@ -475,14 +476,16 @@
     return lax.ppermute(value, axis, [(i, i ^ bits) for i in range(size)])
 
 
-def group_sum(value, axis, size, stride, count):
+def group_sum(value, axis, size, stride, count, beside=None):
     values = [value] + [partner(value, axis, size, k * stride) for k in range(1, count)]
+    if beside is not None:
+        values, _ = lax.optimization_barrier((values, beside))
     while len(values) > 1:
         values = [values[i] + values[i + 1] for i in range(0, len(values), 2)]
     return values[0]
 
 
-def both_by_stages(hidden, parts, parents, units, blocks, blk, mp, prompt, merge):
+def both_by_stages(hidden, parts, parents, units, blocks, blk, mp, prompt, merge, project):
     rows, model = hidden.shape
     half = units // 2
     layers = blocks // 4
@@ -504,15 +507,18 @@
     own = (base.astype(jnp.float32) + jax.nn.silu(inner)).astype(jnp.bfloat16)
     own, heads_out = lax.optimization_barrier((own, heads_out))
     chunks = [own] + [partner(own, "blk", blocks, 4 * k) for k in range(1, layers)]
+    chunks, heads_out = lax.optimization_barrier((chunks, spread(heads_out)))
     quad = stack_part(chunks, place)
-    pieces = [quad] + [partner(quad, "blk", blocks, k) for k in range(1, 4)]
+    pieces = [partner(quad, "blk", blocks, k) for k in range(1, 4)]
+    pieces, attn = lax.optimization_barrier((pieces, project(heads_out)))
+    pieces = [quad] + pieces
     pieces = pieces + [partner(piece, "mp", 2, 1) for piece in pieces]
     places = []
     for side in (mp, 1 - mp):
         for k in range(4):
             which = (blk & 3) ^ k
             places += [which >> 1, side * 2 + (which & 1)]
-    return pieces, jnp.stack(places), heads_out
+    return pieces, jnp.stack(places), attn
 
 
 def spread(value):
@@ -578,18 +584,19 @@
         numer, denom = tree_part(tree_q, tree_key_value, reach, blk * width, width)
         return merge_part(partials, numer, denom)
 
+    def project(heads_out):
+        return project_part(heads_out, out_weight)
+
     if splits == 2 and blocks % 4 == 0 and units % 256 == 0 and drafts == 2:
         parts = draft_part(hidden, medusa_w, blk)
         parts, meta = lax.optimization_barrier((parts, meta))
-        pieces, places, heads_out = both_by_stages(
-            hidden, parts, parents, units, blocks, blk, mp, prompt, merge
+        pieces, places, attn = both_by_stages(
+            hidden, parts, parents, units, blocks, blk, mp, prompt, merge, project
         )
     else:
         pieces = fresh_by_collectives(hidden, medusa_w, blocks, blk, mp)
         places = jnp.zeros((2,), jnp.int32)
-        heads_out = merge(spread(prompt()), parents)
-    heads_out = spread(heads_out)
-    attn = project_part(heads_out, out_weight)
+        attn = project(spread(merge(spread(prompt()), parents)))
     attn, pieces = lax.optimization_barrier((attn, pieces))
     attn = group_sum(attn, "mp", splits, 1, splits)
     normed = attn * lax.rsqrt(jnp.mean(attn * attn, -1, keepdims=True) + 1e-06) * post_gain
@@ -601,7 +608,7 @@
     ids = jnp.pad(ids, ((0, 0), (0, LANES - picks)), constant_values=-1)
     score = score_part(places, pieces, embedding, ids, picks)
     score = group_sum(score, "mp", splits, 1, splits)
-    score = group_sum(score, "blk", blocks, 1, 4)
+    score = group_sum(score, "blk", blocks, 1, 4, layer_out)
     score = group_sum(score, "blk", blocks, 4, blocks // 4)
     draft_logprob = score[:picks] - jnp.log(score[picks : picks + 1])
     draft_logprob = draft_logprob.T.reshape(drafts, rows, picks)

time: 104 us -> 113 us (1.087)
  waiting for transfers between devices: 21.1 us -> 30.9 us
  Pallas kernels: 37.4 us -> 36 us
    ppermute x24, waiting for transfers between devices: 15.4 us -> 30.9 us  [partner(): return lax.ppermute(value, axis, [(i, i ^ bits) for i in range(size)])]
    all_to_all x2, waiting for transfers between devices: 5.67 us -> 0.01 us  [spread(): return lax.all_to_all(value, 'blk', 0, 0, tiled=True)]
  transfers between devices with their start and end apart: 26 -> 26, of which waited for: 14 -> 18; matrix products, arithmetic and copies ran while one was open for 3% -> 3% of each run, Pallas kernels for 17% -> 23%
where the time goes in v9:
time: 113 us; the launch traced here: 112 us
  starting transfers between devices  37.8 us (33%)
  Pallas kernels  36 us (32%)
  waiting for transfers between devices  30.9 us (27%)
  between operations  2.79 us (2%)
  other arithmetic  2.27 us (2%)
  matrix products  1.55 us (1%)
    ppermute x24, waiting for transfers between devices, partner(): return lax.ppermute(value, axis, [(i, i ^ bits) for i in range(size)])  30.9 us
    ppermute x24, starting transfers between devices, partner(): return lax.ppermute(value, axis, [(i, i ^ bits) for i in range(size)])  25 us
    pallas_call x1, Pallas kernels, score_part(): pl.pallas_call(functools.partial(score_kernel, picks, streams), out_shape...  16.3 us
    all_to_all x2, starting transfers between devices, spread(): return lax.all_to_all(value, 'blk', 0, 0, tiled=True)  12.7 us
    pallas_call x1, Pallas kernels, prompt_part(): pl.pallas_call(prompt_kernel, out_shape=jax.ShapeDtypeStruct((blocks, tre...  7.01 us
    pallas_call x1, Pallas kernels, project_part(): pl.pallas_call(project_kernel, out_shape=jax.ShapeDtypeStruct((tokens, mo...  5.95 us
    pallas_call x1, Pallas kernels, draft_part(): pl.pallas_call(draft_kernel, out_shape=[jax.ShapeDtypeStruct((rows, half)...  3.08 us
    pallas_call x1, Pallas kernels, tree_part(): pl.pallas_call(tree_kernel, out_shape=[jax.ShapeDtypeStruct((groups, tree...  2.26 us
  transfers between devices with their start and end apart: 26, of which 18 were waited for; matrix products, arithmetic and copies ran while one was open for 3% of the time, Pallas kernels for 23%

profile of v9, /device:TPU:0, one launch (start us, length us, event | category | flops | bytes accessed | tf_op | source)
XLA Modules:
  0.0 112.3 jit_solution(7982976052982967661)
XLA Ops:
  2.8 3.1 %draft_part.1 = (f32[144,896]{1,0:T(8,128)S(1)}, bf16[144,896]{1,0:T(8,128)(2,1)S(1)}, bf16[144,896]{1,0:T(8,128)(2,1)S(1)}, bf16[144,896]{1,0:T(8,128)(2,1)S(1)}) custom-call(s32[6]{0:T(128)S(1)} %stack.95.meta, bf16[144,3584]{1,0:T(8,128)(2,1)} %hidden_hbm.1, bf16[2,224,1792]{2,1,0:T(8,128)(2,1)} %weight_hbm.2), custom_call_target="tpu_custom_call" | custom-call | tf_op jit(solution)/shard_map/draft_part/pallas_call | solution.py:401
  5.8 7.0 %prompt_part.1 = bf16[16,64,128]{2,1,0:T(8,128)(2,1)} custom-call(s32[3]{0:T(128)S(1)} %pad_add_fusion.meta, bf16[12,48,2048]{2,1,0:T(8,128)(2,1)} %q_hbm.3, bf16[2,1,2048,1024]{3,2,1,0:T(8,128)(2,1)} %kv_hbm.2), custom_call_target="tpu_custom_call" | custom-call | flops 805306368 | bytes 8388608 | tf_op jit(solution)/shard_map/prompt_part/pallas_call | solution.py:115
  12.9 8.3 %all-to-all-start = ((bf16[16,64,128]{2,1,0:T(8,128)(2,1)}), bf16[16,64,128]{2,1,0:T(8,128)(2,1)S(1)}, u32[]{:S(2)}, u32[]{:S(2)}) async-start(bf16[16,64,128]{2,1,0:T(8,128)(2,1)} %prompt_part.1), calls=%async_computation | async-start | bytes 524288 | tf_op jit(solution)/shard_map/all_to_all | solution.py:525
  21.2 1.9 %collective-permute-start = (bf16[144,896]{1,0:T(8,128)(2,1)S(1)}, bf16[144,896]{1,0:T(8,128)(2,1)S(1)}, u32[]{:S(2)}, u32[]{:S(2)}) collective-permute-start(bf16[144,896]{1,0:T(8,128)(2,1)S(1)} %get-tuple-element.58), channel_id=1, source_target_pairs={{0,2},{2,0},{4,6},{6,4},{8,10},{10,8},{12,14},{14,12},{16,18},{18,... | collective-permute-start | bytes 774152 | tf_op jit(solution)/shard_map/ppermute | solution.py:476
  23.1 1.5 %collective-permute-start.1 = (bf16[144,896]{1,0:T(8,128)(2,1)S(1)}, bf16[144,896]{1,0:T(8,128)(2,1)S(1)}, u32[]{:S(2)}, u32[]{:S(2)}) collective-permute-start(bf16[144,896]{1,0:T(8,128)(2,1)S(1)} %get-tuple-element.59), channel_id=1, source_target_pairs={{0,4},{2,6},{4,0},{6,2},{8,12},{10,14},{12,8},{14,10},{16,20},{18,... | collective-permute-start | bytes 774152 | tf_op jit(solution)/shard_map/ppermute | solution.py:476
  24.8 8.3 %collective-permute-done.refs_0_ = bf16[144,896]{1,0:T(8,128)(2,1)S(1)} collective-permute-done((bf16[144,896]{1,0:T(8,128)(2,1)S(1)}, bf16[144,896]{1,0:T(8,128)(2,1)S(1)}, u32[]{:S(2)}, u32[]{:S(2)}) %collective-permute-start) | collective-permute-done | bytes 258080 | tf_op jit(solution)/shard_map/ppermute | solution.py:476
  33.2 3.5 %collective-permute-done.1.refs_1_ = bf16[144,896]{1,0:T(8,128)(2,1)S(1)} collective-permute-done((bf16[144,896]{1,0:T(8,128)(2,1)S(1)}, bf16[144,896]{1,0:T(8,128)(2,1)S(1)}, u32[]{:S(2)}, u32[]{:S(2)}) %collective-permute-start.1) | collective-permute-done | bytes 258080 | tf_op jit(solution)/shard_map/ppermute | solution.py:476
  36.7 1.5 %collective-permute-done.2.refs_2_ = bf16[144,896]{1,0:T(8,128)(2,1)S(1)} collective-permute-done((bf16[144,896]{1,0:T(8,128)(2,1)S(1)}, bf16[144,896]{1,0:T(8,128)(2,1)S(1)}, u32[]{:S(2)}, u32[]{:S(2)}) %collective-permute-start.2) | collective-permute-done | bytes 258080 | tf_op jit(solution)/shard_map/ppermute | solution.py:476
  38.2 0.2 fold_part.1
  38.4 1.5 %collective-permute-start.3 = (bf16[36,896]{1,0:T(8,128)(2,1)S(1)}, bf16[36,896]{1,0:T(8,128)(2,1)S(1)}, u32[]{:S(2)}, u32[]{:S(2)}) collective-permute-start(bf16[36,896]{1,0:T(8,128)(2,1)S(1)} %get-tuple-element.70), channel_id=1, source_target_pairs={{0,8},{2,10},{4,12},{6,14},{8,0},{10,2},{12,4},{14,6},{16,24},{18,... | collective-permute-start | bytes 193544 | tf_op jit(solution)/shard_map/ppermute | solution.py:476
  40.0 2.4 %collective-permute-start.4 = (bf16[36,896]{1,0:T(8,128)(2,1)S(1)}, bf16[36,896]{1,0:T(8,128)(2,1)S(1)}, u32[]{:S(2)}, u32[]{:S(2)}) collective-permute-start(bf16[36,896]{1,0:T(8,128)(2,1)S(1)} %get-tuple-element.71), channel_id=1, source_target_pairs={{0,16},{2,18},{4,20},{6,22},{8,24},{10,26},{12,28},{14,30},{16,0},... | collective-permute-start | bytes 193544 | tf_op jit(solution)/shard_map/ppermute | solution.py:476
  42.3 0.6 collective-permute-start.5
  42.9 0.7 fusion.1
  43.6 0.4 fusion.3
  44.0 0.4 fusion.6.reach_ref
  44.5 2.3 %tree_part.1 = (f32[12,48,128]{2,1,0:T(8,128)S(1)}, f32[12,48,128]{2,1,0:T(8,128)S(1)}) custom-call(s32[3]{0:T(128)S(1)} %pad_add_fusion.1.meta, bf16[12,48,2048]{2,1,0:T(8,128)(2,1)} %q_hbm.3, bf16[2,12,48,1024]{3,2,1,0:T(8,128)(2,1)} %kv_hbm.3, f32[12,48,48]{2,1,0:T(8,128)S(1)} %fusion.6.reach_ref), custom_call_target="tpu_custom_call" | custom-call | tf_op jit(solution)/shard_map/tree_part/pallas_call | solution.py:167
  46.8 1.1 merge_part.1
  47.8 0.6 collective-permute-done.5
  48.5 1.0 add_convert_fusion.1.refs_0_
  49.5 4.4 %all-to-all-start.1 = ((bf16[16,36,128]{2,1,0:T(8,128)(2,1)}), bf16[16,36,128]{2,1,0:T(8,128)(2,1)S(1)}, u32[]{:S(2)}, u32[]{:S(2)}) async-start(bf16[16,36,128]{2,1,0:T(8,128)(2,1)} %merge_part.1), calls=%async_computation.1 | async-start | bytes 327680 | tf_op jit(solution)/shard_map/all_to_all | solution.py:525
  53.9 3.8 %collective-permute-start.8 = (bf16[36,896]{1,0:T(8,128)(2,1)S(1)}, bf16[36,896]{1,0:T(8,128)(2,1)S(1)}, u32[]{:S(2)}, u32[]{:S(2)}) collective-permute-start(bf16[36,896]{1,0:T(8,128)(2,1)S(1)} %add_convert_fusion.1.refs_0_), channel_id=1, source_target_pairs={{0,24},{2,26},{4,28},{6,30},{8,16},{10,18},{12,20},{14,22},{16,8},... | collective-permute-start | bytes 193544 | tf_op jit(solution)/shard_map/ppermute | solution.py:476
  57.6 0.7 collective-permute-start.6
  58.3 4.1 %collective-permute-done.8.refs_3_ = bf16[36,896]{1,0:T(8,128)(2,1)S(1)} collective-permute-done((bf16[36,896]{1,0:T(8,128)(2,1)S(1)}, bf16[36,896]{1,0:T(8,128)(2,1)S(1)}, u32[]{:S(2)}, u32[]{:S(2)}) %collective-permute-start.8) | collective-permute-done | bytes 64544 | tf_op jit(solution)/shard_map/ppermute | solution.py:476
  62.4 3.0 %collective-permute-done.7.refs_2_ = bf16[36,896]{1,0:T(8,128)(2,1)S(1)} collective-permute-done((bf16[36,896]{1,0:T(8,128)(2,1)S(1)}, bf16[36,896]{1,0:T(8,128)(2,1)S(1)}, u32[]{:S(2)}, u32[]{:S(2)}) %collective-permute-start.7) | collective-permute-done | bytes 64544 | tf_op jit(solution)/shard_map/ppermute | solution.py:476
  65.5 2.4 %collective-permute-start.11 = (bf16[144,896]{1,0:T(8,128)(2,1)S(1)}, bf16[144,896]{1,0:T(8,128)(2,1)S(1)}, u32[]{:S(2)}, u32[]{:S(2)}) collective-permute-start(bf16[144,896]{1,0:T(8,128)(2,1)S(1)} %stack_part.1.refs_0_), channel_id=1, source_target_pairs={{0,6},{2,4},{4,2},{6,0},{8,14},{10,12},{12,10},{14,8},{16,22},{18,... | collective-permute-start | bytes 774152 | tf_op jit(solution)/shard_map/ppermute | solution.py:476
  67.9 0.6 collective-permute-start.10
  68.5 0.6 collective-permute-start.9
  69.1 5.9 %project_part.1 = f32[36,3584]{1,0:T(8,128)S(1)} custom-call(bf16[16,36,128]{2,1,0:T(8,128)(2,1)S(1)} %all-to-all-done.1.heads_ref, bf16[2048,3584]{1,0:T(8,128)(2,1)} %weight_hbm.3), custom_call_target="tpu_custom_call" | custom-call | flops 528482304 | bytes 14680064 | tf_op jit(solution)/shard_map/project_part/pallas_call | solution.py:253
  75.0 0.6 collective-permute-done.11.refs_3_
  75.6 2.8 %collective-permute-done.10.refs_2_ = bf16[144,896]{1,0:T(8,128)(2,1)S(1)} collective-permute-done((bf16[144,896]{1,0:T(8,128)(2,1)S(1)}, bf16[144,896]{1,0:T(8,128)(2,1)S(1)}, u32[]{:S(2)}, u32[]{:S(2)}) %collective-permute-start.10) | collective-permute-done | bytes 258080 | tf_op jit(solution)/shard_map/ppermute | solution.py:476
  78.5 0.3 collective-permute-done.9.refs_1_
  78.8 0.5 collective-permute-start.14
  79.6 0.7 collective-permute-done.13.refs_5_
  80.3 0.4 collective-permute-done.14.refs_6_
  80.7 0.4 collective-permute-done.15.refs_7_
  81.2 16.3 %score_part.1 = f32[16,288]{1,0:T(8,128)S(1)} custom-call(s32[16]{0:T(128)S(1)} %stack.88.places, s32[288,128]{1,0:T(8,128)S(1)} %pad.4.ids_ref, bf16[144,896]{1,0:T(8,128)(2,1)S(1)} %stack_part.1.refs_0_, bf16[144,896]{1,0:T(8,128)(2,1)S(1)} %collective-permute-done.9.refs_1_, bf16[144,896]{1,0:T(8,128)(2,1)S(1)} %collective-permute-done.10.refs_2_, ...), custom_call_target="tpu_custom_call" | custom-call | flops 8455716864 | bytes 29360128 | tf_op jit(solution)/shard_map/score_part/pallas_call | solution.py:335
  97.5 0.4 collective-permute-start.16
  98.0 0.8 collective-permute-done.16
  98.8 1.5 %collective-permute-start.19 = (f32[16,288]{1,0:T(8,128)S(1)}, f32[16,288]{1,0:T(8,128)S(1)}, u32[]{:S(2)}, u32[]{:S(2)}) collective-permute-start(f32[16,288]{1,0:T(8,128)S(1)} %add.129), channel_id=1, source_target_pairs={{0,6},{2,4},{4,2},{6,0},{8,14},{10,12},{12,10},{14,8},{16,22},{18,... | collective-permute-start | bytes 55304 | tf_op jit(solution)/shard_map/ppermute | solution.py:476
  100.3 1.2 %collective-permute-start.18 = (f32[16,288]{1,0:T(8,128)S(1)}, f32[16,288]{1,0:T(8,128)S(1)}, u32[]{:S(2)}, u32[]{:S(2)}) collective-permute-start(f32[16,288]{1,0:T(8,128)S(1)} %add.129), channel_id=1, source_target_pairs={{0,4},{2,6},{4,0},{6,2},{8,12},{10,14},{12,8},{14,10},{16,20},{18,... | collective-permute-start | bytes 55304 | tf_op jit(solution)/shard_map/ppermute | solution.py:476
  101.5 0.8 collective-permute-start.17
  102.5 0.9 add_convert_fusion
  103.5 0.6 collective-permute-done.18
  104.1 1.2 %collective-permute-done.17 = f32[16,288]{1,0:T(8,128)S(1)} collective-permute-done((f32[16,288]{1,0:T(8,128)S(1)}, f32[16,288]{1,0:T(8,128)S(1)}, u32[]{:S(2)}, u32[]{:S(2)}) %collective-permute-start.17) | collective-permute-done | bytes 18464 | tf_op jit(solution)/shard_map/ppermute | solution.py:476
  105.5 4.3 %collective-permute-start.21 = (f32[16,288]{1,0:T(8,128)S(1)}, f32[16,288]{1,0:T(8,128)S(1)}, u32[]{:S(2)}, u32[]{:S(2)}) collective-permute-start(f32[16,288]{1,0:T(8,128)S(1)} %add_add_fusion.1), channel_id=1, source_target_pairs={{0,8},{2,10},{4,12},{6,14},{8,0},{10,2},{12,4},{14,6},{16,24},{18,... | collective-permute-start | bytes 55304 | tf_op jit(solution)/shard_map/ppermute | solution.py:476
  109.7 1.2 %collective-permute-done.23 = f32[16,288]{1,0:T(8,128)S(1)} collective-permute-done((f32[16,288]{1,0:T(8,128)S(1)}, f32[16,288]{1,0:T(8,128)S(1)}, u32[]{:S(2)}, u32[]{:S(2)}) %collective-permute-start.23) | collective-permute-done | bytes 18464 | tf_op jit(solution)/shard_map/ppermute | solution.py:476
  111.0 0.6 collective-permute-done.21
  111.6 0.7 reshape.37
  (42 shorter events, 1.5 us)
Async XLA Ops:
  0.6 42.3 %copy-start.3 = (s32[12,48]{1,0:T(8,128)S(1)}, s32[12,48]{1,0:T(8,128)}, u32[]{:S(2)}) copy-start(s32[12,48]{1,0:T(8,128)} %param.24) | copy-start | bytes 6916
  12.9 33.9 %all-to-all-start = ((bf16[16,64,128]{2,1,0:T(8,128)(2,1)}), bf16[16,64,128]{2,1,0:T(8,128)(2,1)S(1)}, u32[]{:S(2)}, u32[]{:S(2)}) async-start(bf16[16,64,128]{2,1,0:T(8,128)(2,1)} %prompt_part.1), calls=%async_computation | async-start | bytes 524288 | tf_op jit(solution)/shard_map/all_to_all | solution.py:525
  21.2 12.0 %collective-permute-start = (bf16[144,896]{1,0:T(8,128)(2,1)S(1)}, bf16[144,896]{1,0:T(8,128)(2,1)S(1)}, u32[]{:S(2)}, u32[]{:S(2)}) collective-permute-start(bf16[144,896]{1,0:T(8,128)(2,1)S(1)} %get-tuple-element.58), channel_id=1, source_target_pairs={{0,2},{2,0},{4,6},{6,4},{8,10},{10,8},{12,14},{14,12},{16,18},{18,... | collective-permute-start | bytes 774152 | tf_op jit(solution)/shard_map/ppermute | solution.py:476
  23.1 13.6 %collective-permute-start.1 = (bf16[144,896]{1,0:T(8,128)(2,1)S(1)}, bf16[144,896]{1,0:T(8,128)(2,1)S(1)}, u32[]{:S(2)}, u32[]{:S(2)}) collective-permute-start(bf16[144,896]{1,0:T(8,128)(2,1)S(1)} %get-tuple-element.59), channel_id=1, source_target_pairs={{0,4},{2,6},{4,0},{6,2},{8,12},{10,14},{12,8},{14,10},{16,20},{18,... | collective-permute-start | bytes 774152 | tf_op jit(solution)/shard_map/ppermute | solution.py:476
  24.6 13.6 %collective-permute-start.2 = (bf16[144,896]{1,0:T(8,128)(2,1)S(1)}, bf16[144,896]{1,0:T(8,128)(2,1)S(1)}, u32[]{:S(2)}, u32[]{:S(2)}) collective-permute-start(bf16[144,896]{1,0:T(8,128)(2,1)S(1)} %get-tuple-element.60), channel_id=1, source_target_pairs={{0,6},{2,4},{4,2},{6,0},{8,14},{10,12},{12,10},{14,8},{16,22},{18,... | collective-permute-start | bytes 774152 | tf_op jit(solution)/shard_map/ppermute | solution.py:476
  38.4 9.4 %collective-permute-start.3 = (bf16[36,896]{1,0:T(8,128)(2,1)S(1)}, bf16[36,896]{1,0:T(8,128)(2,1)S(1)}, u32[]{:S(2)}, u32[]{:S(2)}) collective-permute-start(bf16[36,896]{1,0:T(8,128)(2,1)S(1)} %get-tuple-element.70), channel_id=1, source_target_pairs={{0,8},{2,10},{4,12},{6,14},{8,0},{10,2},{12,4},{14,6},{16,24},{18,... | collective-permute-start | bytes 193544 | tf_op jit(solution)/shard_map/ppermute | solution.py:476
  40.0 7.9 %collective-permute-start.4 = (bf16[36,896]{1,0:T(8,128)(2,1)S(1)}, bf16[36,896]{1,0:T(8,128)(2,1)S(1)}, u32[]{:S(2)}, u32[]{:S(2)}) collective-permute-start(bf16[36,896]{1,0:T(8,128)(2,1)S(1)} %get-tuple-element.71), channel_id=1, source_target_pairs={{0,16},{2,18},{4,20},{6,22},{8,24},{10,26},{12,28},{14,30},{16,0},... | collective-permute-start | bytes 193544 | tf_op jit(solution)/shard_map/ppermute | solution.py:476
  42.3 6.1 %collective-permute-start.5 = (bf16[36,896]{1,0:T(8,128)(2,1)S(1)}, bf16[36,896]{1,0:T(8,128)(2,1)S(1)}, u32[]{:S(2)}, u32[]{:S(2)}) collective-permute-start(bf16[36,896]{1,0:T(8,128)(2,1)S(1)} %get-tuple-element.72), channel_id=1, source_target_pairs={{0,24},{2,26},{4,28},{6,30},{8,16},{10,18},{12,20},{14,22},{16,8},... | collective-permute-start | bytes 193544 | tf_op jit(solution)/shard_map/ppermute | solution.py:476
  47.8 31.5 %copy-start.1 = (s32[2,144,10]{1,0,2:T(2,128)S(1)}, s32[2,144,10]{1,0,2:T(2,128)}, u32[]{:S(2)}) copy-start(s32[2,144,10]{1,0,2:T(2,128)} %param.17) | copy-start | bytes 34564
  49.5 15.9 %all-to-all-start.1 = ((bf16[16,36,128]{2,1,0:T(8,128)(2,1)}), bf16[16,36,128]{2,1,0:T(8,128)(2,1)S(1)}, u32[]{:S(2)}, u32[]{:S(2)}) async-start(bf16[16,36,128]{2,1,0:T(8,128)(2,1)} %merge_part.1), calls=%async_computation.1 | async-start | bytes 327680 | tf_op jit(solution)/shard_map/all_to_all | solution.py:525
  53.9 8.6 %collective-permute-start.8 = (bf16[36,896]{1,0:T(8,128)(2,1)S(1)}, bf16[36,896]{1,0:T(8,128)(2,1)S(1)}, u32[]{:S(2)}, u32[]{:S(2)}) collective-permute-start(bf16[36,896]{1,0:T(8,128)(2,1)S(1)} %add_convert_fusion.1.refs_0_), channel_id=1, source_target_pairs={{0,24},{2,26},{4,28},{6,30},{8,16},{10,18},{12,20},{14,22},{16,8},... | collective-permute-start | bytes 193544 | tf_op jit(solution)/shard_map/ppermute | solution.py:476
  57.6 7.8 %collective-permute-start.7 = (bf16[36,896]{1,0:T(8,128)(2,1)S(1)}, bf16[36,896]{1,0:T(8,128)(2,1)S(1)}, u32[]{:S(2)}, u32[]{:S(2)}) collective-permute-start(bf16[36,896]{1,0:T(8,128)(2,1)S(1)} %add_convert_fusion.1.refs_0_), channel_id=1, source_target_pairs={{0,16},{2,18},{4,20},{6,22},{8,24},{10,26},{12,28},{14,30},{16,0},... | collective-permute-start | bytes 193544 | tf_op jit(solution)/shard_map/ppermute | solution.py:476
  57.6 7.8 %collective-permute-start.6 = (bf16[36,896]{1,0:T(8,128)(2,1)S(1)}, bf16[36,896]{1,0:T(8,128)(2,1)S(1)}, u32[]{:S(2)}, u32[]{:S(2)}) collective-permute-start(bf16[36,896]{1,0:T(8,128)(2,1)S(1)} %add_convert_fusion.1.refs_0_), channel_id=1, source_target_pairs={{0,8},{2,10},{4,12},{6,14},{8,0},{10,2},{12,4},{14,6},{16,24},{18,... | collective-permute-start | bytes 193544 | tf_op jit(solution)/shard_map/ppermute | solution.py:476
  65.5 10.1 %collective-permute-start.11 = (bf16[144,896]{1,0:T(8,128)(2,1)S(1)}, bf16[144,896]{1,0:T(8,128)(2,1)S(1)}, u32[]{:S(2)}, u32[]{:S(2)}) collective-permute-start(bf16[144,896]{1,0:T(8,128)(2,1)S(1)} %stack_part.1.refs_0_), channel_id=1, source_target_pairs={{0,6},{2,4},{4,2},{6,0},{8,14},{10,12},{12,10},{14,8},{16,22},{18,... | collective-permute-start | bytes 774152 | tf_op jit(solution)/shard_map/ppermute | solution.py:476
  67.9 10.6 %collective-permute-start.10 = (bf16[144,896]{1,0:T(8,128)(2,1)S(1)}, bf16[144,896]{1,0:T(8,128)(2,1)S(1)}, u32[]{:S(2)}, u32[]{:S(2)}) collective-permute-start(bf16[144,896]{1,0:T(8,128)(2,1)S(1)} %stack_part.1.refs_0_), channel_id=1, source_target_pairs={{0,4},{2,6},{4,0},{6,2},{8,12},{10,14},{12,8},{14,10},{16,20},{18,... | collective-permute-start | bytes 774152 | tf_op jit(solution)/shard_map/ppermute | solution.py:476
  68.5 10.3 %collective-permute-start.9 = (bf16[144,896]{1,0:T(8,128)(2,1)S(1)}, bf16[144,896]{1,0:T(8,128)(2,1)S(1)}, u32[]{:S(2)}, u32[]{:S(2)}) collective-permute-start(bf16[144,896]{1,0:T(8,128)(2,1)S(1)} %stack_part.1.refs_0_), channel_id=1, source_target_pairs={{0,2},{2,0},{4,6},{6,4},{8,10},{10,8},{12,14},{14,12},{16,18},{18,... | collective-permute-start | bytes 774152 | tf_op jit(solution)/shard_map/ppermute | solution.py:476
  69.0 10.5 %collective-permute-start.12 = (bf16[144,896]{1,0:T(8,128)(2,1)S(1)}, bf16[144,896]{1,0:T(8,128)(2,1)S(1)}, u32[]{:S(2)}, u32[]{:S(2)}) collective-permute-start(bf16[144,896]{1,0:T(8,128)(2,1)S(1)} %stack_part.1.refs_0_), channel_id=1, source_target_pairs={{0,1},{1,0},{2,3},{3,2},{4,5},{5,4},{6,7},{7,6},{8,9},{9,8},{10,11... | collective-permute-start | bytes 774152 | tf_op jit(solution)/shard_map/ppermute | solution.py:476
  78.8 1.5 %collective-permute-start.13 = (bf16[144,896]{1,0:T(8,128)(2,1)S(1)}, bf16[144,896]{1,0:T(8,128)(2,1)S(1)}, u32[]{:S(2)}, u32[]{:S(2)}) collective-permute-start(bf16[144,896]{1,0:T(8,128)(2,1)S(1)} %collective-permute-done.9.refs_1_), channel_id=1, source_target_pairs={{0,1},{1,0},{2,3},{3,2},{4,5},{5,4},{6,7},{7,6},{8,9},{9,8},{10,11... | collective-permute-start | bytes 774152 | tf_op jit(solution)/shard_map/ppermute | solution.py:476
  78.8 1.9 %collective-permute-start.14 = (bf16[144,896]{1,0:T(8,128)(2,1)S(1)}, bf16[144,896]{1,0:T(8,128)(2,1)S(1)}, u32[]{:S(2)}, u32[]{:S(2)}) collective-permute-start(bf16[144,896]{1,0:T(8,128)(2,1)S(1)} %collective-permute-done.10.refs_2_), channel_id=1, source_target_pairs={{0,1},{1,0},{2,3},{3,2},{4,5},{5,4},{6,7},{7,6},{8,9},{9,8},{10,11... | collective-permute-start | bytes 774152 | tf_op jit(solution)/shard_map/ppermute | solution.py:476
  79.3 1.8 %collective-permute-start.15 = (bf16[144,896]{1,0:T(8,128)(2,1)S(1)}, bf16[144,896]{1,0:T(8,128)(2,1)S(1)}, u32[]{:S(2)}, u32[]{:S(2)}) collective-permute-start(bf16[144,896]{1,0:T(8,128)(2,1)S(1)} %collective-permute-done.11.refs_3_), channel_id=1, source_target_pairs={{0,1},{1,0},{2,3},{3,2},{4,5},{5,4},{6,7},{7,6},{8,9},{9,8},{10,11... | collective-permute-start | bytes 774152 | tf_op jit(solution)/shard_map/ppermute | solution.py:476
  79.5 23.0 %copy-start = (bf16[36,3584]{1,0:T(8,128)(2,1)S(1)}, bf16[36,3584]{1,0:T(8,128)(2,1)}, u32[]{:S(2)}) copy-start(bf16[36,3584]{1,0:T(8,128)(2,1)} %param.27) | copy-start | bytes 774148
  79.6 23.0 %copy-start.2 = (f32[3584]{0:T(1024)S(1)}, f32[3584]{0:T(1024)}, u32[]{:S(2)}) copy-start(f32[3584]{0:T(1024)} %param.26) | copy-start | bytes 43012
  81.0 21.3 %collective-permute-start.20 = (f32[36,3584]{1,0:T(8,128)S(1)}, f32[36,3584]{1,0:T(8,128)S(1)}, u32[]{:S(2)}, u32[]{:S(2)}) collective-permute-start(f32[36,3584]{1,0:T(8,128)S(1)} %project_part.1), channel_id=1, source_target_pairs={{0,1},{1,0},{2,3},{3,2},{4,5},{5,4},{6,7},{7,6},{8,9},{9,8},{10,11... | collective-permute-start | bytes 1548296 | tf_op jit(solution)/shard_map/ppermute | solution.py:476
  97.5 1.3 %collective-permute-start.16 = (f32[16,288]{1,0:T(8,128)S(1)}, f32[16,288]{1,0:T(8,128)S(1)}, u32[]{:S(2)}, u32[]{:S(2)}) collective-permute-start(f32[16,288]{1,0:T(8,128)S(1)} %score_part.1), channel_id=1, source_target_pairs={{0,1},{1,0},{2,3},{3,2},{4,5},{5,4},{6,7},{7,6},{8,9},{9,8},{10,11... | collective-permute-start | bytes 55304 | tf_op jit(solution)/shard_map/ppermute | solution.py:476
  98.8 4.7 %collective-permute-start.19 = (f32[16,288]{1,0:T(8,128)S(1)}, f32[16,288]{1,0:T(8,128)S(1)}, u32[]{:S(2)}, u32[]{:S(2)}) collective-permute-start(f32[16,288]{1,0:T(8,128)S(1)} %add.129), channel_id=1, source_target_pairs={{0,6},{2,4},{4,2},{6,0},{8,14},{10,12},{12,10},{14,8},{16,22},{18,... | collective-permute-start | bytes 55304 | tf_op jit(solution)/shard_map/ppermute | solution.py:476
  100.3 3.8 %collective-permute-start.18 = (f32[16,288]{1,0:T(8,128)S(1)}, f32[16,288]{1,0:T(8,128)S(1)}, u32[]{:S(2)}, u32[]{:S(2)}) collective-permute-start(f32[16,288]{1,0:T(8,128)S(1)} %add.129), channel_id=1, source_target_pairs={{0,4},{2,6},{4,0},{6,2},{8,12},{10,14},{12,8},{14,10},{16,20},{18,... | collective-permute-start | bytes 55304 | tf_op jit(solution)/shard_map/ppermute | solution.py:476
  101.5 3.8 %collective-permute-start.17 = (f32[16,288]{1,0:T(8,128)S(1)}, f32[16,288]{1,0:T(8,128)S(1)}, u32[]{:S(2)}, u32[]{:S(2)}) collective-permute-start(f32[16,288]{1,0:T(8,128)S(1)} %add.129), channel_id=1, source_target_pairs={{0,2},{2,0},{4,6},{6,4},{8,10},{10,8},{12,14},{14,12},{16,18},{18,... | collective-permute-start | bytes 55304 | tf_op jit(solution)/shard_map/ppermute | solution.py:476
  105.3 5.7 %collective-permute-start.23 = (f32[16,288]{1,0:T(8,128)S(1)}, f32[16,288]{1,0:T(8,128)S(1)}, u32[]{:S(2)}, u32[]{:S(2)}) collective-permute-start(f32[16,288]{1,0:T(8,128)S(1)} %add_add_fusion.1), channel_id=1, source_target_pairs={{0,24},{2,26},{4,28},{6,30},{8,16},{10,18},{12,20},{14,22},{16,8},... | collective-permute-start | bytes 55304 | tf_op jit(solution)/shard_map/ppermute | solution.py:476
  105.5 5.5 %collective-permute-start.22 = (f32[16,288]{1,0:T(8,128)S(1)}, f32[16,288]{1,0:T(8,128)S(1)}, u32[]{:S(2)}, u32[]{:S(2)}) collective-permute-start(f32[16,288]{1,0:T(8,128)S(1)} %add_add_fusion.1), channel_id=1, source_target_pairs={{0,16},{2,18},{4,20},{6,22},{8,24},{10,26},{12,28},{14,30},{16,0},... | collective-permute-start | bytes 55304 | tf_op jit(solution)/shard_map/ppermute | solution.py:476
  105.5 6.1 %collective-permute-start.21 = (f32[16,288]{1,0:T(8,128)S(1)}, f32[16,288]{1,0:T(8,128)S(1)}, u32[]{:S(2)}, u32[]{:S(2)}) collective-permute-start(f32[16,288]{1,0:T(8,128)S(1)} %add_add_fusion.1), channel_id=1, source_target_pairs={{0,8},{2,10},{4,12},{6,14},{8,0},{10,2},{12,4},{14,6},{16,24},{18,... | collective-permute-start | bytes 55304 | tf_op jit(solution)/shard_map/ppermute | solution.py:476

commit v10 on v8

--- a/solution.py
+++ b/solution.py
@@ -198,7 +198,7 @@
             pltpu.SemaphoreType.DMA((3,)),
         ],
         compiler_params=limit(16),
-        cost_estimate=pl.CostEstimate(flops=0, bytes_accessed=20 * MIB, transcendentals=0),
+        cost_estimate=pl.CostEstimate(flops=0, bytes_accessed=64 * MIB, transcendentals=0),
         name="tree_part",
     )(meta, pin(tree_q), pin(tree_key_value), parents)
 
@@ -523,11 +523,10 @@
     layers = blocks // 4
     place = (blk // 4).reshape(1)
     got = [partner(parts[k], "blk", blocks, k) for k in range(1, 4)]
-    sent = prompt()
+    got, sent = lax.optimization_barrier((got, prompt()))
+    parts = fold_part(parts[4], parts[0], got, place, layers)
+    parts, parents, sent = lax.optimization_barrier((parts, parents, sent))
     partials = spread(sent)
-    got, sent = lax.optimization_barrier((got, sent))
-    parts = fold_part(parts[4], parts[0], got, place, layers)
-    parts, parents = lax.optimization_barrier((parts, parents))
     more = [partner(parts[1 + k], "blk", blocks, 4 * k) for k in range(1, layers)]
     more, heads_out = lax.optimization_barrier((more, merge(partials, parents)))
     inner = parts[1] + sum(one.astype(jnp.float32) for one in more)

time: 111 us -> 105 us (0.946)
  waiting for transfers between devices: 32.9 us -> 26.2 us
    ppermute x24, waiting for transfers between devices: 32.9 us -> 21.7 us  [partner(): return lax.ppermute(value, axis, [(i, i ^ bits) for i in range(size)])]
    all_to_all x2, waiting for transfers between devices: 0.01 us -> 4.48 us  [spread(): return lax.all_to_all(value, 'blk', 0, 0, tiled=True)]
  transfers between devices with their start and end apart: 26 -> 26, of which waited for: 12 -> 11; matrix products, arithmetic and copies ran while one was open for 1% -> 1% of each run, Pallas kernels for 23% -> 31%
where the time goes in v10:
time: 105 us; the launch traced here: 104 us
  starting transfers between devices  36.8 us (35%)
  Pallas kernels  35.9 us (34%)
  waiting for transfers between devices  26.2 us (25%)
  between operations  2.89 us (3%)
  other arithmetic  1.32 us (1%)
    ppermute x24, starting transfers between devices, partner(): return lax.ppermute(value, axis, [(i, i ^ bits) for i in range(size)])  25.3 us
    ppermute x24, waiting for transfers between devices, partner(): return lax.ppermute(value, axis, [(i, i ^ bits) for i in range(size)])  21.7 us
    pallas_call x1, Pallas kernels, score_part(): pl.pallas_call(functools.partial(score_kernel, picks, streams), out_shape...  16.4 us
    all_to_all x2, starting transfers between devices, spread(): return lax.all_to_all(value, 'blk', 0, 0, tiled=True)  11.5 us
    pallas_call x1, Pallas kernels, prompt_part(): pl.pallas_call(prompt_kernel, out_shape=jax.ShapeDtypeStruct((blocks, tre...  6.9 us
    pallas_call x1, Pallas kernels, project_part(): pl.pallas_call(project_kernel, out_shape=jax.ShapeDtypeStruct((tokens, mo...  5.95 us
    all_to_all x2, waiting for transfers between devices, spread(): return lax.all_to_all(value, 'blk', 0, 0, tiled=True)  4.48 us
    pallas_call x1, Pallas kernels, draft_part(): pl.pallas_call(draft_kernel, out_shape=[jax.ShapeDtypeStruct((rows, half)...  3.09 us
  transfers between devices with their start and end apart: 26, of which 11 were waited for; matrix products, arithmetic and copies ran while one was open for 1% of the time, Pallas kernels for 31%

profile of v10, /device:TPU:0, one launch (start us, length us, event | category | flops | bytes accessed | tf_op | source)
XLA Modules:
  0.0 104.2 jit_solution(11416778404384696290)
XLA Ops:
  2.6 0.1 pad_add_fusion.meta
  2.7 0.1 stack.99.meta
  2.8 3.1 %draft_part.1 = (f32[144,896]{1,0:T(8,128)S(1)}, bf16[144,896]{1,0:T(8,128)(2,1)S(1)}, bf16[144,896]{1,0:T(8,128)(2,1)S(1)}, bf16[144,896]{1,0:T(8,128)(2,1)S(1)}, bf16[144,896]{1,0:T(8,128)(2,1)S(1)}) custom-call(s32[7]{0:T(128)S(1)} %stack.99.meta, bf16[144,3584]{1,0:T(8,128)(2,1)} %hidden_hbm.1, bf16[2,224,1792]{2,1,0:T(8,128)(2,1)} %weight_hbm.2), custom_call_target="tpu_custom_call" | custom-call | tf_op jit(solution)/shard_map/draft_part/pallas_call | solution.py:431
  5.9 3.0 %collective-permute-start = (bf16[144,896]{1,0:T(8,128)(2,1)S(1)}, bf16[144,896]{1,0:T(8,128)(2,1)S(1)}, u32[]{:S(2)}, u32[]{:S(2)}) collective-permute-start(bf16[144,896]{1,0:T(8,128)(2,1)S(1)} %get-tuple-element.50), channel_id=1, source_target_pairs={{0,2},{2,0},{4,6},{6,4},{8,10},{10,8},{12,14},{14,12},{16,18},{18,... | collective-permute-start | bytes 774152 | tf_op jit(solution)/shard_map/ppermute | solution.py:510
  8.9 1.5 %collective-permute-start.1 = (bf16[144,896]{1,0:T(8,128)(2,1)S(1)}, bf16[144,896]{1,0:T(8,128)(2,1)S(1)}, u32[]{:S(2)}, u32[]{:S(2)}) collective-permute-start(bf16[144,896]{1,0:T(8,128)(2,1)S(1)} %get-tuple-element.51), channel_id=1, source_target_pairs={{0,4},{2,6},{4,0},{6,2},{8,12},{10,14},{12,8},{14,10},{16,20},{18,... | collective-permute-start | bytes 774152 | tf_op jit(solution)/shard_map/ppermute | solution.py:510
  10.4 6.9 %prompt_part.1 = bf16[16,64,128]{2,1,0:T(8,128)(2,1)} custom-call(s32[3]{0:T(128)S(1)} %pad_add_fusion.meta, bf16[12,48,2048]{2,1,0:T(8,128)(2,1)} %q_hbm.3, bf16[2,1,2048,1024]{3,2,1,0:T(8,128)(2,1)} %kv_hbm.2), custom_call_target="tpu_custom_call" | custom-call | flops 805306368 | bytes 8388608 | tf_op jit(solution)/shard_map/prompt_part/pallas_call | solution.py:124
  17.3 4.7 %collective-permute-done.1.refs_1_ = bf16[144,896]{1,0:T(8,128)(2,1)S(1)} collective-permute-done((bf16[144,896]{1,0:T(8,128)(2,1)S(1)}, bf16[144,896]{1,0:T(8,128)(2,1)S(1)}, u32[]{:S(2)}, u32[]{:S(2)}) %collective-permute-start.1) | collective-permute-done | bytes 258080 | tf_op jit(solution)/shard_map/ppermute | solution.py:510
  22.1 0.3 fold_part.1
  22.4 5.9 %all-to-all-start = ((bf16[16,64,128]{2,1,0:T(8,128)(2,1)}), bf16[16,64,128]{2,1,0:T(8,128)(2,1)S(1)}, u32[]{:S(2)}, u32[]{:S(2)}) async-start(bf16[16,64,128]{2,1,0:T(8,128)(2,1)} %prompt_part.1), calls=%async_computation | async-start | bytes 524288 | tf_op jit(solution)/shard_map/all_to_all | solution.py:548
  28.4 1.9 %collective-permute-start.3 = (bf16[36,896]{1,0:T(8,128)(2,1)S(1)}, bf16[36,896]{1,0:T(8,128)(2,1)S(1)}, u32[]{:S(2)}, u32[]{:S(2)}) collective-permute-start(bf16[36,896]{1,0:T(8,128)(2,1)S(1)} %get-tuple-element.65), channel_id=1, source_target_pairs={{0,8},{2,10},{4,12},{6,14},{8,0},{10,2},{12,4},{14,6},{16,24},{18,... | collective-permute-start | bytes 193544 | tf_op jit(solution)/shard_map/ppermute | solution.py:510
  30.2 2.4 %collective-permute-start.4 = (bf16[36,896]{1,0:T(8,128)(2,1)S(1)}, bf16[36,896]{1,0:T(8,128)(2,1)S(1)}, u32[]{:S(2)}, u32[]{:S(2)}) collective-permute-start(bf16[36,896]{1,0:T(8,128)(2,1)S(1)} %get-tuple-element.66), channel_id=1, source_target_pairs={{0,16},{2,18},{4,20},{6,22},{8,24},{10,26},{12,28},{14,30},{16,0},... | collective-permute-start | bytes 193544 | tf_op jit(solution)/shard_map/ppermute | solution.py:510
  32.6 0.2 collective-permute-start.5
  32.8 0.1 pad_add_fusion.1.meta
  32.9 2.2 %tree_part.1 = (f32[12,48,128]{2,1,0:T(8,128)S(1)}, f32[12,48,128]{2,1,0:T(8,128)S(1)}) custom-call(s32[3]{0:T(128)S(1)} %pad_add_fusion.1.meta, bf16[12,48,2048]{2,1,0:T(8,128)(2,1)} %q_hbm.3, bf16[2,12,48,1024]{3,2,1,0:T(8,128)(2,1)} %kv_hbm.3, s32[12,48]{1,0:T(8,128)S(1)} %copy-done), custom_call_target="tpu_custom_call" | custom-call | bytes 67108864 | tf_op jit(solution)/shard_map/tree_part/pallas_call | solution.py:191
  35.1 4.5 %all-to-all-done.got_ref = bf16[16,64,128]{2,1,0:T(8,128)(2,1)S(1)} async-done(((bf16[16,64,128]{2,1,0:T(8,128)(2,1)}), bf16[16,64,128]{2,1,0:T(8,128)(2,1)S(1)}, u32[]{:S(2)}, u32[]{:S(2)}) %all-to-all-start) | async-done | bytes 262176 | tf_op jit(solution)/shard_map/all_to_all | solution.py:548
  39.6 1.1 %merge_part.1 = bf16[16,36,128]{2,1,0:T(8,128)(2,1)} custom-call(bf16[16,64,128]{2,1,0:T(8,128)(2,1)S(1)} %all-to-all-done.got_ref, f32[12,48,128]{2,1,0:T(8,128)S(1)} %get-tuple-element.70.numer_ref, f32[12,48,128]{2,1,0:T(8,128)S(1)} %get-tuple-element.71.denom_ref), custom_call_target="tpu_custom_call" | custom-call | tf_op jit(solution)/shard_map/merge_part/pallas_call | solution.py:237
  40.7 0.7 collective-permute-done.4
  41.3 0.1 add_convert_fusion.1.refs_0_
  41.4 2.6 %collective-permute-start.8 = (bf16[36,896]{1,0:T(8,128)(2,1)S(1)}, bf16[36,896]{1,0:T(8,128)(2,1)S(1)}, u32[]{:S(2)}, u32[]{:S(2)}) collective-permute-start(bf16[36,896]{1,0:T(8,128)(2,1)S(1)} %add_convert_fusion.1.refs_0_), channel_id=1, source_target_pairs={{0,24},{2,26},{4,28},{6,30},{8,16},{10,18},{12,20},{14,22},{16,8},... | collective-permute-start | bytes 193544 | tf_op jit(solution)/shard_map/ppermute | solution.py:510
  44.0 0.3 collective-permute-start.7
  44.3 1.6 %collective-permute-start.6 = (bf16[36,896]{1,0:T(8,128)(2,1)S(1)}, bf16[36,896]{1,0:T(8,128)(2,1)S(1)}, u32[]{:S(2)}, u32[]{:S(2)}) collective-permute-start(bf16[36,896]{1,0:T(8,128)(2,1)S(1)} %add_convert_fusion.1.refs_0_), channel_id=1, source_target_pairs={{0,8},{2,10},{4,12},{6,14},{8,0},{10,2},{12,4},{14,6},{16,24},{18,... | collective-permute-start | bytes 193544 | tf_op jit(solution)/shard_map/ppermute | solution.py:510
  45.9 1.7 %collective-permute-done.8.refs_3_ = bf16[36,896]{1,0:T(8,128)(2,1)S(1)} collective-permute-done((bf16[36,896]{1,0:T(8,128)(2,1)S(1)}, bf16[36,896]{1,0:T(8,128)(2,1)S(1)}, u32[]{:S(2)}, u32[]{:S(2)}) %collective-permute-start.8) | collective-permute-done | bytes 64544 | tf_op jit(solution)/shard_map/ppermute | solution.py:510
  47.6 1.7 %collective-permute-done.7.refs_2_ = bf16[36,896]{1,0:T(8,128)(2,1)S(1)} collective-permute-done((bf16[36,896]{1,0:T(8,128)(2,1)S(1)}, bf16[36,896]{1,0:T(8,128)(2,1)S(1)}, u32[]{:S(2)}, u32[]{:S(2)}) %collective-permute-start.7) | collective-permute-done | bytes 64544 | tf_op jit(solution)/shard_map/ppermute | solution.py:510
  49.3 0.0 collective-permute-done.6.refs_1_
  49.4 0.1 stack_part.1.refs_0_
  49.4 2.4 %collective-permute-start.11 = (bf16[144,896]{1,0:T(8,128)(2,1)S(1)}, bf16[144,896]{1,0:T(8,128)(2,1)S(1)}, u32[]{:S(2)}, u32[]{:S(2)}) collective-permute-start(bf16[144,896]{1,0:T(8,128)(2,1)S(1)} %stack_part.1.refs_0_), channel_id=1, source_target_pairs={{0,6},{2,4},{4,2},{6,0},{8,14},{10,12},{12,10},{14,8},{16,22},{18,... | collective-permute-start | bytes 774152 | tf_op jit(solution)/shard_map/ppermute | solution.py:510
  51.8 0.6 collective-permute-start.10
  52.4 0.6 collective-permute-start.9
  53.0 4.5 %collective-permute-done.11.refs_3_ = bf16[144,896]{1,0:T(8,128)(2,1)S(1)} collective-permute-done((bf16[144,896]{1,0:T(8,128)(2,1)S(1)}, bf16[144,896]{1,0:T(8,128)(2,1)S(1)}, u32[]{:S(2)}, u32[]{:S(2)}) %collective-permute-start.11) | collective-permute-done | bytes 258080 | tf_op jit(solution)/shard_map/ppermute | solution.py:510
  57.5 2.7 %collective-permute-done.10.refs_2_ = bf16[144,896]{1,0:T(8,128)(2,1)S(1)} collective-permute-done((bf16[144,896]{1,0:T(8,128)(2,1)S(1)}, bf16[144,896]{1,0:T(8,128)(2,1)S(1)}, u32[]{:S(2)}, u32[]{:S(2)}) %collective-permute-start.10) | collective-permute-done | bytes 258080 | tf_op jit(solution)/shard_map/ppermute | solution.py:510
  60.2 0.6 collective-permute-done.9.refs_1_
  60.8 0.1 copy.16
  61.0 0.1 stack.91.places
  61.1 5.6 %all-to-all-start.1 = ((bf16[16,36,128]{2,1,0:T(8,128)(2,1)}), bf16[16,36,128]{2,1,0:T(8,128)(2,1)S(1)}, u32[]{:S(2)}, u32[]{:S(2)}) async-start(bf16[16,36,128]{2,1,0:T(8,128)(2,1)} %merge_part.1), calls=%async_computation.1 | async-start | bytes 327680 | tf_op jit(solution)/shard_map/all_to_all | solution.py:548
  66.7 16.4 %score_part.1 = f32[16,288]{1,0:T(8,128)S(1)} custom-call(s32[16]{0:T(128)S(1)} %stack.91.places, s32[288,128]{1,0:T(8,128)S(1)} %pad.4.ids_ref, bf16[144,896]{1,0:T(8,128)(2,1)S(1)} %stack_part.1.refs_0_, bf16[144,896]{1,0:T(8,128)(2,1)S(1)} %collective-permute-done.9.refs_1_, bf16[144,896]{1,0:T(8,128)(2,1)S(1)} %collective-permute-done.10.refs_2_, ...), custom_call_target="tpu_custom_call" | custom-call | flops 8455716864 | bytes 29360128 | tf_op jit(solution)/shard_map/score_part/pallas_call | solution.py:360
  83.1 0.3 collective-permute-start.16
  83.4 1.0 collective-permute-done.16
  84.4 2.9 %collective-permute-start.19 = (f32[16,288]{1,0:T(8,128)S(1)}, f32[16,288]{1,0:T(8,128)S(1)}, u32[]{:S(2)}, u32[]{:S(2)}) collective-permute-start(f32[16,288]{1,0:T(8,128)S(1)} %add.111), channel_id=1, source_target_pairs={{0,6},{2,4},{4,2},{6,0},{8,14},{10,12},{12,10},{14,8},{16,22},{18,... | collective-permute-start | bytes 55304 | tf_op jit(solution)/shard_map/ppermute | solution.py:510
  87.2 0.6 collective-permute-start.18
  87.8 0.1 collective-permute-start.17
  87.9 5.9 %project_part.1 = f32[36,3584]{1,0:T(8,128)S(1)} custom-call(bf16[16,36,128]{2,1,0:T(8,128)(2,1)S(1)} %all-to-all-done.1.heads_ref, bf16[2048,3584]{1,0:T(8,128)(2,1)} %weight_hbm.3), custom_call_target="tpu_custom_call" | custom-call | flops 528482304 | bytes 14680064 | tf_op jit(solution)/shard_map/project_part/pallas_call | solution.py:278
  93.9 3.8 %collective-permute-start.22 = (f32[16,288]{1,0:T(8,128)S(1)}, f32[16,288]{1,0:T(8,128)S(1)}, u32[]{:S(2)}, u32[]{:S(2)}) collective-permute-start(f32[16,288]{1,0:T(8,128)S(1)} %add_add_fusion.1), channel_id=1, source_target_pairs={{0,24},{2,26},{4,28},{6,30},{8,16},{10,18},{12,20},{14,22},{16,8},... | collective-permute-start | bytes 55304 | tf_op jit(solution)/shard_map/ppermute | solution.py:510
  97.7 0.7 collective-permute-start.20
  98.4 1.5 %collective-permute-done.22 = f32[16,288]{1,0:T(8,128)S(1)} collective-permute-done((f32[16,288]{1,0:T(8,128)S(1)}, f32[16,288]{1,0:T(8,128)S(1)}, u32[]{:S(2)}, u32[]{:S(2)}) %collective-permute-start.22) | collective-permute-done | bytes 18464 | tf_op jit(solution)/shard_map/ppermute | solution.py:510
  99.9 2.6 %collective-permute-done.21 = f32[16,288]{1,0:T(8,128)S(1)} collective-permute-done((f32[16,288]{1,0:T(8,128)S(1)}, f32[16,288]{1,0:T(8,128)S(1)}, u32[]{:S(2)}, u32[]{:S(2)}) %collective-permute-start.21) | collective-permute-done | bytes 18464 | tf_op jit(solution)/shard_map/ppermute | solution.py:510
  102.5 0.7 reshape.23
  103.2 0.2 multiply_reduce_fusion
  103.4 0.9 add_convert_fusion
  (37 shorter events, 0.2 us)
Async XLA Ops:
  0.6 32.3 %copy-start = (s32[12,48]{1,0:T(8,128)S(1)}, s32[12,48]{1,0:T(8,128)}, u32[]{:S(2)}) copy-start(s32[12,48]{1,0:T(8,128)} %parents_ref) | copy-start | bytes 6916
  5.9 11.5 %collective-permute-start = (bf16[144,896]{1,0:T(8,128)(2,1)S(1)}, bf16[144,896]{1,0:T(8,128)(2,1)S(1)}, u32[]{:S(2)}, u32[]{:S(2)}) collective-permute-start(bf16[144,896]{1,0:T(8,128)(2,1)S(1)} %get-tuple-element.50), channel_id=1, source_target_pairs={{0,2},{2,0},{4,6},{6,4},{8,10},{10,8},{12,14},{14,12},{16,18},{18,... | collective-permute-start | bytes 774152 | tf_op jit(solution)/shard_map/ppermute | solution.py:510
  8.9 13.2 %collective-permute-start.1 = (bf16[144,896]{1,0:T(8,128)(2,1)S(1)}, bf16[144,896]{1,0:T(8,128)(2,1)S(1)}, u32[]{:S(2)}, u32[]{:S(2)}) collective-permute-start(bf16[144,896]{1,0:T(8,128)(2,1)S(1)} %get-tuple-element.51), channel_id=1, source_target_pairs={{0,4},{2,6},{4,0},{6,2},{8,12},{10,14},{12,8},{14,10},{16,20},{18,... | collective-permute-start | bytes 774152 | tf_op jit(solution)/shard_map/ppermute | solution.py:510
  10.4 11.7 %collective-permute-start.2 = (bf16[144,896]{1,0:T(8,128)(2,1)S(1)}, bf16[144,896]{1,0:T(8,128)(2,1)S(1)}, u32[]{:S(2)}, u32[]{:S(2)}) collective-permute-start(bf16[144,896]{1,0:T(8,128)(2,1)S(1)} %get-tuple-element.52), channel_id=1, source_target_pairs={{0,6},{2,4},{4,2},{6,0},{8,14},{10,12},{12,10},{14,8},{16,22},{18,... | collective-permute-start | bytes 774152 | tf_op jit(solution)/shard_map/ppermute | solution.py:510
  10.4 50.4 %copy-start.2 = (s32[2,144,10]{1,0,2:T(2,128)S(1)}, s32[2,144,10]{1,0,2:T(2,128)}, u32[]{:S(2)}) copy-start(s32[2,144,10]{1,0,2:T(2,128)} %param.17) | copy-start | bytes 34564
  22.4 17.2 %all-to-all-start = ((bf16[16,64,128]{2,1,0:T(8,128)(2,1)}), bf16[16,64,128]{2,1,0:T(8,128)(2,1)S(1)}, u32[]{:S(2)}, u32[]{:S(2)}) async-start(bf16[16,64,128]{2,1,0:T(8,128)(2,1)} %prompt_part.1), calls=%async_computation | async-start | bytes 524288 | tf_op jit(solution)/shard_map/all_to_all | solution.py:548
  28.4 12.3 %collective-permute-start.3 = (bf16[36,896]{1,0:T(8,128)(2,1)S(1)}, bf16[36,896]{1,0:T(8,128)(2,1)S(1)}, u32[]{:S(2)}, u32[]{:S(2)}) collective-permute-start(bf16[36,896]{1,0:T(8,128)(2,1)S(1)} %get-tuple-element.65), channel_id=1, source_target_pairs={{0,8},{2,10},{4,12},{6,14},{8,0},{10,2},{12,4},{14,6},{16,24},{18,... | collective-permute-start | bytes 193544 | tf_op jit(solution)/shard_map/ppermute | solution.py:510
  30.2 11.1 %collective-permute-start.4 = (bf16[36,896]{1,0:T(8,128)(2,1)S(1)}, bf16[36,896]{1,0:T(8,128)(2,1)S(1)}, u32[]{:S(2)}, u32[]{:S(2)}) collective-permute-start(bf16[36,896]{1,0:T(8,128)(2,1)S(1)} %get-tuple-element.66), channel_id=1, source_target_pairs={{0,16},{2,18},{4,20},{6,22},{8,24},{10,26},{12,28},{14,30},{16,0},... | collective-permute-start | bytes 193544 | tf_op jit(solution)/shard_map/ppermute | solution.py:510
  32.6 8.7 %collective-permute-start.5 = (bf16[36,896]{1,0:T(8,128)(2,1)S(1)}, bf16[36,896]{1,0:T(8,128)(2,1)S(1)}, u32[]{:S(2)}, u32[]{:S(2)}) collective-permute-start(bf16[36,896]{1,0:T(8,128)(2,1)S(1)} %get-tuple-element.67), channel_id=1, source_target_pairs={{0,24},{2,26},{4,28},{6,30},{8,16},{10,18},{12,20},{14,22},{16,8},... | collective-permute-start | bytes 193544 | tf_op jit(solution)/shard_map/ppermute | solution.py:510
  41.4 6.2 %collective-permute-start.8 = (bf16[36,896]{1,0:T(8,128)(2,1)S(1)}, bf16[36,896]{1,0:T(8,128)(2,1)S(1)}, u32[]{:S(2)}, u32[]{:S(2)}) collective-permute-start(bf16[36,896]{1,0:T(8,128)(2,1)S(1)} %add_convert_fusion.1.refs_0_), channel_id=1, source_target_pairs={{0,24},{2,26},{4,28},{6,30},{8,16},{10,18},{12,20},{14,22},{16,8},... | collective-permute-start | bytes 193544 | tf_op jit(solution)/shard_map/ppermute | solution.py:510
  44.0 5.3 %collective-permute-start.7 = (bf16[36,896]{1,0:T(8,128)(2,1)S(1)}, bf16[36,896]{1,0:T(8,128)(2,1)S(1)}, u32[]{:S(2)}, u32[]{:S(2)}) collective-permute-start(bf16[36,896]{1,0:T(8,128)(2,1)S(1)} %add_convert_fusion.1.refs_0_), channel_id=1, source_target_pairs={{0,16},{2,18},{4,20},{6,22},{8,24},{10,26},{12,28},{14,30},{16,0},... | collective-permute-start | bytes 193544 | tf_op jit(solution)/shard_map/ppermute | solution.py:510
  44.3 5.1 %collective-permute-start.6 = (bf16[36,896]{1,0:T(8,128)(2,1)S(1)}, bf16[36,896]{1,0:T(8,128)(2,1)S(1)}, u32[]{:S(2)}, u32[]{:S(2)}) collective-permute-start(bf16[36,896]{1,0:T(8,128)(2,1)S(1)} %add_convert_fusion.1.refs_0_), channel_id=1, source_target_pairs={{0,8},{2,10},{4,12},{6,14},{8,0},{10,2},{12,4},{14,6},{16,24},{18,... | collective-permute-start | bytes 193544 | tf_op jit(solution)/shard_map/ppermute | solution.py:510
  49.4 8.0 %collective-permute-start.11 = (bf16[144,896]{1,0:T(8,128)(2,1)S(1)}, bf16[144,896]{1,0:T(8,128)(2,1)S(1)}, u32[]{:S(2)}, u32[]{:S(2)}) collective-permute-start(bf16[144,896]{1,0:T(8,128)(2,1)S(1)} %stack_part.1.refs_0_), channel_id=1, source_target_pairs={{0,6},{2,4},{4,2},{6,0},{8,14},{10,12},{12,10},{14,8},{16,22},{18,... | collective-permute-start | bytes 774152 | tf_op jit(solution)/shard_map/ppermute | solution.py:510
  51.8 8.3 %collective-permute-start.10 = (bf16[144,896]{1,0:T(8,128)(2,1)S(1)}, bf16[144,896]{1,0:T(8,128)(2,1)S(1)}, u32[]{:S(2)}, u32[]{:S(2)}) collective-permute-start(bf16[144,896]{1,0:T(8,128)(2,1)S(1)} %stack_part.1.refs_0_), channel_id=1, source_target_pairs={{0,4},{2,6},{4,0},{6,2},{8,12},{10,14},{12,8},{14,10},{16,20},{18,... | collective-permute-start | bytes 774152 | tf_op jit(solution)/shard_map/ppermute | solution.py:510
  52.4 8.4 %collective-permute-start.9 = (bf16[144,896]{1,0:T(8,128)(2,1)S(1)}, bf16[144,896]{1,0:T(8,128)(2,1)S(1)}, u32[]{:S(2)}, u32[]{:S(2)}) collective-permute-start(bf16[144,896]{1,0:T(8,128)(2,1)S(1)} %stack_part.1.refs_0_), channel_id=1, source_target_pairs={{0,2},{2,0},{4,6},{6,4},{8,10},{10,8},{12,14},{14,12},{16,18},{18,... | collective-permute-start | bytes 774152 | tf_op jit(solution)/shard_map/ppermute | solution.py:510
  53.0 13.7 %collective-permute-start.12 = (bf16[144,896]{1,0:T(8,128)(2,1)S(1)}, bf16[144,896]{1,0:T(8,128)(2,1)S(1)}, u32[]{:S(2)}, u32[]{:S(2)}) collective-permute-start(bf16[144,896]{1,0:T(8,128)(2,1)S(1)} %stack_part.1.refs_0_), channel_id=1, source_target_pairs={{0,1},{1,0},{2,3},{3,2},{4,5},{5,4},{6,7},{7,6},{8,9},{9,8},{10,11... | collective-permute-start | bytes 774152 | tf_op jit(solution)/shard_map/ppermute | solution.py:510
  57.5 9.2 %collective-permute-start.15 = (bf16[144,896]{1,0:T(8,128)(2,1)S(1)}, bf16[144,896]{1,0:T(8,128)(2,1)S(1)}, u32[]{:S(2)}, u32[]{:S(2)}) collective-permute-start(bf16[144,896]{1,0:T(8,128)(2,1)S(1)} %collective-permute-done.11.refs_3_), channel_id=1, source_target_pairs={{0,1},{1,0},{2,3},{3,2},{4,5},{5,4},{6,7},{7,6},{8,9},{9,8},{10,11... | collective-permute-start | bytes 774152 | tf_op jit(solution)/shard_map/ppermute | solution.py:510
  60.2 6.5 %collective-permute-start.14 = (bf16[144,896]{1,0:T(8,128)(2,1)S(1)}, bf16[144,896]{1,0:T(8,128)(2,1)S(1)}, u32[]{:S(2)}, u32[]{:S(2)}) collective-permute-start(bf16[144,896]{1,0:T(8,128)(2,1)S(1)} %collective-permute-done.10.refs_2_), channel_id=1, source_target_pairs={{0,1},{1,0},{2,3},{3,2},{4,5},{5,4},{6,7},{7,6},{8,9},{9,8},{10,11... | collective-permute-start | bytes 774152 | tf_op jit(solution)/shard_map/ppermute | solution.py:510
  60.8 5.9 %collective-permute-start.13 = (bf16[144,896]{1,0:T(8,128)(2,1)S(1)}, bf16[144,896]{1,0:T(8,128)(2,1)S(1)}, u32[]{:S(2)}, u32[]{:S(2)}) collective-permute-start(bf16[144,896]{1,0:T(8,128)(2,1)S(1)} %collective-permute-done.9.refs_1_), channel_id=1, source_target_pairs={{0,1},{1,0},{2,3},{3,2},{4,5},{5,4},{6,7},{7,6},{8,9},{9,8},{10,11... | collective-permute-start | bytes 774152 | tf_op jit(solution)/shard_map/ppermute | solution.py:510
  61.1 23.3 %all-to-all-start.1 = ((bf16[16,36,128]{2,1,0:T(8,128)(2,1)}), bf16[16,36,128]{2,1,0:T(8,128)(2,1)S(1)}, u32[]{:S(2)}, u32[]{:S(2)}) async-start(bf16[16,36,128]{2,1,0:T(8,128)(2,1)} %merge_part.1), calls=%async_computation.1 | async-start | bytes 327680 | tf_op jit(solution)/shard_map/all_to_all | solution.py:548
  83.1 1.3 %collective-permute-start.16 = (f32[16,288]{1,0:T(8,128)S(1)}, f32[16,288]{1,0:T(8,128)S(1)}, u32[]{:S(2)}, u32[]{:S(2)}) collective-permute-start(f32[16,288]{1,0:T(8,128)S(1)} %score_part.1), channel_id=1, source_target_pairs={{0,1},{1,0},{2,3},{3,2},{4,5},{5,4},{6,7},{7,6},{8,9},{9,8},{10,11... | collective-permute-start | bytes 55304 | tf_op jit(solution)/shard_map/ppermute | solution.py:510
  84.3 19.0 %copy-start.1 = (bf16[36,3584]{1,0:T(8,128)(2,1)S(1)}, bf16[36,3584]{1,0:T(8,128)(2,1)}, u32[]{:S(2)}) copy-start(bf16[36,3584]{1,0:T(8,128)(2,1)} %param.27) | copy-start | bytes 774148
  84.3 19.0 %copy-start.3 = (f32[3584]{0:T(1024)S(1)}, f32[3584]{0:T(1024)}, u32[]{:S(2)}) copy-start(f32[3584]{0:T(1024)} %param.26) | copy-start | bytes 43012
  84.4 9.5 %collective-permute-start.19 = (f32[16,288]{1,0:T(8,128)S(1)}, f32[16,288]{1,0:T(8,128)S(1)}, u32[]{:S(2)}, u32[]{:S(2)}) collective-permute-start(f32[16,288]{1,0:T(8,128)S(1)} %add.111), channel_id=1, source_target_pairs={{0,6},{2,4},{4,2},{6,0},{8,14},{10,12},{12,10},{14,8},{16,22},{18,... | collective-permute-start | bytes 55304 | tf_op jit(solution)/shard_map/ppermute | solution.py:510
  87.2 6.6 %collective-permute-start.18 = (f32[16,288]{1,0:T(8,128)S(1)}, f32[16,288]{1,0:T(8,128)S(1)}, u32[]{:S(2)}, u32[]{:S(2)}) collective-permute-start(f32[16,288]{1,0:T(8,128)S(1)} %add.111), channel_id=1, source_target_pairs={{0,4},{2,6},{4,0},{6,2},{8,12},{10,14},{12,8},{14,10},{16,20},{18,... | collective-permute-start | bytes 55304 | tf_op jit(solution)/shard_map/ppermute | solution.py:510
  87.8 6.1 %collective-permute-start.17 = (f32[16,288]{1,0:T(8,128)S(1)}, f32[16,288]{1,0:T(8,128)S(1)}, u32[]{:S(2)}, u32[]{:S(2)}) collective-permute-start(f32[16,288]{1,0:T(8,128)S(1)} %add.111), channel_id=1, source_target_pairs={{0,2},{2,0},{4,6},{6,4},{8,10},{10,8},{12,14},{14,12},{16,18},{18,... | collective-permute-start | bytes 55304 | tf_op jit(solution)/shard_map/ppermute | solution.py:510
  93.9 5.9 %collective-permute-start.22 = (f32[16,288]{1,0:T(8,128)S(1)}, f32[16,288]{1,0:T(8,128)S(1)}, u32[]{:S(2)}, u32[]{:S(2)}) collective-permute-start(f32[16,288]{1,0:T(8,128)S(1)} %add_add_fusion.1), channel_id=1, source_target_pairs={{0,24},{2,26},{4,28},{6,30},{8,16},{10,18},{12,20},{14,22},{16,8},... | collective-permute-start | bytes 55304 | tf_op jit(solution)/shard_map/ppermute | solution.py:510
  97.7 4.7 %collective-permute-start.21 = (f32[16,288]{1,0:T(8,128)S(1)}, f32[16,288]{1,0:T(8,128)S(1)}, u32[]{:S(2)}, u32[]{:S(2)}) collective-permute-start(f32[16,288]{1,0:T(8,128)S(1)} %add_add_fusion.1), channel_id=1, source_target_pairs={{0,16},{2,18},{4,20},{6,22},{8,24},{10,26},{12,28},{14,30},{16,0},... | collective-permute-start | bytes 55304 | tf_op jit(solution)/shard_map/ppermute | solution.py:510
  97.7 4.7 %collective-permute-start.20 = (f32[16,288]{1,0:T(8,128)S(1)}, f32[16,288]{1,0:T(8,128)S(1)}, u32[]{:S(2)}, u32[]{:S(2)}) collective-permute-start(f32[16,288]{1,0:T(8,128)S(1)} %add_add_fusion.1), channel_id=1, source_target_pairs={{0,8},{2,10},{4,12},{6,14},{8,0},{10,2},{12,4},{14,6},{16,24},{18,... | collective-permute-start | bytes 55304 | tf_op jit(solution)/shard_map/ppermute | solution.py:510
  98.4 4.8 %collective-permute-start.23 = (f32[36,3584]{1,0:T(8,128)S(1)}, f32[36,3584]{1,0:T(8,128)S(1)}, u32[]{:S(2)}, u32[]{:S(2)}) collective-permute-start(f32[36,3584]{1,0:T(8,128)S(1)} %project_part.1), channel_id=1, source_target_pairs={{0,1},{1,0},{2,3},{3,2},{4,5},{5,4},{6,7},{7,6},{8,9},{9,8},{10,11... | collective-permute-start | bytes 1548296 | tf_op jit(solution)/shard_map/ppermute | solution.py:510
